TPU v7x, 32 devices: a whole 2x2x4 slice. The times are simulated.
32 devices in a mesh: seq: 8 (over z, y), fsdp: 4 (over x, core).
Axes of the slice: x: 2, y: 2, z: 4, core: 2. Of those that a mesh axis runs over, the one named last changes fastest.
Arguments:
- inputs: bfloat16 [4, 1024, 2560], P('fsdp', 'seq'), may hold values from -6 to 6
- block_flags: int32 [4, 16], P('fsdp', 'seq'), may hold values from 0 to 1, as said below
- decay_seed: int32 [2560], replicated, may hold values from 0 to 7
- vectors: float32 [10, 2560], replicated, may hold values from -3 to 3, as said below
- in_y: bfloat16 [2560, 2560], P(None, 'fsdp'), may hold values from -0.125 to 0.125
- in_x: bfloat16 [2560, 2560], P(None, 'fsdp'), may hold values from -0.125 to 0.125
- gate_weight: bfloat16 [2560, 512], P(None, 'fsdp'), may hold values from -0.375 to 0.375
- out_proj: bfloat16 [2560, 2560], P(None, 'fsdp'), may hold values from -0.5 to 0.5
- mlp_gate: bfloat16 [2560, 7680], P(None, 'fsdp'), may hold values from -0.125 to 0.125
- mlp_up: bfloat16 [2560, 7680], P(None, 'fsdp'), may hold values from -0.125 to 0.125
- mlp_down: bfloat16 [2560, 7680], P(None, 'fsdp'), may hold values from -0.125 to 0.125
- cotangent: bfloat16 [4, 1024, 2560], P('fsdp', 'seq'), may hold values from -6 to 6
Outputs:
- output: bfloat16 [4, 1024, 2560], P('fsdp', 'seq')
- input_grad: bfloat16 [4, 1024, 2560], P('fsdp', 'seq')
- vectors_grad: float32 [10, 2560], replicated
- in_y_grad: float32 [2560, 2560], P(('seq', 'fsdp'))
- in_x_grad: float32 [2560, 2560], P(('seq', 'fsdp'))
- gate_grad: float32 [2560, 512], P(('seq', 'fsdp'))
- out_proj_grad: float32 [2560, 2560], P(('seq', 'fsdp'))
- mlp_gate_grad: float32 [2560, 7680], P('seq', 'fsdp')
- mlp_up_grad: float32 [2560, 7680], P('seq', 'fsdp')
- mlp_down_grad: float32 [2560, 7680], P('seq', 'fsdp')
Inputs may be any that keep to these rules, and one draw needn't show every extreme that they name: `block_flags`: in each group block 0 is flagged, one more flag may lie among the first 2 blocks and one more among the last 1 block; no other block is flagged. `vectors`: rows 0 and 1 lie in 0.6 to 1.4.
All inputs are finite; a program needn't handle non-finite values.
Results may differ from a plain program's by a relative error of at most 0.015.
Values may be sent and summed in bfloat16 or wider, within the bound.
No kernel may reach another device: no remote copies, remote signals or barrier semaphores. Data moves between devices by JAX's collectives and lax.ppermute only.
A program may use at most 640 MiB of HBM per device.

v0:
```python
import jax
import jax.numpy as jnp
from jax import lax
from jax.sharding import PartitionSpec as P

HEADS = 10
BLK = 256
FBLK = 64


epsilon = 1e-06


def shifted(value, axis, by):
    count = lax.axis_size(axis)
    pairs = [(i, i + by) for i in range(count) if 0 <= i + by < count]
    return lax.ppermute(value, axis, pairs)


def entering(value, axis, join, neutral, backward):
    count, mine = (lax.axis_size(axis), lax.axis_index(axis))
    pieces = jax.tree.map(lambda part: lax.all_gather(part, axis), value)
    if backward:
        pieces = jax.tree.map(lambda part: part[::-1], pieces)
        mine = count - 1 - mine
    running = jax.tree.map(
        lambda part, zero: jnp.full_like(part, 0) + jnp.asarray(zero, part.dtype), value, neutral
    )

    def turn(position, running):
        longer = join(running, jax.tree.map(lambda part: part[position], pieces))
        return jax.tree.map(lambda new, old: jnp.where(position < mine, new, old), longer, running)

    return lax.fori_loop(0, count - 1, turn, running)


def chain_link(earlier, later):
    return (earlier[0] * later[0], later[0] * earlier[1] + later[1])


def gelu_tanh(values):
    return jax.nn.gelu(values, approximate=True)


def norm_scale(values):
    inverse = lax.rsqrt(jnp.mean(values * values, axis=-1, keepdims=True) + epsilon)
    return (values * inverse, inverse)


def norm_back(grad_normed, scaled, inverse, gain_row):
    grad_gain = jnp.sum(grad_normed * scaled, axis=0)
    inner_term = grad_normed * gain_row
    grad_input = inverse * (
        inner_term - scaled * jnp.mean(inner_term * scaled, axis=-1, keepdims=True)
    )
    return (grad_input, grad_gain)


def dot_rows(left, right):
    return lax.dot_general(
        left, right, (((0,), (0,)), ((), ())), preferred_element_type=jnp.float32
    )


def dot_cols(left, right):
    return lax.dot_general(
        left, right, (((1,), (1,)), ((), ())), preferred_element_type=jnp.float32
    )


def local(
    inputs,
    block_flags,
    decay_seed,
    vectors,
    in_y,
    in_x,
    gate_weight,
    out_proj,
    mlp_gate,
    mlp_up,
    mlp_down,
    cotangent,
):
    tokens = inputs.shape[1]
    width = inputs.shape[2]
    ff_each = mlp_gate.shape[1]
    fsdp_count = lax.axis_size("fsdp")
    seq_count = lax.axis_size("seq")
    residual_in = inputs[0].astype(jnp.float32)
    scaled_one, inverse_one = norm_scale(residual_in)
    normed_one = (scaled_one * vectors[0]).astype(jnp.bfloat16)
    weight_y, weight_x, weight_gate, weight_out = (
        lax.all_gather(in_y, "fsdp", axis=1, tiled=True),
        lax.all_gather(in_x, "fsdp", axis=1, tiled=True),
        lax.all_gather(gate_weight, "fsdp", axis=1, tiled=True),
        lax.all_gather(out_proj, "fsdp", axis=1, tiled=True),
    )
    y_pre = jnp.dot(normed_one, weight_y, preferred_element_type=jnp.float32)
    x_low = jnp.dot(normed_one, weight_x, preferred_element_type=jnp.float32).astype(jnp.bfloat16)
    edge_rows = shifted(x_low[tokens - 3 :], "seq", 1)
    extended = jnp.concatenate([edge_rows, x_low], axis=0).astype(jnp.float32)
    token_flag = jnp.repeat(block_flags[0], FBLK)
    offset = jnp.arange(tokens) % FBLK
    start_mask = ((token_flag == 1) & (offset == 0)).astype(jnp.float32)[:, None]
    keep_mask = 1.0 - start_mask
    valid_masks = [
        1.0 - ((token_flag == 1) & (offset < lag)).astype(jnp.float32)[:, None] for lag in range(4)
    ]
    conv_out = vectors[6] + jnp.zeros((tokens, width), jnp.float32)
    for lag in range(4):
        conv_out = (
            conv_out + vectors[2 + lag] * extended[3 - lag : 3 - lag + tokens] * valid_masks[lag]
        )
    conv_low = conv_out.astype(jnp.bfloat16)
    conv_heads = conv_low.reshape(tokens, HEADS, BLK)
    gate_blocks = weight_gate.reshape(HEADS, BLK, 2 * BLK)
    gate_prod = jnp.einsum(
        "thi,hij->thj", conv_heads, gate_blocks, preferred_element_type=jnp.float32
    )
    input_gate = jax.nn.sigmoid(gate_prod[:, :, :BLK].reshape(tokens, width) + vectors[7])
    decay_gate = jax.nn.sigmoid(gate_prod[:, :, BLK:].reshape(tokens, width) + vectors[8])
    base_rate = -5.0 - decay_seed.astype(jnp.float32) + vectors[9]
    rate = jax.nn.softplus(base_rate)
    log_decay = -8.0 * decay_gate * rate
    decay = jnp.exp(log_decay) * keep_mask
    scale_in = jnp.sqrt(keep_mask * -jnp.expm1(2.0 * log_decay) + start_mask)
    conv_float = conv_low.astype(jnp.float32)
    drive = scale_in * input_gate * conv_float
    products, local_state = lax.associative_scan(chain_link, (decay, drive), axis=0)
    identity = (jnp.ones((width,), jnp.float32), jnp.zeros((width,), jnp.float32))
    incoming = entering((products[-1], local_state[-1]), "seq", chain_link, identity, False)
    state_in = incoming[1]
    state = local_state + products * state_in
    gelu_y, gelu_y_back = jax.vjp(gelu_tanh, y_pre)
    mixed_low = (state * gelu_y).astype(jnp.bfloat16)
    residual_mid = residual_in + jnp.dot(mixed_low, weight_out, preferred_element_type=jnp.float32)
    scaled_two, inverse_two = norm_scale(residual_mid)
    normed_two = (scaled_two * vectors[1]).astype(jnp.bfloat16)
    cot_low = cotangent[0]
    rows_each = width // seq_count
    piece_gate = lax.all_gather(mlp_gate, "fsdp", axis=1, tiled=True)
    piece_up = lax.all_gather(mlp_up, "fsdp", axis=1, tiled=True)
    piece_down = lax.all_gather(mlp_down, "fsdp", axis=1, tiled=True)
    gate_val = jnp.dot(normed_two, piece_gate, preferred_element_type=jnp.float32)
    up_val = jnp.dot(normed_two, piece_up, preferred_element_type=jnp.float32)
    hidden_val = (gelu_tanh(gate_val) * up_val).astype(jnp.bfloat16)
    mix_out = dot_cols(hidden_val, piece_down)
    forward_gate_all = gate_val
    forward_up_all = up_val
    output = (residual_mid + mix_out).astype(jnp.bfloat16)[None]
    piece_gate = lax.all_gather(mlp_gate, "fsdp", axis=1, tiled=True)
    piece_up = lax.all_gather(mlp_up, "fsdp", axis=1, tiled=True)
    piece_down = lax.all_gather(mlp_down, "fsdp", axis=1, tiled=True)
    grad_hidden = jnp.dot(cot_low, piece_down, preferred_element_type=jnp.float32)
    gate_val = forward_gate_all
    up_val = forward_up_all
    gelu_val, gelu_back = jax.vjp(gelu_tanh, gate_val)
    grad_gate = gelu_back(grad_hidden * up_val)[0].astype(jnp.bfloat16)
    grad_up = (grad_hidden * gelu_val).astype(jnp.bfloat16)
    grad_normed = dot_cols(grad_gate, piece_gate) + dot_cols(grad_up, piece_up)

    def grad_block(block_index):
        seq_pos = block_index // fsdp_count
        ff_pos = block_index % fsdp_count
        left_normed = lax.dynamic_slice_in_dim(normed_two, seq_pos * rows_each, rows_each, 1)
        left_cot = lax.dynamic_slice_in_dim(cot_low, seq_pos * rows_each, rows_each, 1)
        gate_cols = lax.dynamic_slice_in_dim(grad_gate, ff_pos * ff_each, ff_each, 1)
        up_cols = lax.dynamic_slice_in_dim(grad_up, ff_pos * ff_each, ff_each, 1)
        hidden_cols = lax.dynamic_slice_in_dim(hidden_val, ff_pos * ff_each, ff_each, 1)
        return jnp.concatenate(
            [
                dot_rows(left_normed, gate_cols),
                dot_rows(left_normed, up_cols),
                dot_rows(left_cot, hidden_cols),
            ],
            axis=1,
        )

    blocks = lax.map(
        grad_block, jnp.arange(rows_each * lax.axis_size(("seq", "fsdp")) // rows_each)
    )
    mlp_grads = lax.psum_scatter(
        blocks.reshape(rows_each * lax.axis_size(("seq", "fsdp")), 3 * ff_each),
        ("seq", "fsdp"),
        scatter_dimension=0,
        tiled=True,
    )
    grad_mid_norm, grad_gain_two = norm_back(grad_normed, scaled_two, inverse_two, vectors[1])
    grad_mid = cot_low.astype(jnp.float32) + grad_mid_norm
    grad_branch = grad_mid.astype(jnp.bfloat16)
    grad_mixed = dot_cols(grad_branch, weight_out)
    grad_y_low = gelu_y_back(grad_mixed * state)[0].astype(jnp.bfloat16)
    grad_state_direct = grad_mixed * gelu_y
    next_decay = jnp.concatenate([decay[1:], jnp.ones((1, width), jnp.float32)], axis=0)
    back_prod, back_local = lax.associative_scan(
        chain_link, (jnp.flip(next_decay, 0), jnp.flip(grad_state_direct, 0)), axis=0
    )
    back_prod = jnp.flip(back_prod, 0)
    back_local = jnp.flip(back_local, 0)
    back_summary = (decay[0] * back_prod[0], decay[0] * back_local[0])
    back_in = entering(back_summary, "seq", chain_link, identity, True)
    state_grad = back_local + back_prod * back_in[1]
    prev_state = jnp.concatenate([state_in[None], state[:-1]], axis=0)
    grad_scale = state_grad * input_gate * conv_float
    grad_input_gate = state_grad * scale_in * conv_float
    grad_log = (
        state_grad * prev_state * decay
        - grad_scale * keep_mask * jnp.exp(2.0 * log_decay) / scale_in
    )
    grad_in_pre = grad_input_gate * input_gate * (1.0 - input_gate)
    grad_decay_pre = -8.0 * rate * grad_log * decay_gate * (1.0 - decay_gate)
    grad_base = jnp.sum(-8.0 * decay_gate * grad_log, axis=0) * jax.nn.sigmoid(base_rate)
    grad_prod = jnp.concatenate(
        [grad_in_pre.reshape(tokens, HEADS, BLK), grad_decay_pre.reshape(tokens, HEADS, BLK)],
        axis=2,
    ).astype(jnp.bfloat16)
    grad_conv = state_grad * scale_in * input_gate
    grad_conv = grad_conv + jnp.einsum(
        "thj,hij->thi", grad_prod, gate_blocks, preferred_element_type=jnp.float32
    ).reshape(tokens, width)
    tap_grads = []
    grad_extended = jnp.zeros((tokens + 3, width), jnp.float32)
    for lag in range(4):
        masked = grad_conv * valid_masks[lag]
        tap_grads.append(jnp.sum(masked * extended[3 - lag : 3 - lag + tokens], axis=0))
        grad_extended = grad_extended.at[3 - lag : 3 - lag + tokens].add(vectors[2 + lag] * masked)
    edge_back = shifted(grad_extended[:3], "seq", -1)
    grad_x_pre = grad_extended[3:] + jnp.concatenate(
        [jnp.zeros((tokens - 3, width), jnp.float32), edge_back], axis=0
    )
    grad_x_low = grad_x_pre.astype(jnp.bfloat16)
    rows_mixer = width // (seq_count * fsdp_count)
    fsdp_pos = lax.axis_index("fsdp")
    norm_all, mixed_all, conv_all, grad_y_all, grad_x_all, branch_all, prod_all = (
        lax.all_gather(normed_one, "fsdp", axis=0, tiled=True),
        lax.all_gather(mixed_low, "fsdp", axis=0, tiled=True),
        lax.all_gather(conv_low, "fsdp", axis=0, tiled=True),
        lax.all_gather(grad_y_low, "fsdp", axis=0, tiled=True),
        lax.all_gather(grad_x_low, "fsdp", axis=0, tiled=True),
        lax.all_gather(grad_branch, "fsdp", axis=0, tiled=True),
        lax.all_gather(grad_prod.reshape(tokens, 2 * width), "fsdp", axis=0, tiled=True),
    )
    prod_heads = prod_all.reshape(prod_all.shape[0], HEADS, 2 * BLK)

    def mixer_block(block_index):
        first_row = (block_index * fsdp_count + fsdp_pos) * rows_mixer
        left_one = lax.dynamic_slice_in_dim(norm_all, first_row, rows_mixer, 1)
        left_mixed = lax.dynamic_slice_in_dim(mixed_all, first_row, rows_mixer, 1)
        left_conv = lax.dynamic_slice_in_dim(conv_all, first_row, rows_mixer, 1)
        head_of_row = (first_row + jnp.arange(rows_mixer)) // BLK
        picked = jnp.take(prod_heads, head_of_row, axis=1)
        gate_rows = jnp.einsum("tr,trj->rj", left_conv, picked, preferred_element_type=jnp.float32)
        return jnp.concatenate(
            [
                dot_rows(left_one, grad_y_all),
                dot_rows(left_one, grad_x_all),
                dot_rows(left_mixed, branch_all),
                gate_rows,
            ],
            axis=1,
        )

    blocks = lax.map(mixer_block, jnp.arange(rows_mixer * lax.axis_size("seq") // rows_mixer))
    mixer_grads = lax.psum_scatter(
        blocks.reshape(rows_mixer * lax.axis_size("seq"), 3 * width + 2 * BLK).astype(jnp.bfloat16),
        "seq",
        scatter_dimension=0,
        tiled=True,
    ).astype(jnp.float32)
    grad_normed_one = dot_cols(grad_y_low, weight_y) + dot_cols(grad_x_low, weight_x)
    grad_in_norm, grad_gain_one = norm_back(grad_normed_one, scaled_one, inverse_one, vectors[0])
    input_grad = (grad_mid + grad_in_norm).astype(jnp.bfloat16)[None]
    vector_terms = jnp.stack(
        [
            grad_gain_one,
            grad_gain_two,
            tap_grads[0],
            tap_grads[1],
            tap_grads[2],
            tap_grads[3],
            jnp.sum(grad_conv, axis=0),
            jnp.sum(grad_in_pre, axis=0),
            jnp.sum(grad_decay_pre, axis=0),
            grad_base,
        ]
    )
    vectors_grad = lax.psum(vector_terms, ("seq", "fsdp"))
    in_y_grad = mixer_grads[:, :width]
    in_x_grad = mixer_grads[:, width : 2 * width]
    out_proj_grad = mixer_grads[:, 2 * width : 3 * width]
    gate_grad = mixer_grads[:, 3 * width :]
    mlp_gate_grad = mlp_grads[:, :ff_each]
    mlp_up_grad = mlp_grads[:, ff_each : 2 * ff_each]
    mlp_down_grad = mlp_grads[:, 2 * ff_each :]
    return (
        output,
        input_grad,
        vectors_grad,
        in_y_grad,
        in_x_grad,
        gate_grad,
        out_proj_grad,
        mlp_gate_grad,
        mlp_up_grad,
        mlp_down_grad,
    )


def solution(mesh):
    return jax.shard_map(
        local,
        mesh=mesh,
        in_specs=(
            P("fsdp", "seq", None),
            P("fsdp", "seq"),
            P(),
            P(),
            P(None, "fsdp"),
            P(None, "fsdp"),
            P(None, "fsdp"),
            P(None, "fsdp"),
            P(None, "fsdp"),
            P(None, "fsdp"),
            P(None, "fsdp"),
            P("fsdp", "seq", None),
        ),
        out_specs=(
            P("fsdp", "seq", None),
            P("fsdp", "seq", None),
            P(),
            P(("seq", "fsdp"), None),
            P(("seq", "fsdp"), None),
            P(("seq", "fsdp"), None),
            P(("seq", "fsdp"), None),
            P("seq", "fsdp"),
            P("seq", "fsdp"),
            P("seq", "fsdp"),
        ),
        check_vma=False,
    )
```

profile of v0, /device:TPU:2, one launch (start us, length us, event | category | flops | bytes accessed | tf_op | source)
XLA Modules:
  0.0 4134.0 jit_solution(8492140781680621931)
XLA Ops:
  13.1 81.6 %all-gather.19.cloned.1.call-done = bf16[2560,2560]{1,0:T(8,128)(2,1)} async-done(((bf16[2560,640]{1,0:T(8,128)(2,1)}), bf16[2560,2560]{1,0:T(8,128)(2,1)}) %all-gather.19.cloned.1.call-update) | async-done | bytes 13107216 | tf_op jit(solution)/shard_map/all_gather | solution.py:95
  107.9 14.2 all-gather.21.cloned.1.call-done
  249.9 31.0 all-gather
  288.6 30.7 all-gather.1
  320.8 10.0 slice.697
  347.0 10.7 multiply_convert_fusion.3
  364.8 167.6 %all-gather.29.cloned.1.call-done = bf16[2560,7680]{1,0:T(8,128)(2,1)} async-done(((bf16[2560,1920]{1,0:T(8,128)(2,1)}), bf16[2560,7680]{1,0:T(8,128)(2,1)}) %all-gather.29.cloned.1.call-update) | async-done | bytes 39321616 | tf_op jit(solution)/shard_map/all_gather | solution.py:143
  532.4 20.7 fusion.115
  553.1 216.5 %all-gather.27.cloned.1.call-done = bf16[2560,7680]{1,0:T(8,128)(2,1)} async-done(((bf16[2560,1920]{1,0:T(8,128)(2,1)}), bf16[2560,7680]{1,0:T(8,128)(2,1)}) %all-gather.27.cloned.1.call-update) | async-done | bytes 39321616 | tf_op jit(solution)/shard_map/all_gather | solution.py:142
  769.6 20.6 fusion.114
  790.2 216.7 %all-gather.31.cloned.1.call-done = bf16[2560,7680]{1,0:T(8,128)(2,1)} async-done(((bf16[2560,1920]{1,0:T(8,128)(2,1)}), bf16[2560,7680]{1,0:T(8,128)(2,1)}) %all-gather.31.cloned.1.call-update) | async-done | bytes 39321616 | tf_op jit(solution)/shard_map/all_gather | solution.py:144
  1007.0 21.6 multiply_convert_fusion
  1028.6 19.6 fusion.116
  1048.2 20.5 multiply_reduce_fusion.5
  1071.3 11.1 fusion.70
  1152.1 10.7 rev.15
  1162.8 10.8 rev.16
  1173.8 31.0 all-gather.3
  1205.1 30.5 all-gather.2
  1300.2 19.3 all-gather.33.cloned.1.call-done
  1319.5 27.0 all-gather.43.cloned.1.call-done
  1346.5 27.7 all-gather.39.cloned.1.call-done
  1374.2 27.6 all-gather.35.cloned.1.call-done
  1401.8 27.7 all-gather.41.cloned.1.call-done
  1429.5 27.6 all-gather.37.cloned.1.call-done
  1457.1 346.9 %while.56 = (s32[]{:T(128)}, bf16[8,80,8192]{2,1,0:T(8,128)(2,1)}, s32[8]{0:T(128)S(1)}, s32[]{:T(128)}, bf16[512,2560]{1,0:T(8,128)(2,1)}, /*index=5*/bf16[512,...) while((s32[]{:T(128)}, bf16[8,80,8192]{2,1,0:T(8,128)(2,1)}, ...), condition=%wide.region_20.21_spmd, body=%wide.region_19.20_spmd.sunk | while | flops 697307392 | bytes 161535440 | solution.py:264
  1467.2 17.2 gather_fusion
  1484.4 14.8 fusion.181
  1510.5 17.4 gather_fusion
  1527.9 14.8 fusion.181
  1554.0 17.2 gather_fusion
  1571.2 14.8 fusion.181
  1597.4 17.2 gather_fusion
  1614.6 14.8 fusion.181
  1640.7 17.2 gather_fusion
  1657.9 14.8 fusion.181
  1683.9 17.4 gather_fusion
  1701.3 14.8 fusion.181
  1727.4 17.2 gather_fusion
  1744.6 14.8 fusion.181
  1770.7 17.2 gather_fusion
  1787.9 14.8 fusion.181
  1804.1 371.3 %while.57 = (s32[]{:T(128)}, f32[32,320,5760]{2,1,0:T(8,128)}, s32[32]{0:T(128)S(1)}, bf16[128,2560]{1,0:T(8,128)(2,1)}, bf16[128,7680]{1,0:T(8,128)(2,1)}, /*in...) while((s32[]{:T(128)}, f32[32,320,5760]{2,1,0:T(8,128)}, ...), condition=%wide.region_23.24_spmd, body=%wide.region_22.23_spmd.sunk | while | flops 475545632 | bytes 23888364 | solution.py:180
  2176.7 10.1 fusion.117
  2186.8 27.6 fusion.38
  2214.5 14.1 fusion.62
  2238.1 1760.4 %reduce-scatter.5.cloned.1.call-done = f32[320,5760]{1,0:T(8,128)} async-done(((f32[10240,5760]{1,0:T(8,128)}), f32[320,5760]{1,0:T(8,128)}) %reduce-scatter.5.cloned.1.call-update) | async-done | bytes 7372816 | tf_op jit(solution)/shard_map/reduce_scatter | solution.py:183
  4004.9 120.7 %all-reduce.62.cloned.1.call-done = f32[10,2560]{1,0:T(8,128)} async-done(((f32[10,2560]{1,0:T(8,128)}), f32[10,2560]{1,0:T(8,128)}) %all-reduce.62.cloned.1.call-update) | async-done | bytes 102416 | tf_op jit(solution)/shard_map/psum | solution.py:288
  (883 shorter events, 706.0 us)
Async XLA Ops:
  7.2 87.5 %all-gather.19.cloned.1.call-start = ((), (), s32[]{:S(2)}) async-start(), calls=%async_computation.2 | async-start | bytes 16384000 | tf_op jit(solution)/shard_map/all_gather | solution.py:95
  7.9 114.2 %all-gather.21.cloned.1.call-start = ((), (), s32[]{:S(2)}) async-start(), calls=%async_computation.3 | async-start | bytes 3276800 | tf_op jit(solution)/shard_map/all_gather | solution.py:96
  8.7 338.3 %all-gather.23.cloned.1.call-start = ((), (), s32[]{:S(2)}) async-start(), calls=%async_computation.4 | async-start | bytes 16384000 | tf_op jit(solution)/shard_map/all_gather | solution.py:94
  9.4 348.3 %all-gather.25.cloned.1.call-start = ((), (), s32[]{:S(2)}) async-start(), calls=%async_computation.5 | async-start | bytes 16384000 | tf_op jit(solution)/shard_map/all_gather | solution.py:97
  10.0 522.4 %all-gather.29.cloned.1.call-start = ((), (), s32[]{:S(2)}) async-start(), calls=%async_computation.7 | async-start | bytes 49152000 | tf_op jit(solution)/shard_map/all_gather | solution.py:143
  10.6 759.1 %all-gather.27.cloned.1.call-start = ((), (), s32[]{:S(2)}) async-start(), calls=%async_computation.6 | async-start | bytes 49152000 | tf_op jit(solution)/shard_map/all_gather | solution.py:142
  11.2 995.8 %all-gather.31.cloned.1.call-start = ((), (), s32[]{:S(2)}) async-start(), calls=%async_computation.8 | async-start | bytes 49152000 | tf_op jit(solution)/shard_map/all_gather | solution.py:144
  11.9 1280.4 %all-gather.45.cloned.1.call-start = ((), (), s32[]{:S(2)}) async-start(), calls=%async_computation.16 | async-start | bytes 6553600 | tf_op jit(solution)/shard_map/all_gather | solution.py:242
  12.4 88.8 %copy-start.61 = (f32[2560]{0:T(1024)}, f32[2560]{0:T(1024)S(1)}, u32[]{:S(2)}) copy-start(f32[2560]{0:T(1024)S(1)} %get-tuple-element.565) | copy-start | bytes 30724
  12.4 88.8 %copy-start.63 = (f32[2560]{0:T(1024)}, f32[2560]{0:T(1024)S(1)}, u32[]{:S(2)}) copy-start(f32[2560]{0:T(1024)S(1)} %get-tuple-element.560) | copy-start | bytes 30724
  12.5 124.7 %copy-start.45 = (f32[2560]{0:T(1024)}, f32[2560]{0:T(1024)S(1)}, u32[]{:S(2)}) copy-start(f32[2560]{0:T(1024)S(1)} %get-tuple-element.562) | copy-start | bytes 30724
  12.5 124.7 %copy-start.47 = (f32[2560]{0:T(1024)}, f32[2560]{0:T(1024)S(1)}, u32[]{:S(2)}) copy-start(f32[2560]{0:T(1024)S(1)} %get-tuple-element.563) | copy-start | bytes 30724
  12.5 124.7 %copy-start.49 = (f32[2560]{0:T(1024)}, f32[2560]{0:T(1024)S(1)}, u32[]{:S(2)}) copy-start(f32[2560]{0:T(1024)S(1)} %get-tuple-element.564) | copy-start | bytes 30724
  12.5 124.7 %copy-start.51 = (f32[2560]{0:T(1024)}, f32[2560]{0:T(1024)S(1)}, u32[]{:S(2)}) copy-start(f32[2560]{0:T(1024)S(1)} %get-tuple-element.566) | copy-start | bytes 30724
  12.5 124.7 %copy-start.53 = (f32[2560]{0:T(1024)}, f32[2560]{0:T(1024)S(1)}, u32[]{:S(2)}) copy-start(f32[2560]{0:T(1024)S(1)} %get-tuple-element.568) | copy-start | bytes 30724
  12.5 124.7 %copy-start.55 = (f32[2560]{0:T(1024)}, f32[2560]{0:T(1024)S(1)}, u32[]{:S(2)}) copy-start(f32[2560]{0:T(1024)S(1)} %get-tuple-element.561) | copy-start | bytes 30724
  12.5 124.7 %copy-start.57 = (f32[2560]{0:T(1024)}, f32[2560]{0:T(1024)S(1)}, u32[]{:S(2)}) copy-start(f32[2560]{0:T(1024)S(1)} %get-tuple-element.567) | copy-start | bytes 30724
  12.5 1056.1 %copy-start.43 = (f32[2560]{0:T(1024)}, f32[2560]{0:T(1024)S(1)}, u32[]{:S(2)}) copy-start(f32[2560]{0:T(1024)S(1)} %get-tuple-element.559) | copy-start | bytes 30724
  12.8 81.9 %copy-start.97 = (f32[128]{0:T(128)}, f32[128]{0:T(128)S(1)}, u32[]{:S(2)}) copy-start(f32[128]{0:T(128)S(1)} %add_rsqrt_fusion.1) | copy-start | bytes 1540
  12.8 124.4 %copy-start.89 = (f32[128]{0:T(128)}, f32[128]{0:T(128)S(1)}, u32[]{:S(2)}) copy-start(f32[128]{0:T(128)S(1)} %get-tuple-element.726) | copy-start | bytes 1540
  12.8 124.4 %copy-start.91 = (f32[128]{0:T(128)}, f32[128]{0:T(128)S(1)}, u32[]{:S(2)}) copy-start(f32[128]{0:T(128)S(1)} %get-tuple-element.722) | copy-start | bytes 1540
  12.8 124.4 %copy-start.95 = (f32[128]{0:T(128)}, f32[128]{0:T(128)S(1)}, u32[]{:S(2)}) copy-start(f32[128]{0:T(128)S(1)} %get-tuple-element.723) | copy-start | bytes 1540
  12.8 124.4 %copy-start.59 = (f32[2560]{0:T(1024)}, f32[2560]{0:T(1024)S(1)}, u32[]{:S(2)}) copy-start(f32[2560]{0:T(1024)S(1)} %fusion.79) | copy-start | bytes 30724
  13.1 88.2 %copy-start.11 = (bf16[128,2560]{1,0:T(8,128)(2,1)}, bf16[128,2560]{1,0:T(8,128)(2,1)S(1)}, u32[]{:S(2)}) copy-start(bf16[128,2560]{1,0:T(8,128)(2,1)S(1)} %fusion.56) | copy-start | bytes 1966084
  101.3 5.1 collective-permute-start
  364.6 704.1 %copy-start.2 = (f32[128,2560]{1,0:T(8,128)}, f32[128,2560]{1,0:T(8,128)S(1)}, u32[]{:S(2)}) copy-start(f32[128,2560]{1,0:T(8,128)S(1)} %get-tuple-element.729) | copy-start | bytes 3932164
  364.6 704.1 %copy-start.93 = (f32[128]{0:T(128)}, f32[128]{0:T(128)S(1)}, u32[]{:S(2)}) copy-start(f32[128]{0:T(128)S(1)} %add_rsqrt_fusion) | copy-start | bytes 1540
  364.8 404.8 %copy-start.8 = (bf16[128,2560]{1,0:T(8,128)(2,1)}, bf16[128,2560]{1,0:T(8,128)(2,1)S(1)}, u32[]{:S(2)}) copy-start(bf16[128,2560]{1,0:T(8,128)(2,1)S(1)} %multiply_convert_fusion.2) | copy-start | bytes 1966084
  1162.8 73.1 %copy-start.40 = (f32[2560]{0:T(1024)S(1)}, f32[2560]{0:T(1024)}, u32[]{:S(2)}) copy-start(f32[2560]{0:T(1024)} %custom-call.1) | copy-start | bytes 30724
  1162.8 73.9 %copy-start.6 = (f32[128,2560]{1,0:T(8,128)S(1)}, f32[128,2560]{1,0:T(8,128)}, u32[]{:S(2)}) copy-start(f32[128,2560]{1,0:T(8,128)} %copy-done.5) | copy-start | bytes 3932164
  1173.7 63.1 %copy-start.54 = (f32[2560]{0:T(1024)S(1)}, f32[2560]{0:T(1024)}, u32[]{:S(2)}) copy-start(f32[2560]{0:T(1024)} %copy-done.53) | copy-start | bytes 30724
  1173.7 63.1 %copy-start.56 = (f32[2560]{0:T(1024)S(1)}, f32[2560]{0:T(1024)}, u32[]{:S(2)}) copy-start(f32[2560]{0:T(1024)} %copy-done.55) | copy-start | bytes 30724
  1173.7 63.1 %copy-start.58 = (f32[2560]{0:T(1024)S(1)}, f32[2560]{0:T(1024)}, u32[]{:S(2)}) copy-start(f32[2560]{0:T(1024)} %copy-done.57) | copy-start | bytes 30724
  1173.7 63.1 %copy-start.60 = (f32[2560]{0:T(1024)S(1)}, f32[2560]{0:T(1024)}, u32[]{:S(2)}) copy-start(f32[2560]{0:T(1024)} %copy-done.59) | copy-start | bytes 30724
  1173.7 63.1 %copy-start.77 = (f32[1,2560]{1,0:T(1,128)S(1)}, f32[1,2560]{1,0:T(1,128)}, u32[]{:S(2)}) copy-start(f32[1,2560]{1,0:T(1,128)} %broadcast_in_dim.67) | copy-start | bytes 30724
  1173.7 63.1 %copy-start.90 = (f32[128]{0:T(128)S(1)}, f32[128]{0:T(128)}, u32[]{:S(2)}) copy-start(f32[128]{0:T(128)} %copy-done.89) | copy-start | bytes 1540
  1173.7 63.1 %copy-start.92 = (f32[128]{0:T(128)S(1)}, f32[128]{0:T(128)}, u32[]{:S(2)}) copy-start(f32[128]{0:T(128)} %copy-done.91) | copy-start | bytes 1540
  1173.7 63.1 %copy-start.96 = (f32[128]{0:T(128)S(1)}, f32[128]{0:T(128)}, u32[]{:S(2)}) copy-start(f32[128]{0:T(128)} %copy-done.95) | copy-start | bytes 1540
  1251.4 68.1 %all-gather.33.cloned.1.call-start = ((), (), s32[]{:S(2)}) async-start(), calls=%async_computation.10 | async-start | bytes 3276800 | tf_op jit(solution)/shard_map/all_gather | solution.py:236
  1252.1 94.4 %all-gather.43.cloned.1.call-start = ((), (), s32[]{:S(2)}) async-start(), calls=%async_computation.15 | async-start | bytes 3276800 | tf_op jit(solution)/shard_map/all_gather | solution.py:238
  1252.7 121.5 %all-gather.39.cloned.1.call-start = ((), (), s32[]{:S(2)}) async-start(), calls=%async_computation.13 | async-start | bytes 3276800 | tf_op jit(solution)/shard_map/all_gather | solution.py:237
  1253.4 148.4 %all-gather.35.cloned.1.call-start = ((), (), s32[]{:S(2)}) async-start(), calls=%async_computation.11 | async-start | bytes 3276800 | tf_op jit(solution)/shard_map/all_gather | solution.py:239
  1254.0 175.5 %all-gather.41.cloned.1.call-start = ((), (), s32[]{:S(2)}) async-start(), calls=%async_computation.14 | async-start | bytes 3276800 | tf_op jit(solution)/shard_map/all_gather | solution.py:241
  1257.9 199.3 %all-gather.37.cloned.1.call-start = ((), (), s32[]{:S(2)}) async-start(), calls=%async_computation.12 | async-start | bytes 3276800 | tf_op jit(solution)/shard_map/all_gather | solution.py:240
  1276.9 5.9 collective-permute-start.1
  1283.8 949.8 %reduce-scatter.3.cloned.1.call-start = ((), (), s32[]{:S(2)}) async-start(), calls=%async_computation.17 | async-start | bytes 11796480 | tf_op jit(solution)/shard_map/reduce_scatter | solution.py:265
  1804.0 2194.5 %reduce-scatter.5.cloned.1.call-start = ((), (), s32[]{:S(2)}) async-start(), calls=%async_computation.18 | async-start | bytes 243302400 | tf_op jit(solution)/shard_map/reduce_scatter | solution.py:183
  2175.5 1950.1 %all-reduce.62.cloned.1.call-start = ((), (), s32[]{:S(2)}) async-start(), calls=%async_computation.9 | async-start | bytes 327680 | tf_op jit(solution)/shard_map/psum | solution.py:288
  (103 other events, 1006.3 us)
Sparse Core Ops, SparseCore 0:
  9.6 85.0 all-gather.18
  96.2 25.8 all-gather.20
  123.7 85.0 all-gather.22
  210.2 84.9 all-gather.24
  296.6 235.7 all-gather.28
  533.8 235.7 all-gather.26
  771.2 235.7 all-gather.30
  1251.5 40.7 all-gather.44
  1293.9 25.5 all-gather.32
  1320.9 25.5 all-gather.42
  1348.6 25.5 all-gather.38
  1376.2 25.5 all-gather.34
  1403.9 25.5 all-gather.40
  1431.5 25.5 all-gather.36
  1804.1 179.1 reduce-scatter.2
  2175.6 1822.8 reduce-scatter.4
  4004.5 121.0 all-reduce.61
where the time goes:
time: 4150 us; the launch traced here: 4130 us
  waiting for transfers between devices  2760 us (67%)
  matrix products  533 us (13%)
  local copies, waits for them, and re-layouts  422 us (10%)
  other arithmetic  187 us (5%)
  blocking collectives  123 us (3%)
  loops' own time  90.6 us (2%)
    reduce_scatter x1, waiting for transfers between devices, local(): lax.psum_scatter(blocks.reshape(rows_each * lax.axis_size(('seq', 'fsdp')...  1760 us
    dot_general x120, matrix products, dot_rows(): lax.dot_general(left, right, (((0,), (0,)), ((), ())), preferred_element_...  219 us
    all_gather x1, waiting for transfers between devices, local(): piece_down = lax.all_gather(mlp_down, 'fsdp', axis=1, tiled=True)  217 us
    all_gather x1, waiting for transfers between devices, local(): piece_gate = lax.all_gather(mlp_gate, 'fsdp', axis=1, tiled=True)  216 us
    all_gather x1, waiting for transfers between devices, local(): piece_up = lax.all_gather(mlp_up, 'fsdp', axis=1, tiled=True)  168 us
    gather x8, local copies, waits for them, and re-layouts, mixer_block(): picked = jnp.take(prod_heads, head_of_row, axis=1)  138 us
    all_gather x4, blocking collectives, entering(): pieces = jax.tree.map(lambda part: lax.all_gather(part, axis), value)  123 us
    psum x1, waiting for transfers between devices, local(): vectors_grad = lax.psum(vector_terms, ('seq', 'fsdp'))  121 us
  transfers between devices with their start and end apart: 19, of which 16 were waited for; matrix products, arithmetic and copies ran while one was open for 15% of the time, Pallas kernels for 0%

commit v1 on v0

v1 whole, which is shorter than its diff:
```python
import functools

import jax
import jax.numpy as jnp
from jax import lax
from jax.experimental import pallas as pl
from jax.experimental.pallas import tpu as pltpu
from jax.sharding import PartitionSpec as P

HEADS = 10
BLK = 256
FBLK = 64
EPS = 1e-06
ALL = ("seq", "fsdp")
F32 = jnp.float32
BF16 = jnp.bfloat16
GELU_C = 0.7978845608028654
GELU_A = 0.044715


def norm_scale(values):
    inverse = lax.rsqrt(jnp.mean(values * values, axis=-1, keepdims=True) + EPS)
    return (values * inverse, inverse)


def norm_back(grad_normed, scaled, inverse, gain_row):
    grad_gain = jnp.sum(grad_normed * scaled, axis=0)
    inner_term = grad_normed * gain_row
    grad_input = inverse * (
        inner_term - scaled * jnp.mean(inner_term * scaled, axis=-1, keepdims=True)
    )
    return (grad_input, grad_gain)


def gelu_pair(values):
    square = values * values
    t = jnp.tanh(GELU_C * values * (1.0 + GELU_A * square))
    half = 0.5 * (1.0 + t)
    slope = half + 0.5 * values * (1.0 - t * t) * GELU_C * (1.0 + 3.0 * GELU_A * square)
    return (values * half, slope)


def dot(left, right):
    return jnp.dot(left, right, preferred_element_type=F32)


def dot_rows(left, right):
    return lax.dot_general(left, right, (((0,), (0,)), ((), ())), preferred_element_type=F32)


def dot_cols(left, right):
    return lax.dot_general(left, right, (((1,), (1,)), ((), ())), preferred_element_type=F32)


class Lay:
    def __init__(self):
        self.seq = lax.axis_size("seq")
        self.nz = self.seq // 2
        seq, fsdp = (lax.axis_index("seq"), lax.axis_index("fsdp"))
        self.z, self.y = (seq // 2, seq % 2)
        self.x, self.c = (fsdp // 2, fsdp % 2)

    def pairs(self, target):
        found = []
        for s in range(self.seq):
            for f in range(4):
                z, y, x, c = (s // 2, s % 2, f // 2, f % 2)
                to = target(z, y, x, c)
                if to is not None:
                    found.append((s * 4 + f, ((to[0] * 2 + to[1]) * 2 + to[2]) * 2 + to[3]))
        return found

    def send(self, value, target):
        return lax.ppermute(value, ALL, self.pairs(target))

    def over_c(self, value):
        return self.send(value, lambda z, y, x, c: (z, y, x, 1 - c))

    def over_x(self, value):
        return self.send(value, lambda z, y, x, c: (z, y, 1 - x, c))

    def over_y(self, value):
        return self.send(value, lambda z, y, x, c: (z, 1 - y, x, c))

    def over_seq_bit(self, value, bit):
        def to(z, y, x, c):
            other = (2 * z + y) ^ bit
            return (other // 2, other % 2, x, c)

        return self.send(value, to)

    def over_seq(self, value, by):
        def to(z, y, x, c):
            other = 2 * z + y + by
            return (other // 2, other % 2, x, c) if 0 <= other < self.seq else None

        return self.send(value, to)


def row_iota(rows, cols):
    return lax.broadcasted_iota(jnp.int32, (rows, cols), 0)


def token_masks(flags_ref, g, rows, cols):
    row = row_iota(rows, cols)
    block = row // FBLK
    offset = row % FBLK
    flagged = jnp.zeros((rows, cols), F32)
    for b in range(rows // FBLK):
        flagged = jnp.where(block == b, flags_ref[g, b], flagged)
    valid = [jnp.where(offset < lag, 1.0 - flagged, 1.0) for lag in range(4)]
    start = jnp.where(offset == 0, flagged, 0.0)
    return start, valid


def neg_expm1(v):
    series = 1.0 + v * (1.0 / 6.0)
    for n in (5.0, 4.0, 3.0, 2.0):
        series = 1.0 + v * (1.0 / n) * series
    return jnp.where(v > -0.25, -v * series, 1.0 - jnp.exp(v))


def shifted_inputs(xl_ref, halo_ref, g):
    ext = jnp.concatenate([halo_ref[g].astype(F32), xl_ref[g].astype(F32)], axis=0)
    pad = halo_ref.shape[1]
    return [ext[pad:] if k == 0 else pltpu.roll(ext, k, 0)[pad:] for k in range(4)]


def mixer_forward(flags_ref, xl_ref, halo_ref, gw_ref, vec_ref, rate_ref,
                  conv_ref, ig_ref, dg_ref, prod_ref, local_ref, sum_ref):
    groups, rows, cols = xl_ref.shape
    row = row_iota(rows, cols)
    for g in range(groups):
        start, valid = token_masks(flags_ref, g, rows, cols)
        lagged = shifted_inputs(xl_ref, halo_ref, g)
        conv = vec_ref[6:7, :] + jnp.zeros((rows, cols), F32)
        for k in range(4):
            conv = conv + vec_ref[2 + k : 3 + k, :] * lagged[k] * valid[k]
        conv_low = conv.astype(BF16)
        conv_ref[g] = conv_low
        prod = jnp.dot(conv_low, gw_ref[...], preferred_element_type=F32)
        ig = jax.nn.sigmoid(prod[:, :cols] + vec_ref[7:8, :])
        dg = jax.nn.sigmoid(prod[:, cols:] + vec_ref[8:9, :])
        ig_ref[g] = ig
        dg_ref[g] = dg
        keep = 1.0 - start
        log_decay = -8.0 * dg * rate_ref[0:1, :]
        p = jnp.exp(log_decay) * keep
        s = jnp.sqrt(keep * neg_expm1(2.0 * log_decay) + start) * ig * conv_low.astype(F32)
        step = 1
        while step < rows:
            inside = row >= step
            p_prev = jnp.where(inside, pltpu.roll(p, step, 0), 1.0)
            s_prev = jnp.where(inside, pltpu.roll(s, step, 0), 0.0)
            s = p * s_prev + s
            p = p * p_prev
            step *= 2
        prod_ref[g] = p
        local_ref[g] = s
        sum_ref[g : g + 1, :] = p[rows - 1 :, :]
        sum_ref[groups + g : groups + g + 1, :] = s[rows - 1 :, :]


def mixer_back_scan(flags_ref, gm_ref, y_ref, dg_ref, prod_ref, local_ref, sin_ref, rate_ref,
                    gy_ref, bprod_ref, blocal_ref, sum_ref):
    groups, rows, cols = gm_ref.shape
    row = row_iota(rows, cols)
    for g in range(groups):
        start, _ = token_masks(flags_ref, g, rows, cols)
        state = local_ref[g] + prod_ref[g] * sin_ref[g : g + 1, :]
        gelu, slope = gelu_pair(y_ref[g])
        gm = gm_ref[g]
        gy_ref[g] = (gm * state * slope).astype(BF16)
        decay = jnp.exp(-8.0 * dg_ref[g] * rate_ref[0:1, :]) * (1.0 - start)
        s = gm * gelu
        p = jnp.where(row == rows - 1, 1.0, pltpu.roll(decay, rows - 1, 0))
        step = 1
        while step < rows:
            inside = row < rows - step
            p_next = jnp.where(inside, pltpu.roll(p, rows - step, 0), 1.0)
            s_next = jnp.where(inside, pltpu.roll(s, rows - step, 0), 0.0)
            s = p * s_next + s
            p = p * p_next
            step *= 2
        bprod_ref[g] = p
        blocal_ref[g] = s
        sum_ref[g : g + 1, :] = decay[:1, :] * p[:1, :]
        sum_ref[groups + g : groups + g + 1, :] = decay[:1, :] * s[:1, :]


def mixer_backward(flags_ref, bprod_ref, blocal_ref, bin_ref, prod_ref, local_ref, sin_ref,
                   ig_ref, dg_ref, conv_ref, xl_ref, halo_ref, gw_ref, vec_ref, rate_ref,
                   gip_ref, gdp_ref, gx_ref, tail_ref, edge_ref, rows_ref):
    groups, rows, cols = xl_ref.shape
    row = row_iota(rows, cols)
    sums = [jnp.zeros((1, cols), F32) for _ in range(8)]
    tail = tail_ref.shape[1]
    pad = edge_ref.shape[1]
    for g in range(groups):
        start, valid = token_masks(flags_ref, g, rows, cols)
        keep = 1.0 - start
        rate = rate_ref[0:1, :]
        state_in = sin_ref[g : g + 1, :]
        state = local_ref[g] + prod_ref[g] * state_in
        prev = jnp.where(row == 0, state_in, pltpu.roll(state, 1, 0))
        sg = blocal_ref[g] + bprod_ref[g] * bin_ref[g : g + 1, :]
        ig, dg = (ig_ref[g], dg_ref[g])
        cf = conv_ref[g].astype(F32)
        log_decay = -8.0 * dg * rate
        decay = jnp.exp(log_decay) * keep
        scale = jnp.sqrt(keep * neg_expm1(2.0 * log_decay) + start)
        gscale = sg * ig * cf
        glog = sg * prev * decay - gscale * keep * jnp.exp(2.0 * log_decay) / scale
        gip = sg * scale * cf * ig * (1.0 - ig)
        gdp = -8.0 * rate * glog * dg * (1.0 - dg)
        gip_low, gdp_low = (gip.astype(BF16), gdp.astype(BF16))
        gip_ref[g] = gip_low
        gdp_ref[g] = gdp_low
        gconv = sg * scale * ig + lax.dot_general(
            jnp.concatenate([gip_low, gdp_low], axis=1), gw_ref[...],
            (((1,), (1,)), ((), ())), preferred_element_type=F32)
        lagged = shifted_inputs(xl_ref, halo_ref, g)
        spread = jnp.zeros((rows + pad, cols), F32)
        for k in range(4):
            masked = gconv * valid[k]
            sums[k] = sums[k] + jnp.sum(masked * lagged[k], axis=0, keepdims=True)
            full = jnp.concatenate(
                [jnp.zeros((pad, cols), F32), vec_ref[2 + k : 3 + k, :] * masked], axis=0)
            spread = spread + (full if k == 0 else pltpu.roll(full, rows + pad - k, 0))
        gx_ref[g] = spread[pad:].astype(BF16)
        tail_ref[g] = spread[pad + rows - tail :]
        edge_ref[g] = spread[:pad]
        sums[4] = sums[4] + jnp.sum(gconv, axis=0, keepdims=True)
        sums[5] = sums[5] + jnp.sum(gip, axis=0, keepdims=True)
        sums[6] = sums[6] + jnp.sum(gdp, axis=0, keepdims=True)
        sums[7] = sums[7] + jnp.sum(-8.0 * dg * glog, axis=0, keepdims=True) * rate_ref[1:2, :]
    rows_ref[...] = jnp.concatenate(sums, axis=0)


def by_head(body, flags, operands, outs):
    def spec(shape, rows_are_channels):
        if rows_are_channels:
            return pl.BlockSpec((BLK, shape[1]), lambda h: (h, 0))
        lead = shape[:-1]
        return pl.BlockSpec(lead + (BLK,), lambda h: (0,) * len(lead) + (h,))

    heads = outs[0].shape[-1] // BLK
    in_specs = [pl.BlockSpec(memory_space=pltpu.SMEM)]
    values = [flags]
    for value, is_gate in operands:
        in_specs.append(spec(value.shape, is_gate))
        values.append(value)
    size = sum(v.size * v.dtype.itemsize for v in values) + sum(
        o.size * o.dtype.itemsize for o in outs)
    return pl.pallas_call(
        body,
        grid=(heads,),
        in_specs=in_specs,
        out_specs=[spec(o.shape, False) for o in outs],
        out_shape=outs,
        compiler_params=pltpu.CompilerParams(vmem_limit_bytes=48 * 1024 * 1024),
        cost_estimate=pl.CostEstimate(
            flops=200 * outs[0].size, bytes_accessed=size, transcendentals=4 * outs[0].size),
    )(*values)


def entering(lay, summary, groups, backward):
    prod, state = (summary[:groups], summary[groups : 2 * groups])
    before_p, before_s = (jnp.ones_like(prod), jnp.zeros_like(state))
    mine = lax.axis_index("seq")
    bit = 1
    while bit < lay.seq:
        other = lay.over_seq_bit(jnp.concatenate([prod, state], axis=0), bit)
        other_p, other_s = (other[:groups], other[groups:])
        is_later = (mine & bit) != 0
        take = jnp.logical_not(is_later) if backward else is_later
        before_s = jnp.where(take, before_p * other_s + before_s, before_s)
        before_p = jnp.where(take, before_p * other_p, before_p)
        state = jnp.where(take, prod * other_s + state, other_p * state + other_s)
        prod = prod * other_p
        bit *= 2
    return before_s


def line_sum(lay, blocks):
    nz, z = (lay.nz, lay.z)

    def pick(t):
        return lax.dynamic_index_in_dim(blocks, jnp.clip(t, 0, nz - 1), 0, keepdims=False).astype(F32)

    right = left = None
    for dist in range(nz - 1, 0, -1):
        up, down = (pick(z + dist), pick(z - dist))
        if right is not None:
            up, down = (up + right.astype(F32), down + left.astype(F32))
        right = lay.send(
            up.astype(BF16), lambda z, y, x, c: (z + 1, y, x, c) if z + dist < nz else None)
        left = lay.send(
            down.astype(BF16), lambda z, y, x, c: (z - 1, y, x, c) if z - dist >= 0 else None)
    return pick(z) + right.astype(F32) + left.astype(F32)


def local(inputs, block_flags, decay_seed, vectors, in_y, in_x, gate_weight, out_proj,
          mlp_gate, mlp_up, mlp_down, cotangent):
    lay = Lay()
    nz, x, y, z, c = (lay.nz, lay.x, lay.y, lay.z, lay.c)
    tokens, width = inputs.shape[1:]
    half = width // 2
    quarter = width // 4
    first = c == 0

    def order_c(own, other, axis):
        return jnp.where(first, jnp.concatenate([own, other], axis),
                         jnp.concatenate([other, own], axis))

    def order_f(rel):
        b = rel.shape[-1] // 4
        p = [rel[..., i * b : (i + 1) * b] for i in range(4)]
        by_c = jnp.where(first, rel, jnp.concatenate([p[1], p[0], p[3], p[2]], -1))
        return jnp.where(x == 0, by_c, jnp.concatenate([by_c[..., 2 * b :], by_c[..., : 2 * b]], -1))

    halo_raw = lay.over_seq(inputs[0, tokens - 16 :], 1)
    residual = inputs[0].astype(F32)
    scaled_one, inverse_one = norm_scale(residual)
    normed_own = (scaled_one * vectors[0]).astype(BF16)
    normed_x = lay.over_x(normed_own)
    halo_own = (norm_scale(halo_raw.astype(F32))[0] * vectors[0]).astype(BF16)
    flag_row = jnp.pad(block_flags.astype(BF16), ((0, 0), (0, width - block_flags.shape[1])))
    halo_x = lay.over_x(jnp.concatenate([flag_row, halo_own[1:]], axis=0))
    n_flags = block_flags.shape[1]
    flags = jnp.concatenate(
        [block_flags.astype(F32), halo_x[:1, :n_flags].astype(F32)], axis=0)

    wy, wx = (in_y, in_x)
    wy_c, wx_c = (lay.over_c(in_y), lay.over_c(in_x))
    rows_mine = lax.dynamic_slice_in_dim(gate_weight, x * half, half, 0)
    rows_theirs = lax.dynamic_slice_in_dim(gate_weight, (1 - x) * half, half, 0)
    gate_x = lay.over_x(rows_theirs)
    gate_c, gate_xc = (lay.over_c(rows_mine), lay.over_c(gate_x))
    gates = order_f(jnp.concatenate([rows_mine, gate_c, gate_x, gate_xc], axis=1))
    out_mine = lax.dynamic_slice_in_dim(out_proj, x * half, half, 0)
    out_x = lay.over_x(lax.dynamic_slice_in_dim(out_proj, (1 - x) * half, half, 0))
    out_c, out_xc = (lay.over_c(out_mine), lay.over_c(out_x))
    out_rel = jnp.concatenate([out_mine, out_c, out_x, out_xc], axis=1)
    cot = cotangent[0]
    cot_c = lay.over_c(cot)
    cot_x = lay.over_x(cot)
    cot_xc = lay.over_c(cot_x)

    normed = jnp.concatenate([normed_own, normed_x, halo_own, halo_x], axis=0)
    two = 2 * tokens
    y_pre = order_c(dot(normed[:two], wy), dot(normed[:two], wy_c), 1).reshape(2, tokens, half)
    x_all = order_c(dot(normed, wx).astype(BF16), dot(normed, wx_c).astype(BF16), 1)
    x_low = x_all[:two].reshape(2, tokens, half)
    halo = x_all[two:].reshape(2, 16, half)
    vec_half = lax.dynamic_slice_in_dim(vectors, x * half, half, 1)
    base = -5.0 - decay_seed.astype(F32) + vectors[9]
    rates = lax.dynamic_slice_in_dim(
        jnp.stack([jax.nn.softplus(base), jax.nn.sigmoid(base)]), x * half, half, 1)
    shape3 = lambda dt: jax.ShapeDtypeStruct((2, tokens, half), dt)
    summary_shape = jax.ShapeDtypeStruct((4, half), F32)
    conv_low, ig, dg, prods, local_state, summary = by_head(
        mixer_forward, flags,
        [(x_low, False), (halo, False), (gates, True), (vec_half, False), (rates, False)],
        [shape3(BF16), shape3(F32), shape3(F32), shape3(F32), shape3(F32), summary_shape])
    state_in = entering(lay, summary, 2, False)
    state = local_state + prods * state_in[:, None, :]
    mixed = (state * jax.nn.gelu(y_pre, approximate=True)).astype(BF16)
    part_x = dot(mixed[1], out_rel).astype(BF16)
    part_x = lay.over_x(part_x)
    part_own = dot(mixed[0], out_rel)
    swapped = jnp.concatenate([part_x[:, half:], part_x[:, :half]], axis=1)
    mid = residual + order_f(part_own + swapped.astype(F32))

    scaled_two, inverse_two = norm_scale(mid)
    n2 = (scaled_two * vectors[1]).astype(BF16)
    n2_c = lay.over_c(n2)
    n2_x = lay.over_x(n2)
    n2_xc = lay.over_c(n2_x)

    def mlp(normed_in, cot_in):
        gate_val = dot(normed_in, mlp_gate)
        up_val = dot(normed_in, mlp_up)
        grad_hidden = dot(cot_in, mlp_down)
        gelu, slope = gelu_pair(gate_val)
        hidden = (gelu * up_val).astype(BF16)
        grad_gate = (grad_hidden * up_val * slope).astype(BF16)
        grad_up = (grad_hidden * gelu).astype(BF16)
        return hidden, grad_gate, grad_up

    near_n2, near_cot = (jnp.concatenate([n2, n2_c], 0), jnp.concatenate([cot, cot_c], 0))
    far_n2, far_cot = (jnp.concatenate([n2_x, n2_xc], 0), jnp.concatenate([cot_x, cot_xc], 0))
    near = mlp(near_n2, near_cot)
    far = mlp(far_n2, far_cot)

    def to_owners(of):
        far_part = of(far)
        far_sum = far_part[:tokens] + lay.over_c(far_part[tokens:].astype(BF16)).astype(F32)
        arriving = lay.over_x(far_sum.astype(BF16))
        near_part = of(near)
        near_sum = near_part[:tokens] + lay.over_c(near_part[tokens:].astype(BF16)).astype(F32)
        return near_sum + arriving.astype(F32)

    grad_n2 = to_owners(lambda t: dot_cols(t[1], mlp_gate) + dot_cols(t[2], mlp_up))
    output = (mid + to_owners(lambda t: dot_cols(t[0], mlp_down))).astype(BF16)[None]

    n2_y = lay.over_y(jnp.concatenate([n2, n2_x], 0))
    cot_y = lay.over_y(jnp.concatenate([cot, cot_x], 0))
    n2_y = jnp.concatenate([n2_y, lay.over_c(n2_y)], 0)
    cot_y = jnp.concatenate([cot_y, lay.over_c(cot_y)], 0)
    side = mlp(n2_y, cot_y)
    each = width // lay.seq

    def rows_of_y(value, which):
        return lax.dynamic_index_in_dim(
            value.reshape(value.shape[0], nz, 2, each), which, 2, keepdims=False
        ).reshape(value.shape[0], nz * each)

    n2_rows = rows_of_y(jnp.concatenate([near_n2, far_n2, n2_y], 0), y)
    cot_rows = rows_of_y(jnp.concatenate([near_cot, far_cot, cot_y], 0), y)
    hidden_all, gg_all, gu_all = [
        jnp.concatenate([near[i], far[i], side[i]], 0) for i in range(3)]
    mlp_grads = []
    for left, right in ((cot_rows, hidden_all), (n2_rows, gg_all), (n2_rows, gu_all)):
        part = dot_rows(left, right).astype(BF16).reshape(nz, each, right.shape[1])
        mlp_grads.append(line_sum(lay, part))
    mlp_down_grad, mlp_gate_grad, mlp_up_grad = mlp_grads

    grad_mid_norm, grad_gain_two = norm_back(grad_n2, scaled_two, inverse_two, vectors[1])
    grad_mid = cot.astype(F32) + grad_mid_norm
    branch = grad_mid.astype(BF16)
    branch_rel = order_f(branch)
    arriving = lay.over_x(branch_rel)
    branch_x_rel = jnp.concatenate([arriving[:, half:], arriving[:, :half]], axis=1)
    grad_mixed = dot_cols(jnp.concatenate([branch_rel, branch_x_rel], 0), out_rel)
    gy, bprod, blocal, back_summary = by_head(
        mixer_back_scan, flags,
        [(grad_mixed.reshape(2, tokens, half), False), (y_pre, False), (dg, False), (prods, False),
         (local_state, False), (state_in, False), (rates, False)],
        [shape3(BF16), shape3(F32), shape3(F32), summary_shape])
    back_in = entering(lay, back_summary, 2, True)
    gip, gdp, gx_main, gx_tail, edge, vec_rows = by_head(
        mixer_backward, flags,
        [(bprod, False), (blocal, False), (back_in, False), (prods, False), (local_state, False),
         (state_in, False), (ig, False), (dg, False), (conv_low, False), (x_low, False),
         (halo, False), (gates, True), (vec_half, False), (rates, False)],
        [shape3(BF16), shape3(BF16), shape3(BF16), jax.ShapeDtypeStruct((2, 16, half), F32),
         jax.ShapeDtypeStruct((2, 8, half), F32), jax.ShapeDtypeStruct((8, half), F32)])
    edge_next = lay.over_seq(edge, -1)
    gx_last = (gx_tail + jnp.pad(edge_next, ((0, 0), (8, 0), (0, 0)))).astype(BF16)
    gx = jnp.concatenate([gx_main[:, : tokens - 16], gx_last], axis=1).reshape(two, half)
    gy = gy.reshape(two, half)

    def own_cols(value, which):
        return lax.dynamic_slice_in_dim(value, which * quarter, quarter, 1)

    gy_o, gy_c, gx_o, gx_c = (
        own_cols(gy, c), own_cols(gy, 1 - c), own_cols(gx, c), own_cols(gx, 1 - c))

    def grad_n1_of(rows):
        return (dot_cols(gy_o[rows], wy) + dot_cols(gy_c[rows], wy_c)
                + dot_cols(gx_o[rows], wx) + dot_cols(gx_c[rows], wx_c))

    arriving = lay.over_x(grad_n1_of(slice(tokens, two)).astype(BF16))
    grad_n1 = grad_n1_of(slice(0, tokens)) + arriving.astype(F32)
    grad_in_norm, grad_gain_one = norm_back(grad_n1, scaled_one, inverse_one, vectors[0])
    input_grad = (grad_mid + grad_in_norm).astype(BF16)[None]

    rows_full = lax.dynamic_update_slice_in_dim(
        jnp.zeros((8, width), F32), vec_rows, x * half, 1)
    vec = jnp.concatenate([grad_gain_one[None], grad_gain_two[None], rows_full], axis=0)
    vec = vec + lay.over_c(vec)
    vec = vec + lay.over_x(vec)
    bit = 1
    while bit < lay.seq:
        vec = vec + lay.over_seq_bit(vec, bit)
        bit *= 2

    n1_two = jnp.concatenate([normed_own, normed_x], 0)
    n1_four = jnp.concatenate([n1_two, lay.over_c(n1_two)], 0)
    n1_rows = jnp.concatenate(
        [rows_of_y(n1_four, y), lay.over_y(rows_of_y(n1_four, 1 - y))], 0)
    keep = jnp.where(first, gy, gx)
    g_four = jnp.concatenate([keep, lay.over_c(jnp.where(first, gx, gy))], 0)
    g_all = jnp.concatenate([g_four, lay.over_y(g_four)], 0)
    in_part = dot_rows(n1_rows, g_all).astype(BF16).reshape(nz, each, half)

    mixed_two = mixed.reshape(two, half)
    mixed_four = jnp.concatenate([mixed_two, lay.over_c(mixed_two)], 0)
    branch_two = jnp.concatenate([branch, order_f(branch_x_rel)], 0)

    def half_cols(value, which, n):
        return lax.dynamic_slice_in_dim(value, which * n, n, 1)

    branch_four = jnp.concatenate(
        [half_cols(branch_two, c, half), lay.over_c(half_cols(branch_two, 1 - c, half))], 0)
    mixed_rows = jnp.concatenate(
        [half_cols(mixed_four, y, quarter), lay.over_y(half_cols(mixed_four, 1 - y, quarter))], 0)
    branch_all = jnp.concatenate([branch_four, lay.over_y(branch_four)], 0)
    fine = quarter // nz
    out_part = dot_rows(mixed_rows, branch_all).astype(BF16).reshape(nz, fine, half)

    conv_two = conv_low.reshape(two, half)
    conv_four = jnp.concatenate([conv_two, lay.over_c(conv_two)], 0)
    gip2, gdp2 = (gip.reshape(two, half), gdp.reshape(two, half))
    gp_four = jnp.concatenate(
        [jnp.where(first, gip2, gdp2), lay.over_c(jnp.where(first, gdp2, gip2))], 0)
    heads = half // BLK
    gate_part = jnp.einsum(
        "thi,thj->hij", conv_four.reshape(2 * two, heads, BLK),
        gp_four.reshape(2 * two, heads, BLK), preferred_element_type=F32).reshape(half, BLK)
    gate_keep = lax.dynamic_slice_in_dim(gate_part, y * quarter, quarter, 0)
    gate_send = lax.dynamic_slice_in_dim(gate_part, (1 - y) * quarter, quarter, 0).astype(BF16)
    gate_sum = (gate_keep + lay.over_y(gate_send).astype(F32)).astype(BF16)
    gate_sum = gate_sum.reshape(nz, fine * BLK // half, half)

    done = line_sum(lay, jnp.concatenate([in_part, out_part, gate_sum], axis=1)).astype(BF16)
    own80 = each // 4
    in_done = done[:each].reshape(2, 2, own80, half)
    out_done = done[each : each + fine].reshape(2, own80, half)
    gate_done = done[each + fine :].reshape(2, own80, BLK)

    def by_core(value, axis):
        mine = lax.dynamic_index_in_dim(value, c, axis, keepdims=False)
        theirs = lax.dynamic_index_in_dim(value, 1 - c, axis, keepdims=False)
        return mine, lay.over_c(theirs)

    in_keep, in_recv = by_core(in_done, 1)
    out_keep, out_recv = by_core(out_done, 0)
    gate_keep, gate_recv = by_core(gate_done, 0)
    both = jnp.stack([jnp.where(first, in_keep, in_recv), jnp.where(first, in_recv, in_keep)])
    mine = lax.dynamic_index_in_dim(both, x, 1, keepdims=False)
    theirs = lay.over_x(lax.dynamic_index_in_dim(both, 1 - x, 1, keepdims=False))
    in_full = jnp.where(x == 0, jnp.concatenate([mine, theirs], -1),
                        jnp.concatenate([theirs, mine], -1)).astype(F32)
    last = jnp.concatenate(
        [order_c(out_keep, out_recv, 1), order_c(gate_keep, gate_recv, 1)], axis=1)

    def final(z, y, x, c):
        at = ((x * 2 + y) * nz + z) * 2 + c
        s, f = (at // 4, at % 4)
        return (s // 2, s % 2, f // 2, f % 2)

    last = lay.send(last, final).astype(F32)
    return (output, input_grad, vec, in_full[0], in_full[1], last[:, width:], last[:, :width],
            mlp_gate_grad, mlp_up_grad, mlp_down_grad)


def solution(mesh):
    return jax.shard_map(
        local,
        mesh=mesh,
        in_specs=(
            P("fsdp", "seq", None),
            P("fsdp", "seq"),
            P(),
            P(),
            P(None, "fsdp"),
            P(None, "fsdp"),
            P(None, "fsdp"),
            P(None, "fsdp"),
            P(None, "fsdp"),
            P(None, "fsdp"),
            P(None, "fsdp"),
            P("fsdp", "seq", None),
        ),
        out_specs=(
            P("fsdp", "seq", None),
            P("fsdp", "seq", None),
            P(),
            P(("seq", "fsdp"), None),
            P(("seq", "fsdp"), None),
            P(("seq", "fsdp"), None),
            P(("seq", "fsdp"), None),
            P("seq", "fsdp"),
            P("seq", "fsdp"),
            P("seq", "fsdp"),
        ),
        check_vma=False,
    )
```

time: 4150 us -> 892 us (0.21)
  waiting for transfers between devices: 2760 us -> 308 us
  matrix products: 533 us -> 184 us
  local copies, waits for them, and re-layouts: 422 us -> 82.9 us
  starting transfers between devices: 6.2 us -> 213 us
  blocking collectives: 123 us -> 0 us
  other arithmetic: 187 us -> 65.5 us
  loops' own time: 90.6 us -> 0 us
    reduce_scatter x2 -> x0, waiting for transfers between devices: 1760 us -> none  [the longest x1 1760 us: local(): lax.psum_scatter(blocks.reshape(rows_each * lax.axis_size(('seq', 'fsdp')...]
    all_gather x14 -> x0, waiting for transfers between devices: 862 us -> none  [the longest x1 217 us: local(): piece_down = lax.all_gather(mlp_down, 'fsdp', axis=1, tiled=True)]
    ppermute x2 -> x82, waiting for transfers between devices: 5.84 us -> 308 us  [send(): return lax.ppermute(value, ALL, self.pairs(target))]
    ppermute x2 -> x82, starting transfers between devices: 5.07 us -> 213 us  [send(): return lax.ppermute(value, ALL, self.pairs(target))]
    dot_general x120 -> x5, matrix products: 219 us -> 31.4 us  [dot_rows(): lax.dot_general(left, right, (((0,), (0,)), ((), ())), preferred_element_...]
    gather x8 -> x0, local copies, waits for them, and re-layouts: 138 us -> none  [mixer_block(): picked = jnp.take(prod_heads, head_of_row, axis=1)]
    slice x103 -> x23, local copies, waits for them, and re-layouts: 139 us -> 6.64 us  [the longest x4 1.31 us: order_f(): by_c[..., 2 * b:]]
    all_gather x4 -> x0, blocking collectives: 123 us -> none  [entering(): pieces = jax.tree.map(lambda part: lax.all_gather(part, axis), value)]
  transfers between devices with their start and end apart: 19 -> 82, of which waited for: 16 -> 26; matrix products, arithmetic and copies ran while one was open for 15% -> 37% of each run, Pallas kernels for 0% -> 2%
where the time goes in v1:
time: 892 us; the launch traced here: 877 us
  waiting for transfers between devices  308 us (35%)
  starting transfers between devices  213 us (24%)
  matrix products  184 us (21%)
  local copies, waits for them, and re-layouts  82.9 us (9%)
  other arithmetic  65.5 us (7%)
  Pallas kernels  20 us (2%)
    ppermute x82, waiting for transfers between devices, send(): return lax.ppermute(value, ALL, self.pairs(target))  308 us
    ppermute x82, starting transfers between devices, send(): return lax.ppermute(value, ALL, self.pairs(target))  213 us
    dot_general x15, matrix products, dot(): return jnp.dot(left, right, preferred_element_type=F32)  93.1 us
    dot_general x15, matrix products, dot_cols(): lax.dot_general(left, right, (((1,), (1,)), ((), ())), preferred_element_...  58.7 us
    dot_general x5, matrix products, dot_rows(): lax.dot_general(left, right, (((0,), (0,)), ((), ())), preferred_element_...  31.4 us
    unnamed x212, local copies, waits for them, and re-layouts  21 us
    pallas_call x3, Pallas kernels, by_head(): pl.pallas_call(body, grid=(heads,), in_specs=in_specs, out_specs=[spec(o....  20 us
  transfers between devices with their start and end apart: 82, of which 26 were waited for; matrix products, arithmetic and copies ran while one was open for 37% of the time, Pallas kernels for 2%

profile of v1, /device:TPU:2, one launch (start us, length us, event | category | flops | bytes accessed | tf_op | source)
XLA Modules:
  0.0 877.1 jit_solution(7816230540679694302)
XLA Ops:
  18.6 14.6 %collective-permute-done.1 = bf16[16,2560]{1,0:T(8,128)(2,1)S(1)} collective-permute-done((bf16[16,2560]{1,0:T(8,128)(2,1)S(1)}, bf16[16,2560]{1,0:T(8,128)(2,1)S(1)}, u32[]{:S(2)}, u32[]{:S(2)}) %collective-permute-start.1) | collective-permute-done | bytes 81952 | tf_op jit(solution)/shard_map/ppermute | solution.py:74
  35.8 6.2 collective-permute-done.5
  64.9 7.2 shard_map.195
  80.8 5.3 collective-permute-done.12
  111.9 6.2 collective-permute-done.62
  122.1 6.7 convolution_add_fusion.8
  132.4 9.2 %fusion.31 = f32[512,1920]{1,0:T(8,128)} fusion(bf16[2560,1920]{1,0:T(8,128)(2,1)S(1)} %bitcast.280, bf16[256,2560]{1,0:T(8,128)(2,1)} %collective-permute-done.63, bf16[256,2560]{1,0:T(8,128)(2,1)} %collective-permute-done.62), kind=kOutput, calls=%fused_computation.54 | convolution fusion | flops 5038407680 | bytes 16384000 | tf_op jit(solution)/shard_map/dot_general | solution.py:44
  151.4 7.2 fusion.105
  158.6 7.2 fusion.104
  165.9 5.9 multiply_convert_fusion.5
  174.8 6.0 convolution_add_fusion.1
  181.0 5.6 fusion.169
  191.1 6.8 fusion.170
  198.0 6.8 fusion.171
  204.8 6.1 multiply_convert_fusion.3
  210.9 6.3 fusion.174
  217.2 5.8 convolution_add_fusion
  223.5 5.8 fusion.172
  236.0 11.3 %collective-permute-done.26 = bf16[128,2560]{1,0:T(8,128)(2,1)S(1)} collective-permute-done((bf16[128,2560]{1,0:T(8,128)(2,1)S(1)}, bf16[128,2560]{1,0:T(8,128)(2,1)S(1)}, u32[]{:S(2)}, u32[]{:S(2)}) %collective-permute-start.26) | collective-permute-done | bytes 655392 | tf_op jit(solution)/shard_map/ppermute | solution.py:74
  249.9 11.1 %collective-permute-done.20 = bf16[128,2560]{1,0:T(8,128)(2,1)S(1)} collective-permute-done((bf16[128,2560]{1,0:T(8,128)(2,1)S(1)}, bf16[128,2560]{1,0:T(8,128)(2,1)S(1)}, u32[]{:S(2)}, u32[]{:S(2)}) %collective-permute-start.20) | collective-permute-done | bytes 655392 | tf_op jit(solution)/shard_map/ppermute | solution.py:74
  286.9 5.5 shard_map.196
  303.2 7.9 copy.32
  313.6 8.7 fusion.175
  322.3 10.8 %multiply_convert_fusion = (bf16[512,1920]{1,0:T(8,128)(2,1)S(1)}, bf16[512,1920]{1,0:T(8,128)(2,1)S(1)}, bf16[512,1920]{1,0:T(8,128)(2,1)S(1)}) fusion(f32[512,1920]{1,0:T(8,128)S(1)} %fusion.175, f32[512,1920]{1,0:T(8,128)S(1)} %copy-done.78, bf16[512,2560]{1,0:T(8,128)(2,1)S(1)} %copy-done.52, bf16[2560,1920]{1,0:T(8,128)(2,1)} %param.21), kind=kOutput, calls=%fused_computation.23 | convolution fusion | flops 5056757760 | bytes 26214400 | tf_op jit(solution)/shard_map/dot_general | solution.py:44
  333.2 5.8 convolution_convert_fusion.2
  339.1 5.8 convolution_convert_fusion.1
  345.0 7.7 convolution_convert_fusion
  370.2 7.3 shard_map.197
  400.8 7.3 collective-permute-done.32
  424.6 39.2 %collective-permute-done.48 = bf16[640,256]{1,0:T(8,128)(2,1)S(1)} collective-permute-done((bf16[640,256]{1,0:T(8,128)(2,1)S(1)}, bf16[640,256]{1,0:T(8,128)(2,1)S(1)}, u32[]{:S(2)}, u32[]{:S(2)}) %collective-permute-start.48) | collective-permute-done | bytes 327712 | tf_op jit(solution)/shard_map/ppermute | solution.py:74
  480.7 5.1 convolution_convert_fusion.5
  485.8 7.0 convolution_convert_fusion.3
  502.8 28.5 %collective-permute-done.36 = f32[10,2560]{1,0:T(8,128)S(1)} collective-permute-done((f32[10,2560]{1,0:T(8,128)}, f32[10,2560]{1,0:T(8,128)S(1)}, u32[]{:S(2)}, u32[]{:S(2)}) %collective-permute-start.36) | collective-permute-done | bytes 102432 | tf_op jit(solution)/shard_map/ppermute | solution.py:74
  542.9 16.4 %collective-permute-done.49 = bf16[512,1280]{1,0:T(8,128)(2,1)S(1)} collective-permute-done((bf16[512,1280]{1,0:T(8,128)(2,1)S(1)}, bf16[512,1280]{1,0:T(8,128)(2,1)S(1)}, u32[]{:S(2)}, u32[]{:S(2)}) %collective-permute-start.49) | collective-permute-done | bytes 1310752 | tf_op jit(solution)/shard_map/ppermute | solution.py:74
  564.1 21.5 %collective-permute-done.76 = bf16[320,1920]{1,0:T(8,128)(2,1)S(1)} collective-permute-done((bf16[320,1920]{1,0:T(8,128)(2,1)S(1)}, bf16[320,1920]{1,0:T(8,128)(2,1)S(1)}, u32[]{:S(2)}, u32[]{:S(2)}) %collective-permute-start.76) | collective-permute-done | bytes 1228832 | tf_op jit(solution)/shard_map/ppermute | solution.py:74
  586.5 29.0 %collective-permute-done.37 = f32[10,2560]{1,0:T(8,128)S(1)} collective-permute-done((f32[10,2560]{1,0:T(8,128)S(1)}, f32[10,2560]{1,0:T(8,128)S(1)}, u32[]{:S(2)}, u32[]{:S(2)}) %collective-permute-start.37) | collective-permute-done | bytes 102432 | tf_op jit(solution)/shard_map/ppermute | solution.py:74
  620.6 7.4 collective-permute-start.77
  628.0 13.8 %collective-permute-done.71 = bf16[320,1920]{1,0:T(8,128)(2,1)S(1)} collective-permute-done((bf16[320,1920]{1,0:T(8,128)(2,1)S(1)}, bf16[320,1920]{1,0:T(8,128)(2,1)S(1)}, u32[]{:S(2)}, u32[]{:S(2)}) %collective-permute-start.71) | collective-permute-done | bytes 1228832 | tf_op jit(solution)/shard_map/ppermute | solution.py:74
  645.5 5.0 collective-permute-start.66
  650.5 19.4 %collective-permute-done.50 = bf16[512,1280]{1,0:T(8,128)(2,1)S(1)} collective-permute-done((bf16[512,1280]{1,0:T(8,128)(2,1)S(1)}, bf16[512,1280]{1,0:T(8,128)(2,1)S(1)}, u32[]{:S(2)}, u32[]{:S(2)}) %collective-permute-start.50) | collective-permute-done | bytes 1310752 | tf_op jit(solution)/shard_map/ppermute | solution.py:74
  671.4 5.0 collective-permute-start.72
  676.4 19.8 %collective-permute-done.77 = bf16[320,1920]{1,0:T(8,128)(2,1)} collective-permute-done((bf16[320,1920]{1,0:T(8,128)(2,1)S(1)}, bf16[320,1920]{1,0:T(8,128)(2,1)}, u32[]{:S(2)}, u32[]{:S(2)}) %collective-permute-start.77) | collective-permute-done | bytes 1228832 | tf_op jit(solution)/shard_map/ppermute | solution.py:74
  704.8 17.7 %collective-permute-done.66 = bf16[320,1920]{1,0:T(8,128)(2,1)S(1)} collective-permute-done((bf16[320,1920]{1,0:T(8,128)(2,1)S(1)}, bf16[320,1920]{1,0:T(8,128)(2,1)S(1)}, u32[]{:S(2)}, u32[]{:S(2)}) %collective-permute-start.66) | collective-permute-done | bytes 1228832 | tf_op jit(solution)/shard_map/ppermute | solution.py:74
  722.6 14.3 %collective-permute-start.51 = (bf16[512,1280]{1,0:T(8,128)(2,1)S(1)}, bf16[512,1280]{1,0:T(8,128)(2,1)S(1)}, u32[]{:S(2)}, u32[]{:S(2)}) collective-permute-start(bf16[512,1280]{1,0:T(8,128)(2,1)S(1)} %get-tuple-element.60), channel_id=1, source_target_pairs={{0,8},{1,9},{2,10},{3,11},{4,12},{5,13},{6,14},{7,15},{8,16},{9,17... | collective-permute-start | bytes 3932168 | tf_op jit(solution)/shard_map/ppermute | solution.py:74
  738.6 49.7 %collective-permute-start.78 = (bf16[320,1920]{1,0:T(8,128)(2,1)}, bf16[320,1920]{1,0:T(8,128)(2,1)}, u32[]{:S(2)}, u32[]{:S(2)}) collective-permute-start(bf16[320,1920]{1,0:T(8,128)(2,1)} %get-tuple-element.64), channel_id=1, source_target_pairs={{0,8},{1,9},{2,10},{3,11},{4,12},{5,13},{6,14},{7,15},{8,16},{9,17... | collective-permute-start | bytes 3686408 | tf_op jit(solution)/shard_map/ppermute | solution.py:74
  795.9 49.5 %collective-permute-start.59 = (bf16[80,3072]{1,0:T(8,128)(2,1)S(1)}, bf16[80,3072]{1,0:T(8,128)(2,1)S(1)}, u32[]{:S(2)}, u32[]{:S(2)}) collective-permute-start(bf16[80,3072]{1,0:T(8,128)(2,1)S(1)} %pad_maximum_fusion.16), channel_id=1, source_target_pairs={{0,0},{1,1},{2,16},{3,17},{4,8},{5,9},{6,24},{7,25},{8,2},{9,3},{1... | collective-permute-start | bytes 1474568 | tf_op jit(solution)/shard_map/ppermute | solution.py:74
  849.6 12.1 %collective-permute-done.59 = bf16[80,3072]{1,0:T(8,128)(2,1)S(1)} collective-permute-done((bf16[80,3072]{1,0:T(8,128)(2,1)S(1)}, bf16[80,3072]{1,0:T(8,128)(2,1)S(1)}, u32[]{:S(2)}, u32[]{:S(2)}) %collective-permute-start.59) | collective-permute-done | bytes 491552 | tf_op jit(solution)/shard_map/ppermute | solution.py:74
  863.3 12.0 %collective-permute-done.56 = bf16[2,80,1280]{2,1,0:T(8,128)(2,1)S(1)} collective-permute-done((bf16[2,80,1280]{2,1,0:T(8,128)(2,1)S(1)}, bf16[2,80,1280]{2,1,0:T(8,128)(2,1)S(1)}, u32[]{:S(2)}, u32[]{:S(2)}) %collective-permute-start.56) | collective-permute-done | bytes 409632 | tf_op jit(solution)/shard_map/ppermute | solution.py:74
  (521 shorter events, 286.8 us)
Async XLA Ops:
  0.7 54.2 %collective-permute-start.23 = (bf16[128,2560]{1,0:T(8,128)(2,1)}, bf16[128,2560]{1,0:T(8,128)(2,1)}, u32[]{:S(2)}, u32[]{:S(2)}) collective-permute-start(bf16[128,2560]{1,0:T(8,128)(2,1)} %bitcast.250), channel_id=1, source_target_pairs={{0,2},{1,3},{2,0},{3,1},{4,6},{5,7},{6,4},{7,5},{8,10},{9,11},{10,... | collective-permute-start | bytes 1966088 | tf_op jit(solution)/shard_map/ppermute | solution.py:74
  0.8 32.8 %collective-permute-start.21 = (bf16[128,2560]{1,0:T(8,128)(2,1)}, bf16[128,2560]{1,0:T(8,128)(2,1)}, u32[]{:S(2)}, u32[]{:S(2)}) collective-permute-start(bf16[128,2560]{1,0:T(8,128)(2,1)} %bitcast.251), channel_id=1, source_target_pairs={{0,1},{1,0},{2,3},{3,2},{4,5},{5,4},{6,7},{7,6},{8,9},{9,8},{10,11... | collective-permute-start | bytes 1966088 | tf_op jit(solution)/shard_map/ppermute | solution.py:74
  5.6 55.6 %collective-permute-start.3 = (bf16[2560,640]{1,0:T(8,128)(2,1)}, bf16[2560,640]{1,0:T(8,128)(2,1)}, u32[]{:S(2)}, u32[]{:S(2)}) collective-permute-start(bf16[2560,640]{1,0:T(8,128)(2,1)} %param.17), channel_id=1, source_target_pairs={{0,1},{1,0},{2,3},{3,2},{4,5},{5,4},{6,7},{7,6},{8,9},{9,8},{10,11... | collective-permute-start | bytes 9830408 | tf_op jit(solution)/shard_map/ppermute | solution.py:74
  9.6 32.4 %collective-permute-start.2 = (bf16[128,2560]{1,0:T(8,128)(2,1)S(1)}, bf16[128,2560]{1,0:T(8,128)(2,1)S(1)}, u32[]{:S(2)}, u32[]{:S(2)}) collective-permute-start(bf16[128,2560]{1,0:T(8,128)(2,1)S(1)} %fusion.72), channel_id=1, source_target_pairs={{0,2},{1,3},{2,0},{3,1},{4,6},{5,7},{6,4},{7,5},{8,10},{9,11},{10,... | collective-permute-start | bytes 1966088 | tf_op jit(solution)/shard_map/ppermute | solution.py:74
  42.0 45.7 %collective-permute-start.10 = (bf16[2560,640]{1,0:T(8,128)(2,1)}, bf16[2560,640]{1,0:T(8,128)(2,1)}, u32[]{:S(2)}, u32[]{:S(2)}) collective-permute-start(bf16[2560,640]{1,0:T(8,128)(2,1)} %param.16), channel_id=1, source_target_pairs={{0,1},{1,0},{2,3},{3,2},{4,5},{5,4},{6,7},{7,6},{8,9},{9,8},{10,11... | collective-permute-start | bytes 9830408 | tf_op jit(solution)/shard_map/ppermute | solution.py:74
  47.9 38.2 %collective-permute-start.12 = (bf16[1280,640]{1,0:T(8,128)(2,1)}, bf16[1280,640]{1,0:T(8,128)(2,1)}, u32[]{:S(2)}, u32[]{:S(2)}) collective-permute-start(bf16[1280,640]{1,0:T(8,128)(2,1)} %get-tuple-element.83), channel_id=1, source_target_pairs={{0,2},{1,3},{2,0},{3,1},{4,6},{5,7},{6,4},{7,5},{8,10},{9,11},{10,... | collective-permute-start | bytes 4915208 | tf_op jit(solution)/shard_map/ppermute | solution.py:74
  48.6 46.8 %collective-permute-start.11 = (bf16[1280,640]{1,0:T(8,128)(2,1)}, bf16[1280,640]{1,0:T(8,128)(2,1)}, u32[]{:S(2)}, u32[]{:S(2)}) collective-permute-start(bf16[1280,640]{1,0:T(8,128)(2,1)} %get-tuple-element.82), channel_id=1, source_target_pairs={{0,1},{1,0},{2,3},{3,2},{4,5},{5,4},{6,7},{7,6},{8,9},{9,8},{10,11... | collective-permute-start | bytes 4915208 | tf_op jit(solution)/shard_map/ppermute | solution.py:74
  86.1 32.0 %collective-permute-start.62 = (bf16[256,2560]{1,0:T(8,128)(2,1)}, bf16[256,2560]{1,0:T(8,128)(2,1)}, u32[]{:S(2)}, u32[]{:S(2)}) collective-permute-start(bf16[256,2560]{1,0:T(8,128)(2,1)} %pad_maximum_fusion.5), channel_id=1, source_target_pairs={{0,4},{1,5},{2,6},{3,7},{4,0},{5,1},{6,2},{7,3},{8,12},{9,13},{10,... | collective-permute-start | bytes 3932168 | tf_op jit(solution)/shard_map/ppermute | solution.py:74
  111.4 374.4 %collective-permute-start.39 = (bf16[512,1280]{0,1:T(8,128)(2,1)}, bf16[512,1280]{0,1:T(8,128)(2,1)}, u32[]{:S(2)}, u32[]{:S(2)}) collective-permute-start(bf16[512,1280]{0,1:T(8,128)(2,1)} %bitcast.17), channel_id=1, source_target_pairs={{0,4},{1,5},{2,6},{3,7},{4,0},{5,1},{6,2},{7,3},{8,12},{9,13},{10,... | collective-permute-start | bytes 3932168 | tf_op jit(solution)/shard_map/ppermute | solution.py:74
  151.3 35.9 %collective-permute-start.17 = (bf16[128,2560]{1,0:T(8,128)(2,1)}, bf16[128,2560]{1,0:T(8,128)(2,1)S(1)}, u32[]{:S(2)}, u32[]{:S(2)}) collective-permute-start(bf16[128,2560]{1,0:T(8,128)(2,1)} %get-tuple-element.50), channel_id=1, source_target_pairs={{0,2},{1,3},{2,0},{3,1},{4,6},{5,7},{6,4},{7,5},{8,10},{9,11},{10,... | collective-permute-start | bytes 1966088 | tf_op jit(solution)/shard_map/ppermute | solution.py:74
  180.9 55.1 %collective-permute-start.22 = (bf16[128,2560]{1,0:T(8,128)(2,1)S(1)}, bf16[128,2560]{1,0:T(8,128)(2,1)S(1)}, u32[]{:S(2)}, u32[]{:S(2)}) collective-permute-start(bf16[128,2560]{1,0:T(8,128)(2,1)S(1)} %slice.427), channel_id=1, source_target_pairs={{0,1},{1,0},{2,3},{3,2},{4,5},{5,4},{6,7},{7,6},{8,9},{9,8},{10,11... | collective-permute-start | bytes 1966088 | tf_op jit(solution)/shard_map/ppermute | solution.py:74
  186.7 61.2 %collective-permute-start.16 = (bf16[128,2560]{1,0:T(8,128)(2,1)S(1)}, bf16[128,2560]{1,0:T(8,128)(2,1)}, u32[]{:S(2)}, u32[]{:S(2)}) collective-permute-start(bf16[128,2560]{1,0:T(8,128)(2,1)S(1)} %slice.429), channel_id=1, source_target_pairs={{0,1},{1,0},{2,3},{3,2},{4,5},{5,4},{6,7},{7,6},{8,9},{9,8},{10,11... | collective-permute-start | bytes 1966088 | tf_op jit(solution)/shard_map/ppermute | solution.py:74
  236.0 33.0 %collective-permute-start.46 = (bf16[256,1280]{1,0:T(8,128)(2,1)S(1)}, bf16[256,1280]{1,0:T(8,128)(2,1)}, u32[]{:S(2)}, u32[]{:S(2)}) collective-permute-start(bf16[256,1280]{1,0:T(8,128)(2,1)S(1)} %bitcast.213), channel_id=1, source_target_pairs={{0,1},{1,0},{2,3},{3,2},{4,5},{5,4},{6,7},{7,6},{8,9},{9,8},{10,11... | collective-permute-start | bytes 1966088 | tf_op jit(solution)/shard_map/ppermute | solution.py:74
  247.9 32.0 %collective-permute-start.60 = (bf16[256,2560]{1,0:T(8,128)(2,1)}, bf16[256,2560]{1,0:T(8,128)(2,1)}, u32[]{:S(2)}, u32[]{:S(2)}) collective-permute-start(bf16[256,2560]{1,0:T(8,128)(2,1)} %pad_maximum_fusion.3), channel_id=1, source_target_pairs={{0,4},{1,5},{2,6},{3,7},{4,0},{5,1},{6,2},{7,3},{8,12},{9,13},{10,... | collective-permute-start | bytes 3932168 | tf_op jit(solution)/shard_map/ppermute | solution.py:74
  273.7 202.8 %collective-permute-start.43 = (bf16[512,640]{1,0:T(8,128)(2,1)}, bf16[512,640]{1,0:T(8,128)(2,1)}, u32[]{:S(2)}, u32[]{:S(2)}) collective-permute-start(bf16[512,640]{1,0:T(8,128)(2,1)} %get-tuple-element.95), channel_id=1, source_target_pairs={{0,4},{1,5},{2,6},{3,7},{4,0},{5,1},{6,2},{7,3},{8,12},{9,13},{10,... | collective-permute-start | bytes 1966088 | tf_op jit(solution)/shard_map/ppermute | solution.py:74
  292.4 68.8 %collective-permute-start.28 = (f32[4,1280]{1,0:T(4,128)S(1)}, f32[4,1280]{1,0:T(4,128)S(1)}, u32[]{:S(2)}, u32[]{:S(2)}) collective-permute-start(f32[4,1280]{1,0:T(4,128)S(1)} %get-tuple-element.33), channel_id=1, source_target_pairs={{0,4},{1,5},{2,6},{3,7},{4,0},{5,1},{6,2},{7,3},{8,12},{9,13},{10,... | collective-permute-start | bytes 61448 | tf_op jit(solution)/shard_map/ppermute | solution.py:74
  296.6 97.9 %collective-permute-start.44 = (bf16[256,1280]{1,0:T(8,128)(2,1)}, bf16[256,1280]{1,0:T(8,128)(2,1)}, u32[]{:S(2)}, u32[]{:S(2)}) collective-permute-start(bf16[256,1280]{1,0:T(8,128)(2,1)} %get-tuple-element.97), channel_id=1, source_target_pairs={{0,1},{1,0},{2,3},{3,2},{4,5},{5,4},{6,7},{7,6},{8,9},{9,8},{10,11... | collective-permute-start | bytes 1966088 | tf_op jit(solution)/shard_map/ppermute | solution.py:74
  396.9 81.3 %collective-permute-start.45 = (bf16[512,1280]{1,0:T(8,128)(2,1)}, bf16[512,1280]{1,0:T(8,128)(2,1)}, u32[]{:S(2)}, u32[]{:S(2)}) collective-permute-start(bf16[512,1280]{1,0:T(8,128)(2,1)} %pad_maximum_fusion.11), channel_id=1, source_target_pairs={{0,4},{1,5},{2,6},{3,7},{4,0},{5,1},{6,2},{7,3},{8,12},{9,13},{10,... | collective-permute-start | bytes 3932168 | tf_op jit(solution)/shard_map/ppermute | solution.py:74
  412.9 72.9 %collective-permute-start.41 = (bf16[512,1280]{1,0:T(8,128)(2,1)}, bf16[512,1280]{1,0:T(8,128)(2,1)}, u32[]{:S(2)}, u32[]{:S(2)}) collective-permute-start(bf16[512,1280]{1,0:T(8,128)(2,1)} %pad_maximum_fusion.10), channel_id=1, source_target_pairs={{0,4},{1,5},{2,6},{3,7},{4,0},{5,1},{6,2},{7,3},{8,12},{9,13},{10,... | collective-permute-start | bytes 3932168 | tf_op jit(solution)/shard_map/ppermute | solution.py:74
  421.9 41.8 %collective-permute-start.48 = (bf16[640,256]{1,0:T(8,128)(2,1)S(1)}, bf16[640,256]{1,0:T(8,128)(2,1)S(1)}, u32[]{:S(2)}, u32[]{:S(2)}) collective-permute-start(bf16[640,256]{1,0:T(8,128)(2,1)S(1)} %dynamic-slice_convert_fusion), channel_id=1, source_target_pairs={{0,4},{1,5},{2,6},{3,7},{4,0},{5,1},{6,2},{7,3},{8,12},{9,13},{10,... | collective-permute-start | bytes 983048 | tf_op jit(solution)/shard_map/ppermute | solution.py:74
  470.1 62.9 %collective-permute-start.64 = (bf16[320,1920]{1,0:T(8,128)(2,1)}, bf16[320,1920]{1,0:T(8,128)(2,1)}, u32[]{:S(2)}, u32[]{:S(2)}) collective-permute-start(bf16[320,1920]{1,0:T(8,128)(2,1)} %get-tuple-element.74), channel_id=1, source_target_pairs={{0,8},{1,9},{2,10},{3,11},{4,12},{5,13},{6,14},{7,15}} | collective-permute-start | bytes 3686408 | tf_op jit(solution)/shard_map/ppermute | solution.py:74
  476.4 66.4 %collective-permute-start.67 = (bf16[320,1920]{1,0:T(8,128)(2,1)}, bf16[320,1920]{1,0:T(8,128)(2,1)}, u32[]{:S(2)}, u32[]{:S(2)}) collective-permute-start(bf16[320,1920]{1,0:T(8,128)(2,1)} %get-tuple-element.75), channel_id=1, source_target_pairs={{24,16},{25,17},{26,18},{27,19},{28,20},{29,21},{30,22},{31,23}} | collective-permute-start | bytes 3686408 | tf_op jit(solution)/shard_map/ppermute | solution.py:74
  478.2 61.4 %collective-permute-start.70 = (bf16[320,1920]{1,0:T(8,128)(2,1)}, bf16[320,1920]{1,0:T(8,128)(2,1)}, u32[]{:S(2)}, u32[]{:S(2)}) collective-permute-start(bf16[320,1920]{1,0:T(8,128)(2,1)} %get-tuple-element.70), channel_id=1, source_target_pairs={{0,8},{1,9},{2,10},{3,11},{4,12},{5,13},{6,14},{7,15}} | collective-permute-start | bytes 3686408 | tf_op jit(solution)/shard_map/ppermute | solution.py:74
  485.8 45.6 %collective-permute-start.36 = (f32[10,2560]{1,0:T(8,128)}, f32[10,2560]{1,0:T(8,128)S(1)}, u32[]{:S(2)}, u32[]{:S(2)}) collective-permute-start(f32[10,2560]{1,0:T(8,128)} %add.458), channel_id=1, source_target_pairs={{0,8},{1,9},{2,10},{3,11},{4,12},{5,13},{6,14},{7,15},{8,0},{9,1},... | collective-permute-start | bytes 307208 | tf_op jit(solution)/shard_map/ppermute | solution.py:74
  495.8 63.6 %collective-permute-start.49 = (bf16[512,1280]{1,0:T(8,128)(2,1)S(1)}, bf16[512,1280]{1,0:T(8,128)(2,1)S(1)}, u32[]{:S(2)}, u32[]{:S(2)}) collective-permute-start(bf16[512,1280]{1,0:T(8,128)(2,1)S(1)} %get-tuple-element.62), channel_id=1, source_target_pairs={{0,8},{1,9},{2,10},{3,11},{4,12},{5,13},{6,14},{7,15}} | collective-permute-start | bytes 3932168 | tf_op jit(solution)/shard_map/ppermute | solution.py:74
  531.3 89.2 %collective-permute-start.73 = (bf16[320,1920]{1,0:T(8,128)(2,1)S(1)}, bf16[320,1920]{1,0:T(8,128)(2,1)S(1)}, u32[]{:S(2)}, u32[]{:S(2)}) collective-permute-start(bf16[320,1920]{1,0:T(8,128)(2,1)S(1)} %copy-done.42), channel_id=1, source_target_pairs={{24,16},{25,17},{26,18},{27,19},{28,20},{29,21},{30,22},{31,23}} | collective-permute-start | bytes 3686408 | tf_op jit(solution)/shard_map/ppermute | solution.py:74
  533.0 52.6 %collective-permute-start.76 = (bf16[320,1920]{1,0:T(8,128)(2,1)S(1)}, bf16[320,1920]{1,0:T(8,128)(2,1)S(1)}, u32[]{:S(2)}, u32[]{:S(2)}) collective-permute-start(bf16[320,1920]{1,0:T(8,128)(2,1)S(1)} %copy-done.44), channel_id=1, source_target_pairs={{0,8},{1,9},{2,10},{3,11},{4,12},{5,13},{6,14},{7,15}} | collective-permute-start | bytes 3686408 | tf_op jit(solution)/shard_map/ppermute | solution.py:74
  539.5 78.4 %collective-permute-start.65 = (bf16[320,1920]{1,0:T(8,128)(2,1)S(1)}, bf16[320,1920]{1,0:T(8,128)(2,1)S(1)}, u32[]{:S(2)}, u32[]{:S(2)}) collective-permute-start(bf16[320,1920]{1,0:T(8,128)(2,1)S(1)} %fusion.53), channel_id=1, source_target_pairs={{0,8},{1,9},{2,10},{3,11},{4,12},{5,13},{6,14},{7,15},{8,16},{9,17... | collective-permute-start | bytes 3686408 | tf_op jit(solution)/shard_map/ppermute | solution.py:74
  542.8 72.7 %collective-permute-start.37 = (f32[10,2560]{1,0:T(8,128)S(1)}, f32[10,2560]{1,0:T(8,128)S(1)}, u32[]{:S(2)}, u32[]{:S(2)}) collective-permute-start(f32[10,2560]{1,0:T(8,128)S(1)} %add.459), channel_id=1, source_target_pairs={{0,16},{1,17},{2,18},{3,19},{4,20},{5,21},{6,22},{7,23},{8,24},{9,... | collective-permute-start | bytes 307208 | tf_op jit(solution)/shard_map/ppermute | solution.py:74
  559.3 82.5 %collective-permute-start.71 = (bf16[320,1920]{1,0:T(8,128)(2,1)S(1)}, bf16[320,1920]{1,0:T(8,128)(2,1)S(1)}, u32[]{:S(2)}, u32[]{:S(2)}) collective-permute-start(bf16[320,1920]{1,0:T(8,128)(2,1)S(1)} %fusion.48), channel_id=1, source_target_pairs={{0,8},{1,9},{2,10},{3,11},{4,12},{5,13},{6,14},{7,15},{8,16},{9,17... | collective-permute-start | bytes 3686408 | tf_op jit(solution)/shard_map/ppermute | solution.py:74
  585.7 59.8 %collective-permute-start.52 = (bf16[512,1280]{1,0:T(8,128)(2,1)S(1)}, bf16[512,1280]{1,0:T(8,128)(2,1)S(1)}, u32[]{:S(2)}, u32[]{:S(2)}) collective-permute-start(bf16[512,1280]{1,0:T(8,128)(2,1)S(1)} %get-tuple-element.63), channel_id=1, source_target_pairs={{24,16},{25,17},{26,18},{27,19},{28,20},{29,21},{30,22},{31,23}} | collective-permute-start | bytes 3932168 | tf_op jit(solution)/shard_map/ppermute | solution.py:74
  615.5 54.4 %collective-permute-start.50 = (bf16[512,1280]{1,0:T(8,128)(2,1)S(1)}, bf16[512,1280]{1,0:T(8,128)(2,1)S(1)}, u32[]{:S(2)}, u32[]{:S(2)}) collective-permute-start(bf16[512,1280]{1,0:T(8,128)(2,1)S(1)} %fusion.37), channel_id=1, source_target_pairs={{0,8},{1,9},{2,10},{3,11},{4,12},{5,13},{6,14},{7,15},{8,16},{9,17... | collective-permute-start | bytes 3932168 | tf_op jit(solution)/shard_map/ppermute | solution.py:74
  617.9 53.5 %collective-permute-start.79 = (bf16[320,1920]{1,0:T(8,128)(2,1)S(1)}, bf16[320,1920]{1,0:T(8,128)(2,1)S(1)}, u32[]{:S(2)}, u32[]{:S(2)}) collective-permute-start(bf16[320,1920]{1,0:T(8,128)(2,1)S(1)} %copy-done.43), channel_id=1, source_target_pairs={{24,16},{25,17},{26,18},{27,19},{28,20},{29,21},{30,22},{31,23}} | collective-permute-start | bytes 3686408 | tf_op jit(solution)/shard_map/ppermute | solution.py:74
  620.6 75.7 %collective-permute-start.77 = (bf16[320,1920]{1,0:T(8,128)(2,1)S(1)}, bf16[320,1920]{1,0:T(8,128)(2,1)}, u32[]{:S(2)}, u32[]{:S(2)}) collective-permute-start(bf16[320,1920]{1,0:T(8,128)(2,1)S(1)} %fusion.43), channel_id=1, source_target_pairs={{0,8},{1,9},{2,10},{3,11},{4,12},{5,13},{6,14},{7,15},{8,16},{9,17... | collective-permute-start | bytes 3686408 | tf_op jit(solution)/shard_map/ppermute | solution.py:74
  642.9 57.6 %collective-permute-start.68 = (bf16[320,1920]{1,0:T(8,128)(2,1)S(1)}, bf16[320,1920]{1,0:T(8,128)(2,1)S(1)}, u32[]{:S(2)}, u32[]{:S(2)}) collective-permute-start(bf16[320,1920]{1,0:T(8,128)(2,1)S(1)} %get-tuple-element.73), channel_id=1, source_target_pairs={{16,8},{17,9},{18,10},{19,11},{20,12},{21,13},{22,14},{23,15},{24,... | collective-permute-start | bytes 3686408 | tf_op jit(solution)/shard_map/ppermute | solution.py:74
  645.5 77.1 %collective-permute-start.66 = (bf16[320,1920]{1,0:T(8,128)(2,1)S(1)}, bf16[320,1920]{1,0:T(8,128)(2,1)S(1)}, u32[]{:S(2)}, u32[]{:S(2)}) collective-permute-start(bf16[320,1920]{1,0:T(8,128)(2,1)S(1)} %get-tuple-element.72), channel_id=1, source_target_pairs={{0,8},{1,9},{2,10},{3,11},{4,12},{5,13},{6,14},{7,15},{8,16},{9,17... | collective-permute-start | bytes 3686408 | tf_op jit(solution)/shard_map/ppermute | solution.py:74
  669.9 31.6 %collective-permute-start.74 = (bf16[320,1920]{1,0:T(8,128)(2,1)S(1)}, bf16[320,1920]{1,0:T(8,128)(2,1)S(1)}, u32[]{:S(2)}, u32[]{:S(2)}) collective-permute-start(bf16[320,1920]{1,0:T(8,128)(2,1)S(1)} %get-tuple-element.69), channel_id=1, source_target_pairs={{16,8},{17,9},{18,10},{19,11},{20,12},{21,13},{22,14},{23,15},{24,... | collective-permute-start | bytes 3686408 | tf_op jit(solution)/shard_map/ppermute | solution.py:74
  671.4 118.7 %collective-permute-start.72 = (bf16[320,1920]{1,0:T(8,128)(2,1)S(1)}, bf16[320,1920]{1,0:T(8,128)(2,1)S(1)}, u32[]{:S(2)}, u32[]{:S(2)}) collective-permute-start(bf16[320,1920]{1,0:T(8,128)(2,1)S(1)} %get-tuple-element.68), channel_id=1, source_target_pairs={{0,8},{1,9},{2,10},{3,11},{4,12},{5,13},{6,14},{7,15},{8,16},{9,17... | collective-permute-start | bytes 3686408 | tf_op jit(solution)/shard_map/ppermute | solution.py:74
  700.5 36.4 %collective-permute-start.80 = (bf16[320,1920]{1,0:T(8,128)(2,1)}, bf16[320,1920]{1,0:T(8,128)(2,1)S(1)}, u32[]{:S(2)}, u32[]{:S(2)}) collective-permute-start(bf16[320,1920]{1,0:T(8,128)(2,1)} %get-tuple-element.65), channel_id=1, source_target_pairs={{16,8},{17,9},{18,10},{19,11},{20,12},{21,13},{22,14},{23,15},{24,... | collective-permute-start | bytes 3686408 | tf_op jit(solution)/shard_map/ppermute | solution.py:74
  701.6 37.0 %collective-permute-start.69 = (bf16[320,1920]{1,0:T(8,128)(2,1)S(1)}, bf16[320,1920]{1,0:T(8,128)(2,1)S(1)}, u32[]{:S(2)}, u32[]{:S(2)}) collective-permute-start(bf16[320,1920]{1,0:T(8,128)(2,1)S(1)} %fusion.52), channel_id=1, source_target_pairs={{8,0},{9,1},{10,2},{11,3},{12,4},{13,5},{14,6},{15,7},{16,8},{17,9... | collective-permute-start | bytes 3686408 | tf_op jit(solution)/shard_map/ppermute | solution.py:74
  703.2 88.2 %collective-permute-start.75 = (bf16[320,1920]{1,0:T(8,128)(2,1)S(1)}, bf16[320,1920]{1,0:T(8,128)(2,1)S(1)}, u32[]{:S(2)}, u32[]{:S(2)}) collective-permute-start(bf16[320,1920]{1,0:T(8,128)(2,1)S(1)} %fusion.47), channel_id=1, source_target_pairs={{8,0},{9,1},{10,2},{11,3},{12,4},{13,5},{14,6},{15,7},{16,8},{17,9... | collective-permute-start | bytes 3686408 | tf_op jit(solution)/shard_map/ppermute | solution.py:74
  722.6 70.7 %collective-permute-start.51 = (bf16[512,1280]{1,0:T(8,128)(2,1)S(1)}, bf16[512,1280]{1,0:T(8,128)(2,1)S(1)}, u32[]{:S(2)}, u32[]{:S(2)}) collective-permute-start(bf16[512,1280]{1,0:T(8,128)(2,1)S(1)} %get-tuple-element.60), channel_id=1, source_target_pairs={{0,8},{1,9},{2,10},{3,11},{4,12},{5,13},{6,14},{7,15},{8,16},{9,17... | collective-permute-start | bytes 3932168 | tf_op jit(solution)/shard_map/ppermute | solution.py:74
  737.0 56.3 %collective-permute-start.54 = (bf16[512,1280]{1,0:T(8,128)(2,1)S(1)}, bf16[512,1280]{1,0:T(8,128)(2,1)S(1)}, u32[]{:S(2)}, u32[]{:S(2)}) collective-permute-start(bf16[512,1280]{1,0:T(8,128)(2,1)S(1)} %fusion.36), channel_id=1, source_target_pairs={{8,0},{9,1},{10,2},{11,3},{12,4},{13,5},{14,6},{15,7},{16,8},{17,9... | collective-permute-start | bytes 3932168 | tf_op jit(solution)/shard_map/ppermute | solution.py:74
  738.6 107.2 %collective-permute-start.78 = (bf16[320,1920]{1,0:T(8,128)(2,1)}, bf16[320,1920]{1,0:T(8,128)(2,1)}, u32[]{:S(2)}, u32[]{:S(2)}) collective-permute-start(bf16[320,1920]{1,0:T(8,128)(2,1)} %get-tuple-element.64), channel_id=1, source_target_pairs={{0,8},{1,9},{2,10},{3,11},{4,12},{5,13},{6,14},{7,15},{8,16},{9,17... | collective-permute-start | bytes 3686408 | tf_op jit(solution)/shard_map/ppermute | solution.py:74
  790.1 55.6 %collective-permute-start.81 = (bf16[320,1920]{1,0:T(8,128)(2,1)S(1)}, bf16[320,1920]{1,0:T(8,128)(2,1)}, u32[]{:S(2)}, u32[]{:S(2)}) collective-permute-start(bf16[320,1920]{1,0:T(8,128)(2,1)S(1)} %fusion.42), channel_id=1, source_target_pairs={{8,0},{9,1},{10,2},{11,3},{12,4},{13,5},{14,6},{15,7},{16,8},{17,9... | collective-permute-start | bytes 3686408 | tf_op jit(solution)/shard_map/ppermute | solution.py:74
  794.7 50.7 %collective-permute-start.55 = (bf16[2,80,1280]{2,1,0:T(8,128)(2,1)S(1)}, bf16[2,80,1280]{2,1,0:T(8,128)(2,1)S(1)}, u32[]{:S(2)}, u32[]{:S(2)}) collective-permute-start(bf16[2,80,1280]{2,1,0:T(8,128)(2,1)S(1)} %dynamic-slice_bitcast_fusion.8), channel_id=1, source_target_pairs={{0,1},{1,0},{2,3},{3,2},{4,5},{5,4},{6,7},{7,6},{8,9},{9,8},{10,11... | collective-permute-start | bytes 1228808 | tf_op jit(solution)/shard_map/ppermute | solution.py:74
  795.9 65.8 %collective-permute-start.59 = (bf16[80,3072]{1,0:T(8,128)(2,1)S(1)}, bf16[80,3072]{1,0:T(8,128)(2,1)S(1)}, u32[]{:S(2)}, u32[]{:S(2)}) collective-permute-start(bf16[80,3072]{1,0:T(8,128)(2,1)S(1)} %pad_maximum_fusion.16), channel_id=1, source_target_pairs={{0,0},{1,1},{2,16},{3,17},{4,8},{5,9},{6,24},{7,25},{8,2},{9,3},{1... | collective-permute-start | bytes 1474568 | tf_op jit(solution)/shard_map/ppermute | solution.py:74
  845.6 29.7 %collective-permute-start.56 = (bf16[2,80,1280]{2,1,0:T(8,128)(2,1)S(1)}, bf16[2,80,1280]{2,1,0:T(8,128)(2,1)S(1)}, u32[]{:S(2)}, u32[]{:S(2)}) collective-permute-start(bf16[2,80,1280]{2,1,0:T(8,128)(2,1)S(1)} %get-tuple-element.112), channel_id=1, source_target_pairs={{0,2},{1,3},{2,0},{3,1},{4,6},{5,7},{6,4},{7,5},{8,10},{9,11},{10,... | collective-permute-start | bytes 1228808 | tf_op jit(solution)/shard_map/ppermute | solution.py:74
  (135 other events, 1852.4 us)

commit v2 on v1

--- a/solution.py
+++ b/solution.py
@@ -88,6 +88,9 @@
             return (other // 2, other % 2, x, c)
 
         return self.send(value, to)
+
+    def over_z(self, value):
+        return self.send(value, lambda z, y, x, c: (self.nz - 1 - z, y, x, c))
 
     def over_seq(self, value, by):
         def to(z, y, x, c):
@@ -388,42 +391,68 @@
         grad_up = (grad_hidden * gelu).astype(BF16)
         return hidden, grad_gate, grad_up
 
-    near_n2, near_cot = (jnp.concatenate([n2, n2_c], 0), jnp.concatenate([cot, cot_c], 0))
-    far_n2, far_cot = (jnp.concatenate([n2_x, n2_xc], 0), jnp.concatenate([cot_x, cot_xc], 0))
-    near = mlp(near_n2, near_cot)
-    far = mlp(far_n2, far_cot)
+    main_n2 = jnp.concatenate([n2, n2_c, n2_x, n2_xc], 0)
+    main_cot = jnp.concatenate([cot, cot_c, cot_x, cot_xc], 0)
+    main = mlp(main_n2, main_cot)
 
     def to_owners(of):
-        far_part = of(far)
+        far_part = of(slice(two, 2 * two))
         far_sum = far_part[:tokens] + lay.over_c(far_part[tokens:].astype(BF16)).astype(F32)
         arriving = lay.over_x(far_sum.astype(BF16))
-        near_part = of(near)
+        near_part = of(slice(0, two))
         near_sum = near_part[:tokens] + lay.over_c(near_part[tokens:].astype(BF16)).astype(F32)
         return near_sum + arriving.astype(F32)
 
-    grad_n2 = to_owners(lambda t: dot_cols(t[1], mlp_gate) + dot_cols(t[2], mlp_up))
-    output = (mid + to_owners(lambda t: dot_cols(t[0], mlp_down))).astype(BF16)[None]
-
-    n2_y = lay.over_y(jnp.concatenate([n2, n2_x], 0))
-    cot_y = lay.over_y(jnp.concatenate([cot, cot_x], 0))
-    n2_y = jnp.concatenate([n2_y, lay.over_c(n2_y)], 0)
-    cot_y = jnp.concatenate([cot_y, lay.over_c(cot_y)], 0)
-    side = mlp(n2_y, cot_y)
+    grad_n2 = to_owners(
+        lambda rows: dot_cols(main[1][rows], mlp_gate) + dot_cols(main[2][rows], mlp_up))
+    output = (mid + to_owners(lambda rows: dot_cols(main[0][rows], mlp_down))).astype(BF16)[None]
+
+    n2_z, n2_xz = (lay.over_z(n2), lay.over_z(n2_x))
+    cot_z, cot_xz = (lay.over_z(cot), lay.over_z(cot_x))
+    side_n2 = jnp.concatenate([n2_z, lay.over_c(n2_z), n2_xz, lay.over_c(n2_xz)], 0)
+    side_cot = jnp.concatenate([cot_z, lay.over_c(cot_z), cot_xz, lay.over_c(cot_xz)], 0)
+    side = mlp(side_n2, side_cot)
     each = width // lay.seq
-
-    def rows_of_y(value, which):
-        return lax.dynamic_index_in_dim(
-            value.reshape(value.shape[0], nz, 2, each), which, 2, keepdims=False
-        ).reshape(value.shape[0], nz * each)
-
-    n2_rows = rows_of_y(jnp.concatenate([near_n2, far_n2, n2_y], 0), y)
-    cot_rows = rows_of_y(jnp.concatenate([near_cot, far_cot, cot_y], 0), y)
-    hidden_all, gg_all, gu_all = [
-        jnp.concatenate([near[i], far[i], side[i]], 0) for i in range(3)]
+    seq_at = 2 * z + y
+    upper = seq_at // nz
+
+    def window(value):
+        return lax.dynamic_slice_in_dim(value, upper * half, half, 1)
+
+    n2_rows = jnp.concatenate([window(main_n2), window(side_n2)], 0)
+    cot_rows = jnp.concatenate([window(main_cot), window(side_cot)], 0)
+    hidden_all, gg_all, gu_all = [jnp.concatenate([main[i], side[i]], 0) for i in range(3)]
+
+    def halve(blocks, bits):
+        own = seq_at % nz
+
+        def pick(j):
+            return lax.dynamic_index_in_dim(blocks, own ^ j, 0, keepdims=False).astype(F32)
+
+        def joined(old, come, at):
+            return old() + come[at].astype(F32)
+
+        held = {j: functools.partial(pick, j) for j in range(nz)}
+        for bit in bits:
+            leaving = sorted(j for j in held if j & bit)
+            sent = jnp.stack([held[j]().astype(BF16) for j in leaving])
+            come = lay.over_seq_bit(sent, bit)
+            held = {
+                j ^ bit: functools.partial(joined, held[j ^ bit], come, i)
+                for i, j in enumerate(leaving)
+            }
+        return held[0]()
+
+    bits = []
+    bit = 1
+    while bit < nz:
+        bits.append(bit)
+        bit *= 2
     mlp_grads = []
-    for left, right in ((cot_rows, hidden_all), (n2_rows, gg_all), (n2_rows, gu_all)):
+    for left, right, order in (
+        (cot_rows, hidden_all, bits), (n2_rows, gg_all, bits[::-1]), (n2_rows, gu_all, bits)):
         part = dot_rows(left, right).astype(BF16).reshape(nz, each, right.shape[1])
-        mlp_grads.append(line_sum(lay, part))
+        mlp_grads.append(halve(part, order))
     mlp_down_grad, mlp_gate_grad, mlp_up_grad = mlp_grads
 
     grad_mid_norm, grad_gain_two = norm_back(grad_n2, scaled_two, inverse_two, vectors[1])
@@ -476,73 +505,68 @@
         vec = vec + lay.over_seq_bit(vec, bit)
         bit *= 2
 
-    n1_two = jnp.concatenate([normed_own, normed_x], 0)
-    n1_four = jnp.concatenate([n1_two, lay.over_c(n1_two)], 0)
-    n1_rows = jnp.concatenate(
-        [rows_of_y(n1_four, y), lay.over_y(rows_of_y(n1_four, 1 - y))], 0)
-    keep = jnp.where(first, gy, gx)
-    g_four = jnp.concatenate([keep, lay.over_c(jnp.where(first, gx, gy))], 0)
-    g_all = jnp.concatenate([g_four, lay.over_y(g_four)], 0)
-    in_part = dot_rows(n1_rows, g_all).astype(BF16).reshape(nz, each, half)
-
-    mixed_two = mixed.reshape(two, half)
-    mixed_four = jnp.concatenate([mixed_two, lay.over_c(mixed_two)], 0)
-    branch_two = jnp.concatenate([branch, order_f(branch_x_rel)], 0)
-
-    def half_cols(value, which, n):
-        return lax.dynamic_slice_in_dim(value, which * n, n, 1)
-
-    branch_four = jnp.concatenate(
-        [half_cols(branch_two, c, half), lay.over_c(half_cols(branch_two, 1 - c, half))], 0)
-    mixed_rows = jnp.concatenate(
-        [half_cols(mixed_four, y, quarter), lay.over_y(half_cols(mixed_four, 1 - y, quarter))], 0)
-    branch_all = jnp.concatenate([branch_four, lay.over_y(branch_four)], 0)
-    fine = quarter // nz
-    out_part = dot_rows(mixed_rows, branch_all).astype(BF16).reshape(nz, fine, half)
-
-    conv_two = conv_low.reshape(two, half)
-    conv_four = jnp.concatenate([conv_two, lay.over_c(conv_two)], 0)
-    gip2, gdp2 = (gip.reshape(two, half), gdp.reshape(two, half))
-    gp_four = jnp.concatenate(
-        [jnp.where(first, gip2, gdp2), lay.over_c(jnp.where(first, gdp2, gip2))], 0)
+    own80 = each // 4
+
+    def spread_rows(value, where):
+        by_yc = where(value.T)
+        by_c = lax.dynamic_index_in_dim(by_yc, c, 1, keepdims=False)
+        other_c = lax.dynamic_index_in_dim(by_yc, 1 - c, 1, keepdims=False)
+        pair = jnp.concatenate([by_c, lay.over_c(other_c)], axis=2)
+        by_y = lax.dynamic_index_in_dim(pair, y, 0, keepdims=False)
+        other_y = lax.dynamic_index_in_dim(pair, 1 - y, 0, keepdims=False)
+        return jnp.concatenate([by_y, lay.over_y(other_y)], axis=1)
+
+    def all_tokens(value):
+        other_y = lay.over_y(value)
+        return jnp.concatenate([value, lay.over_c(value), other_y, lay.over_c(other_y)], 0)
+
+    def where_n1(rows):
+        split = rows.reshape(nz, 2, 2, 2, own80, two)
+        return split.transpose(1, 3, 0, 2, 4, 5).reshape(2, 2, nz * 2 * own80, two)
+
+    def where_mixed(rows):
+        split = rows.reshape(2, nz, 2, own80, two)
+        return split.transpose(0, 2, 1, 3, 4).reshape(2, 2, nz * own80, two)
+
+    n1_rows = spread_rows(jnp.concatenate([normed_own, normed_x], 0), where_n1)
+    mixed_rows = spread_rows(mixed.reshape(two, half), where_mixed)
+    branch_all = all_tokens(jnp.concatenate([branch, order_f(branch_x_rel)], 0))
+    out_part = dot(mixed_rows, branch_all).astype(BF16).reshape(nz, 2 * own80, half)
+    in_y_part = dot(n1_rows, all_tokens(gy)).astype(BF16).reshape(nz, 2 * own80, half)
+    done_one = line_sum(lay, jnp.concatenate([in_y_part, out_part], axis=1)).astype(BF16)
+
     heads = half // BLK
     gate_part = jnp.einsum(
-        "thi,thj->hij", conv_four.reshape(2 * two, heads, BLK),
-        gp_four.reshape(2 * two, heads, BLK), preferred_element_type=F32).reshape(half, BLK)
-    gate_keep = lax.dynamic_slice_in_dim(gate_part, y * quarter, quarter, 0)
-    gate_send = lax.dynamic_slice_in_dim(gate_part, (1 - y) * quarter, quarter, 0).astype(BF16)
-    gate_sum = (gate_keep + lay.over_y(gate_send).astype(F32)).astype(BF16)
-    gate_sum = gate_sum.reshape(nz, fine * BLK // half, half)
-
-    done = line_sum(lay, jnp.concatenate([in_part, out_part, gate_sum], axis=1)).astype(BF16)
-    own80 = each // 4
-    in_done = done[:each].reshape(2, 2, own80, half)
-    out_done = done[each : each + fine].reshape(2, own80, half)
-    gate_done = done[each + fine :].reshape(2, own80, BLK)
-
-    def by_core(value, axis):
-        mine = lax.dynamic_index_in_dim(value, c, axis, keepdims=False)
-        theirs = lax.dynamic_index_in_dim(value, 1 - c, axis, keepdims=False)
-        return mine, lay.over_c(theirs)
-
-    in_keep, in_recv = by_core(in_done, 1)
-    out_keep, out_recv = by_core(out_done, 0)
-    gate_keep, gate_recv = by_core(gate_done, 0)
-    both = jnp.stack([jnp.where(first, in_keep, in_recv), jnp.where(first, in_recv, in_keep)])
-    mine = lax.dynamic_index_in_dim(both, x, 1, keepdims=False)
-    theirs = lay.over_x(lax.dynamic_index_in_dim(both, 1 - x, 1, keepdims=False))
-    in_full = jnp.where(x == 0, jnp.concatenate([mine, theirs], -1),
-                        jnp.concatenate([theirs, mine], -1)).astype(F32)
-    last = jnp.concatenate(
-        [order_c(out_keep, out_recv, 1), order_c(gate_keep, gate_recv, 1)], axis=1)
-
+        "thi,thj->hij", conv_low.reshape(two, heads, BLK),
+        jnp.concatenate([gip.reshape(two, heads, BLK), gdp.reshape(two, heads, BLK)], 2),
+        preferred_element_type=F32).reshape(2, nz, 2, own80, 2 * BLK)
+    keep = lax.dynamic_index_in_dim(gate_part, c, 2, keepdims=False)
+    away = lax.dynamic_index_in_dim(gate_part, 1 - c, 2, keepdims=False)
+    gate_part = keep + lay.over_c(away.astype(BF16)).astype(F32)
+    keep = lax.dynamic_index_in_dim(gate_part, y, 0, keepdims=False)
+    away = lax.dynamic_index_in_dim(gate_part, 1 - y, 0, keepdims=False)
+    gate_part = (keep + lay.over_y(away.astype(BF16)).astype(F32)).astype(BF16)
+    in_x_part = dot(n1_rows, all_tokens(gx)).astype(BF16).reshape(nz, 2 * own80, half)
+    done_two = line_sum(lay, jnp.concatenate(
+        [in_x_part, gate_part.reshape(nz, own80 * 2 * BLK // half, half)], axis=1)).astype(BF16)
+
+    def over_columns(value):
+        split = value.reshape(2, own80, half)
+        mine = lax.dynamic_index_in_dim(split, x, 0, keepdims=False)
+        theirs = lay.over_x(lax.dynamic_index_in_dim(split, 1 - x, 0, keepdims=False))
+        return jnp.where(x == 0, jnp.concatenate([mine, theirs], -1),
+                         jnp.concatenate([theirs, mine], -1)).astype(F32)
+
+    in_y_grad = over_columns(done_one[: 2 * own80])
+    in_x_grad = over_columns(done_two[: 2 * own80])
     def final(z, y, x, c):
         at = ((x * 2 + y) * nz + z) * 2 + c
         s, f = (at // 4, at % 4)
         return (s // 2, s % 2, f // 2, f % 2)
 
-    last = lay.send(last, final).astype(F32)
-    return (output, input_grad, vec, in_full[0], in_full[1], last[:, width:], last[:, :width],
+    out_grad = lay.send(done_one[2 * own80 :].reshape(own80, width), final).astype(F32)
+    gate_grad = lay.send(done_two[2 * own80 :].reshape(own80, 2 * BLK), final).astype(F32)
+    return (output, input_grad, vec, in_y_grad, in_x_grad, gate_grad, out_grad,
             mlp_gate_grad, mlp_up_grad, mlp_down_grad)
 
 

time: 892 us -> 795 us (0.89)
  starting transfers between devices: 213 us -> 147 us
  local copies, waits for them, and re-layouts: 82.9 us -> 54.4 us
    ppermute x82 -> x83, starting transfers between devices: 213 us -> 147 us  [send(): return lax.ppermute(value, ALL, self.pairs(target))]
    concatenate x5 -> x3, local copies, waits for them, and re-layouts: 19.2 us -> 1.09 us  [the longest x1 0.96 us: local(): jnp.concatenate([cot_z, lay.over_c(cot_z), cot_xz, lay.over_c(cot_xz)], 0)]
    concatenate x11 -> x3, other arithmetic: 19.6 us -> 6.22 us  [the longest x1 3.26 us: local(): main_cot = jnp.concatenate([cot, cot_c, cot_x, cot_xc], 0)]
    ppermute x6 -> x0, local copies, waits for them, and re-layouts: 11.9 us -> none  [send(): return lax.ppermute(value, ALL, self.pairs(target))]
    reshape x2 -> x10, local copies, waits for them, and re-layouts: 0.31 us -> 11.6 us  [the longest x2 3.87 us: local(): gdp.reshape(two, heads, BLK)]
    convert_element_type x8 -> x11, other arithmetic: 5.39 us -> 16.6 us  [the longest x3 8.95 us: halve(): sent = jnp.stack([held[j]().astype(BF16) for j in leaving])]
    dot_general x5 -> x3, matrix products: 31.4 us -> 23.4 us  [dot_rows(): lax.dot_general(left, right, (((0,), (0,)), ((), ())), preferred_element_...]
    ppermute x82 -> x83, waiting for transfers between devices: 308 us -> 302 us  [send(): return lax.ppermute(value, ALL, self.pairs(target))]
  transfers between devices with their start and end apart: 82 -> 83, of which waited for: 26 -> 22; matrix products, arithmetic and copies ran while one was open for 37% -> 39% of each run, Pallas kernels for 2% -> 3%
where the time goes in v2:
time: 795 us; the launch traced here: 784 us
  waiting for transfers between devices  302 us (38%)
  matrix products  189 us (24%)
  starting transfers between devices  147 us (18%)
  other arithmetic  68.4 us (9%)
  local copies, waits for them, and re-layouts  54.4 us (7%)
  Pallas kernels  20.5 us (3%)
    ppermute x83, waiting for transfers between devices, send(): return lax.ppermute(value, ALL, self.pairs(target))  302 us
    ppermute x83, starting transfers between devices, send(): return lax.ppermute(value, ALL, self.pairs(target))  147 us
    dot_general x15, matrix products, dot(): return jnp.dot(left, right, preferred_element_type=F32)  101 us
    dot_general x15, matrix products, dot_cols(): lax.dot_general(left, right, (((1,), (1,)), ((), ())), preferred_element_...  62.3 us
    dot_general x3, matrix products, dot_rows(): lax.dot_general(left, right, (((0,), (0,)), ((), ())), preferred_element_...  23.4 us
    pallas_call x3, Pallas kernels, by_head(): pl.pallas_call(body, grid=(heads,), in_specs=in_specs, out_specs=[spec(o....  20.5 us
  transfers between devices with their start and end apart: 83, of which 22 were waited for; matrix products, arithmetic and copies ran while one was open for 39% of the time, Pallas kernels for 3%

profile of v2, /device:TPU:2, one launch (start us, length us, event | category | flops | bytes accessed | tf_op | source)
XLA Modules:
  0.0 784.4 jit_solution(14661255009296247560)
XLA Ops:
  0.7 4.1 collective-permute-start.73
  18.7 3.9 constant_dynamic-slice_fusion.11
  24.0 9.6 %collective-permute-done.1 = bf16[16,2560]{1,0:T(8,128)(2,1)} collective-permute-done((bf16[16,2560]{1,0:T(8,128)(2,1)S(1)}, bf16[16,2560]{1,0:T(8,128)(2,1)}, u32[]{:S(2)}, u32[]{:S(2)}) %collective-permute-start.1) | collective-permute-done | bytes 81952 | tf_op jit(solution)/shard_map/ppermute | solution.py:74
  42.2 4.4 fusion.132
  65.3 7.1 shard_map.195
  79.7 15.1 %collective-permute-done.75 = bf16[128,2560]{1,0:T(8,128)(2,1)S(1)} collective-permute-done((bf16[128,2560]{1,0:T(8,128)(2,1)}, bf16[128,2560]{1,0:T(8,128)(2,1)S(1)}, u32[]{:S(2)}, u32[]{:S(2)}) %collective-permute-start.75) | collective-permute-done | bytes 655392 | tf_op jit(solution)/shard_map/ppermute | solution.py:74
  94.7 14.6 %collective-permute-start.8 = (f32[4,1280]{1,0:T(4,128)S(1)}, f32[4,1280]{1,0:T(4,128)S(1)}, u32[]{:S(2)}, u32[]{:S(2)}) collective-permute-start(f32[4,1280]{1,0:T(4,128)S(1)} %pad_maximum_fusion.21), channel_id=1, source_target_pairs={{0,8},{1,9},{2,10},{3,11},{4,12},{5,13},{6,14},{7,15},{8,0},{9,1},... | collective-permute-start | bytes 61448 | tf_op jit(solution)/shard_map/ppermute | solution.py:74
  119.3 7.1 convolution_convert_fusion.4
  132.4 11.1 %collective-permute-done.14 = bf16[128,2560]{1,0:T(8,128)(2,1)} collective-permute-done((bf16[128,2560]{1,0:T(8,128)(2,1)}, bf16[128,2560]{1,0:T(8,128)(2,1)}, u32[]{:S(2)}, u32[]{:S(2)}) %collective-permute-start.14) | collective-permute-done | bytes 655392 | tf_op jit(solution)/shard_map/ppermute | solution.py:74
  144.7 6.2 convolution_add_fusion.8
  155.6 7.6 fusion.187
  163.2 6.8 collective-permute-done.16
  179.9 10.7 %fusion.175 = f32[512,1920]{1,0:T(8,128)} fusion(bf16[2560,1920]{1,0:T(8,128)(2,1)} %param.20, bf16[128,2560]{1,0:T(8,128)(2,1)} %collective-permute-done.17, bf16[128,2560]{1,0:T(8,128)(2,1)} %collective-permute-done.16, bf16[128,2560]{1,0:T(8,128)(2,1)} %collective-permute-done.15, bf16[128,2560]{1,0:T(8,128)(2,1)} %multiply_convert_fusion.6), kind=kOutput, calls=%fused_computation.378 | convolution fusion | flops 5043650560 | bytes 16384000 | tf_op jit(solution)/shard_map/dot_general | solution.py:44
  190.7 9.3 %fusion.174 = f32[512,1920]{1,0:T(8,128)} fusion(bf16[2560,1920]{1,0:T(8,128)(2,1)S(1)} %bitcast.238, bf16[128,2560]{1,0:T(8,128)(2,1)} %collective-permute-done.17, bf16[128,2560]{1,0:T(8,128)(2,1)} %collective-permute-done.16, bf16[128,2560]{1,0:T(8,128)(2,1)} %collective-permute-done.15, bf16[128,2560]{1,0:T(8,128)(2,1)} %multiply_convert_fusion.6), kind=kOutput, calls=%fused_computation.377 | convolution fusion | flops 5043650560 | bytes 16384000 | tf_op jit(solution)/shard_map/dot_general | solution.py:44
  200.1 13.7 %multiply_convert_fusion.3 = (bf16[512,1920]{1,0:T(8,128)(2,1)S(1)}, bf16[512,1920]{1,0:T(8,128)(2,1)S(1)}, bf16[512,1920]{1,0:T(8,128)(2,1)S(1)}) fusion(f32[512,1920]{1,0:T(8,128)} %fusion.175, f32[512,1920]{1,0:T(8,128)} %fusion.174, bf16[2560,1920]{1,0:T(8,128)(2,1)} %param.22, bf16[128,2560]{1,0:T(8,128)(2,1)S(1)} %copy-done.48, ...), kind=kOutput, calls=%fused_computation.43 | convolution fusion | flops 5067243520 | bytes 26214400 | tf_op jit(solution)/shard_map/dot_general | solution.py:44
  213.8 7.6 fusion.74
  221.4 8.2 %fusion.77 = f32[256,2560]{1,0:T(8,128)} fusion(bf16[2560,1920]{1,0:T(8,128)(2,1)} %param.20, bf16[512,1920]{1,0:T(8,128)(2,1)S(1)} %get-tuple-element.62), kind=kOutput, calls=%fused_computation.183 | convolution fusion | flops 2516582400 | bytes 13434880 | tf_op jit(solution)/shard_map/dot_general | solution.py:52
  229.6 5.7 fusion.79
  235.4 8.2 %fusion.81 = f32[256,2560]{1,0:T(8,128)} fusion(bf16[2560,1920]{1,0:T(8,128)(2,1)} %param.22, bf16[512,1920]{1,0:T(8,128)(2,1)S(1)} %get-tuple-element.63), kind=kOutput, calls=%fused_computation.187 | convolution fusion | flops 2516582400 | bytes 13434880 | tf_op jit(solution)/shard_map/dot_general | solution.py:52
  243.6 5.6 convolution_add_fusion
  250.3 7.5 convolution_add_fusion.1
  265.3 10.1 %fusion.188 = f32[512,1920]{1,0:T(8,128)} fusion(bf16[512,2560]{1,0:T(8,128)(2,1)S(1)} %constant_dynamic-update-slice_fusion.5, bf16[2560,1920]{1,0:T(8,128)(2,1)} %param.20), kind=kOutput, calls=%fused_computation.391 | convolution fusion | flops 5033164800 | bytes 16384000 | tf_op jit(solution)/shard_map/dot_general | solution.py:44
  277.0 14.2 %multiply_convert_fusion = (bf16[512,1920]{1,0:T(8,128)(2,1)}, bf16[512,1920]{1,0:T(8,128)(2,1)}, bf16[512,1920]{1,0:T(8,128)(2,1)S(1)}) fusion(f32[512,1920]{1,0:T(8,128)} %fusion.188, f32[512,1920]{1,0:T(8,128)} %fusion.187, bf16[512,2560]{1,0:T(8,128)(2,1)S(1)} %constant_dynamic-update-slice_fusion.5, bf16[2560,1920]{1,0:T(8,128)(2,1)} %param.21), kind=kOutput, calls=%fused_computation.37 | convolution fusion | flops 5056757760 | bytes 26214400 | tf_op jit(solution)/shard_map/dot_general | solution.py:44
  291.1 7.4 convolution_convert_fusion.2
  302.6 21.9 %collective-permute-start.77 = (bf16[2,320,1920]{2,1,0:T(8,128)(2,1)}, bf16[2,320,1920]{2,1,0:T(8,128)(2,1)}, u32[]{:S(2)}, u32[]{:S(2)}) collective-permute-start(bf16[2,320,1920]{2,1,0:T(8,128)(2,1)} %pad_maximum_fusion.4), channel_id=1, source_target_pairs={{0,8},{1,9},{2,10},{3,11},{4,12},{5,13},{6,14},{7,15},{8,0},{9,1},... | collective-permute-start | bytes 7372808 | tf_op jit(solution)/shard_map/ppermute | solution.py:74
  324.5 5.9 convolution_convert_fusion.1
  330.5 10.0 %convolution_convert_fusion = bf16[1280,1920]{1,0:T(8,128)(2,1)S(1)} fusion(bf16[512,1920]{1,0:T(8,128)(2,1)} %get-tuple-element.58, bf16[512,1920]{1,0:T(8,128)(2,1)} %copy-done.66, bf16[512,1280]{1,0:T(8,128)(2,1)S(1)} %copy-done.43, bf16[512,1280]{1,0:T(8,128)(2,1)S(1)} %copy-done.42), kind=kOutput, calls=%fused_computation | convolution fusion | flops 5048729600 | bytes 11468800 | tf_op jit(solution)/shard_map/dot_general | solution.py:48
  351.9 9.5 %collective-permute-done.27 = bf16[128,2560]{1,0:T(8,128)(2,1)S(1)} collective-permute-done((bf16[128,2560]{1,0:T(8,128)(2,1)S(1)}, bf16[128,2560]{1,0:T(8,128)(2,1)S(1)}, u32[]{:S(2)}, u32[]{:S(2)}) %collective-permute-start.27) | collective-permute-done | bytes 655392 | tf_op jit(solution)/shard_map/ppermute | solution.py:74
  365.4 5.5 shard_map.196
  376.4 4.2 convolution_add_fusion.4
  380.6 75.2 %collective-permute-done.28 = f32[4,1280]{1,0:T(4,128)S(1)} collective-permute-done((f32[4,1280]{1,0:T(4,128)S(1)}, f32[4,1280]{1,0:T(4,128)S(1)}, u32[]{:S(2)}, u32[]{:S(2)}) %collective-permute-start.28) | collective-permute-done | bytes 20512 | tf_op jit(solution)/shard_map/ppermute | solution.py:74
  461.1 4.2 convolution_add_fusion.7
  465.4 7.9 %shard_map.197 = (bf16[2,128,1280]{2,1,0:T(8,128)(2,1)S(1)}, bf16[2,128,1280]{2,1,0:T(8,128)(2,1)S(1)}, bf16[2,128,1280]{2,1,0:T(8,128)(2,1)S(1)}, f32[2,16,1280...) custom-call(f32[2,2]{1,0:T(2,128)S(1)} %copy-done.15, ...), custom_call_target="tpu_custom_call" | custom-call | flops 65536000 | bytes 12902416 | tf_op jit(solution)/shard_map/pallas_call | solution.py:258
  491.6 10.6 %collective-permute-done.32 = bf16[128,2560]{1,0:T(8,128)(2,1)S(1)} collective-permute-done((bf16[128,2560]{1,0:T(8,128)(2,1)S(1)}, bf16[128,2560]{1,0:T(8,128)(2,1)S(1)}, u32[]{:S(2)}, u32[]{:S(2)}) %collective-permute-start.32) | collective-permute-done | bytes 655392 | tf_op jit(solution)/shard_map/ppermute | solution.py:74
  507.3 4.2 collective-permute-done.34
  514.6 17.2 %collective-permute-done.35 = f32[10,2560]{1,0:T(8,128)S(1)} collective-permute-done((f32[10,2560]{1,0:T(8,128)S(1)}, f32[10,2560]{1,0:T(8,128)S(1)}, u32[]{:S(2)}, u32[]{:S(2)}) %collective-permute-start.35) | collective-permute-done | bytes 102432 | tf_op jit(solution)/shard_map/ppermute | solution.py:74
  548.3 29.4 %collective-permute-done.39 = bf16[640,512]{1,0:T(8,128)(2,1)S(1)} collective-permute-done((bf16[640,512]{1,0:T(8,128)(2,1)S(1)}, bf16[640,512]{1,0:T(8,128)(2,1)S(1)}, u32[]{:S(2)}, u32[]{:S(2)}) %collective-permute-start.39) | collective-permute-done | bytes 655392 | tf_op jit(solution)/shard_map/ppermute | solution.py:74
  577.8 13.7 %collective-permute-done.56 = bf16[256,1280]{1,0:T(8,128)(2,1)S(1)} collective-permute-done((bf16[256,1280]{1,0:T(8,128)(2,1)S(1)}, bf16[256,1280]{1,0:T(8,128)(2,1)S(1)}, u32[]{:S(2)}, u32[]{:S(2)}) %collective-permute-start.56) | collective-permute-done | bytes 655392 | tf_op jit(solution)/shard_map/ppermute | solution.py:74
  599.7 5.4 collective-permute-done.37
  622.0 48.0 %collective-permute-done.60 = bf16[192,1280]{1,0:T(8,128)(2,1)} collective-permute-done((bf16[192,1280]{1,0:T(8,128)(2,1)}, bf16[192,1280]{1,0:T(8,128)(2,1)}, u32[]{:S(2)}, u32[]{:S(2)}) %collective-permute-start.60) | collective-permute-done | bytes 491552 | tf_op jit(solution)/shard_map/ppermute | solution.py:74
  670.0 4.4 collective-permute-start.48
  681.9 11.2 %collective-permute-done.48 = bf16[320,1280]{1,0:T(8,128)(2,1)S(1)} collective-permute-done((bf16[320,1280]{1,0:T(8,128)(2,1)S(1)}, bf16[320,1280]{1,0:T(8,128)(2,1)S(1)}, u32[]{:S(2)}, u32[]{:S(2)}) %collective-permute-start.48) | collective-permute-done | bytes 819232 | tf_op jit(solution)/shard_map/ppermute | solution.py:74
  694.2 5.0 collective-permute-start.49
  705.4 9.8 %collective-permute-start.62 = (bf16[192,1280]{1,0:T(8,128)(2,1)S(1)}, bf16[192,1280]{1,0:T(8,128)(2,1)S(1)}, u32[]{:S(2)}, u32[]{:S(2)}) collective-permute-start(bf16[192,1280]{1,0:T(8,128)(2,1)S(1)} %get-tuple-element.78), channel_id=1, source_target_pairs={{0,8},{1,9},{2,10},{3,11},{4,12},{5,13},{6,14},{7,15},{8,16},{9,17... | collective-permute-start | bytes 1474568 | tf_op jit(solution)/shard_map/ppermute | solution.py:74
  715.3 5.9 collective-permute-done.49
  724.1 11.0 %collective-permute-start.50 = (bf16[320,1280]{1,0:T(8,128)(2,1)}, bf16[320,1280]{1,0:T(8,128)(2,1)}, u32[]{:S(2)}, u32[]{:S(2)}) collective-permute-start(bf16[320,1280]{1,0:T(8,128)(2,1)} %get-tuple-element.70), channel_id=1, source_target_pairs={{0,8},{1,9},{2,10},{3,11},{4,12},{5,13},{6,14},{7,15},{8,16},{9,17... | collective-permute-start | bytes 2457608 | tf_op jit(solution)/shard_map/ppermute | solution.py:74
  751.7 8.4 %collective-permute-start.68 = (bf16[80,2560]{1,0:T(8,128)(2,1)S(1)}, bf16[80,2560]{1,0:T(8,128)(2,1)S(1)}, u32[]{:S(2)}, u32[]{:S(2)}) collective-permute-start(bf16[80,2560]{1,0:T(8,128)(2,1)S(1)} %reshape.199), channel_id=1, source_target_pairs={{0,0},{1,1},{2,16},{3,17},{4,8},{5,9},{6,24},{7,25},{8,2},{9,3},{1... | collective-permute-start | bytes 1228808 | tf_op jit(solution)/shard_map/ppermute | solution.py:74
  763.1 19.9 %collective-permute-done.68 = bf16[80,2560]{1,0:T(8,128)(2,1)S(1)} collective-permute-done((bf16[80,2560]{1,0:T(8,128)(2,1)S(1)}, bf16[80,2560]{1,0:T(8,128)(2,1)S(1)}, u32[]{:S(2)}, u32[]{:S(2)}) %collective-permute-start.68) | collective-permute-done | bytes 409632 | tf_op jit(solution)/shard_map/ppermute | solution.py:74
  (458 shorter events, 226.8 us)
Async XLA Ops:
  0.6 49.9 %collective-permute-start.22 = (bf16[128,2560]{1,0:T(8,128)(2,1)}, bf16[128,2560]{1,0:T(8,128)(2,1)}, u32[]{:S(2)}, u32[]{:S(2)}) collective-permute-start(bf16[128,2560]{1,0:T(8,128)(2,1)} %bitcast.223), channel_id=1, source_target_pairs={{0,2},{1,3},{2,0},{3,1},{4,6},{5,7},{6,4},{7,5},{8,10},{9,11},{10,... | collective-permute-start | bytes 1966088 | tf_op jit(solution)/shard_map/ppermute | solution.py:74
  0.7 46.4 %collective-permute-start.73 = (bf16[128,2560]{1,0:T(8,128)(2,1)}, bf16[128,2560]{1,0:T(8,128)(2,1)}, u32[]{:S(2)}, u32[]{:S(2)}) collective-permute-start(bf16[128,2560]{1,0:T(8,128)(2,1)} %bitcast.224), channel_id=1, source_target_pairs={{0,24},{1,25},{2,26},{3,27},{4,28},{5,29},{6,30},{7,31},{8,16},{9,... | collective-permute-start | bytes 1966088 | tf_op jit(solution)/shard_map/ppermute | solution.py:74
  9.2 52.0 %collective-permute-start.3 = (bf16[2560,640]{1,0:T(8,128)(2,1)}, bf16[2560,640]{1,0:T(8,128)(2,1)S(1)}, u32[]{:S(2)}, u32[]{:S(2)}) collective-permute-start(bf16[2560,640]{1,0:T(8,128)(2,1)} %param.17), channel_id=1, source_target_pairs={{0,1},{1,0},{2,3},{3,2},{4,5},{5,4},{6,7},{7,6},{8,9},{9,8},{10,11... | collective-permute-start | bytes 9830408 | tf_op jit(solution)/shard_map/ppermute | solution.py:74
  14.3 21.4 %collective-permute-start.2 = (bf16[128,2560]{1,0:T(8,128)(2,1)}, bf16[128,2560]{1,0:T(8,128)(2,1)}, u32[]{:S(2)}, u32[]{:S(2)}) collective-permute-start(bf16[128,2560]{1,0:T(8,128)(2,1)} %fusion.49), channel_id=1, source_target_pairs={{0,2},{1,3},{2,0},{3,1},{4,6},{5,7},{6,4},{7,5},{8,10},{9,11},{10,... | collective-permute-start | bytes 1966088 | tf_op jit(solution)/shard_map/ppermute | solution.py:74
  35.8 75.4 %collective-permute-start.10 = (bf16[2560,640]{1,0:T(8,128)(2,1)}, bf16[2560,640]{1,0:T(8,128)(2,1)}, u32[]{:S(2)}, u32[]{:S(2)}) collective-permute-start(bf16[2560,640]{1,0:T(8,128)(2,1)} %param.16), channel_id=1, source_target_pairs={{0,1},{1,0},{2,3},{3,2},{4,5},{5,4},{6,7},{7,6},{8,9},{9,8},{10,11... | collective-permute-start | bytes 9830408 | tf_op jit(solution)/shard_map/ppermute | solution.py:74
  50.0 60.2 %collective-permute-start.12 = (bf16[1280,640]{1,0:T(8,128)(2,1)}, bf16[1280,640]{1,0:T(8,128)(2,1)}, u32[]{:S(2)}, u32[]{:S(2)}) collective-permute-start(bf16[1280,640]{1,0:T(8,128)(2,1)} %get-tuple-element.77), channel_id=1, source_target_pairs={{0,2},{1,3},{2,0},{3,1},{4,6},{5,7},{6,4},{7,5},{8,10},{9,11},{10,... | collective-permute-start | bytes 4915208 | tf_op jit(solution)/shard_map/ppermute | solution.py:74
  57.2 62.1 %collective-permute-start.11 = (bf16[1280,640]{1,0:T(8,128)(2,1)S(1)}, bf16[1280,640]{1,0:T(8,128)(2,1)}, u32[]{:S(2)}, u32[]{:S(2)}) collective-permute-start(bf16[1280,640]{1,0:T(8,128)(2,1)S(1)} %copy-done.37), channel_id=1, source_target_pairs={{0,1},{1,0},{2,3},{3,2},{4,5},{5,4},{6,7},{7,6},{8,9},{9,8},{10,11... | collective-permute-start | bytes 4915208 | tf_op jit(solution)/shard_map/ppermute | solution.py:74
  57.8 70.3 %collective-permute-start.38 = (bf16[2,640,256]{2,1,0:T(8,128)(2,1)}, bf16[2,640,256]{2,1,0:T(8,128)(2,1)}, u32[]{:S(2)}, u32[]{:S(2)}) collective-permute-start(bf16[2,640,256]{2,1,0:T(8,128)(2,1)} %get-tuple-element.86), channel_id=1, source_target_pairs={{0,1},{1,0},{2,3},{3,2},{4,5},{5,4},{6,7},{7,6},{8,9},{9,8},{10,11... | collective-permute-start | bytes 1966088 | tf_op jit(solution)/shard_map/ppermute | solution.py:74
  76.3 18.4 %collective-permute-start.75 = (bf16[128,2560]{1,0:T(8,128)(2,1)}, bf16[128,2560]{1,0:T(8,128)(2,1)S(1)}, u32[]{:S(2)}, u32[]{:S(2)}) collective-permute-start(bf16[128,2560]{1,0:T(8,128)(2,1)} %collective-permute-done.22), channel_id=1, source_target_pairs={{0,24},{1,25},{2,26},{3,27},{4,28},{5,29},{6,30},{7,31},{8,16},{9,... | collective-permute-start | bytes 1966088 | tf_op jit(solution)/shard_map/ppermute | solution.py:74
  110.2 20.1 %collective-permute-start.76 = (bf16[128,2560]{1,0:T(8,128)(2,1)S(1)}, bf16[128,2560]{1,0:T(8,128)(2,1)S(1)}, u32[]{:S(2)}, u32[]{:S(2)}) collective-permute-start(bf16[128,2560]{1,0:T(8,128)(2,1)S(1)} %collective-permute-done.75), channel_id=1, source_target_pairs={{0,1},{1,0},{2,3},{3,2},{4,5},{5,4},{6,7},{7,6},{8,9},{9,8},{10,11... | collective-permute-start | bytes 1966088 | tf_op jit(solution)/shard_map/ppermute | solution.py:74
  132.4 43.3 %collective-permute-start.43 = (bf16[2,320,256]{2,1,0:T(8,128)(2,1)}, bf16[2,320,256]{2,1,0:T(8,128)(2,1)}, u32[]{:S(2)}, u32[]{:S(2)}) collective-permute-start(bf16[2,320,256]{2,1,0:T(8,128)(2,1)} %get-tuple-element.101), channel_id=1, source_target_pairs={{0,1},{1,0},{2,3},{3,2},{4,5},{5,4},{6,7},{7,6},{8,9},{9,8},{10,11... | collective-permute-start | bytes 983048 | tf_op jit(solution)/shard_map/ppermute | solution.py:74
  154.2 24.2 %collective-permute-start.69 = (bf16[128,2560]{1,0:T(8,128)(2,1)}, bf16[128,2560]{1,0:T(8,128)(2,1)}, u32[]{:S(2)}, u32[]{:S(2)}) collective-permute-start(bf16[128,2560]{1,0:T(8,128)(2,1)} %multiply_convert_fusion.6), channel_id=1, source_target_pairs={{0,24},{1,25},{2,26},{3,27},{4,28},{5,29},{6,30},{7,31},{8,16},{9,... | collective-permute-start | bytes 1966088 | tf_op jit(solution)/shard_map/ppermute | solution.py:74
  177.8 84.2 %collective-permute-start.71 = (bf16[128,2560]{1,0:T(8,128)(2,1)}, bf16[128,2560]{1,0:T(8,128)(2,1)}, u32[]{:S(2)}, u32[]{:S(2)}) collective-permute-start(bf16[128,2560]{1,0:T(8,128)(2,1)} %collective-permute-done.16), channel_id=1, source_target_pairs={{0,24},{1,25},{2,26},{3,27},{4,28},{5,29},{6,30},{7,31},{8,16},{9,... | collective-permute-start | bytes 1966088 | tf_op jit(solution)/shard_map/ppermute | solution.py:74
  178.4 83.4 %collective-permute-start.70 = (bf16[128,2560]{1,0:T(8,128)(2,1)}, bf16[128,2560]{1,0:T(8,128)(2,1)S(1)}, u32[]{:S(2)}, u32[]{:S(2)}) collective-permute-start(bf16[128,2560]{1,0:T(8,128)(2,1)} %collective-permute-done.69), channel_id=1, source_target_pairs={{0,1},{1,0},{2,3},{3,2},{4,5},{5,4},{6,7},{7,6},{8,9},{9,8},{10,11... | collective-permute-start | bytes 1966088 | tf_op jit(solution)/shard_map/ppermute | solution.py:74
  257.9 82.7 %collective-permute-start.24 = (bf16[128,2560]{1,0:T(8,128)(2,1)S(1)}, bf16[128,2560]{1,0:T(8,128)(2,1)S(1)}, u32[]{:S(2)}, u32[]{:S(2)}) collective-permute-start(bf16[128,2560]{1,0:T(8,128)(2,1)S(1)} %slice.488), channel_id=1, source_target_pairs={{0,1},{1,0},{2,3},{3,2},{4,5},{5,4},{6,7},{7,6},{8,9},{9,8},{10,11... | collective-permute-start | bytes 1966088 | tf_op jit(solution)/shard_map/ppermute | solution.py:74
  261.8 78.8 %collective-permute-start.18 = (bf16[128,2560]{1,0:T(8,128)(2,1)S(1)}, bf16[128,2560]{1,0:T(8,128)(2,1)S(1)}, u32[]{:S(2)}, u32[]{:S(2)}) collective-permute-start(bf16[128,2560]{1,0:T(8,128)(2,1)S(1)} %slice.490), channel_id=1, source_target_pairs={{0,1},{1,0},{2,3},{3,2},{4,5},{5,4},{6,7},{7,6},{8,9},{9,8},{10,11... | collective-permute-start | bytes 1966088 | tf_op jit(solution)/shard_map/ppermute | solution.py:74
  263.8 76.7 %collective-permute-start.26 = (bf16[128,2560]{1,0:T(8,128)(2,1)S(1)}, bf16[128,2560]{1,0:T(8,128)(2,1)S(1)}, u32[]{:S(2)}, u32[]{:S(2)}) collective-permute-start(bf16[128,2560]{1,0:T(8,128)(2,1)S(1)} %fusion.57), channel_id=1, source_target_pairs={{0,2},{1,3},{2,0},{3,1},{4,6},{5,7},{6,4},{7,5},{8,10},{9,11},{10,... | collective-permute-start | bytes 1966088 | tf_op jit(solution)/shard_map/ppermute | solution.py:74
  275.7 64.9 %collective-permute-start.20 = (bf16[128,2560]{1,0:T(8,128)(2,1)S(1)}, bf16[128,2560]{1,0:T(8,128)(2,1)S(1)}, u32[]{:S(2)}, u32[]{:S(2)}) collective-permute-start(bf16[128,2560]{1,0:T(8,128)(2,1)S(1)} %fusion.59), channel_id=1, source_target_pairs={{0,2},{1,3},{2,0},{3,1},{4,6},{5,7},{6,4},{7,5},{8,10},{9,11},{10,... | collective-permute-start | bytes 1966088 | tf_op jit(solution)/shard_map/ppermute | solution.py:74
  302.6 229.3 %collective-permute-start.77 = (bf16[2,320,1920]{2,1,0:T(8,128)(2,1)}, bf16[2,320,1920]{2,1,0:T(8,128)(2,1)}, u32[]{:S(2)}, u32[]{:S(2)}) collective-permute-start(bf16[2,320,1920]{2,1,0:T(8,128)(2,1)} %pad_maximum_fusion.4), channel_id=1, source_target_pairs={{0,8},{1,9},{2,10},{3,11},{4,12},{5,13},{6,14},{7,15},{8,0},{9,1},... | collective-permute-start | bytes 7372808 | tf_op jit(solution)/shard_map/ppermute | solution.py:74
  348.2 188.5 %collective-permute-start.79 = (bf16[2,320,1920]{2,1,0:T(8,128)(2,1)}, bf16[2,320,1920]{2,1,0:T(8,128)(2,1)}, u32[]{:S(2)}, u32[]{:S(2)}) collective-permute-start(bf16[2,320,1920]{2,1,0:T(8,128)(2,1)} %pad_maximum_fusion.5), channel_id=1, source_target_pairs={{0,4},{1,5},{2,6},{3,7},{4,0},{5,1},{6,2},{7,3},{8,12},{9,13},{10,... | collective-permute-start | bytes 7372808 | tf_op jit(solution)/shard_map/ppermute | solution.py:74
  351.4 189.3 %collective-permute-start.81 = (bf16[2,320,1920]{2,1,0:T(8,128)(2,1)}, bf16[2,320,1920]{2,1,0:T(8,128)(2,1)}, u32[]{:S(2)}, u32[]{:S(2)}) collective-permute-start(bf16[2,320,1920]{2,1,0:T(8,128)(2,1)} %pad_maximum_fusion.6), channel_id=1, source_target_pairs={{0,4},{1,5},{2,6},{3,7},{4,0},{5,1},{6,2},{7,3},{8,12},{9,13},{10,... | collective-permute-start | bytes 7372808 | tf_op jit(solution)/shard_map/ppermute | solution.py:74
  370.9 84.9 %collective-permute-start.28 = (f32[4,1280]{1,0:T(4,128)S(1)}, f32[4,1280]{1,0:T(4,128)S(1)}, u32[]{:S(2)}, u32[]{:S(2)}) collective-permute-start(f32[4,1280]{1,0:T(4,128)S(1)} %get-tuple-element.33), channel_id=1, source_target_pairs={{0,4},{1,5},{2,6},{3,7},{4,0},{5,1},{6,2},{7,3},{8,12},{9,13},{10,... | collective-permute-start | bytes 61448 | tf_op jit(solution)/shard_map/ppermute | solution.py:74
  488.9 25.2 %collective-permute-start.59 = (bf16[4,80,512]{2,1,0:T(8,128)(2,1)S(1)}, bf16[4,80,512]{2,1,0:T(8,128)(2,1)S(1)}, u32[]{:S(2)}, u32[]{:S(2)}) collective-permute-start(bf16[4,80,512]{2,1,0:T(8,128)(2,1)S(1)} %fusion.133), channel_id=1, source_target_pairs={{0,4},{1,5},{2,6},{3,7},{4,0},{5,1},{6,2},{7,3},{8,12},{9,13},{10,... | collective-permute-start | bytes 983048 | tf_op jit(solution)/shard_map/ppermute | solution.py:74
  511.5 35.1 %collective-permute-start.41 = (bf16[256,1280]{1,0:T(8,128)(2,1)S(1)}, bf16[256,1280]{1,0:T(8,128)(2,1)S(1)}, u32[]{:S(2)}, u32[]{:S(2)}) collective-permute-start(bf16[256,1280]{1,0:T(8,128)(2,1)S(1)} %bitcast.188), channel_id=1, source_target_pairs={{0,4},{1,5},{2,6},{3,7},{4,0},{5,1},{6,2},{7,3},{8,12},{9,13},{10,... | collective-permute-start | bytes 1966088 | tf_op jit(solution)/shard_map/ppermute | solution.py:74
  514.2 17.7 %collective-permute-start.35 = (f32[10,2560]{1,0:T(8,128)S(1)}, f32[10,2560]{1,0:T(8,128)S(1)}, u32[]{:S(2)}, u32[]{:S(2)}) collective-permute-start(f32[10,2560]{1,0:T(8,128)S(1)} %add.458), channel_id=1, source_target_pairs={{0,4},{1,5},{2,6},{3,7},{4,0},{5,1},{6,2},{7,3},{8,12},{9,13},{10,... | collective-permute-start | bytes 307208 | tf_op jit(solution)/shard_map/ppermute | solution.py:74
  531.9 59.6 %collective-permute-start.46 = (bf16[256,2560]{1,0:T(8,128)(2,1)}, bf16[256,2560]{1,0:T(8,128)(2,1)S(1)}, u32[]{:S(2)}, u32[]{:S(2)}) collective-permute-start(bf16[256,2560]{1,0:T(8,128)(2,1)} %pad_maximum_fusion.12), channel_id=1, source_target_pairs={{0,4},{1,5},{2,6},{3,7},{4,0},{5,1},{6,2},{7,3},{8,12},{9,13},{10,... | collective-permute-start | bytes 3932168 | tf_op jit(solution)/shard_map/ppermute | solution.py:74
  540.7 37.1 %collective-permute-start.39 = (bf16[640,512]{1,0:T(8,128)(2,1)S(1)}, bf16[640,512]{1,0:T(8,128)(2,1)S(1)}, u32[]{:S(2)}, u32[]{:S(2)}) collective-permute-start(bf16[640,512]{1,0:T(8,128)(2,1)S(1)} %copy-done.50), channel_id=1, source_target_pairs={{0,4},{1,5},{2,6},{3,7},{4,0},{5,1},{6,2},{7,3},{8,12},{9,13},{10,... | collective-permute-start | bytes 1966088 | tf_op jit(solution)/shard_map/ppermute | solution.py:74
  543.0 48.5 %collective-permute-start.56 = (bf16[256,1280]{1,0:T(8,128)(2,1)S(1)}, bf16[256,1280]{1,0:T(8,128)(2,1)S(1)}, u32[]{:S(2)}, u32[]{:S(2)}) collective-permute-start(bf16[256,1280]{1,0:T(8,128)(2,1)S(1)} %bitcast.218), channel_id=1, source_target_pairs={{0,4},{1,5},{2,6},{3,7},{4,0},{5,1},{6,2},{7,3},{8,12},{9,13},{10,... | collective-permute-start | bytes 1966088 | tf_op jit(solution)/shard_map/ppermute | solution.py:74
  546.6 46.5 %collective-permute-start.40 = (bf16[256,1280]{1,0:T(8,128)(2,1)S(1)}, bf16[256,1280]{1,0:T(8,128)(2,1)S(1)}, u32[]{:S(2)}, u32[]{:S(2)}) collective-permute-start(bf16[256,1280]{1,0:T(8,128)(2,1)S(1)} %bitcast.189), channel_id=1, source_target_pairs={{0,1},{1,0},{2,3},{3,2},{4,5},{5,4},{6,7},{7,6},{8,9},{9,8},{10,11... | collective-permute-start | bytes 1966088 | tf_op jit(solution)/shard_map/ppermute | solution.py:74
  546.7 48.2 %collective-permute-start.42 = (bf16[256,1280]{1,0:T(8,128)(2,1)S(1)}, bf16[256,1280]{1,0:T(8,128)(2,1)S(1)}, u32[]{:S(2)}, u32[]{:S(2)}) collective-permute-start(bf16[256,1280]{1,0:T(8,128)(2,1)S(1)} %collective-permute-done.41), channel_id=1, source_target_pairs={{0,1},{1,0},{2,3},{3,2},{4,5},{5,4},{6,7},{7,6},{8,9},{9,8},{10,11... | collective-permute-start | bytes 1966088 | tf_op jit(solution)/shard_map/ppermute | solution.py:74
  577.8 28.4 %collective-permute-start.55 = (bf16[256,1280]{1,0:T(8,128)(2,1)S(1)}, bf16[256,1280]{1,0:T(8,128)(2,1)S(1)}, u32[]{:S(2)}, u32[]{:S(2)}) collective-permute-start(bf16[256,1280]{1,0:T(8,128)(2,1)S(1)} %bitcast.219), channel_id=1, source_target_pairs={{0,1},{1,0},{2,3},{3,2},{4,5},{5,4},{6,7},{7,6},{8,9},{9,8},{10,11... | collective-permute-start | bytes 1966088 | tf_op jit(solution)/shard_map/ppermute | solution.py:74
  591.4 19.7 %collective-permute-start.47 = (bf16[256,2560]{1,0:T(8,128)(2,1)S(1)}, bf16[256,2560]{1,0:T(8,128)(2,1)S(1)}, u32[]{:S(2)}, u32[]{:S(2)}) collective-permute-start(bf16[256,2560]{1,0:T(8,128)(2,1)S(1)} %collective-permute-done.46), channel_id=1, source_target_pairs={{0,1},{1,0},{2,3},{3,2},{4,5},{5,4},{6,7},{7,6},{8,9},{9,8},{10,11... | collective-permute-start | bytes 3932168 | tf_op jit(solution)/shard_map/ppermute | solution.py:74
  593.1 21.6 %collective-permute-start.44 = (bf16[320,512]{1,0:T(8,128)(2,1)S(1)}, bf16[320,512]{1,0:T(8,128)(2,1)S(1)}, u32[]{:S(2)}, u32[]{:S(2)}) collective-permute-start(bf16[320,512]{1,0:T(8,128)(2,1)S(1)} %copy-done.53), channel_id=1, source_target_pairs={{0,4},{1,5},{2,6},{3,7},{4,0},{5,1},{6,2},{7,3},{8,12},{9,13},{10,... | collective-permute-start | bytes 983048 | tf_op jit(solution)/shard_map/ppermute | solution.py:74
  605.1 71.6 %collective-permute-start.78 = (bf16[1,320,1920]{2,1,0:T(8,128)(2,1)}, bf16[1,320,1920]{2,1,0:T(8,128)(2,1)}, u32[]{:S(2)}, u32[]{:S(2)}) collective-permute-start(bf16[1,320,1920]{2,1,0:T(8,128)(2,1)} %add_convert_fusion.2), channel_id=1, source_target_pairs={{0,4},{1,5},{2,6},{3,7},{4,0},{5,1},{6,2},{7,3},{8,12},{9,13},{10,... | collective-permute-start | bytes 3686408 | tf_op jit(solution)/shard_map/ppermute | solution.py:74
  606.2 93.1 %collective-permute-start.80 = (bf16[1,320,1920]{2,1,0:T(8,128)(2,1)}, bf16[1,320,1920]{2,1,0:T(8,128)(2,1)}, u32[]{:S(2)}, u32[]{:S(2)}) collective-permute-start(bf16[1,320,1920]{2,1,0:T(8,128)(2,1)} %add_convert_fusion.1), channel_id=1, source_target_pairs={{0,8},{1,9},{2,10},{3,11},{4,12},{5,13},{6,14},{7,15},{8,0},{9,1},... | collective-permute-start | bytes 3686408 | tf_op jit(solution)/shard_map/ppermute | solution.py:74
  606.7 128.4 %collective-permute-start.82 = (bf16[1,320,1920]{2,1,0:T(8,128)(2,1)}, bf16[1,320,1920]{2,1,0:T(8,128)(2,1)}, u32[]{:S(2)}, u32[]{:S(2)}) collective-permute-start(bf16[1,320,1920]{2,1,0:T(8,128)(2,1)} %add_convert_fusion), channel_id=1, source_target_pairs={{0,8},{1,9},{2,10},{3,11},{4,12},{5,13},{6,14},{7,15},{8,0},{9,1},... | collective-permute-start | bytes 3686408 | tf_op jit(solution)/shard_map/ppermute | solution.py:74
  611.1 58.9 %collective-permute-start.60 = (bf16[192,1280]{1,0:T(8,128)(2,1)}, bf16[192,1280]{1,0:T(8,128)(2,1)}, u32[]{:S(2)}, u32[]{:S(2)}) collective-permute-start(bf16[192,1280]{1,0:T(8,128)(2,1)} %get-tuple-element.82), channel_id=1, source_target_pairs={{0,8},{1,9},{2,10},{3,11},{4,12},{5,13},{6,14},{7,15}} | collective-permute-start | bytes 1474568 | tf_op jit(solution)/shard_map/ppermute | solution.py:74
  614.7 59.8 %collective-permute-start.63 = (bf16[192,1280]{1,0:T(8,128)(2,1)}, bf16[192,1280]{1,0:T(8,128)(2,1)}, u32[]{:S(2)}, u32[]{:S(2)}) collective-permute-start(bf16[192,1280]{1,0:T(8,128)(2,1)} %get-tuple-element.83), channel_id=1, source_target_pairs={{24,16},{25,17},{26,18},{27,19},{28,20},{29,21},{30,22},{31,23}} | collective-permute-start | bytes 1474568 | tf_op jit(solution)/shard_map/ppermute | solution.py:74
  670.0 23.1 %collective-permute-start.48 = (bf16[320,1280]{1,0:T(8,128)(2,1)S(1)}, bf16[320,1280]{1,0:T(8,128)(2,1)S(1)}, u32[]{:S(2)}, u32[]{:S(2)}) collective-permute-start(bf16[320,1280]{1,0:T(8,128)(2,1)S(1)} %get-tuple-element.74), channel_id=1, source_target_pairs={{0,8},{1,9},{2,10},{3,11},{4,12},{5,13},{6,14},{7,15}} | collective-permute-start | bytes 2457608 | tf_op jit(solution)/shard_map/ppermute | solution.py:74
  674.5 19.3 %collective-permute-start.51 = (bf16[320,1280]{1,0:T(8,128)(2,1)S(1)}, bf16[320,1280]{1,0:T(8,128)(2,1)S(1)}, u32[]{:S(2)}, u32[]{:S(2)}) collective-permute-start(bf16[320,1280]{1,0:T(8,128)(2,1)S(1)} %get-tuple-element.75), channel_id=1, source_target_pairs={{24,16},{25,17},{26,18},{27,19},{28,20},{29,21},{30,22},{31,23}} | collective-permute-start | bytes 2457608 | tf_op jit(solution)/shard_map/ppermute | solution.py:74
  676.7 27.2 %collective-permute-start.61 = (bf16[192,1280]{1,0:T(8,128)(2,1)S(1)}, bf16[192,1280]{1,0:T(8,128)(2,1)S(1)}, u32[]{:S(2)}, u32[]{:S(2)}) collective-permute-start(bf16[192,1280]{1,0:T(8,128)(2,1)S(1)} %get-tuple-element.80), channel_id=1, source_target_pairs={{0,8},{1,9},{2,10},{3,11},{4,12},{5,13},{6,14},{7,15},{8,16},{9,17... | collective-permute-start | bytes 1474568 | tf_op jit(solution)/shard_map/ppermute | solution.py:74
  694.2 26.9 %collective-permute-start.49 = (bf16[320,1280]{1,0:T(8,128)(2,1)S(1)}, bf16[320,1280]{1,0:T(8,128)(2,1)S(1)}, u32[]{:S(2)}, u32[]{:S(2)}) collective-permute-start(bf16[320,1280]{1,0:T(8,128)(2,1)S(1)} %get-tuple-element.72), channel_id=1, source_target_pairs={{0,8},{1,9},{2,10},{3,11},{4,12},{5,13},{6,14},{7,15},{8,16},{9,17... | collective-permute-start | bytes 2457608 | tf_op jit(solution)/shard_map/ppermute | solution.py:74
  699.3 21.9 %collective-permute-start.52 = (bf16[320,1280]{1,0:T(8,128)(2,1)S(1)}, bf16[320,1280]{1,0:T(8,128)(2,1)S(1)}, u32[]{:S(2)}, u32[]{:S(2)}) collective-permute-start(bf16[320,1280]{1,0:T(8,128)(2,1)S(1)} %get-tuple-element.73), channel_id=1, source_target_pairs={{16,8},{17,9},{18,10},{19,11},{20,12},{21,13},{22,14},{23,15},{24,... | collective-permute-start | bytes 2457608 | tf_op jit(solution)/shard_map/ppermute | solution.py:74
  704.1 34.8 %collective-permute-start.65 = (bf16[192,1280]{1,0:T(8,128)(2,1)S(1)}, bf16[192,1280]{1,0:T(8,128)(2,1)S(1)}, u32[]{:S(2)}, u32[]{:S(2)}) collective-permute-start(bf16[192,1280]{1,0:T(8,128)(2,1)S(1)} %get-tuple-element.79), channel_id=1, source_target_pairs={{8,0},{9,1},{10,2},{11,3},{12,4},{13,5},{14,6},{15,7},{16,8},{17,9... | collective-permute-start | bytes 1474568 | tf_op jit(solution)/shard_map/ppermute | solution.py:74
  705.4 33.5 %collective-permute-start.62 = (bf16[192,1280]{1,0:T(8,128)(2,1)S(1)}, bf16[192,1280]{1,0:T(8,128)(2,1)S(1)}, u32[]{:S(2)}, u32[]{:S(2)}) collective-permute-start(bf16[192,1280]{1,0:T(8,128)(2,1)S(1)} %get-tuple-element.78), channel_id=1, source_target_pairs={{0,8},{1,9},{2,10},{3,11},{4,12},{5,13},{6,14},{7,15},{8,16},{9,17... | collective-permute-start | bytes 1474568 | tf_op jit(solution)/shard_map/ppermute | solution.py:74
  722.8 26.8 %collective-permute-start.53 = (bf16[320,1280]{1,0:T(8,128)(2,1)}, bf16[320,1280]{1,0:T(8,128)(2,1)}, u32[]{:S(2)}, u32[]{:S(2)}) collective-permute-start(bf16[320,1280]{1,0:T(8,128)(2,1)} %get-tuple-element.71), channel_id=1, source_target_pairs={{8,0},{9,1},{10,2},{11,3},{12,4},{13,5},{14,6},{15,7},{16,8},{17,9... | collective-permute-start | bytes 2457608 | tf_op jit(solution)/shard_map/ppermute | solution.py:74
  724.1 25.6 %collective-permute-start.50 = (bf16[320,1280]{1,0:T(8,128)(2,1)}, bf16[320,1280]{1,0:T(8,128)(2,1)}, u32[]{:S(2)}, u32[]{:S(2)}) collective-permute-start(bf16[320,1280]{1,0:T(8,128)(2,1)} %get-tuple-element.70), channel_id=1, source_target_pairs={{0,8},{1,9},{2,10},{3,11},{4,12},{5,13},{6,14},{7,15},{8,16},{9,17... | collective-permute-start | bytes 2457608 | tf_op jit(solution)/shard_map/ppermute | solution.py:74
  751.7 31.4 %collective-permute-start.68 = (bf16[80,2560]{1,0:T(8,128)(2,1)S(1)}, bf16[80,2560]{1,0:T(8,128)(2,1)S(1)}, u32[]{:S(2)}, u32[]{:S(2)}) collective-permute-start(bf16[80,2560]{1,0:T(8,128)(2,1)S(1)} %reshape.199), channel_id=1, source_target_pairs={{0,0},{1,1},{2,16},{3,17},{4,8},{5,9},{6,24},{7,25},{8,2},{9,3},{1... | collective-permute-start | bytes 1228808 | tf_op jit(solution)/shard_map/ppermute | solution.py:74
  (112 other events, 1517.9 us)

commit v3 on v2

--- a/solution.py
+++ b/solution.py
@@ -16,6 +16,8 @@
 BF16 = jnp.bfloat16
 GELU_C = 0.7978845608028654
 GELU_A = 0.044715
+VMEM_MAX = 60 * 1024 * 1024
+ANY = pl.BlockSpec(memory_space=pl.ANY)
 
 
 def norm_scale(values):
@@ -34,9 +36,9 @@
 
 def gelu_pair(values):
     square = values * values
-    t = jnp.tanh(GELU_C * values * (1.0 + GELU_A * square))
-    half = 0.5 * (1.0 + t)
-    slope = half + 0.5 * values * (1.0 - t * t) * GELU_C * (1.0 + 3.0 * GELU_A * square)
+    t = jnp.tanh(values * (GELU_C + GELU_C * GELU_A * square))
+    half = 0.5 + 0.5 * t
+    slope = half * (1.0 + (1.0 - t) * values * (GELU_C + 3.0 * GELU_C * GELU_A * square))
     return (values * half, slope)
 
 
@@ -267,6 +269,286 @@
     )(*values)
 
 
+def grad_hidden_of(parts, w_down):
+    count = len(parts)
+    rows, width = parts[0].shape
+    total = count * rows
+    ff = w_down.shape[1]
+
+    def body(*refs):
+        c_refs, (w_ref, out_ref, held, sem) = (refs[:count], refs[count:])
+
+        @pl.when(pl.program_id(0) == 0)
+        def _():
+            copies = [
+                pltpu.make_async_copy(c_refs[i], held.at[pl.ds(i * rows, rows)], sem.at[i])
+                for i in range(count)
+            ]
+            for copy in copies:
+                copy.start()
+            for copy in copies:
+                copy.wait()
+
+        out_ref[...] = dot(held[...], w_ref[...])
+
+    return pl.pallas_call(
+        body,
+        grid=(pl.cdiv(ff, BLK),),
+        in_specs=[ANY] * count + [pl.BlockSpec((width, BLK), lambda j: (0, j))],
+        out_specs=pl.BlockSpec((total, BLK), lambda j: (0, j)),
+        out_shape=jax.ShapeDtypeStruct((total, ff), F32),
+        scratch_shapes=[pltpu.VMEM((total, width), BF16), pltpu.SemaphoreType.DMA((count,))],
+        compiler_params=pltpu.CompilerParams(vmem_limit_bytes=VMEM_MAX),
+        cost_estimate=pl.CostEstimate(
+            flops=2 * total * width * ff, bytes_accessed=2 * width * ff + 4 * total * ff,
+            transcendentals=0),
+    )(*parts, w_down)
+
+
+def sections_of(total):
+    found, at = ([], 0)
+    while at < total:
+        size = min(768, total - at)
+        found.append((at, size))
+        at += size
+    return found
+
+
+def mlp_forward(n2_parts, grad_hidden, w_gate, w_up):
+    count = len(n2_parts)
+    rows, width = n2_parts[0].shape
+    total = count * rows
+    ff = w_gate.shape[1]
+    parts = sections_of(ff)
+    widest = parts[0][1]
+    far = total // 2
+
+    def body(*refs):
+        n_refs = refs[:count]
+        gh_ref, wg_ref, wu_ref = refs[count : count + 3]
+        hid_ref, gg_ref, gu_ref, far_ref, far_c_ref = refs[count + 3 : count + 8]
+        n2_s, gh_s, wg_s, wu_s, acc, sem_n, sem_w = refs[count + 8 :]
+
+        def load(k):
+            at, size = parts[k]
+            slot = k % 2
+            return [
+                pltpu.make_async_copy(
+                    wg_ref.at[:, pl.ds(at, size)], wg_s.at[slot, :, pl.ds(0, size)], sem_w.at[slot, 0]),
+                pltpu.make_async_copy(
+                    wu_ref.at[:, pl.ds(at, size)], wu_s.at[slot, :, pl.ds(0, size)], sem_w.at[slot, 1]),
+                pltpu.make_async_copy(
+                    gh_ref.at[:, pl.ds(at, size)], gh_s.at[slot, :, pl.ds(0, size)], sem_w.at[slot, 2]),
+            ]
+
+        first = [
+            pltpu.make_async_copy(n_refs[i], n2_s.at[pl.ds(i * rows, rows)], sem_n.at[i])
+            for i in range(count)
+        ]
+        for copy in first + load(0):
+            copy.start()
+        for copy in first:
+            copy.wait()
+        for k, (at, size) in enumerate(parts):
+            if k + 1 < len(parts):
+                for copy in load(k + 1):
+                    copy.start()
+            for copy in load(k):
+                copy.wait()
+            slot = k % 2
+            wg, wu = (wg_s[slot, :, :size], wu_s[slot, :, :size])
+            gelu, slope = gelu_pair(dot(n2_s[...], wg))
+            up = dot(n2_s[...], wu)
+            gh = gh_s[slot, :, :size]
+            hid_ref[:, at : at + size] = (gelu * up).astype(BF16)
+            gg = (gh * up * slope).astype(BF16)
+            gu = (gh * gelu).astype(BF16)
+            gg_ref[:, at : at + size] = gg
+            gu_ref[:, at : at + size] = gu
+
+            def far_rows(v):
+                return jnp.concatenate([v[rows : 2 * rows], v[3 * rows :]], axis=0)
+
+            part = dot_cols(far_rows(gg), wg) + dot_cols(far_rows(gu), wu)
+            if k == 0:
+                acc[...] = part
+            else:
+                acc[...] += part
+        far_ref[...] = acc[:rows]
+        far_c_ref[...] = acc[rows:].astype(BF16)
+
+    act = jax.ShapeDtypeStruct((total, ff), BF16)
+    return pl.pallas_call(
+        body,
+        in_specs=[ANY] * (count + 3),
+        out_shape=[act, act, act, jax.ShapeDtypeStruct((rows, width), F32),
+                   jax.ShapeDtypeStruct((rows, width), BF16)],
+        scratch_shapes=[
+            pltpu.VMEM((total, width), BF16),
+            pltpu.VMEM((2, total, widest), F32),
+            pltpu.VMEM((2, width, widest), BF16),
+            pltpu.VMEM((2, width, widest), BF16),
+            pltpu.VMEM((far, width), F32),
+            pltpu.SemaphoreType.DMA((count,)),
+            pltpu.SemaphoreType.DMA((2, 3)),
+        ],
+        compiler_params=pltpu.CompilerParams(vmem_limit_bytes=VMEM_MAX),
+        cost_estimate=pl.CostEstimate(
+            flops=6 * total * width * ff, bytes_accessed=4 * width * ff + 16 * total * ff,
+            transcendentals=total * ff),
+    )(*n2_parts, grad_hidden, w_gate, w_up)
+
+
+def mlp_rest(hidden, grad_gate, grad_up, w_gate, w_up, w_down, rows):
+    total, ff = hidden.shape
+    width = w_gate.shape[0]
+    block = 512
+
+    def body(hid_ref, gg_ref, gu_ref, wg_ref, wu_ref, wd_ref, gn_ref, gn_c_ref, out_ref, out_c_ref):
+        def near(ref):
+            return jnp.concatenate([ref[:rows], ref[2 * rows : 3 * rows]], axis=0)
+
+        gn = dot_cols(near(gg_ref), wg_ref[...]) + dot_cols(near(gu_ref), wu_ref[...])
+        gn_ref[...] = gn[:rows]
+        gn_c_ref[...] = gn[rows:].astype(BF16)
+        out = dot_cols(hid_ref[...], wd_ref[...])
+        out_ref[...] = out[: total // 2]
+        out_c_ref[...] = out[total // 2 :].astype(BF16)
+
+    whole = pl.BlockSpec((total, ff), lambda j: (0, 0))
+    weight = pl.BlockSpec((block, ff), lambda j: (j, 0))
+    tall = lambda n: pl.BlockSpec((n, block), lambda j: (0, j))
+    shape = lambda n, dt: jax.ShapeDtypeStruct((n, width), dt)
+    return pl.pallas_call(
+        body,
+        grid=(width // block,),
+        in_specs=[whole] * 3 + [weight] * 3,
+        out_specs=[tall(rows), tall(rows), tall(total // 2), tall(total // 2)],
+        out_shape=[shape(rows, F32), shape(rows, BF16), shape(total // 2, F32), shape(total // 2, BF16)],
+        compiler_params=pltpu.CompilerParams(vmem_limit_bytes=VMEM_MAX),
+        cost_estimate=pl.CostEstimate(
+            flops=4 * total * width * ff, bytes_accessed=6 * width * ff + 6 * total * ff,
+            transcendentals=0),
+    )(hidden, grad_gate, grad_up, w_gate, w_up, w_down)
+
+
+def rows_of_tokens(parts, place, rows_out, each):
+    tokens, width = parts[0].shape
+    half = width // 2
+    count = len(parts)
+
+    def body(place_ref, *refs):
+        out_ref, turned = (refs[count], refs[count + 1])
+        for k in range(count):
+            turned[...] = refs[k][...].T
+            for i in range(rows_out // each):
+                at = pl.multiple_of((2 * i + place_ref[1]) * each, 16)
+                out_ref[i * each : (i + 1) * each, k * tokens : (k + 1) * tokens] = turned[pl.ds(at, each), :]
+
+    return pl.pallas_call(
+        body,
+        grid_spec=pltpu.PrefetchScalarGridSpec(
+            num_scalar_prefetch=1,
+            grid=(1,),
+            in_specs=[pl.BlockSpec((tokens, half), lambda i, place: (0, place[0]))] * count,
+            out_specs=pl.BlockSpec((rows_out, count * tokens), lambda i, place: (0, 0)),
+            scratch_shapes=[pltpu.VMEM((half, tokens), BF16)],
+        ),
+        out_shape=jax.ShapeDtypeStruct((rows_out, count * tokens), BF16),
+        compiler_params=pltpu.CompilerParams(vmem_limit_bytes=VMEM_MAX),
+        cost_estimate=pl.CostEstimate(
+            flops=0, bytes_accessed=6 * rows_out * count * tokens, transcendentals=0),
+    )(place, *parts)
+
+
+def mlp_weight_grads(n2_parts, grad_hiddens, acts, n2_rows, cot_rows, weights, at, size):
+    groups = len(n2_parts)
+    per = len(n2_parts[0])
+    tokens, width = n2_parts[0][0].shape
+    group = per * tokens
+    both = group // 2
+    rows = n2_rows[0].shape[0]
+    ff = weights[0].shape[1]
+    flat_n = [p for g in n2_parts for p in g]
+    total = len(flat_n)
+
+    def body(*refs):
+        n_refs, h_refs = (refs[:total], refs[total : total + groups])
+        wg_ref, wu_ref, hid_ref, gg_ref, gu_ref, nm, no, cm, co = refs[total + groups : total + groups + 9]
+        out_ref = refs[total + groups + 9]
+        n2_s, gh_s, acc, sem = refs[total + groups + 10 :]
+
+        def load(g, slot):
+            found = []
+            for i in range(per):
+                to = pl.ds(i * tokens, tokens)
+                found.append(pltpu.make_async_copy(n_refs[g * per + i], n2_s.at[slot, to], sem.at[slot, i]))
+            found.append(pltpu.make_async_copy(
+                h_refs[g].at[:, pl.ds(at, size)], gh_s.at[slot], sem.at[slot, per]))
+            return found
+
+        for copy in load(0, 0):
+            copy.start()
+
+        def add(g, act, fresh):
+            start = g * both if isinstance(g, int) else pl.multiple_of(g * both, both)
+            for i, (mine, other) in enumerate(((cm, co), (nm, no), (nm, no))):
+                part = dot(mine[:, pl.ds(start, both)], act[i][:both]) + dot(
+                    other[:, pl.ds(start, both)], act[i][both:])
+                if fresh:
+                    acc[i] = part
+                else:
+                    acc[i] += part
+
+        add(0, (hid_ref[...], gg_ref[...], gu_ref[...]), True)
+
+        def step(g, carry):
+            slot = lax.rem(g, 2)
+            for k in range(1, groups):
+                @pl.when(g + 1 == k)
+                def _():
+                    for copy in load(k, k % 2):
+                        copy.start()
+
+            for copy in load(0, slot):
+                copy.wait()
+            gelu, slope = gelu_pair(dot(n2_s[slot], wg_ref[...]))
+            up = dot(n2_s[slot], wu_ref[...])
+            gh = gh_s[slot]
+            add(g + 1, ((gelu * up).astype(BF16), (gh * up * slope).astype(BF16), (gh * gelu).astype(BF16)), False)
+            return carry
+
+        lax.fori_loop(0, groups, step, 0)
+        for i in range(3):
+            out_ref[:, i * size : (i + 1) * size] = acc[i].astype(BF16)
+
+    index = at // size
+    column = lambda n: pl.BlockSpec((n, size), lambda j: (0, index))
+    whole = pl.BlockSpec(n2_rows[0].shape, lambda j: (0, 0))
+    return pl.pallas_call(
+        body,
+        grid=(1,),
+        in_specs=[ANY] * (total + groups) + [column(width)] * 2 + [column(group)] * 3 + [whole] * 4,
+        out_specs=pl.BlockSpec((rows, 3 * size), lambda j: (0, 0)),
+        out_shape=jax.ShapeDtypeStruct((rows, 3 * size), BF16),
+        scratch_shapes=[
+            pltpu.VMEM((2, group, width), BF16),
+            pltpu.VMEM((2, group, size), F32),
+            pltpu.VMEM((3, rows, size), F32),
+            pltpu.SemaphoreType.DMA((2, per + 1)),
+        ],
+        compiler_params=pltpu.CompilerParams(vmem_limit_bytes=VMEM_MAX),
+        cost_estimate=pl.CostEstimate(
+            flops=4 * groups * group * width * size + 6 * (groups + 1) * group * rows * size,
+            bytes_accessed=4 * width * size + 4 * groups * group * width,
+            transcendentals=groups * group * size),
+    )(*flat_n, *grad_hiddens, *weights, *acts, *n2_rows, *cot_rows)
+
+
+def after(value, *others):
+    return lax.optimization_barrier((value, others))[0]
+
+
 def entering(lay, summary, groups, backward):
     prod, state = (summary[:groups], summary[groups : 2 * groups])
     before_p, before_s = (jnp.ones_like(prod), jnp.zeros_like(state))
@@ -341,14 +623,15 @@
     gate_x = lay.over_x(rows_theirs)
     gate_c, gate_xc = (lay.over_c(rows_mine), lay.over_c(gate_x))
     gates = order_f(jnp.concatenate([rows_mine, gate_c, gate_x, gate_xc], axis=1))
-    out_mine = lax.dynamic_slice_in_dim(out_proj, x * half, half, 0)
-    out_x = lay.over_x(lax.dynamic_slice_in_dim(out_proj, (1 - x) * half, half, 0))
+    out_later = after(out_proj, halo_own)
+    out_mine = lax.dynamic_slice_in_dim(out_later, x * half, half, 0)
+    out_x = lay.over_x(lax.dynamic_slice_in_dim(out_later, (1 - x) * half, half, 0))
     out_c, out_xc = (lay.over_c(out_mine), lay.over_c(out_x))
     out_rel = jnp.concatenate([out_mine, out_c, out_x, out_xc], axis=1)
     cot = cotangent[0]
-    cot_c = lay.over_c(cot)
-    cot_x = lay.over_x(cot)
-    cot_xc = lay.over_c(cot_x)
+    cot_y, cot_z = (lay.over_y(cot), lay.over_z(cot))
+    cot_x = lay.over_x(after(cot, normed_own))
+    cot_xz, cot_xy = (lay.over_x(cot_z), lay.over_y(cot_x))
 
     normed = jnp.concatenate([normed_own, normed_x, halo_own, halo_x], axis=0)
     two = 2 * tokens
@@ -367,6 +650,12 @@
         [(x_low, False), (halo, False), (gates, True), (vec_half, False), (rates, False)],
         [shape3(BF16), shape3(F32), shape3(F32), shape3(F32), shape3(F32), summary_shape])
     state_in = entering(lay, summary, 2, False)
+    cot_yz = lay.over_y(after(cot_z, state_in))
+    cot_xyz = lay.over_y(after(cot_xz, state_in))
+    cots = [[cot, cot_x], [cot_y, cot_xy], [cot_z, cot_xz], [cot_yz, cot_xyz]]
+    cots_c = [[lay.over_c(part) for part in group] for group in cots]
+    grad_hiddens = [
+        grad_hidden_of(group + group_c, mlp_down) for group, group_c in zip(cots, cots_c)]
     state = local_state + prods * state_in[:, None, :]
     mixed = (state * jax.nn.gelu(y_pre, approximate=True)).astype(BF16)
     part_x = dot(mixed[1], out_rel).astype(BF16)
@@ -377,83 +666,19 @@
 
     scaled_two, inverse_two = norm_scale(mid)
     n2 = (scaled_two * vectors[1]).astype(BF16)
-    n2_c = lay.over_c(n2)
     n2_x = lay.over_x(n2)
-    n2_xc = lay.over_c(n2_x)
-
-    def mlp(normed_in, cot_in):
-        gate_val = dot(normed_in, mlp_gate)
-        up_val = dot(normed_in, mlp_up)
-        grad_hidden = dot(cot_in, mlp_down)
-        gelu, slope = gelu_pair(gate_val)
-        hidden = (gelu * up_val).astype(BF16)
-        grad_gate = (grad_hidden * up_val * slope).astype(BF16)
-        grad_up = (grad_hidden * gelu).astype(BF16)
-        return hidden, grad_gate, grad_up
-
-    main_n2 = jnp.concatenate([n2, n2_c, n2_x, n2_xc], 0)
-    main_cot = jnp.concatenate([cot, cot_c, cot_x, cot_xc], 0)
-    main = mlp(main_n2, main_cot)
-
-    def to_owners(of):
-        far_part = of(slice(two, 2 * two))
-        far_sum = far_part[:tokens] + lay.over_c(far_part[tokens:].astype(BF16)).astype(F32)
-        arriving = lay.over_x(far_sum.astype(BF16))
-        near_part = of(slice(0, two))
-        near_sum = near_part[:tokens] + lay.over_c(near_part[tokens:].astype(BF16)).astype(F32)
-        return near_sum + arriving.astype(F32)
-
-    grad_n2 = to_owners(
-        lambda rows: dot_cols(main[1][rows], mlp_gate) + dot_cols(main[2][rows], mlp_up))
-    output = (mid + to_owners(lambda rows: dot_cols(main[0][rows], mlp_down))).astype(BF16)[None]
-
-    n2_z, n2_xz = (lay.over_z(n2), lay.over_z(n2_x))
-    cot_z, cot_xz = (lay.over_z(cot), lay.over_z(cot_x))
-    side_n2 = jnp.concatenate([n2_z, lay.over_c(n2_z), n2_xz, lay.over_c(n2_xz)], 0)
-    side_cot = jnp.concatenate([cot_z, lay.over_c(cot_z), cot_xz, lay.over_c(cot_xz)], 0)
-    side = mlp(side_n2, side_cot)
-    each = width // lay.seq
-    seq_at = 2 * z + y
-    upper = seq_at // nz
-
-    def window(value):
-        return lax.dynamic_slice_in_dim(value, upper * half, half, 1)
-
-    n2_rows = jnp.concatenate([window(main_n2), window(side_n2)], 0)
-    cot_rows = jnp.concatenate([window(main_cot), window(side_cot)], 0)
-    hidden_all, gg_all, gu_all = [jnp.concatenate([main[i], side[i]], 0) for i in range(3)]
-
-    def halve(blocks, bits):
-        own = seq_at % nz
-
-        def pick(j):
-            return lax.dynamic_index_in_dim(blocks, own ^ j, 0, keepdims=False).astype(F32)
-
-        def joined(old, come, at):
-            return old() + come[at].astype(F32)
-
-        held = {j: functools.partial(pick, j) for j in range(nz)}
-        for bit in bits:
-            leaving = sorted(j for j in held if j & bit)
-            sent = jnp.stack([held[j]().astype(BF16) for j in leaving])
-            come = lay.over_seq_bit(sent, bit)
-            held = {
-                j ^ bit: functools.partial(joined, held[j ^ bit], come, i)
-                for i, j in enumerate(leaving)
-            }
-        return held[0]()
-
-    bits = []
-    bit = 1
-    while bit < nz:
-        bits.append(bit)
-        bit *= 2
-    mlp_grads = []
-    for left, right, order in (
-        (cot_rows, hidden_all, bits), (n2_rows, gg_all, bits[::-1]), (n2_rows, gu_all, bits)):
-        part = dot_rows(left, right).astype(BF16).reshape(nz, each, right.shape[1])
-        mlp_grads.append(halve(part, order))
-    mlp_down_grad, mlp_gate_grad, mlp_up_grad = mlp_grads
+    n2_y, n2_z = (lay.over_y(n2), lay.over_z(n2))
+    n2_xy, n2_xz = (lay.over_y(n2_x), lay.over_z(n2_x))
+    n2_yz, n2_xyz = (lay.over_y(n2_z), lay.over_y(n2_xz))
+    n2s = [[n2, n2_x], [n2_y, n2_xy], [n2_z, n2_xz], [n2_yz, n2_xyz]]
+    n2s_c = [[lay.over_c(part) for part in group] for group in n2s]
+    hidden, grad_gate, grad_up, far, far_c = mlp_forward(
+        n2s[0] + n2s_c[0], grad_hiddens[0], mlp_gate, mlp_up)
+    arriving = lay.over_x((far + lay.over_c(far_c).astype(F32)).astype(BF16))
+    near, near_c, out, out_c = mlp_rest(
+        hidden, grad_gate, grad_up, mlp_gate, mlp_up, mlp_down, tokens)
+    grad_n2 = near + lay.over_c(near_c).astype(F32) + arriving.astype(F32)
+    out_sum = out + lay.over_c(out_c).astype(F32)
 
     grad_mid_norm, grad_gain_two = norm_back(grad_n2, scaled_two, inverse_two, vectors[1])
     grad_mid = cot.astype(F32) + grad_mid_norm
@@ -461,6 +686,8 @@
     branch_rel = order_f(branch)
     arriving = lay.over_x(branch_rel)
     branch_x_rel = jnp.concatenate([arriving[:, half:], arriving[:, :half]], axis=1)
+    out_arriving = lay.over_x(after(out_sum[tokens:].astype(BF16), branch))
+    output = (mid + out_sum[:tokens] + out_arriving.astype(F32)).astype(BF16)[None]
     grad_mixed = dot_cols(jnp.concatenate([branch_rel, branch_x_rel], 0), out_rel)
     gy, bprod, blocal, back_summary = by_head(
         mixer_back_scan, flags,
@@ -490,10 +717,34 @@
         return (dot_cols(gy_o[rows], wy) + dot_cols(gy_c[rows], wy_c)
                 + dot_cols(gx_o[rows], wx) + dot_cols(gx_c[rows], wx_c))
 
-    arriving = lay.over_x(grad_n1_of(slice(tokens, two)).astype(BF16))
+    grad_n1_far = grad_n1_of(slice(tokens, two)).astype(BF16)
+    arriving = lay.over_x(grad_n1_far)
     grad_n1 = grad_n1_of(slice(0, tokens)) + arriving.astype(F32)
     grad_in_norm, grad_gain_one = norm_back(grad_n1, scaled_one, inverse_one, vectors[0])
     input_grad = (grad_mid + grad_in_norm).astype(BF16)[None]
+
+    each = width // lay.seq
+    seq_at = 2 * z + y
+    place = jnp.stack([seq_at // nz, y]).astype(jnp.int32)
+    n2_rows = rows_of_tokens([p for group in n2s for p in group], place, half // 2, each)
+    cot_rows = rows_of_tokens([p for group in cots for p in group], place, half // 2, each)
+    row_pairs = ((n2_rows, lay.over_c(n2_rows)), (cot_rows, lay.over_c(cot_rows)))
+    acts = (hidden, grad_gate, grad_up)
+    sides = [group + group_c for group, group_c in zip(n2s[1:], n2s_c[1:])]
+    share = [
+        [2 * (upper * (nz // 2) + low) + side for low in range(nz // 2)]
+        for upper in range(2) for side in range(2)]
+    ties = (branch, grad_n1_far, input_grad)
+    columns = [[], [], []]
+    for (at, size), tie in zip(sections_of(mlp_gate.shape[1]), ties):
+        part = mlp_weight_grads(
+            sides, grad_hiddens[1:], after(acts, tie), *row_pairs, (mlp_gate, mlp_up), at, size)
+        part = lax.psum_scatter(
+            part, "seq", scatter_dimension=0, axis_index_groups=share, tiled=True)
+        for i in range(3):
+            columns[i].append(part[:, i * size : (i + 1) * size])
+    mlp_down_grad, mlp_gate_grad, mlp_up_grad = [
+        jnp.concatenate(parts, axis=1).astype(F32) for parts in columns]
 
     rows_full = lax.dynamic_update_slice_in_dim(
         jnp.zeros((8, width), F32), vec_rows, x * half, 1)

time: 795 us -> 749 us (0.942)
  Pallas kernels: 20.5 us -> 200 us
  matrix products: 189 us -> 54.8 us
  waiting for transfers between devices: 302 us -> 241 us
  starting transfers between devices: 147 us -> 122 us
  between operations: 3.22 us -> 15.9 us
  other arithmetic: 68.4 us -> 56.1 us
    pallas_call x0 -> x11, Pallas kernels: none -> 180 us  [the longest x3 76.9 us: mlp_weight_grads(): pl.pallas_call(body, grid=(1,), in_specs=[ANY] * (total + groups) + [colu...]
    dot_general x15 -> x9, matrix products: 101 us -> 32.2 us  [dot(): return jnp.dot(left, right, preferred_element_type=F32)]
    ppermute x83 -> x94, waiting for transfers between devices: 302 us -> 241 us  [send(): return lax.ppermute(value, ALL, self.pairs(target))]
    dot_general x15 -> x9, matrix products: 62.3 us -> 22.1 us  [dot_cols(): lax.dot_general(left, right, (((1,), (1,)), ((), ())), preferred_element_...]
    ppermute x83 -> x94, starting transfers between devices: 147 us -> 121 us  [send(): return lax.ppermute(value, ALL, self.pairs(target))]
    dot_general x3 -> x0, matrix products: 23.4 us -> none  [dot_rows(): lax.dot_general(left, right, (((0,), (0,)), ((), ())), preferred_element_...]
    add x3 -> x1, other arithmetic: 11.6 us -> 1.7 us  [local(): out_sum = out + lay.over_c(out_c).astype(F32)]
  transfers between devices with their start and end apart: 83 -> 97, of which waited for: 22 -> 29; matrix products, arithmetic and copies ran while one was open for 39% -> 19% of each run, Pallas kernels for 3% -> 24%
where the time goes in v3:
time: 749 us; the launch traced here: 741 us
  waiting for transfers between devices  241 us (32%)
  Pallas kernels  200 us (27%)
  starting transfers between devices  122 us (16%)
  other arithmetic  56.1 us (7%)
  matrix products  54.8 us (7%)
  local copies, waits for them, and re-layouts  51.6 us (7%)
  between operations  15.9 us (2%)
    ppermute x94, waiting for transfers between devices, send(): return lax.ppermute(value, ALL, self.pairs(target))  241 us
    ppermute x94, starting transfers between devices, send(): return lax.ppermute(value, ALL, self.pairs(target))  121 us
    pallas_call x3, Pallas kernels, mlp_weight_grads(): pl.pallas_call(body, grid=(1,), in_specs=[ANY] * (total + groups) + [colu...  76.9 us
    pallas_call x4, Pallas kernels, grad_hidden_of(): pl.pallas_call(body, grid=(pl.cdiv(ff, BLK),), in_specs=[ANY] * count + [...  51.3 us
    dot_general x9, matrix products, dot(): return jnp.dot(left, right, preferred_element_type=F32)  32.2 us
    pallas_call x1, Pallas kernels, mlp_forward(): pl.pallas_call(body, in_specs=[ANY] * (count + 3), out_shape=[act, act, a...  23.4 us
    dot_general x9, matrix products, dot_cols(): lax.dot_general(left, right, (((1,), (1,)), ((), ())), preferred_element_...  22.1 us
    pallas_call x3, Pallas kernels, by_head(): pl.pallas_call(body, grid=(heads,), in_specs=in_specs, out_specs=[spec(o....  20.5 us
  transfers between devices with their start and end apart: 97, of which 29 were waited for; matrix products, arithmetic and copies ran while one was open for 19% of the time, Pallas kernels for 24%

profile of v3, /device:TPU:2, one launch (start us, length us, event | category | flops | bytes accessed | tf_op | source)
XLA Modules:
  0.0 741.4 jit_solution(4247881393085060786)
XLA Ops:
  8.8 3.5 collective-permute-start
  22.9 3.9 constant_dynamic-slice_fusion.1
  26.8 16.2 %collective-permute-done.1 = bf16[16,2560]{1,0:T(8,128)(2,1)S(1)} collective-permute-done((bf16[16,2560]{1,0:T(8,128)(2,1)S(1)}, bf16[16,2560]{1,0:T(8,128)(2,1)S(1)}, u32[]{:S(2)}, u32[]{:S(2)}) %collective-permute-start.1) | collective-permute-done | bytes 81952 | tf_op jit(solution)/shard_map/ppermute | solution.py:76
  44.2 5.0 collective-permute-done.6
  55.7 3.5 convolution_convert_fusion.4
  59.5 7.4 shard_map.195
  78.1 3.6 collective-permute-done.12
  89.4 4.4 convolution_convert_fusion.1
  95.9 15.5 %collective-permute-done.14 = bf16[128,2560]{1,0:T(8,128)(2,1)S(1)} collective-permute-done((bf16[128,2560]{1,0:T(8,128)(2,1)S(1)}, bf16[128,2560]{1,0:T(8,128)(2,1)S(1)}, u32[]{:S(2)}, u32[]{:S(2)}) %collective-permute-start.14) | collective-permute-done | bytes 655392 | tf_op jit(solution)/shard_map/ppermute | solution.py:76
  111.5 4.6 convolution_add_fusion.6
  121.9 3.7 collective-permute-done.18.refs_1_
  126.1 12.8 %collective-permute-done.15.refs_1_ = bf16[128,2560]{1,0:T(8,128)(2,1)} collective-permute-done((bf16[128,2560]{1,0:T(8,128)(2,1)}, bf16[128,2560]{1,0:T(8,128)(2,1)}, u32[]{:S(2)}, u32[]{:S(2)}) %collective-permute-start.15) | collective-permute-done | bytes 655392 | tf_op jit(solution)/shard_map/ppermute | solution.py:76
  142.0 13.0 %shard_map.196.refs_4_ = f32[512,1920]{1,0:T(8,128)} custom-call(bf16[128,2560]{1,0:T(8,128)(2,1)} %bitcast.9.refs_0_, bf16[128,2560]{1,0:T(8,128)(2,1)} %collective-permute-done.18.refs_1_, bf16[128,2560]{1,0:T(8,128)(2,1)} %collective-permute-done.19.refs_2_, bf16[128,2560]{1,0:T(8,128)(2,1)} %collective-permute-done.20.refs_3_, bf16[2560,1920]{1,0:T(8,128)(2,1)} %refs_4_.7), custom_call_target="tpu_custom_call" | custom-call | flops 5033164800 | bytes 13762560 | tf_op jit(solution)/shard_map/pallas_call | solution.py:294
  154.9 23.4 %shard_map.197 = (bf16[512,1920]{1,0:T(8,128)(2,1)}, bf16[512,1920]{1,0:T(8,128)(2,1)}, bf16[512,1920]{1,0:T(8,128)(2,1)}, f32[128,2560]{1,0:T(8,128)}, bf16[128,2560]{1,0:T(8,128)(2,1)}) custom-call(bf16[128,2560]{1,0:T(8,128)(2,1)} %multiply_convert_fusion.refs_0_, bf16[128,2560]{1,0:T(8,128)(2,1)} %collective-permute-done.15.refs_1_, ...), custom_call_target="tpu_custom_call" | custom-call | flops 15099494400 | bytes 35389440 | tf_op jit(solution)/shard_map/pallas_call | solution.py:381
  178.4 19.2 %shard_map.198 = (f32[128,2560]{1,0:T(8,128)}, bf16[128,2560]{1,0:T(8,128)(2,1)}, f32[256,2560]{1,0:T(8,128)}, bf16[256,2560]{1,0:T(8,128)(2,1)}) custom-call(bf16[512,1920]{1,0:T(8,128)(2,1)} %get-tuple-element.82.hid_ref.refs_17_, bf16[512,1920]{1,0:T(8,128)(2,1)} %get-tuple-element.83.gg_ref.refs_18_, ...), custom_call_target="tpu_custom_call" | custom-call | flops 10066329600 | bytes 35389440 | tf_op jit(solution)/shard_map/pallas_call | solution.py:422
  203.2 14.3 %collective-permute-done.24 = bf16[128,2560]{1,0:T(8,128)(2,1)} collective-permute-done((bf16[128,2560]{1,0:T(8,128)(2,1)}, bf16[128,2560]{1,0:T(8,128)(2,1)}, u32[]{:S(2)}, u32[]{:S(2)}) %collective-permute-start.24) | collective-permute-done | bytes 655392 | tf_op jit(solution)/shard_map/ppermute | solution.py:76
  228.6 12.8 %shard_map.201.refs_12_ = f32[512,1920]{1,0:T(8,128)} custom-call(bf16[128,2560]{1,0:T(8,128)(2,1)} %collective-permute-done.80.refs_0_.refs_2_, bf16[128,2560]{1,0:T(8,128)(2,1)} %collective-permute-done.81.refs_1_.refs_3_, bf16[128,2560]{1,0:T(8,128)(2,1)} %copy-done.53, bf16[128,2560]{1,0:T(8,128)(2,1)} %copy-done.54, bf16[2560,1920]{1,0:T(8,128)(2,1)} %refs_4_.7), custom_call_target="tpu_custom_call" | custom-call | flops 5033164800 | bytes 13762560 | tf_op jit(solution)/shard_map/pallas_call | solution.py:294
  245.5 12.8 %shard_map.202.refs_13_ = f32[512,1920]{1,0:T(8,128)} custom-call(bf16[128,2560]{1,0:T(8,128)(2,1)} %collective-permute-done.84.refs_0_.refs_4_, bf16[128,2560]{1,0:T(8,128)(2,1)} %collective-permute-done.85.refs_1_.refs_5_, bf16[128,2560]{1,0:T(8,128)(2,1)} %collective-permute-done.86.refs_2_, bf16[128,2560]{1,0:T(8,128)(2,1)} %collective-permute-done.87.refs_3_, ...), custom_call_target="tpu_custom_call" | custom-call | flops 5033164800 | bytes 13762560 | tf_op jit(solution)/shard_map/pallas_call | solution.py:294
  258.3 4.4 shard_map.205.refs_22_
  266.2 8.8 %collective-permute-done.73.refs_5_ = bf16[128,2560]{1,0:T(8,128)(2,1)} collective-permute-done((bf16[128,2560]{1,0:T(8,128)(2,1)}, bf16[128,2560]{1,0:T(8,128)(2,1)}, u32[]{:S(2)}, u32[]{:S(2)}) %collective-permute-start.73) | collective-permute-done | bytes 655392 | tf_op jit(solution)/shard_map/ppermute | solution.py:76
  276.2 4.5 fusion.45
  280.7 5.4 shard_map.199
  288.9 12.8 %shard_map.203.refs_14_ = f32[512,1920]{1,0:T(8,128)} custom-call(bf16[128,2560]{1,0:T(8,128)(2,1)} %collective-permute-done.88.refs_0_.refs_6_, bf16[128,2560]{1,0:T(8,128)(2,1)} %collective-permute-done.89.refs_1_.refs_7_, bf16[128,2560]{1,0:T(8,128)(2,1)} %collective-permute-done.90.refs_2_, bf16[128,2560]{1,0:T(8,128)(2,1)} %collective-permute-done.91.refs_3_, ...), custom_call_target="tpu_custom_call" | custom-call | flops 5033164800 | bytes 13762560 | tf_op jit(solution)/shard_map/pallas_call | solution.py:294
  302.3 6.4 collective-permute-done.76.refs_6_.refs_8_
  308.7 13.9 %collective-permute-done.77.refs_7_.refs_9_ = bf16[128,2560]{1,0:T(8,128)(2,1)} collective-permute-done((bf16[128,2560]{1,0:T(8,128)(2,1)}, bf16[128,2560]{1,0:T(8,128)(2,1)}, u32[]{:S(2)}, u32[]{:S(2)}) %collective-permute-start.77) | collective-permute-done | bytes 655392 | tf_op jit(solution)/shard_map/ppermute | solution.py:76
  322.6 4.4 shard_map.204.refs_20_
  327.0 10.4 %collective-permute-start.28 = (f32[4,1280]{1,0:T(4,128)S(1)}, f32[4,1280]{1,0:T(4,128)S(1)}, u32[]{:S(2)}, u32[]{:S(2)}) collective-permute-start(f32[4,1280]{1,0:T(4,128)S(1)} %pad_maximum_fusion.15), channel_id=1, source_target_pairs={{0,8},{1,9},{2,10},{3,11},{4,12},{5,13},{6,14},{7,15},{8,0},{9,1},... | collective-permute-start | bytes 61448 | tf_op jit(solution)/shard_map/ppermute | solution.py:76
  345.7 7.7 %shard_map.200 = (bf16[2,128,1280]{2,1,0:T(8,128)(2,1)S(1)}, bf16[2,128,1280]{2,1,0:T(8,128)(2,1)S(1)}, bf16[2,128,1280]{2,1,0:T(8,128)(2,1)S(1)}, f32[2,16,1280...) custom-call(f32[2,2]{1,0:T(2,128)S(1)} %pad_maximum_fusion.17.flags_ref, ...), custom_call_target="tpu_custom_call" | custom-call | flops 65536000 | bytes 12902416 | tf_op jit(solution)/shard_map/pallas_call | solution.py:260
  369.1 8.5 %collective-permute-done.31 = bf16[128,2560]{1,0:T(8,128)(2,1)S(1)} collective-permute-done((bf16[128,2560]{1,0:T(8,128)(2,1)S(1)}, bf16[128,2560]{1,0:T(8,128)(2,1)S(1)}, u32[]{:S(2)}, u32[]{:S(2)}) %collective-permute-start.31) | collective-permute-done | bytes 655392 | tf_op jit(solution)/shard_map/ppermute | solution.py:76
  383.8 19.9 %shard_map.208 = bf16[640,1152]{1,0:T(8,128)(2,1)} custom-call(bf16[128,2560]{1,0:T(8,128)(2,1)} %collective-permute-done.68.refs_2_.refs_0_, bf16[128,2560]{1,0:T(8,128)(2,1)} %collective-permute-done.69.refs_3_.refs_1_, bf16[128,2560]{1,0:T(8,128)(2,1)} %collective-permute-done.70.refs_2_, bf16[128,2560]{1,0:T(8,128)(2,1)} %collective-permute-done.71.refs_3_, ...), custom_call_target="tpu_custom_call" | custom-call | flops 9059696640 | bytes 19660800 | tf_op jit(solution)/shard_map/pallas_call | solution.py:528
  415.6 28.5 %shard_map.206 = bf16[640,2304]{1,0:T(8,128)(2,1)} custom-call(bf16[128,2560]{1,0:T(8,128)(2,1)} %collective-permute-done.68.refs_2_.refs_0_, bf16[128,2560]{1,0:T(8,128)(2,1)} %collective-permute-done.69.refs_3_.refs_1_, bf16[128,2560]{1,0:T(8,128)(2,1)} %collective-permute-done.70.refs_2_, bf16[128,2560]{1,0:T(8,128)(2,1)} %collective-permute-done.71.refs_3_, ...), custom_call_target="tpu_custom_call" | custom-call | flops 18119393280 | bytes 23592960 | tf_op jit(solution)/shard_map/pallas_call | solution.py:528
  465.6 36.2 %collective-permute-done.55 = bf16[256,1280]{1,0:T(8,128)(2,1)} collective-permute-done((bf16[256,1280]{1,0:T(8,128)(2,1)S(1)}, bf16[256,1280]{1,0:T(8,128)(2,1)}, u32[]{:S(2)}, u32[]{:S(2)}) %collective-permute-start.55) | collective-permute-done | bytes 655392 | tf_op jit(solution)/shard_map/ppermute | solution.py:76
  503.9 4.9 collective-permute-done.58
  514.8 8.1 %collective-permute-done.38 = bf16[640,512]{1,0:T(8,128)(2,1)} collective-permute-done((bf16[640,512]{1,0:T(8,128)(2,1)}, bf16[640,512]{1,0:T(8,128)(2,1)}, u32[]{:S(2)}, u32[]{:S(2)}) %collective-permute-start.38) | collective-permute-done | bytes 655392 | tf_op jit(solution)/shard_map/ppermute | solution.py:76
  522.9 13.7 %collective-permute-done.40 = bf16[256,1280]{1,0:T(8,128)(2,1)} collective-permute-done((bf16[256,1280]{1,0:T(8,128)(2,1)S(1)}, bf16[256,1280]{1,0:T(8,128)(2,1)}, u32[]{:S(2)}, u32[]{:S(2)}) %collective-permute-start.40) | collective-permute-done | bytes 655392 | tf_op jit(solution)/shard_map/ppermute | solution.py:76
  537.1 3.7 convolution_convert_fusion.2
  540.9 4.3 collective-permute-start.59
  551.6 4.2 collective-permute-done.59
  558.0 5.3 collective-permute-start.60
  576.4 28.6 %shard_map.207 = bf16[640,2304]{1,0:T(8,128)(2,1)} custom-call(bf16[128,2560]{1,0:T(8,128)(2,1)} %collective-permute-done.68.refs_2_.refs_0_, bf16[128,2560]{1,0:T(8,128)(2,1)} %collective-permute-done.69.refs_3_.refs_1_, bf16[128,2560]{1,0:T(8,128)(2,1)} %collective-permute-done.70.refs_2_, bf16[128,2560]{1,0:T(8,128)(2,1)} %collective-permute-done.71.refs_3_, ...), custom_call_target="tpu_custom_call" | custom-call | flops 18119393280 | bytes 23592960 | tf_op jit(solution)/shard_map/pallas_call | solution.py:528
  609.1 4.6 collective-permute-start.61
  616.8 5.4 collective-permute-start.48
  631.0 7.1 collective-permute-start.36
  643.5 27.4 %collective-permute-done.48 = bf16[320,1280]{1,0:T(8,128)(2,1)} collective-permute-done((bf16[320,1280]{1,0:T(8,128)(2,1)}, bf16[320,1280]{1,0:T(8,128)(2,1)}, u32[]{:S(2)}, u32[]{:S(2)}) %collective-permute-start.48) | collective-permute-done | bytes 819232 | tf_op jit(solution)/shard_map/ppermute | solution.py:76
  675.9 5.1 collective-permute-start.49
  687.6 5.4 collective-permute-done.52
  695.1 4.1 collective-permute-start.53
  708.4 17.9 %collective-permute-done.67 = bf16[80,2560]{1,0:T(8,128)(2,1)S(1)} collective-permute-done((bf16[80,2560]{1,0:T(8,128)(2,1)S(1)}, bf16[80,2560]{1,0:T(8,128)(2,1)S(1)}, u32[]{:S(2)}, u32[]{:S(2)}) %collective-permute-start.67) | collective-permute-done | bytes 409632 | tf_op jit(solution)/shard_map/ppermute | solution.py:76
  (419 shorter events, 224.3 us)
Async XLA Ops:
  7.2 695.8 %reduce-scatter.8.cloned.1.call-start = ((), (), s32[]{:S(2)}) async-start(), calls=%async_computation.5 | async-start | bytes 2211840 | tf_op jit(solution)/shard_map/reduce_scatter | solution.py:742
  12.3 43.4 %collective-permute-start.3 = (bf16[2560,640]{1,0:T(8,128)(2,1)}, bf16[2560,640]{1,0:T(8,128)(2,1)S(1)}, u32[]{:S(2)}, u32[]{:S(2)}) collective-permute-start(bf16[2560,640]{1,0:T(8,128)(2,1)} %param.17), channel_id=1, source_target_pairs={{0,1},{1,0},{2,3},{3,2},{4,5},{5,4},{6,7},{7,6},{8,9},{9,8},{10,11... | collective-permute-start | bytes 9830408 | tf_op jit(solution)/shard_map/ppermute | solution.py:76
  16.9 34.5 %collective-permute-start.2 = (bf16[128,2560]{1,0:T(8,128)(2,1)}, bf16[128,2560]{1,0:T(8,128)(2,1)}, u32[]{:S(2)}, u32[]{:S(2)}) collective-permute-start(bf16[128,2560]{1,0:T(8,128)(2,1)} %fusion.35), channel_id=1, source_target_pairs={{0,2},{1,3},{2,0},{3,1},{4,6},{5,7},{6,4},{7,5},{8,10},{9,11},{10,... | collective-permute-start | bytes 1966088 | tf_op jit(solution)/shard_map/ppermute | solution.py:76
  43.0 41.3 %collective-permute-start.10 = (bf16[2560,640]{1,0:T(8,128)(2,1)}, bf16[2560,640]{1,0:T(8,128)(2,1)}, u32[]{:S(2)}, u32[]{:S(2)}) collective-permute-start(bf16[2560,640]{1,0:T(8,128)(2,1)} %param.16), channel_id=1, source_target_pairs={{0,1},{1,0},{2,3},{3,2},{4,5},{5,4},{6,7},{7,6},{8,9},{9,8},{10,11... | collective-permute-start | bytes 9830408 | tf_op jit(solution)/shard_map/ppermute | solution.py:76
  43.6 38.1 %collective-permute-start.12 = (bf16[1280,640]{1,0:T(8,128)(2,1)}, bf16[1280,640]{1,0:T(8,128)(2,1)}, u32[]{:S(2)}, u32[]{:S(2)}) collective-permute-start(bf16[1280,640]{1,0:T(8,128)(2,1)} %get-tuple-element.111), channel_id=1, source_target_pairs={{0,2},{1,3},{2,0},{3,1},{4,6},{5,7},{6,4},{7,5},{8,10},{9,11},{10,... | collective-permute-start | bytes 4915208 | tf_op jit(solution)/shard_map/ppermute | solution.py:76
  94.4 31.2 %collective-permute-start.18 = (bf16[128,2560]{1,0:T(8,128)(2,1)}, bf16[128,2560]{1,0:T(8,128)(2,1)}, u32[]{:S(2)}, u32[]{:S(2)}) collective-permute-start(bf16[128,2560]{1,0:T(8,128)(2,1)} %bitcast.9.refs_0_), channel_id=1, source_target_pairs={{0,2},{1,3},{2,0},{3,1},{4,6},{5,7},{6,4},{7,5},{8,10},{9,11},{10,... | collective-permute-start | bytes 1966088 | tf_op jit(solution)/shard_map/ppermute | solution.py:76
  125.6 29.3 %collective-permute-start.16 = (bf16[128,2560]{1,0:T(8,128)(2,1)}, bf16[128,2560]{1,0:T(8,128)(2,1)}, u32[]{:S(2)}, u32[]{:S(2)}) collective-permute-start(bf16[128,2560]{1,0:T(8,128)(2,1)} %multiply_convert_fusion.refs_0_), channel_id=1, source_target_pairs={{0,1},{1,0},{2,3},{3,2},{4,5},{5,4},{6,7},{7,6},{8,9},{9,8},{10,11... | collective-permute-start | bytes 1966088 | tf_op jit(solution)/shard_map/ppermute | solution.py:76
  138.9 63.2 %collective-permute-start.80 = (bf16[128,2560]{1,0:T(8,128)(2,1)}, bf16[128,2560]{1,0:T(8,128)(2,1)}, u32[]{:S(2)}, u32[]{:S(2)}) collective-permute-start(bf16[128,2560]{1,0:T(8,128)(2,1)} %bitcast.9.refs_0_), channel_id=1, source_target_pairs={{0,4},{1,5},{2,6},{3,7},{4,0},{5,1},{6,2},{7,3},{8,12},{9,13},{10,... | collective-permute-start | bytes 1966088 | tf_op jit(solution)/shard_map/ppermute | solution.py:76
  140.5 62.2 %collective-permute-start.81 = (bf16[128,2560]{1,0:T(8,128)(2,1)}, bf16[128,2560]{1,0:T(8,128)(2,1)}, u32[]{:S(2)}, u32[]{:S(2)}) collective-permute-start(bf16[128,2560]{1,0:T(8,128)(2,1)} %collective-permute-done.18.refs_1_), channel_id=1, source_target_pairs={{0,4},{1,5},{2,6},{3,7},{4,0},{5,1},{6,2},{7,3},{8,12},{9,13},{10,... | collective-permute-start | bytes 1966088 | tf_op jit(solution)/shard_map/ppermute | solution.py:76
  141.0 61.2 %collective-permute-start.85 = (bf16[128,2560]{1,0:T(8,128)(2,1)}, bf16[128,2560]{1,0:T(8,128)(2,1)}, u32[]{:S(2)}, u32[]{:S(2)}) collective-permute-start(bf16[128,2560]{1,0:T(8,128)(2,1)} %collective-permute-done.84.refs_0_.refs_4_), channel_id=1, source_target_pairs={{0,2},{1,3},{2,0},{3,1},{4,6},{5,7},{6,4},{7,5},{8,10},{9,11},{10,... | collective-permute-start | bytes 1966088 | tf_op jit(solution)/shard_map/ppermute | solution.py:76
  202.1 39.4 %collective-permute-start.86 = (bf16[128,2560]{1,0:T(8,128)(2,1)}, bf16[128,2560]{1,0:T(8,128)(2,1)}, u32[]{:S(2)}, u32[]{:S(2)}) collective-permute-start(bf16[128,2560]{1,0:T(8,128)(2,1)} %collective-permute-done.84.refs_0_.refs_4_), channel_id=1, source_target_pairs={{0,1},{1,0},{2,3},{3,2},{4,5},{5,4},{6,7},{7,6},{8,9},{9,8},{10,11... | collective-permute-start | bytes 1966088 | tf_op jit(solution)/shard_map/ppermute | solution.py:76
  202.7 40.3 %collective-permute-start.87 = (bf16[128,2560]{1,0:T(8,128)(2,1)}, bf16[128,2560]{1,0:T(8,128)(2,1)}, u32[]{:S(2)}, u32[]{:S(2)}) collective-permute-start(bf16[128,2560]{1,0:T(8,128)(2,1)} %collective-permute-done.85.refs_1_.refs_5_), channel_id=1, source_target_pairs={{0,1},{1,0},{2,3},{3,2},{4,5},{5,4},{6,7},{7,6},{8,9},{9,8},{10,11... | collective-permute-start | bytes 1966088 | tf_op jit(solution)/shard_map/ppermute | solution.py:76
  225.4 32.9 %collective-permute-start.89 = (bf16[128,2560]{1,0:T(8,128)(2,1)}, bf16[128,2560]{1,0:T(8,128)(2,1)}, u32[]{:S(2)}, u32[]{:S(2)}) collective-permute-start(bf16[128,2560]{1,0:T(8,128)(2,1)} %collective-permute-done.85.refs_1_.refs_5_), channel_id=1, source_target_pairs={{0,4},{1,5},{2,6},{3,7},{4,0},{5,1},{6,2},{7,3},{8,12},{9,13},{10,... | collective-permute-start | bytes 1966088 | tf_op jit(solution)/shard_map/ppermute | solution.py:76
  227.3 35.5 %collective-permute-start.26 = (bf16[128,2560]{1,0:T(8,128)(2,1)S(1)}, bf16[128,2560]{1,0:T(8,128)(2,1)S(1)}, u32[]{:S(2)}, u32[]{:S(2)}) collective-permute-start(bf16[128,2560]{1,0:T(8,128)(2,1)S(1)} %maximum_select_fusion.7), channel_id=1, source_target_pairs={{0,2},{1,3},{2,0},{3,1},{4,6},{5,7},{6,4},{7,5},{8,10},{9,11},{10,... | collective-permute-start | bytes 1966088 | tf_op jit(solution)/shard_map/ppermute | solution.py:76
  243.0 32.0 %collective-permute-start.73 = (bf16[128,2560]{1,0:T(8,128)(2,1)}, bf16[128,2560]{1,0:T(8,128)(2,1)}, u32[]{:S(2)}, u32[]{:S(2)}) collective-permute-start(bf16[128,2560]{1,0:T(8,128)(2,1)} %collective-permute-done.15.refs_1_), channel_id=1, source_target_pairs={{0,24},{1,25},{2,26},{3,27},{4,28},{5,29},{6,30},{7,31},{8,16},{9,... | collective-permute-start | bytes 1966088 | tf_op jit(solution)/shard_map/ppermute | solution.py:76
  258.3 29.9 %collective-permute-start.91 = (bf16[128,2560]{1,0:T(8,128)(2,1)}, bf16[128,2560]{1,0:T(8,128)(2,1)}, u32[]{:S(2)}, u32[]{:S(2)}) collective-permute-start(bf16[128,2560]{1,0:T(8,128)(2,1)} %collective-permute-done.89.refs_1_.refs_7_), channel_id=1, source_target_pairs={{0,1},{1,0},{2,3},{3,2},{4,5},{5,4},{6,7},{7,6},{8,9},{9,8},{10,11... | collective-permute-start | bytes 1966088 | tf_op jit(solution)/shard_map/ppermute | solution.py:76
  262.7 39.0 %collective-permute-start.68 = (bf16[128,2560]{1,0:T(8,128)(2,1)}, bf16[128,2560]{1,0:T(8,128)(2,1)}, u32[]{:S(2)}, u32[]{:S(2)}) collective-permute-start(bf16[128,2560]{1,0:T(8,128)(2,1)} %multiply_convert_fusion.refs_0_), channel_id=1, source_target_pairs={{0,4},{1,5},{2,6},{3,7},{4,0},{5,1},{6,2},{7,3},{8,12},{9,13},{10,... | collective-permute-start | bytes 1966088 | tf_op jit(solution)/shard_map/ppermute | solution.py:76
  264.1 37.8 %collective-permute-start.69 = (bf16[128,2560]{1,0:T(8,128)(2,1)}, bf16[128,2560]{1,0:T(8,128)(2,1)}, u32[]{:S(2)}, u32[]{:S(2)}) collective-permute-start(bf16[128,2560]{1,0:T(8,128)(2,1)} %collective-permute-done.15.refs_1_), channel_id=1, source_target_pairs={{0,4},{1,5},{2,6},{3,7},{4,0},{5,1},{6,2},{7,3},{8,12},{9,13},{10,... | collective-permute-start | bytes 1966088 | tf_op jit(solution)/shard_map/ppermute | solution.py:76
  265.0 43.8 %collective-permute-start.76 = (bf16[128,2560]{1,0:T(8,128)(2,1)}, bf16[128,2560]{1,0:T(8,128)(2,1)}, u32[]{:S(2)}, u32[]{:S(2)}) collective-permute-start(bf16[128,2560]{1,0:T(8,128)(2,1)} %collective-permute-done.72.refs_4_), channel_id=1, source_target_pairs={{0,4},{1,5},{2,6},{3,7},{4,0},{5,1},{6,2},{7,3},{8,12},{9,13},{10,... | collective-permute-start | bytes 1966088 | tf_op jit(solution)/shard_map/ppermute | solution.py:76
  275.0 47.6 %collective-permute-start.77 = (bf16[128,2560]{1,0:T(8,128)(2,1)}, bf16[128,2560]{1,0:T(8,128)(2,1)}, u32[]{:S(2)}, u32[]{:S(2)}) collective-permute-start(bf16[128,2560]{1,0:T(8,128)(2,1)} %collective-permute-done.73.refs_5_), channel_id=1, source_target_pairs={{0,4},{1,5},{2,6},{3,7},{4,0},{5,1},{6,2},{7,3},{8,12},{9,13},{10,... | collective-permute-start | bytes 1966088 | tf_op jit(solution)/shard_map/ppermute | solution.py:76
  288.1 38.9 %collective-permute-start.27 = (f32[4,1280]{1,0:T(4,128)S(1)}, f32[4,1280]{1,0:T(4,128)S(1)}, u32[]{:S(2)}, u32[]{:S(2)}) collective-permute-start(f32[4,1280]{1,0:T(4,128)S(1)} %get-tuple-element.68), channel_id=1, source_target_pairs={{0,4},{1,5},{2,6},{3,7},{4,0},{5,1},{6,2},{7,3},{8,12},{9,13},{10,... | collective-permute-start | bytes 61448 | tf_op jit(solution)/shard_map/ppermute | solution.py:76
  301.7 77.3 %collective-permute-start.93 = (bf16[640,1024]{1,0:T(8,128)(2,1)}, bf16[640,1024]{1,0:T(8,128)(2,1)}, u32[]{:S(2)}, u32[]{:S(2)}) collective-permute-start(bf16[640,1024]{1,0:T(8,128)(2,1)} %shard_map.205.refs_22_), channel_id=1, source_target_pairs={{0,1},{1,0},{2,3},{3,2},{4,5},{5,4},{6,7},{7,6},{8,9},{9,8},{10,11... | collective-permute-start | bytes 3932168 | tf_op jit(solution)/shard_map/ppermute | solution.py:76
  301.8 77.9 %collective-permute-start.74 = (bf16[128,2560]{1,0:T(8,128)(2,1)}, bf16[128,2560]{1,0:T(8,128)(2,1)}, u32[]{:S(2)}, u32[]{:S(2)}) collective-permute-start(bf16[128,2560]{1,0:T(8,128)(2,1)} %collective-permute-done.72.refs_4_), channel_id=1, source_target_pairs={{0,1},{1,0},{2,3},{3,2},{4,5},{5,4},{6,7},{7,6},{8,9},{9,8},{10,11... | collective-permute-start | bytes 1966088 | tf_op jit(solution)/shard_map/ppermute | solution.py:76
  308.7 70.9 %collective-permute-start.70 = (bf16[128,2560]{1,0:T(8,128)(2,1)}, bf16[128,2560]{1,0:T(8,128)(2,1)}, u32[]{:S(2)}, u32[]{:S(2)}) collective-permute-start(bf16[128,2560]{1,0:T(8,128)(2,1)} %collective-permute-done.68.refs_2_.refs_0_), channel_id=1, source_target_pairs={{0,1},{1,0},{2,3},{3,2},{4,5},{5,4},{6,7},{7,6},{8,9},{9,8},{10,11... | collective-permute-start | bytes 1966088 | tf_op jit(solution)/shard_map/ppermute | solution.py:76
  322.6 58.9 %collective-permute-start.71 = (bf16[128,2560]{1,0:T(8,128)(2,1)}, bf16[128,2560]{1,0:T(8,128)(2,1)}, u32[]{:S(2)}, u32[]{:S(2)}) collective-permute-start(bf16[128,2560]{1,0:T(8,128)(2,1)} %collective-permute-done.69.refs_3_.refs_1_), channel_id=1, source_target_pairs={{0,1},{1,0},{2,3},{3,2},{4,5},{5,4},{6,7},{7,6},{8,9},{9,8},{10,11... | collective-permute-start | bytes 1966088 | tf_op jit(solution)/shard_map/ppermute | solution.py:76
  403.7 323.6 %reduce-scatter.4.cloned.1.call-start = ((), (), s32[]{:S(2)}) async-start(), calls=%async_computation.3 | async-start | bytes 4423680 | tf_op jit(solution)/shard_map/reduce_scatter | solution.py:742
  411.5 47.1 %collective-permute-start.37 = (bf16[2,640,256]{2,1,0:T(8,128)(2,1)}, bf16[2,640,256]{2,1,0:T(8,128)(2,1)}, u32[]{:S(2)}, u32[]{:S(2)}) collective-permute-start(bf16[2,640,256]{2,1,0:T(8,128)(2,1)} %get-tuple-element.126), channel_id=1, source_target_pairs={{0,1},{1,0},{2,3},{3,2},{4,5},{5,4},{6,7},{7,6},{8,9},{9,8},{10,11... | collective-permute-start | bytes 1966088 | tf_op jit(solution)/shard_map/ppermute | solution.py:76
  415.2 46.0 %collective-permute-start.42 = (bf16[2,320,256]{2,1,0:T(8,128)(2,1)}, bf16[2,320,256]{2,1,0:T(8,128)(2,1)}, u32[]{:S(2)}, u32[]{:S(2)}) collective-permute-start(bf16[2,320,256]{2,1,0:T(8,128)(2,1)} %get-tuple-element.143), channel_id=1, source_target_pairs={{0,1},{1,0},{2,3},{3,2},{4,5},{5,4},{6,7},{7,6},{8,9},{9,8},{10,11... | collective-permute-start | bytes 983048 | tf_op jit(solution)/shard_map/ppermute | solution.py:76
  444.1 284.6 %reduce-scatter.6.cloned.1.call-start = ((), (), s32[]{:S(2)}) async-start(), calls=%async_computation.4 | async-start | bytes 4423680 | tf_op jit(solution)/shard_map/reduce_scatter | solution.py:742
  455.9 52.9 %collective-permute-start.44 = (bf16[256,2560]{1,0:T(8,128)(2,1)S(1)}, bf16[256,2560]{1,0:T(8,128)(2,1)S(1)}, u32[]{:S(2)}, u32[]{:S(2)}) collective-permute-start(bf16[256,2560]{1,0:T(8,128)(2,1)S(1)} %pad_maximum_fusion.4), channel_id=1, source_target_pairs={{0,1},{1,0},{2,3},{3,2},{4,5},{5,4},{6,7},{7,6},{8,9},{9,8},{10,11... | collective-permute-start | bytes 3932168 | tf_op jit(solution)/shard_map/ppermute | solution.py:76
  456.1 80.5 %collective-permute-start.45 = (bf16[256,2560]{1,0:T(8,128)(2,1)S(1)}, bf16[256,2560]{1,0:T(8,128)(2,1)}, u32[]{:S(2)}, u32[]{:S(2)}) collective-permute-start(bf16[256,2560]{1,0:T(8,128)(2,1)S(1)} %pad_maximum_fusion.4), channel_id=1, source_target_pairs={{0,4},{1,5},{2,6},{3,7},{4,0},{5,1},{6,2},{7,3},{8,12},{9,13},{10,... | collective-permute-start | bytes 3932168 | tf_op jit(solution)/shard_map/ppermute | solution.py:76
  459.2 42.7 %collective-permute-start.55 = (bf16[256,1280]{1,0:T(8,128)(2,1)S(1)}, bf16[256,1280]{1,0:T(8,128)(2,1)}, u32[]{:S(2)}, u32[]{:S(2)}) collective-permute-start(bf16[256,1280]{1,0:T(8,128)(2,1)S(1)} %bitcast.187), channel_id=1, source_target_pairs={{0,4},{1,5},{2,6},{3,7},{4,0},{5,1},{6,2},{7,3},{8,12},{9,13},{10,... | collective-permute-start | bytes 1966088 | tf_op jit(solution)/shard_map/ppermute | solution.py:76
  459.9 48.9 %collective-permute-start.58 = (bf16[4,80,512]{2,1,0:T(8,128)(2,1)S(1)}, bf16[4,80,512]{2,1,0:T(8,128)(2,1)S(1)}, u32[]{:S(2)}, u32[]{:S(2)}) collective-permute-start(bf16[4,80,512]{2,1,0:T(8,128)(2,1)S(1)} %fusion.105), channel_id=1, source_target_pairs={{0,4},{1,5},{2,6},{3,7},{4,0},{5,1},{6,2},{7,3},{8,12},{9,13},{10,... | collective-permute-start | bytes 983048 | tf_op jit(solution)/shard_map/ppermute | solution.py:76
  461.2 42.6 %collective-permute-start.33 = (f32[10,2560]{1,0:T(8,128)S(1)}, f32[10,2560]{1,0:T(8,128)S(1)}, u32[]{:S(2)}, u32[]{:S(2)}) collective-permute-start(f32[10,2560]{1,0:T(8,128)S(1)} %fusion.141), channel_id=1, source_target_pairs={{0,2},{1,3},{2,0},{3,1},{4,6},{5,7},{6,4},{7,5},{8,10},{9,11},{10,... | collective-permute-start | bytes 307208 | tf_op jit(solution)/shard_map/ppermute | solution.py:76
  503.8 32.8 %collective-permute-start.40 = (bf16[256,1280]{1,0:T(8,128)(2,1)S(1)}, bf16[256,1280]{1,0:T(8,128)(2,1)}, u32[]{:S(2)}, u32[]{:S(2)}) collective-permute-start(bf16[256,1280]{1,0:T(8,128)(2,1)S(1)} %bitcast.166), channel_id=1, source_target_pairs={{0,4},{1,5},{2,6},{3,7},{4,0},{5,1},{6,2},{7,3},{8,12},{9,13},{10,... | collective-permute-start | bytes 1966088 | tf_op jit(solution)/shard_map/ppermute | solution.py:76
  508.8 28.3 %collective-permute-start.54 = (bf16[256,1280]{1,0:T(8,128)(2,1)S(1)}, bf16[256,1280]{1,0:T(8,128)(2,1)}, u32[]{:S(2)}, u32[]{:S(2)}) collective-permute-start(bf16[256,1280]{1,0:T(8,128)(2,1)S(1)} %bitcast.188), channel_id=1, source_target_pairs={{0,1},{1,0},{2,3},{3,2},{4,5},{5,4},{6,7},{7,6},{8,9},{9,8},{10,11... | collective-permute-start | bytes 1966088 | tf_op jit(solution)/shard_map/ppermute | solution.py:76
  508.8 28.3 %collective-permute-start.56 = (bf16[256,1280]{1,0:T(8,128)(2,1)}, bf16[256,1280]{1,0:T(8,128)(2,1)}, u32[]{:S(2)}, u32[]{:S(2)}) collective-permute-start(bf16[256,1280]{1,0:T(8,128)(2,1)} %collective-permute-done.55), channel_id=1, source_target_pairs={{0,1},{1,0},{2,3},{3,2},{4,5},{5,4},{6,7},{7,6},{8,9},{9,8},{10,11... | collective-permute-start | bytes 1966088 | tf_op jit(solution)/shard_map/ppermute | solution.py:76
  548.4 73.8 %collective-permute-start.21 = (bf16[256,2560]{1,0:T(8,128)(2,1)}, bf16[256,2560]{1,0:T(8,128)(2,1)}, u32[]{:S(2)}, u32[]{:S(2)}) collective-permute-start(bf16[256,2560]{1,0:T(8,128)(2,1)} %get-tuple-element.58), channel_id=1, source_target_pairs={{0,1},{1,0},{2,3},{3,2},{4,5},{5,4},{6,7},{7,6},{8,9},{9,8},{10,11... | collective-permute-start | bytes 3932168 | tf_op jit(solution)/shard_map/ppermute | solution.py:76
  558.0 47.9 %collective-permute-start.60 = (bf16[192,1280]{1,0:T(8,128)(2,1)}, bf16[192,1280]{1,0:T(8,128)(2,1)}, u32[]{:S(2)}, u32[]{:S(2)}) collective-permute-start(bf16[192,1280]{1,0:T(8,128)(2,1)} %get-tuple-element.114), channel_id=1, source_target_pairs={{0,8},{1,9},{2,10},{3,11},{4,12},{5,13},{6,14},{7,15},{8,16},{9,17... | collective-permute-start | bytes 1474568 | tf_op jit(solution)/shard_map/ppermute | solution.py:76
  563.3 42.7 %collective-permute-start.63 = (bf16[192,1280]{1,0:T(8,128)(2,1)}, bf16[192,1280]{1,0:T(8,128)(2,1)}, u32[]{:S(2)}, u32[]{:S(2)}) collective-permute-start(bf16[192,1280]{1,0:T(8,128)(2,1)} %get-tuple-element.115), channel_id=1, source_target_pairs={{16,8},{17,9},{18,10},{19,11},{20,12},{21,13},{22,14},{23,15},{24,... | collective-permute-start | bytes 1474568 | tf_op jit(solution)/shard_map/ppermute | solution.py:76
  571.8 37.3 %collective-permute-start.47 = (bf16[320,1280]{1,0:T(8,128)(2,1)}, bf16[320,1280]{1,0:T(8,128)(2,1)}, u32[]{:S(2)}, u32[]{:S(2)}) collective-permute-start(bf16[320,1280]{1,0:T(8,128)(2,1)} %get-tuple-element.108), channel_id=1, source_target_pairs={{0,8},{1,9},{2,10},{3,11},{4,12},{5,13},{6,14},{7,15}} | collective-permute-start | bytes 2457608 | tf_op jit(solution)/shard_map/ppermute | solution.py:76
  574.6 39.1 %collective-permute-start.50 = (bf16[320,1280]{1,0:T(8,128)(2,1)}, bf16[320,1280]{1,0:T(8,128)(2,1)}, u32[]{:S(2)}, u32[]{:S(2)}) collective-permute-start(bf16[320,1280]{1,0:T(8,128)(2,1)} %get-tuple-element.109), channel_id=1, source_target_pairs={{24,16},{25,17},{26,18},{27,19},{28,20},{29,21},{30,22},{31,23}} | collective-permute-start | bytes 2457608 | tf_op jit(solution)/shard_map/ppermute | solution.py:76
  609.1 29.1 %collective-permute-start.61 = (bf16[192,1280]{1,0:T(8,128)(2,1)S(1)}, bf16[192,1280]{1,0:T(8,128)(2,1)S(1)}, u32[]{:S(2)}, u32[]{:S(2)}) collective-permute-start(bf16[192,1280]{1,0:T(8,128)(2,1)S(1)} %get-tuple-element.112), channel_id=1, source_target_pairs={{0,8},{1,9},{2,10},{3,11},{4,12},{5,13},{6,14},{7,15},{8,16},{9,17... | collective-permute-start | bytes 1474568 | tf_op jit(solution)/shard_map/ppermute | solution.py:76
  616.8 54.1 %collective-permute-start.48 = (bf16[320,1280]{1,0:T(8,128)(2,1)}, bf16[320,1280]{1,0:T(8,128)(2,1)}, u32[]{:S(2)}, u32[]{:S(2)}) collective-permute-start(bf16[320,1280]{1,0:T(8,128)(2,1)} %get-tuple-element.106), channel_id=1, source_target_pairs={{0,8},{1,9},{2,10},{3,11},{4,12},{5,13},{6,14},{7,15},{8,16},{9,17... | collective-permute-start | bytes 2457608 | tf_op jit(solution)/shard_map/ppermute | solution.py:76
  622.2 50.6 %collective-permute-start.51 = (bf16[320,1280]{1,0:T(8,128)(2,1)}, bf16[320,1280]{1,0:T(8,128)(2,1)}, u32[]{:S(2)}, u32[]{:S(2)}) collective-permute-start(bf16[320,1280]{1,0:T(8,128)(2,1)} %get-tuple-element.107), channel_id=1, source_target_pairs={{16,8},{17,9},{18,10},{19,11},{20,12},{21,13},{22,14},{23,15},{24,... | collective-permute-start | bytes 2457608 | tf_op jit(solution)/shard_map/ppermute | solution.py:76
  626.4 49.5 %collective-permute-start.25 = (bf16[128,2560]{1,0:T(8,128)(2,1)}, bf16[128,2560]{1,0:T(8,128)(2,1)}, u32[]{:S(2)}, u32[]{:S(2)}) collective-permute-start(bf16[128,2560]{1,0:T(8,128)(2,1)} %slice.401), channel_id=1, source_target_pairs={{0,2},{1,3},{2,0},{3,1},{4,6},{5,7},{6,4},{7,5},{8,10},{9,11},{10,... | collective-permute-start | bytes 1966088 | tf_op jit(solution)/shard_map/ppermute | solution.py:76
  631.0 52.2 %collective-permute-start.36 = (f32[10,2560]{1,0:T(8,128)}, f32[10,2560]{1,0:T(8,128)}, u32[]{:S(2)}, u32[]{:S(2)}) collective-permute-start(f32[10,2560]{1,0:T(8,128)} %add.352), channel_id=1, source_target_pairs={{0,16},{1,17},{2,18},{3,19},{4,20},{5,21},{6,22},{7,23},{8,24},{9,... | collective-permute-start | bytes 307208 | tf_op jit(solution)/shard_map/ppermute | solution.py:76
  639.8 45.8 %collective-permute-start.65 = (bf16[80,1280]{1,0:T(8,128)(2,1)}, bf16[80,1280]{1,0:T(8,128)(2,1)}, u32[]{:S(2)}, u32[]{:S(2)}) collective-permute-start(bf16[80,1280]{1,0:T(8,128)(2,1)} %get-tuple-element.164), channel_id=1, source_target_pairs={{0,2},{1,3},{2,0},{3,1},{4,6},{5,7},{6,4},{7,5},{8,10},{9,11},{10,... | collective-permute-start | bytes 614408 | tf_op jit(solution)/shard_map/ppermute | solution.py:76
  (105 other events, 1458.4 us)
Sparse Core Ops, SparseCore 0:
  403.9 25.8 reduce-scatter.7
  444.2 42.2 reduce-scatter.3
  605.1 70.1 reduce-scatter.5

commit v4 on v3

--- a/solution.py
+++ b/solution.py
@@ -18,6 +18,7 @@
 GELU_A = 0.044715
 VMEM_MAX = 60 * 1024 * 1024
 ANY = pl.BlockSpec(memory_space=pl.ANY)
+SMALL = pl.CostEstimate(flops=1, bytes_accessed=1, transcendentals=0)
 
 
 def norm_scale(values):
@@ -61,6 +62,7 @@
         seq, fsdp = (lax.axis_index("seq"), lax.axis_index("fsdp"))
         self.z, self.y = (seq // 2, seq % 2)
         self.x, self.c = (fsdp // 2, fsdp % 2)
+        self.seq_at = seq
 
     def pairs(self, target):
         found = []
@@ -264,8 +266,7 @@
         out_specs=[spec(o.shape, False) for o in outs],
         out_shape=outs,
         compiler_params=pltpu.CompilerParams(vmem_limit_bytes=48 * 1024 * 1024),
-        cost_estimate=pl.CostEstimate(
-            flops=200 * outs[0].size, bytes_accessed=size, transcendentals=4 * outs[0].size),
+        cost_estimate=SMALL,
     )(*values)
 
 
@@ -299,9 +300,7 @@
         out_shape=jax.ShapeDtypeStruct((total, ff), F32),
         scratch_shapes=[pltpu.VMEM((total, width), BF16), pltpu.SemaphoreType.DMA((count,))],
         compiler_params=pltpu.CompilerParams(vmem_limit_bytes=VMEM_MAX),
-        cost_estimate=pl.CostEstimate(
-            flops=2 * total * width * ff, bytes_accessed=2 * width * ff + 4 * total * ff,
-            transcendentals=0),
+        cost_estimate=SMALL,
     )(*parts, w_down)
 
 
@@ -393,9 +392,7 @@
             pltpu.SemaphoreType.DMA((2, 3)),
         ],
         compiler_params=pltpu.CompilerParams(vmem_limit_bytes=VMEM_MAX),
-        cost_estimate=pl.CostEstimate(
-            flops=6 * total * width * ff, bytes_accessed=4 * width * ff + 16 * total * ff,
-            transcendentals=total * ff),
+        cost_estimate=SMALL,
     )(*n2_parts, grad_hidden, w_gate, w_up)
 
 
@@ -426,9 +423,7 @@
         out_specs=[tall(rows), tall(rows), tall(total // 2), tall(total // 2)],
         out_shape=[shape(rows, F32), shape(rows, BF16), shape(total // 2, F32), shape(total // 2, BF16)],
         compiler_params=pltpu.CompilerParams(vmem_limit_bytes=VMEM_MAX),
-        cost_estimate=pl.CostEstimate(
-            flops=4 * total * width * ff, bytes_accessed=6 * width * ff + 6 * total * ff,
-            transcendentals=0),
+        cost_estimate=SMALL,
     )(hidden, grad_gate, grad_up, w_gate, w_up, w_down)
 
 
@@ -456,93 +451,156 @@
         ),
         out_shape=jax.ShapeDtypeStruct((rows_out, count * tokens), BF16),
         compiler_params=pltpu.CompilerParams(vmem_limit_bytes=VMEM_MAX),
-        cost_estimate=pl.CostEstimate(
-            flops=0, bytes_accessed=6 * rows_out * count * tokens, transcendentals=0),
+        cost_estimate=SMALL,
     )(place, *parts)
 
 
-def mlp_weight_grads(n2_parts, grad_hiddens, acts, n2_rows, cot_rows, weights, at, size):
-    groups = len(n2_parts)
+def mlp_weight_grads(place, n2_parts, given, cot_parts, acts, n2_rows, cot_rows, weights, at, size, each):
+    groups, ready = (len(n2_parts), len(given))
     per = len(n2_parts[0])
     tokens, width = n2_parts[0][0].shape
     group = per * tokens
     both = group // 2
     rows = n2_rows[0].shape[0]
-    ff = weights[0].shape[1]
     flat_n = [p for g in n2_parts for p in g]
-    total = len(flat_n)
-
-    def body(*refs):
-        n_refs, h_refs = (refs[:total], refs[total : total + groups])
-        wg_ref, wu_ref, hid_ref, gg_ref, gu_ref, nm, no, cm, co = refs[total + groups : total + groups + 9]
-        out_ref = refs[total + groups + 9]
-        n2_s, gh_s, acc, sem = refs[total + groups + 10 :]
+    flat_c = [p for g in cot_parts for p in g]
+    lead = [len(flat_n), len(flat_c), ready]
+
+    def body(place_ref, *refs):
+        n_refs, refs = (refs[: lead[0]], refs[lead[0] :])
+        c_refs, refs = (refs[: lead[1]], refs[lead[1] :])
+        h_refs, refs = (refs[: lead[2]], refs[lead[2] :])
+        wg_ref, wu_ref, wd_ref, hid_ref, gg_ref, gu_ref, nm, no, cm, co = refs[:10]
+        own_ref, rest_ref, n2_s, cot_s, gh_s, acc, sem = refs[10:]
 
         def load(g, slot):
             found = []
             for i in range(per):
                 to = pl.ds(i * tokens, tokens)
                 found.append(pltpu.make_async_copy(n_refs[g * per + i], n2_s.at[slot, to], sem.at[slot, i]))
-            found.append(pltpu.make_async_copy(
-                h_refs[g].at[:, pl.ds(at, size)], gh_s.at[slot], sem.at[slot, per]))
+                if g >= ready:
+                    found.append(pltpu.make_async_copy(
+                        c_refs[(g - ready) * per + i], cot_s.at[slot, to], sem.at[slot, per + i]))
+            if g < ready:
+                found.append(pltpu.make_async_copy(
+                    h_refs[g].at[:, pl.ds(at, size)], gh_s, sem.at[slot, per]))
             return found
 
         for copy in load(0, 0):
             copy.start()
 
         def add(g, act, fresh):
-            start = g * both if isinstance(g, int) else pl.multiple_of(g * both, both)
+            span = slice(g * both, (g + 1) * both)
             for i, (mine, other) in enumerate(((cm, co), (nm, no), (nm, no))):
-                part = dot(mine[:, pl.ds(start, both)], act[i][:both]) + dot(
-                    other[:, pl.ds(start, both)], act[i][both:])
+                part = dot(mine[:, span], act[i][:both]) + dot(other[:, span], act[i][both:])
                 if fresh:
                     acc[i] = part
                 else:
                     acc[i] += part
 
-        add(0, (hid_ref[...], gg_ref[...], gu_ref[...]), True)
-
-        def step(g, carry):
-            slot = lax.rem(g, 2)
-            for k in range(1, groups):
-                @pl.when(g + 1 == k)
-                def _():
-                    for copy in load(k, k % 2):
-                        copy.start()
-
-            for copy in load(0, slot):
+        add(0, (hid_ref, gg_ref, gu_ref), True)
+        for g in range(groups):
+            slot = g % 2
+            if g + 1 < groups:
+                for copy in load(g + 1, 1 - slot):
+                    copy.start()
+            for copy in load(g, slot):
                 copy.wait()
             gelu, slope = gelu_pair(dot(n2_s[slot], wg_ref[...]))
             up = dot(n2_s[slot], wu_ref[...])
-            gh = gh_s[slot]
+            gh = gh_s[...] if g < ready else dot(cot_s[slot], wd_ref[...])
             add(g + 1, ((gelu * up).astype(BF16), (gh * up * slope).astype(BF16), (gh * gelu).astype(BF16)), False)
-            return carry
-
-        lax.fori_loop(0, groups, step, 0)
-        for i in range(3):
-            out_ref[:, i * size : (i + 1) * size] = acc[i].astype(BF16)
+        for j in range(rows // each):
+            start = pl.multiple_of((place_ref[0] ^ j) * each, 8)
+            for i in range(3):
+                block = acc[i, pl.ds(start, each), :]
+                if j == 0:
+                    own_ref[:, i * size : (i + 1) * size] = block
+                else:
+                    rest_ref[(j - 1) * each : j * each, i * size : (i + 1) * size] = block.astype(BF16)
 
     index = at // size
-    column = lambda n: pl.BlockSpec((n, size), lambda j: (0, index))
-    whole = pl.BlockSpec(n2_rows[0].shape, lambda j: (0, 0))
+    column = lambda n: pl.BlockSpec((n, size), lambda j, place: (0, index))
+    whole = pl.BlockSpec(n2_rows[0].shape, lambda j, place: (0, 0))
     return pl.pallas_call(
         body,
-        grid=(1,),
-        in_specs=[ANY] * (total + groups) + [column(width)] * 2 + [column(group)] * 3 + [whole] * 4,
-        out_specs=pl.BlockSpec((rows, 3 * size), lambda j: (0, 0)),
-        out_shape=jax.ShapeDtypeStruct((rows, 3 * size), BF16),
-        scratch_shapes=[
-            pltpu.VMEM((2, group, width), BF16),
-            pltpu.VMEM((2, group, size), F32),
-            pltpu.VMEM((3, rows, size), F32),
-            pltpu.SemaphoreType.DMA((2, per + 1)),
-        ],
+        grid_spec=pltpu.PrefetchScalarGridSpec(
+            num_scalar_prefetch=1,
+            grid=(1,),
+            in_specs=[ANY] * sum(lead) + [column(width)] * 3 + [column(group)] * 3 + [whole] * 4,
+            out_specs=[pl.BlockSpec((each, 3 * size), lambda j, place: (0, 0)),
+                       pl.BlockSpec((rows - each, 3 * size), lambda j, place: (0, 0))],
+            scratch_shapes=[
+                pltpu.VMEM((2, group, width), BF16),
+                pltpu.VMEM((2, group, width), BF16),
+                pltpu.VMEM((group, size), F32),
+                pltpu.VMEM((3, rows, size), F32),
+                pltpu.SemaphoreType.DMA((2, 2 * per)),
+            ],
+        ),
+        out_shape=[jax.ShapeDtypeStruct((each, 3 * size), F32),
+                   jax.ShapeDtypeStruct((rows - each, 3 * size), BF16)],
         compiler_params=pltpu.CompilerParams(vmem_limit_bytes=VMEM_MAX),
-        cost_estimate=pl.CostEstimate(
-            flops=4 * groups * group * width * size + 6 * (groups + 1) * group * rows * size,
-            bytes_accessed=4 * width * size + 4 * groups * group * width,
-            transcendentals=groups * group * size),
-    )(*flat_n, *grad_hiddens, *weights, *acts, *n2_rows, *cot_rows)
+        cost_estimate=SMALL,
+    )(place, *flat_n, *flat_c, *given, *weights, *acts, *n2_rows, *cot_rows)
+
+
+def rows_by_device(place, parts, starts, block):
+    count = len(parts)
+    tokens, n = parts[0].shape
+    rows = len(starts(0, 0)) * block
+    if block % 16:
+        turned = jnp.concatenate(parts, axis=0).T
+
+        def taken(dc):
+            return jnp.stack([
+                jnp.concatenate([
+                    lax.dynamic_slice_in_dim(turned, start, block, 0)
+                    for start in starts(place[0] ^ dy, place[1] ^ dc)])
+                for dy in range(2)])
+
+        return taken(0), taken(1)
+
+    def body(place_ref, *refs):
+        keep_ref, send_ref, turned = refs[count:]
+        for k in range(count):
+            turned[:, k * tokens : (k + 1) * tokens] = refs[k][...].T
+        for dy in range(2):
+            for dc, ref in ((0, keep_ref), (1, send_ref)):
+                for i, start in enumerate(starts(place_ref[0] ^ dy, place_ref[1] ^ dc)):
+                    ref[dy, i * block : (i + 1) * block, :] = turned[pl.ds(pl.multiple_of(start, 16), block), :]
+
+    shape = (2, rows, count * tokens)
+    return pl.pallas_call(
+        body,
+        grid_spec=pltpu.PrefetchScalarGridSpec(
+            num_scalar_prefetch=1,
+            grid=(1,),
+            in_specs=[pl.BlockSpec((tokens, n), lambda i, place: (0, 0))] * count,
+            out_specs=[pl.BlockSpec(shape, lambda i, place: (0, 0, 0))] * 2,
+            scratch_shapes=[pltpu.VMEM((n, count * tokens), BF16)],
+        ),
+        out_shape=[jax.ShapeDtypeStruct(shape, BF16)] * 2,
+        compiler_params=pltpu.CompilerParams(vmem_limit_bytes=VMEM_MAX),
+        cost_estimate=SMALL,
+    )(place, *parts)
+
+
+def sum_of_dots(rows, values):
+    count = len(rows)
+
+    def body(*refs):
+        total = dot(refs[0][...], refs[count][...])
+        for k in range(1, count):
+            total = total + dot(refs[k][...], refs[count + k][...])
+        refs[2 * count][...] = total.astype(BF16)
+
+    return pl.pallas_call(
+        body,
+        out_shape=jax.ShapeDtypeStruct((rows[0].shape[0], values[0].shape[1]), BF16),
+        compiler_params=pltpu.CompilerParams(vmem_limit_bytes=VMEM_MAX),
+        cost_estimate=SMALL,
+    )(*rows, *values)
 
 
 def after(value, *others):
@@ -567,22 +625,17 @@
     return before_s
 
 
-def line_sum(lay, blocks):
+def owner_sum(lay, blocks, tie=None):
     nz, z = (lay.nz, lay.z)
 
     def pick(t):
-        return lax.dynamic_index_in_dim(blocks, jnp.clip(t, 0, nz - 1), 0, keepdims=False).astype(F32)
-
-    right = left = None
-    for dist in range(nz - 1, 0, -1):
-        up, down = (pick(z + dist), pick(z - dist))
-        if right is not None:
-            up, down = (up + right.astype(F32), down + left.astype(F32))
-        right = lay.send(
-            up.astype(BF16), lambda z, y, x, c: (z + 1, y, x, c) if z + dist < nz else None)
-        left = lay.send(
-            down.astype(BF16), lambda z, y, x, c: (z - 1, y, x, c) if z - dist >= 0 else None)
-    return pick(z) + right.astype(F32) + left.astype(F32)
+        return lax.dynamic_index_in_dim(blocks, t, 0, keepdims=False)
+
+    total = pick(z).astype(F32)
+    for step in range(1, nz):
+        come = lay.send(pick((z + step) % nz), lambda z, y, x, c: ((z + step) % nz, y, x, c))
+        total = total + come.astype(F32)
+    return total
 
 
 def local(inputs, block_flags, decay_seed, vectors, in_y, in_x, gate_weight, out_proj,
@@ -604,12 +657,16 @@
         by_c = jnp.where(first, rel, jnp.concatenate([p[1], p[0], p[3], p[2]], -1))
         return jnp.where(x == 0, by_c, jnp.concatenate([by_c[..., 2 * b :], by_c[..., : 2 * b]], -1))
 
+    cot = cotangent[0]
+    cot_y, cot_z = (lay.over_y(cot), lay.over_z(cot))
     halo_raw = lay.over_seq(inputs[0, tokens - 16 :], 1)
-    residual = inputs[0].astype(F32)
+    rows_theirs = lax.dynamic_slice_in_dim(gate_weight, (1 - x) * half, half, 0)
+    gate_x = lay.over_x(rows_theirs)
+    residual = after(inputs[0], rows_theirs).astype(F32)
     scaled_one, inverse_one = norm_scale(residual)
     normed_own = (scaled_one * vectors[0]).astype(BF16)
     normed_x = lay.over_x(normed_own)
-    halo_own = (norm_scale(halo_raw.astype(F32))[0] * vectors[0]).astype(BF16)
+    halo_own = (norm_scale(after(halo_raw, normed_own).astype(F32))[0] * vectors[0]).astype(BF16)
     flag_row = jnp.pad(block_flags.astype(BF16), ((0, 0), (0, width - block_flags.shape[1])))
     halo_x = lay.over_x(jnp.concatenate([flag_row, halo_own[1:]], axis=0))
     n_flags = block_flags.shape[1]
@@ -618,24 +675,19 @@
 
     wy, wx = (in_y, in_x)
     wy_c, wx_c = (lay.over_c(in_y), lay.over_c(in_x))
-    rows_mine = lax.dynamic_slice_in_dim(gate_weight, x * half, half, 0)
-    rows_theirs = lax.dynamic_slice_in_dim(gate_weight, (1 - x) * half, half, 0)
-    gate_x = lay.over_x(rows_theirs)
+    out_later = after(out_proj, halo_own)
+    out_theirs = lax.dynamic_slice_in_dim(out_later, (1 - x) * half, half, 0)
+    out_x = lay.over_x(out_theirs)
+    out_mine = lax.dynamic_slice_in_dim(out_later, x * half, half, 0)
+    rows_mine = lax.dynamic_slice_in_dim(after(gate_weight, out_theirs), x * half, half, 0)
     gate_c, gate_xc = (lay.over_c(rows_mine), lay.over_c(gate_x))
     gates = order_f(jnp.concatenate([rows_mine, gate_c, gate_x, gate_xc], axis=1))
-    out_later = after(out_proj, halo_own)
-    out_mine = lax.dynamic_slice_in_dim(out_later, x * half, half, 0)
-    out_x = lay.over_x(lax.dynamic_slice_in_dim(out_later, (1 - x) * half, half, 0))
     out_c, out_xc = (lay.over_c(out_mine), lay.over_c(out_x))
     out_rel = jnp.concatenate([out_mine, out_c, out_x, out_xc], axis=1)
-    cot = cotangent[0]
-    cot_y, cot_z = (lay.over_y(cot), lay.over_z(cot))
-    cot_x = lay.over_x(after(cot, normed_own))
-    cot_xz, cot_xy = (lay.over_x(cot_z), lay.over_y(cot_x))
+    cot_x = lay.over_x(after(cot, out_theirs))
 
     normed = jnp.concatenate([normed_own, normed_x, halo_own, halo_x], axis=0)
     two = 2 * tokens
-    y_pre = order_c(dot(normed[:two], wy), dot(normed[:two], wy_c), 1).reshape(2, tokens, half)
     x_all = order_c(dot(normed, wx).astype(BF16), dot(normed, wx_c).astype(BF16), 1)
     x_low = x_all[:two].reshape(2, tokens, half)
     halo = x_all[two:].reshape(2, 16, half)
@@ -647,47 +699,86 @@
     summary_shape = jax.ShapeDtypeStruct((4, half), F32)
     conv_low, ig, dg, prods, local_state, summary = by_head(
         mixer_forward, flags,
-        [(x_low, False), (halo, False), (gates, True), (vec_half, False), (rates, False)],
+        [(after(x_low, cot_y), False), (halo, False), (gates, True), (vec_half, False), (rates, False)],
         [shape3(BF16), shape3(F32), shape3(F32), shape3(F32), shape3(F32), summary_shape])
     state_in = entering(lay, summary, 2, False)
+    normed_two = after(normed[:two], summary)
+    y_pre = order_c(dot(normed_two, wy), dot(normed_two, wy_c), 1).reshape(2, tokens, half)
+    state_tied = after(state_in, cot_z)
+    cot_xy = lay.over_y(after(cot_x, state_in))
+    cot_xz = lay.over_z(after(cot_x, state_in))
     cot_yz = lay.over_y(after(cot_z, state_in))
-    cot_xyz = lay.over_y(after(cot_xz, state_in))
+    cot_xyz = lay.over_y(cot_xz)
     cots = [[cot, cot_x], [cot_y, cot_xy], [cot_z, cot_xz], [cot_yz, cot_xyz]]
     cots_c = [[lay.over_c(part) for part in group] for group in cots]
-    grad_hiddens = [
-        grad_hidden_of(group + group_c, mlp_down) for group, group_c in zip(cots, cots_c)]
-    state = local_state + prods * state_in[:, None, :]
+    state = local_state + prods * state_tied[:, None, :]
     mixed = (state * jax.nn.gelu(y_pre, approximate=True)).astype(BF16)
-    part_x = dot(mixed[1], out_rel).astype(BF16)
-    part_x = lay.over_x(part_x)
-    part_own = dot(mixed[0], out_rel)
+    part_x_low = dot(mixed[1], out_rel).astype(BF16)
+    part_x = lay.over_x(part_x_low)
+    gh_main = grad_hidden_of(after(cots[0] + cots_c[0], part_x_low), mlp_down)
+    part_own = after(dot(after(mixed[0], part_x_low), out_rel), gh_main, cot_xy)
     swapped = jnp.concatenate([part_x[:, half:], part_x[:, :half]], axis=1)
     mid = residual + order_f(part_own + swapped.astype(F32))
 
     scaled_two, inverse_two = norm_scale(mid)
     n2 = (scaled_two * vectors[1]).astype(BF16)
     n2_x = lay.over_x(n2)
-    n2_y, n2_z = (lay.over_y(n2), lay.over_z(n2))
-    n2_xy, n2_xz = (lay.over_y(n2_x), lay.over_z(n2_x))
-    n2_yz, n2_xyz = (lay.over_y(n2_z), lay.over_y(n2_xz))
+    n2_c, n2_xc = (lay.over_c(n2), lay.over_c(n2_x))
+    n2_z = lay.over_z(n2)
+    gh_y = grad_hidden_of(after(cots[1] + cots_c[1], n2), mlp_down)
+    place = jnp.stack([lay.seq_at // nz, y]).astype(jnp.int32)
+    each = width // lay.seq
+    cot_rows = rows_of_tokens(
+        after([p for group in cots for p in group], gh_y), place, half // 2, each)
+    n2_y = lay.over_y(after(n2, cot_xyz))
+    hidden, grad_gate, grad_up, far, far_c = mlp_forward(
+        after([n2, n2_x, n2_c, n2_xc], gh_y, cot_rows), gh_main, mlp_gate, mlp_up)
+    n2_xy = lay.over_x(after(n2_y, far))
+    n2_xz = lay.over_z(n2_x)
+    n2_yz = lay.over_y(n2_z)
+    n2_xyz = lay.over_y(n2_xz)
+    far_sum = (far + lay.over_c(far_c).astype(F32)).astype(BF16)
+    arriving = lay.over_x(far_sum)
+    near, near_c, out, out_c = mlp_rest(
+        after(hidden, far_sum, n2_y, n2_z), grad_gate, grad_up, mlp_gate, mlp_up, mlp_down, tokens)
+    near_sum = after(near + lay.over_c(near_c).astype(F32), n2_xz, n2_yz)
+    grad_n2 = near_sum + arriving.astype(F32)
+    out_sum = out + lay.over_c(out_c).astype(F32)
     n2s = [[n2, n2_x], [n2_y, n2_xy], [n2_z, n2_xz], [n2_yz, n2_xyz]]
-    n2s_c = [[lay.over_c(part) for part in group] for group in n2s]
-    hidden, grad_gate, grad_up, far, far_c = mlp_forward(
-        n2s[0] + n2s_c[0], grad_hiddens[0], mlp_gate, mlp_up)
-    arriving = lay.over_x((far + lay.over_c(far_c).astype(F32)).astype(BF16))
-    near, near_c, out, out_c = mlp_rest(
-        hidden, grad_gate, grad_up, mlp_gate, mlp_up, mlp_down, tokens)
-    grad_n2 = near + lay.over_c(near_c).astype(F32) + arriving.astype(F32)
-    out_sum = out + lay.over_c(out_c).astype(F32)
+    n2s_c = [[n2_c, n2_xc]] + [[lay.over_c(part) for part in group] for group in n2s[1:]]
+    acts = (hidden, grad_gate, grad_up)
+    low = (lay.z % (nz // 2)).astype(jnp.int32).reshape(1)
+    cot_row_pair = (cot_rows, lay.over_c(cot_rows))
+
+    def weight_piece(at, size, n2_row_pair, *ties):
+        own, rest = mlp_weight_grads(
+            low, [group + group_c for group, group_c in zip(n2s[1:], n2s_c[1:])], [gh_y],
+            [group + group_c for group, group_c in zip(cots[2:], cots_c[2:])],
+            after(acts, ties), n2_row_pair, cot_row_pair, (mlp_gate, mlp_up, mlp_down), at, size, each)
+        blocks = [own] + [rest[j * each : (j + 1) * each] for j in range(nz // 2 - 1)]
+        bit = nz // 4
+        while bit >= 1:
+            gone = blocks[bit] if bit == 1 else jnp.concatenate(
+                [b.astype(BF16) for b in blocks[bit : 2 * bit]], axis=0)
+            come = lay.over_seq_bit(gone.astype(BF16), 2 * bit)
+            blocks = [blocks[j].astype(F32) + come[j * each : (j + 1) * each].astype(F32) for j in range(bit)]
+            bit //= 2
+        return own, blocks[0]
 
     grad_mid_norm, grad_gain_two = norm_back(grad_n2, scaled_two, inverse_two, vectors[1])
     grad_mid = cot.astype(F32) + grad_mid_norm
     branch = grad_mid.astype(BF16)
     branch_rel = order_f(branch)
     arriving = lay.over_x(branch_rel)
+    n2_rows = rows_of_tokens(
+        after([p for group in n2s for p in group], branch_rel), place, half // 2, each)
+    n2_row_pair = (n2_rows, lay.over_c(n2_rows))
+    cuts = sections_of(mlp_gate.shape[1])
+    cuts = cuts[-1:] + cuts[:-1]
+    first_own, first_piece = weight_piece(*cuts[0], n2_row_pair, branch_rel)
+    arriving = after(arriving, first_own)
     branch_x_rel = jnp.concatenate([arriving[:, half:], arriving[:, :half]], axis=1)
-    out_arriving = lay.over_x(after(out_sum[tokens:].astype(BF16), branch))
-    output = (mid + out_sum[:tokens] + out_arriving.astype(F32)).astype(BF16)[None]
+    branch_two = jnp.concatenate([branch, order_f(branch_x_rel)], 0)
     grad_mixed = dot_cols(jnp.concatenate([branch_rel, branch_x_rel], 0), out_rel)
     gy, bprod, blocal, back_summary = by_head(
         mixer_back_scan, flags,
@@ -695,6 +786,29 @@
          (local_state, False), (state_in, False), (rates, False)],
         [shape3(BF16), shape3(F32), shape3(F32), summary_shape])
     back_in = entering(lay, back_summary, 2, True)
+
+    own80 = each // 4
+    at_yc = jnp.stack([y, c]).astype(jnp.int32)
+
+    def spread(parts, starts):
+        keep, away = rows_by_device(at_yc, parts, starts, own80)
+        come = lay.over_c(away)
+        keep_y, come_y = (lay.over_y(keep[1]), lay.over_y(come[1]))
+        return [keep[0], come[0], keep_y, come_y]
+
+    def n1_starts(at_y, at_c):
+        return [((2 * i + at_y) * 4 + 2 * j + at_c) * own80 for i in range(nz) for j in range(2)]
+
+    def mixed_starts(at_y, at_c):
+        return [((at_y * nz + i) * 2 + at_c) * own80 for i in range(nz)]
+
+    def all_tokens(value, tie):
+        other_y = lay.over_y(after(value, tie))
+        return [value, lay.over_c(value), other_y, lay.over_c(other_y)]
+
+    n1_rows = spread([normed_own, normed_x], n1_starts)
+    mixed_rows = spread([after(mixed, back_summary)[i] for i in range(2)], mixed_starts)
+
     gip, gdp, gx_main, gx_tail, edge, vec_rows = by_head(
         mixer_backward, flags,
         [(bprod, False), (blocal, False), (back_in, False), (prods, False), (local_state, False),
@@ -719,73 +833,17 @@
 
     grad_n1_far = grad_n1_of(slice(tokens, two)).astype(BF16)
     arriving = lay.over_x(grad_n1_far)
-    grad_n1 = grad_n1_of(slice(0, tokens)) + arriving.astype(F32)
+    grad_n1_near = grad_n1_of(slice(0, tokens))
+    second_own, second_piece = weight_piece(*cuts[1], n2_row_pair, grad_n1_far)
+    grad_n1 = after(grad_n1_near, second_own) + arriving.astype(F32)
     grad_in_norm, grad_gain_one = norm_back(grad_n1, scaled_one, inverse_one, vectors[0])
     input_grad = (grad_mid + grad_in_norm).astype(BF16)[None]
 
-    each = width // lay.seq
-    seq_at = 2 * z + y
-    place = jnp.stack([seq_at // nz, y]).astype(jnp.int32)
-    n2_rows = rows_of_tokens([p for group in n2s for p in group], place, half // 2, each)
-    cot_rows = rows_of_tokens([p for group in cots for p in group], place, half // 2, each)
-    row_pairs = ((n2_rows, lay.over_c(n2_rows)), (cot_rows, lay.over_c(cot_rows)))
-    acts = (hidden, grad_gate, grad_up)
-    sides = [group + group_c for group, group_c in zip(n2s[1:], n2s_c[1:])]
-    share = [
-        [2 * (upper * (nz // 2) + low) + side for low in range(nz // 2)]
-        for upper in range(2) for side in range(2)]
-    ties = (branch, grad_n1_far, input_grad)
-    columns = [[], [], []]
-    for (at, size), tie in zip(sections_of(mlp_gate.shape[1]), ties):
-        part = mlp_weight_grads(
-            sides, grad_hiddens[1:], after(acts, tie), *row_pairs, (mlp_gate, mlp_up), at, size)
-        part = lax.psum_scatter(
-            part, "seq", scatter_dimension=0, axis_index_groups=share, tiled=True)
-        for i in range(3):
-            columns[i].append(part[:, i * size : (i + 1) * size])
-    mlp_down_grad, mlp_gate_grad, mlp_up_grad = [
-        jnp.concatenate(parts, axis=1).astype(F32) for parts in columns]
-
-    rows_full = lax.dynamic_update_slice_in_dim(
-        jnp.zeros((8, width), F32), vec_rows, x * half, 1)
-    vec = jnp.concatenate([grad_gain_one[None], grad_gain_two[None], rows_full], axis=0)
-    vec = vec + lay.over_c(vec)
-    vec = vec + lay.over_x(vec)
-    bit = 1
-    while bit < lay.seq:
-        vec = vec + lay.over_seq_bit(vec, bit)
-        bit *= 2
-
-    own80 = each // 4
-
-    def spread_rows(value, where):
-        by_yc = where(value.T)
-        by_c = lax.dynamic_index_in_dim(by_yc, c, 1, keepdims=False)
-        other_c = lax.dynamic_index_in_dim(by_yc, 1 - c, 1, keepdims=False)
-        pair = jnp.concatenate([by_c, lay.over_c(other_c)], axis=2)
-        by_y = lax.dynamic_index_in_dim(pair, y, 0, keepdims=False)
-        other_y = lax.dynamic_index_in_dim(pair, 1 - y, 0, keepdims=False)
-        return jnp.concatenate([by_y, lay.over_y(other_y)], axis=1)
-
-    def all_tokens(value):
-        other_y = lay.over_y(value)
-        return jnp.concatenate([value, lay.over_c(value), other_y, lay.over_c(other_y)], 0)
-
-    def where_n1(rows):
-        split = rows.reshape(nz, 2, 2, 2, own80, two)
-        return split.transpose(1, 3, 0, 2, 4, 5).reshape(2, 2, nz * 2 * own80, two)
-
-    def where_mixed(rows):
-        split = rows.reshape(2, nz, 2, own80, two)
-        return split.transpose(0, 2, 1, 3, 4).reshape(2, 2, nz * own80, two)
-
-    n1_rows = spread_rows(jnp.concatenate([normed_own, normed_x], 0), where_n1)
-    mixed_rows = spread_rows(mixed.reshape(two, half), where_mixed)
-    branch_all = all_tokens(jnp.concatenate([branch, order_f(branch_x_rel)], 0))
-    out_part = dot(mixed_rows, branch_all).astype(BF16).reshape(nz, 2 * own80, half)
-    in_y_part = dot(n1_rows, all_tokens(gy)).astype(BF16).reshape(nz, 2 * own80, half)
-    done_one = line_sum(lay, jnp.concatenate([in_y_part, out_part], axis=1)).astype(BF16)
-
+    branch_all = all_tokens(branch_two, edge)
+    out_part = sum_of_dots(mixed_rows, branch_all)
+    out_sum_z = owner_sum(lay, out_part.reshape(nz, own80, width))
+    in_y_part = sum_of_dots(n1_rows, all_tokens(gy, edge))
+    in_y_sum = owner_sum(lay, in_y_part.reshape(nz, 2 * own80, half)).astype(BF16)
     heads = half // BLK
     gate_part = jnp.einsum(
         "thi,thj->hij", conv_low.reshape(two, heads, BLK),
@@ -797,9 +855,16 @@
     keep = lax.dynamic_index_in_dim(gate_part, y, 0, keepdims=False)
     away = lax.dynamic_index_in_dim(gate_part, 1 - y, 0, keepdims=False)
     gate_part = (keep + lay.over_y(away.astype(BF16)).astype(F32)).astype(BF16)
-    in_x_part = dot(n1_rows, all_tokens(gx)).astype(BF16).reshape(nz, 2 * own80, half)
-    done_two = line_sum(lay, jnp.concatenate(
-        [in_x_part, gate_part.reshape(nz, own80 * 2 * BLK // half, half)], axis=1)).astype(BF16)
+    in_x_part = sum_of_dots(n1_rows, all_tokens(gx, edge))
+    in_x_sum = owner_sum(lay, in_x_part.reshape(nz, 2 * own80, half)).astype(BF16)
+    gate_sum = owner_sum(lay, gate_part).astype(BF16)
+
+    third_own, third_piece = weight_piece(*cuts[2], n2_row_pair, in_x_part)
+    pieces = [second_piece, third_piece, first_piece]
+    widths = [cuts[1][1], cuts[2][1], cuts[0][1]]
+    mlp_down_grad, mlp_gate_grad, mlp_up_grad = [
+        jnp.concatenate([p[:, i * n : (i + 1) * n] for p, n in zip(pieces, widths)], axis=1)
+        for i in range(3)]
 
     def over_columns(value):
         split = value.reshape(2, own80, half)
@@ -808,15 +873,29 @@
         return jnp.where(x == 0, jnp.concatenate([mine, theirs], -1),
                          jnp.concatenate([theirs, mine], -1)).astype(F32)
 
-    in_y_grad = over_columns(done_one[: 2 * own80])
-    in_x_grad = over_columns(done_two[: 2 * own80])
+    in_y_grad = over_columns(in_y_sum)
+    in_x_grad = over_columns(in_x_sum)
+
     def final(z, y, x, c):
         at = ((x * 2 + y) * nz + z) * 2 + c
         s, f = (at // 4, at % 4)
         return (s // 2, s % 2, f // 2, f % 2)
 
-    out_grad = lay.send(done_one[2 * own80 :].reshape(own80, width), final).astype(F32)
-    gate_grad = lay.send(done_two[2 * own80 :].reshape(own80, 2 * BLK), final).astype(F32)
+    out_grad = lay.send(out_sum_z.astype(BF16), final).astype(F32)
+    gate_grad = lay.send(gate_sum, final).astype(F32)
+    out_arriving = lay.over_x(after(out_sum[tokens:].astype(BF16), input_grad))
+    output = (mid + out_sum[:tokens] + out_arriving.astype(F32)).astype(BF16)[None]
+
+    rows_full = lax.dynamic_update_slice_in_dim(
+        jnp.zeros((8, width), F32), vec_rows, x * half, 1)
+    vec = jnp.concatenate([grad_gain_one[None], grad_gain_two[None], rows_full], axis=0)
+    vec = vec + lay.over_c(vec)
+    vec = vec + lay.over_x(vec)
+    bit = 1
+    while bit < lay.seq:
+        vec = vec + lay.over_seq_bit(vec, bit)
+        bit *= 2
+
     return (output, input_grad, vec, in_y_grad, in_x_grad, gate_grad, out_grad,
             mlp_gate_grad, mlp_up_grad, mlp_down_grad)
 

time: 749 us -> 692 us (0.924)
  starting transfers between devices: 122 us -> 103 us
  matrix products: 54.8 us -> 39.5 us
  Pallas kernels: 200 us -> 214 us
  other arithmetic: 56.1 us -> 42.6 us
  between operations: 15.9 us -> 2.72 us
  waiting for transfers between devices: 241 us -> 233 us
    pallas_call x3 -> x8, Pallas kernels: 76.9 us -> 117 us  [the longest x3 94.3 us: mlp_weight_grads(): pl.pallas_call(body, grid_spec=pltpu.PrefetchScalarGridSpec(num_scalar_pr...]
    pallas_call x4 -> x2, Pallas kernels: 51.3 us -> 25.8 us  [grad_hidden_of(): pl.pallas_call(body, grid=(pl.cdiv(ff, BLK),), in_specs=[ANY] * count + [...]
    dot_general x9 -> x6, matrix products: 32.2 us -> 13.8 us  [dot(): return jnp.dot(left, right, preferred_element_type=F32)]
    ppermute x94 -> x99, starting transfers between devices: 121 us -> 103 us  [send(): return lax.ppermute(value, ALL, self.pairs(target))]
    squeeze x2 -> x10, local copies, waits for them, and re-layouts: 2.04 us -> 11.2 us  [the longest x4 6.44 us: spread(): keep_y, come_y = (lay.over_y(keep[1]), lay.over_y(come[1]))]
    ppermute x94 -> x99, waiting for transfers between devices: 241 us -> 233 us  [send(): return lax.ppermute(value, ALL, self.pairs(target))]
    convert_element_type x12 -> x8, other arithmetic: 16.7 us -> 9.78 us  [the longest x1 2.72 us: local(): branch = grad_mid.astype(BF16)]
  transfers between devices with their start and end apart: 97 -> 99, of which waited for: 29 -> 32; matrix products, arithmetic and copies ran while one was open for 19% -> 17% of each run, Pallas kernels for 24% -> 25%
where the time goes in v4:
time: 692 us; the launch traced here: 685 us
  waiting for transfers between devices  233 us (34%)
  Pallas kernels  214 us (31%)
  starting transfers between devices  103 us (15%)
  local copies, waits for them, and re-layouts  49.4 us (7%)
  other arithmetic  42.6 us (6%)
  matrix products  39.5 us (6%)
    ppermute x99, waiting for transfers between devices, send(): return lax.ppermute(value, ALL, self.pairs(target))  233 us
    ppermute x99, starting transfers between devices, send(): return lax.ppermute(value, ALL, self.pairs(target))  103 us
    pallas_call x3, Pallas kernels, mlp_weight_grads(): pl.pallas_call(body, grid_spec=pltpu.PrefetchScalarGridSpec(num_scalar_pr...  94.3 us
    pallas_call x2, Pallas kernels, grad_hidden_of(): pl.pallas_call(body, grid=(pl.cdiv(ff, BLK),), in_specs=[ANY] * count + [...  25.8 us
    dot_general x9, matrix products, dot_cols(): lax.dot_general(left, right, (((1,), (1,)), ((), ())), preferred_element_...  25.2 us
    pallas_call x1, Pallas kernels, mlp_forward(): pl.pallas_call(body, in_specs=[ANY] * (count + 3), out_shape=[act, act, a...  23.3 us
    pallas_call x3, Pallas kernels, by_head(): pl.pallas_call(body, grid=(heads,), in_specs=in_specs, out_specs=[spec(o....  20.6 us
    pallas_call x1, Pallas kernels, mlp_rest(): pl.pallas_call(body, grid=(width // block,), in_specs=[whole] * 3 + [weig...  19 us
  transfers between devices with their start and end apart: 99, of which 32 were waited for; matrix products, arithmetic and copies ran while one was open for 17% of the time, Pallas kernels for 25%

profile of v4, /device:TPU:2, one launch (start us, length us, event | category | flops | bytes accessed | tf_op | source)
XLA Modules:
  0.0 685.2 jit_solution(4698580386897044606)
XLA Ops:
  1.7 3.4 collective-permute-start
  11.7 4.2 constant_dynamic-slice_fusion
  15.9 15.3 %collective-permute-done.1 = bf16[16,2560]{1,0:T(8,128)(2,1)S(1)} collective-permute-done((bf16[16,2560]{1,0:T(8,128)(2,1)S(1)}, bf16[16,2560]{1,0:T(8,128)(2,1)S(1)}, u32[]{:S(2)}, u32[]{:S(2)}) %collective-permute-start.1) | collective-permute-done | bytes 81952 | tf_op jit(solution)/shard_map/ppermute | solution.py:78
  32.8 3.6 collective-permute-start.11
  41.5 3.3 convolution_convert_fusion.1
  45.1 7.1 %shard_map.195 = (bf16[2,128,1280]{2,1,0:T(8,128)(2,1)S(1)}, f32[2,128,1280]{2,1,0:T(8,128)S(1)}, f32[2,128,1280]{2,1,0:T(8,128)S(1)}, f32[2,128,1280]{2,1,0:T(8...) custom-call(f32[2,2]{1,0:T(2,128)S(1)} %pad_maximum_fusion.15.flags_ref, bf16[2,128,1280]{2,1,0:T(8,128)(2,1)S(1)} %bitcast.128, ...), custom_call_target="tpu_custom_call" | custom-call | flops 1 | bytes 1 | tf_op jit(solution)/shard_map/pallas_call | solution.py:262
  59.2 17.8 %collective-permute-done.14 = bf16[1280,640]{1,0:T(8,128)(2,1)} collective-permute-done((bf16[1280,640]{1,0:T(8,128)(2,1)}, bf16[1280,640]{1,0:T(8,128)(2,1)}, u32[]{:S(2)}, u32[]{:S(2)}) %collective-permute-start.14) | collective-permute-done | bytes 1638432 | tf_op jit(solution)/shard_map/ppermute | solution.py:78
  83.0 10.7 %collective-permute-done.16.refs_1_ = bf16[128,2560]{1,0:T(8,128)(2,1)} collective-permute-done((bf16[128,2560]{1,0:T(8,128)(2,1)}, bf16[128,2560]{1,0:T(8,128)(2,1)}, u32[]{:S(2)}, u32[]{:S(2)}) %collective-permute-start.16) | collective-permute-done | bytes 655392 | tf_op jit(solution)/shard_map/ppermute | solution.py:78
  100.8 12.8 %shard_map.196.refs_4_ = f32[512,1920]{1,0:T(8,128)} custom-call(bf16[128,2560]{1,0:T(8,128)(2,1)} %bitcast.3.refs_0_, bf16[128,2560]{1,0:T(8,128)(2,1)} %collective-permute-done.16.refs_1_, bf16[128,2560]{1,0:T(8,128)(2,1)} %copy-done.62, bf16[128,2560]{1,0:T(8,128)(2,1)} %collective-permute-done.18.refs_3_, bf16[2560,1920]{1,0:T(8,128)(2,1)} %refs_23_.5), custom_call_target="tpu_custom_call" | custom-call | flops 1 | bytes 1 | tf_op jit(solution)/shard_map/pallas_call | solution.py:295
  113.6 3.6 fusion.80
  123.9 13.1 %collective-permute-done.21.refs_1_ = bf16[128,2560]{1,0:T(8,128)(2,1)} collective-permute-done((bf16[128,2560]{1,0:T(8,128)(2,1)}, bf16[128,2560]{1,0:T(8,128)(2,1)}, u32[]{:S(2)}, u32[]{:S(2)}) %collective-permute-start.21) | collective-permute-done | bytes 655392 | tf_op jit(solution)/shard_map/ppermute | solution.py:78
  137.6 13.0 %shard_map.197.refs_20_ = f32[512,1920]{1,0:T(8,128)} custom-call(bf16[128,2560]{1,0:T(8,128)(2,1)} %collective-permute-done.4.refs_0_.refs_2_, bf16[128,2560]{1,0:T(8,128)(2,1)} %collective-permute-done.19.refs_1_.refs_3_, bf16[128,2560]{1,0:T(8,128)(2,1)} %collective-permute-done.24.refs_2_, bf16[128,2560]{1,0:T(8,128)(2,1)} %collective-permute-done.25.refs_3_, ...), custom_call_target="tpu_custom_call" | custom-call | flops 1 | bytes 1 | tf_op jit(solution)/shard_map/pallas_call | solution.py:295
  153.4 4.4 shard_map.198.refs_29_
  157.8 23.3 %shard_map.199 = (bf16[512,1920]{1,0:T(8,128)(2,1)}, bf16[512,1920]{1,0:T(8,128)(2,1)}, bf16[512,1920]{1,0:T(8,128)(2,1)}, f32[128,2560]{1,0:T(8,128)}, bf16[128,2560]{1,0:T(8,128)(2,1)}) custom-call(bf16[128,2560]{1,0:T(8,128)(2,1)} %multiply_convert_fusion.refs_0_, bf16[128,2560]{1,0:T(8,128)(2,1)} %collective-permute-done.21.refs_1_, ...), custom_call_target="tpu_custom_call" | custom-call | flops 1 | bytes 1 | tf_op jit(solution)/shard_map/pallas_call | solution.py:380
  187.7 12.9 %collective-permute-done.31.refs_4_ = bf16[128,2560]{1,0:T(8,128)(2,1)} collective-permute-done((bf16[128,2560]{1,0:T(8,128)(2,1)}, bf16[128,2560]{1,0:T(8,128)(2,1)}, u32[]{:S(2)}, u32[]{:S(2)}) %collective-permute-start.31) | collective-permute-done | bytes 655392 | tf_op jit(solution)/shard_map/ppermute | solution.py:78
  200.8 19.0 %shard_map.200 = (f32[128,2560]{1,0:T(8,128)}, bf16[128,2560]{1,0:T(8,128)(2,1)}, f32[256,2560]{1,0:T(8,128)}, bf16[256,2560]{1,0:T(8,128)(2,1)}) custom-call(bf16[512,1920]{1,0:T(8,128)(2,1)} %get-tuple-element.194.hid_ref.refs_24_, bf16[512,1920]{1,0:T(8,128)(2,1)} %get-tuple-element.195.gg_ref.refs_25_, ...), custom_call_target="tpu_custom_call" | custom-call | flops 1 | bytes 1 | tf_op jit(solution)/shard_map/pallas_call | solution.py:419
  220.6 3.4 shard_map.206
  230.6 13.2 %collective-permute-done.34.refs_5_ = bf16[128,2560]{1,0:T(8,128)(2,1)} collective-permute-done((bf16[128,2560]{1,0:T(8,128)(2,1)}, bf16[128,2560]{1,0:T(8,128)(2,1)}, u32[]{:S(2)}, u32[]{:S(2)}) %collective-permute-start.34) | collective-permute-done | bytes 655392 | tf_op jit(solution)/shard_map/ppermute | solution.py:78
  251.0 14.8 %collective-permute-done.38.refs_3_.refs_1_ = bf16[128,2560]{1,0:T(8,128)(2,1)S(1)} collective-permute-done((bf16[128,2560]{1,0:T(8,128)(2,1)}, bf16[128,2560]{1,0:T(8,128)(2,1)S(1)}, u32[]{:S(2)}, u32[]{:S(2)}) %collective-permute-start.38) | collective-permute-done | bytes 655392 | tf_op jit(solution)/shard_map/ppermute | solution.py:78
  267.4 4.4 shard_map.201.refs_27_
  287.5 23.1 %shard_map.202 = (f32[320,1152]{1,0:T(8,128)}, bf16[320,1152]{1,0:T(8,128)(2,1)}) custom-call(s32[1]{0:T(128)} %bitcast.11.place_ref, bf16[128,2560]{1,0:T(8,128)(2,1)} %collective-permute-done.30.refs_2_.refs_0_, bf16[128,2560]{1,0:T(8,128)(2,1)} %copy-done.27, bf16[128,2560]{1,0:T(8,128)(2,1)} %collective-permute-done.39.refs_2_, ...), custom_call_target="tpu_custom_call" | custom-call | flops 1 | bytes 1 | tf_op jit(solution)/shard_map/pallas_call | solution.py:525
  312.0 4.5 fusion.24
  316.5 5.6 shard_map.203
  337.3 3.6 convolution_add_fusion.2
  341.2 14.5 %collective-permute-start.53 = (f32[4,1280]{1,0:T(4,128)S(1)}, f32[4,1280]{1,0:T(4,128)S(1)}, u32[]{:S(2)}, u32[]{:S(2)}) collective-permute-start(f32[4,1280]{1,0:T(4,128)S(1)} %pad_maximum_fusion.13), channel_id=1, source_target_pairs={{0,8},{1,9},{2,10},{3,11},{4,12},{5,13},{6,14},{7,15},{8,0},{9,1},... | collective-permute-start | bytes 61448 | tf_op jit(solution)/shard_map/ppermute | solution.py:78
  362.6 7.9 %shard_map.204 = (bf16[2,128,1280]{2,1,0:T(8,128)(2,1)S(1)}, bf16[2,128,1280]{2,1,0:T(8,128)(2,1)S(1)}, bf16[2,128,1280]{2,1,0:T(8,128)(2,1)S(1)}, f32[2,16,1280...) custom-call(f32[2,2]{1,0:T(2,128)S(1)} %pad_maximum_fusion.15.flags_ref, ...), custom_call_target="tpu_custom_call" | custom-call | flops 1 | bytes 1 | tf_op jit(solution)/shard_map/pallas_call | solution.py:262
  385.0 3.2 fusion
  391.3 35.7 %shard_map.205 = (f32[320,2304]{1,0:T(8,128)}, bf16[320,2304]{1,0:T(8,128)(2,1)}) custom-call(s32[1]{0:T(128)} %bitcast.11.place_ref, bf16[128,2560]{1,0:T(8,128)(2,1)} %collective-permute-done.30.refs_2_.refs_0_, bf16[128,2560]{1,0:T(8,128)(2,1)} %copy-done.27, bf16[128,2560]{1,0:T(8,128)(2,1)} %collective-permute-done.39.refs_2_, ...), custom_call_target="tpu_custom_call" | custom-call | flops 1 | bytes 1 | tf_op jit(solution)/shard_map/pallas_call | solution.py:525
  427.0 3.6 convolution_add_fusion.3
  438.7 3.3 collective-permute-done.59
  444.1 4.5 collective-permute-start.84
  452.2 3.6 collective-permute-done.83
  457.5 16.7 %collective-permute-done.61 = f32[10,2560]{1,0:T(8,128)S(1)} collective-permute-done((f32[10,2560]{1,0:T(8,128)S(1)}, f32[10,2560]{1,0:T(8,128)S(1)}, u32[]{:S(2)}, u32[]{:S(2)}) %collective-permute-start.61) | collective-permute-done | bytes 102432 | tf_op jit(solution)/shard_map/ppermute | solution.py:78
  478.8 3.2 collective-permute-start.74
  484.1 8.3 %collective-permute-done.62 = f32[10,2560]{1,0:T(8,128)S(1)} collective-permute-done((f32[10,2560]{1,0:T(8,128)S(1)}, f32[10,2560]{1,0:T(8,128)S(1)}, u32[]{:S(2)}, u32[]{:S(2)}) %collective-permute-start.62) | collective-permute-done | bytes 102432 | tf_op jit(solution)/shard_map/ppermute | solution.py:78
  498.3 5.3 shard_map.207
  512.3 5.1 shard_map.208
  517.4 35.5 %shard_map.211 = (f32[320,2304]{1,0:T(8,128)}, bf16[320,2304]{1,0:T(8,128)(2,1)}) custom-call(s32[1]{0:T(128)} %bitcast.11.place_ref, bf16[128,2560]{1,0:T(8,128)(2,1)} %collective-permute-done.30.refs_2_.refs_0_, bf16[128,2560]{1,0:T(8,128)(2,1)} %copy-done.27, bf16[128,2560]{1,0:T(8,128)(2,1)} %collective-permute-done.39.refs_2_, ...), custom_call_target="tpu_custom_call" | custom-call | flops 1 | bytes 1 | tf_op jit(solution)/shard_map/pallas_call | solution.py:525
  564.8 25.9 %collective-permute-done.77 = bf16[160,1280]{1,0:T(8,128)(2,1)S(1)} collective-permute-done((bf16[160,1280]{1,0:T(8,128)(2,1)S(1)}, bf16[160,1280]{1,0:T(8,128)(2,1)S(1)}, u32[]{:S(2)}, u32[]{:S(2)}) %collective-permute-start.77) | collective-permute-done | bytes 409632 | tf_op jit(solution)/shard_map/ppermute | solution.py:78
  592.6 3.3 collective-permute-start.72
  595.9 4.0 collective-permute-done.72
  606.9 4.1 collective-permute-done.88.refs_3_
  611.7 5.8 shard_map.210
  623.0 4.9 collective-permute-done.97
  630.6 5.7 collective-permute-done.94
  636.2 18.6 %collective-permute-done.93 = bf16[80,2560]{1,0:T(8,128)(2,1)S(1)} collective-permute-done((bf16[80,2560]{1,0:T(8,128)(2,1)S(1)}, bf16[80,2560]{1,0:T(8,128)(2,1)S(1)}, u32[]{:S(2)}, u32[]{:S(2)}) %collective-permute-start.93) | collective-permute-done | bytes 409632 | tf_op jit(solution)/shard_map/ppermute | solution.py:78
  656.1 5.1 collective-permute-start.95
  665.7 18.3 %collective-permute-done.95 = bf16[80,2560]{1,0:T(8,128)(2,1)S(1)} collective-permute-done((bf16[80,2560]{1,0:T(8,128)(2,1)S(1)}, bf16[80,2560]{1,0:T(8,128)(2,1)S(1)}, u32[]{:S(2)}, u32[]{:S(2)}) %collective-permute-start.95) | collective-permute-done | bytes 409632 | tf_op jit(solution)/shard_map/ppermute | solution.py:78
  (465 shorter events, 196.1 us)
Async XLA Ops:
  5.1 35.9 %collective-permute-start.3 = (bf16[2560,640]{1,0:T(8,128)(2,1)}, bf16[2560,640]{1,0:T(8,128)(2,1)}, u32[]{:S(2)}, u32[]{:S(2)}) collective-permute-start(bf16[2560,640]{1,0:T(8,128)(2,1)} %param.17), channel_id=1, source_target_pairs={{0,1},{1,0},{2,3},{3,2},{4,5},{5,4},{6,7},{7,6},{8,9},{9,8},{10,11... | collective-permute-start | bytes 9830408 | tf_op jit(solution)/shard_map/ppermute | solution.py:78
  5.3 25.9 %collective-permute-start.6 = (bf16[1280,128]{1,0:T(8,128)(2,1)S(1)}, bf16[1280,128]{1,0:T(8,128)(2,1)S(1)}, u32[]{:S(2)}, u32[]{:S(2)}) collective-permute-start(bf16[1280,128]{1,0:T(8,128)(2,1)S(1)} %constant_dynamic-slice_fusion.4), channel_id=1, source_target_pairs={{0,2},{1,3},{2,0},{3,1},{4,6},{5,7},{6,4},{7,5},{8,10},{9,11},{10,... | collective-permute-start | bytes 983048 | tf_op jit(solution)/shard_map/ppermute | solution.py:78
  7.4 31.1 %collective-permute-start.2 = (bf16[128,2560]{1,0:T(8,128)(2,1)S(1)}, bf16[128,2560]{1,0:T(8,128)(2,1)S(1)}, u32[]{:S(2)}, u32[]{:S(2)}) collective-permute-start(bf16[128,2560]{1,0:T(8,128)(2,1)S(1)} %fusion.5.refs_0_), channel_id=1, source_target_pairs={{0,2},{1,3},{2,0},{3,1},{4,6},{5,7},{6,4},{7,5},{8,10},{9,11},{10,... | collective-permute-start | bytes 1966088 | tf_op jit(solution)/shard_map/ppermute | solution.py:78
  9.0 36.1 %collective-permute-start.4 = (bf16[128,2560]{1,0:T(8,128)(2,1)}, bf16[128,2560]{1,0:T(8,128)(2,1)}, u32[]{:S(2)}, u32[]{:S(2)}) collective-permute-start(bf16[128,2560]{1,0:T(8,128)(2,1)} %bitcast.3.refs_0_), channel_id=1, source_target_pairs={{0,4},{1,5},{2,6},{3,7},{4,0},{5,1},{6,2},{7,3},{8,12},{9,13},{10,... | collective-permute-start | bytes 1966088 | tf_op jit(solution)/shard_map/ppermute | solution.py:78
  11.1 20.2 %collective-permute-start.1 = (bf16[16,2560]{1,0:T(8,128)(2,1)S(1)}, bf16[16,2560]{1,0:T(8,128)(2,1)S(1)}, u32[]{:S(2)}, u32[]{:S(2)}) collective-permute-start(bf16[16,2560]{1,0:T(8,128)(2,1)S(1)} %fusion.67), channel_id=1, source_target_pairs={{0,2},{1,3},{2,0},{3,1},{4,6},{5,7},{6,4},{7,5},{8,10},{9,11},{10,... | collective-permute-start | bytes 245768 | tf_op jit(solution)/shard_map/ppermute | solution.py:78
  32.8 49.6 %collective-permute-start.11 = (bf16[128,2560]{1,0:T(8,128)(2,1)}, bf16[128,2560]{1,0:T(8,128)(2,1)}, u32[]{:S(2)}, u32[]{:S(2)}) collective-permute-start(bf16[128,2560]{1,0:T(8,128)(2,1)} %bitcast.3.refs_0_), channel_id=1, source_target_pairs={{0,24},{1,25},{2,26},{3,27},{4,28},{5,29},{6,30},{7,31},{8,16},{9,... | collective-permute-start | bytes 1966088 | tf_op jit(solution)/shard_map/ppermute | solution.py:78
  36.4 41.2 %collective-permute-start.12 = (bf16[2560,640]{1,0:T(8,128)(2,1)S(1)}, bf16[2560,640]{1,0:T(8,128)(2,1)S(1)}, u32[]{:S(2)}, u32[]{:S(2)}) collective-permute-start(bf16[2560,640]{1,0:T(8,128)(2,1)S(1)} %copy-done.24), channel_id=1, source_target_pairs={{0,1},{1,0},{2,3},{3,2},{4,5},{5,4},{6,7},{7,6},{8,9},{9,8},{10,11... | collective-permute-start | bytes 9830408 | tf_op jit(solution)/shard_map/ppermute | solution.py:78
  38.5 38.5 %collective-permute-start.14 = (bf16[1280,640]{1,0:T(8,128)(2,1)}, bf16[1280,640]{1,0:T(8,128)(2,1)}, u32[]{:S(2)}, u32[]{:S(2)}) collective-permute-start(bf16[1280,640]{1,0:T(8,128)(2,1)} %get-tuple-element.214), channel_id=1, source_target_pairs={{0,2},{1,3},{2,0},{3,1},{4,6},{5,7},{6,4},{7,5},{8,10},{9,11},{10,... | collective-permute-start | bytes 4915208 | tf_op jit(solution)/shard_map/ppermute | solution.py:78
  41.0 53.4 %collective-permute-start.13 = (bf16[1280,640]{1,0:T(8,128)(2,1)}, bf16[1280,640]{1,0:T(8,128)(2,1)}, u32[]{:S(2)}, u32[]{:S(2)}) collective-permute-start(bf16[1280,640]{1,0:T(8,128)(2,1)} %get-tuple-element.213), channel_id=1, source_target_pairs={{0,1},{1,0},{2,3},{3,2},{4,5},{5,4},{6,7},{7,6},{8,9},{9,8},{10,11... | collective-permute-start | bytes 4915208 | tf_op jit(solution)/shard_map/ppermute | solution.py:78
  58.0 19.6 %collective-permute-start.9 = (f32[4,1280]{1,0:T(4,128)S(1)}, f32[4,1280]{1,0:T(4,128)S(1)}, u32[]{:S(2)}, u32[]{:S(2)}) collective-permute-start(f32[4,1280]{1,0:T(4,128)S(1)} %pad_maximum_fusion.11), channel_id=1, source_target_pairs={{0,8},{1,9},{2,10},{3,11},{4,12},{5,13},{6,14},{7,15},{8,0},{9,1},... | collective-permute-start | bytes 61448 | tf_op jit(solution)/shard_map/ppermute | solution.py:78
  82.5 41.4 %collective-permute-start.24 = (bf16[128,2560]{1,0:T(8,128)(2,1)}, bf16[128,2560]{1,0:T(8,128)(2,1)}, u32[]{:S(2)}, u32[]{:S(2)}) collective-permute-start(bf16[128,2560]{1,0:T(8,128)(2,1)} %collective-permute-done.4.refs_0_.refs_2_), channel_id=1, source_target_pairs={{0,1},{1,0},{2,3},{3,2},{4,5},{5,4},{6,7},{7,6},{8,9},{9,8},{10,11... | collective-permute-start | bytes 1966088 | tf_op jit(solution)/shard_map/ppermute | solution.py:78
  94.4 22.9 %collective-permute-start.19 = (bf16[128,2560]{1,0:T(8,128)(2,1)}, bf16[128,2560]{1,0:T(8,128)(2,1)}, u32[]{:S(2)}, u32[]{:S(2)}) collective-permute-start(bf16[128,2560]{1,0:T(8,128)(2,1)} %collective-permute-done.16.refs_1_), channel_id=1, source_target_pairs={{0,4},{1,5},{2,6},{3,7},{4,0},{5,1},{6,2},{7,3},{8,12},{9,13},{10,... | collective-permute-start | bytes 1966088 | tf_op jit(solution)/shard_map/ppermute | solution.py:78
  94.5 28.2 %collective-permute-start.26 = (bf16[128,2560]{1,0:T(8,128)(2,1)}, bf16[128,2560]{1,0:T(8,128)(2,1)}, u32[]{:S(2)}, u32[]{:S(2)}) collective-permute-start(bf16[128,2560]{1,0:T(8,128)(2,1)} %collective-permute-done.16.refs_1_), channel_id=1, source_target_pairs={{0,24},{1,25},{2,26},{3,27},{4,28},{5,29},{6,30},{7,31},{8,16},{9,... | collective-permute-start | bytes 1966088 | tf_op jit(solution)/shard_map/ppermute | solution.py:78
  121.9 28.7 %collective-permute-start.27 = (bf16[128,2560]{1,0:T(8,128)(2,1)}, bf16[128,2560]{1,0:T(8,128)(2,1)}, u32[]{:S(2)}, u32[]{:S(2)}) collective-permute-start(bf16[128,2560]{1,0:T(8,128)(2,1)} %collective-permute-done.11.refs_4_.refs_12_), channel_id=1, source_target_pairs={{0,4},{1,5},{2,6},{3,7},{4,0},{5,1},{6,2},{7,3},{8,12},{9,13},{10,... | collective-permute-start | bytes 1966088 | tf_op jit(solution)/shard_map/ppermute | solution.py:78
  122.7 30.6 %collective-permute-start.28 = (bf16[128,2560]{1,0:T(8,128)(2,1)}, bf16[128,2560]{1,0:T(8,128)(2,1)}, u32[]{:S(2)}, u32[]{:S(2)}) collective-permute-start(bf16[128,2560]{1,0:T(8,128)(2,1)} %collective-permute-done.26.refs_5_.refs_13_), channel_id=1, source_target_pairs={{0,4},{1,5},{2,6},{3,7},{4,0},{5,1},{6,2},{7,3},{8,12},{9,13},{10,... | collective-permute-start | bytes 1966088 | tf_op jit(solution)/shard_map/ppermute | solution.py:78
  123.9 33.9 %collective-permute-start.22 = (bf16[128,2560]{1,0:T(8,128)(2,1)}, bf16[128,2560]{1,0:T(8,128)(2,1)}, u32[]{:S(2)}, u32[]{:S(2)}) collective-permute-start(bf16[128,2560]{1,0:T(8,128)(2,1)} %multiply_convert_fusion.refs_0_), channel_id=1, source_target_pairs={{0,1},{1,0},{2,3},{3,2},{4,5},{5,4},{6,7},{7,6},{8,9},{9,8},{10,11... | collective-permute-start | bytes 1966088 | tf_op jit(solution)/shard_map/ppermute | solution.py:78
  137.0 20.8 %collective-permute-start.23 = (bf16[128,2560]{1,0:T(8,128)(2,1)}, bf16[128,2560]{1,0:T(8,128)(2,1)}, u32[]{:S(2)}, u32[]{:S(2)}) collective-permute-start(bf16[128,2560]{1,0:T(8,128)(2,1)} %collective-permute-done.21.refs_1_), channel_id=1, source_target_pairs={{0,1},{1,0},{2,3},{3,2},{4,5},{5,4},{6,7},{7,6},{8,9},{9,8},{10,11... | collective-permute-start | bytes 1966088 | tf_op jit(solution)/shard_map/ppermute | solution.py:78
  181.2 19.4 %collective-permute-start.31 = (bf16[128,2560]{1,0:T(8,128)(2,1)}, bf16[128,2560]{1,0:T(8,128)(2,1)}, u32[]{:S(2)}, u32[]{:S(2)}) collective-permute-start(bf16[128,2560]{1,0:T(8,128)(2,1)} %multiply_convert_fusion.refs_0_), channel_id=1, source_target_pairs={{0,24},{1,25},{2,26},{3,27},{4,28},{5,29},{6,30},{7,31},{8,16},{9,... | collective-permute-start | bytes 1966088 | tf_op jit(solution)/shard_map/ppermute | solution.py:78
  224.1 25.0 %collective-permute-start.63 = (bf16[2,640,256]{2,1,0:T(8,128)(2,1)}, bf16[2,640,256]{2,1,0:T(8,128)(2,1)S(1)}, u32[]{:S(2)}, u32[]{:S(2)}) collective-permute-start(bf16[2,640,256]{2,1,0:T(8,128)(2,1)} %get-tuple-element.184), channel_id=1, source_target_pairs={{0,1},{1,0},{2,3},{3,2},{4,5},{5,4},{6,7},{7,6},{8,9},{9,8},{10,11... | collective-permute-start | bytes 1966088 | tf_op jit(solution)/shard_map/ppermute | solution.py:78
  224.4 24.0 %collective-permute-start.46 = (bf16[128,2560]{1,0:T(8,128)(2,1)}, bf16[128,2560]{1,0:T(8,128)(2,1)S(1)}, u32[]{:S(2)}, u32[]{:S(2)}) collective-permute-start(bf16[128,2560]{1,0:T(8,128)(2,1)} %collective-permute-done.11.refs_4_.refs_12_), channel_id=1, source_target_pairs={{0,1},{1,0},{2,3},{3,2},{4,5},{5,4},{6,7},{7,6},{8,9},{9,8},{10,11... | collective-permute-start | bytes 1966088 | tf_op jit(solution)/shard_map/ppermute | solution.py:78
  224.6 19.2 %collective-permute-start.34 = (bf16[128,2560]{1,0:T(8,128)(2,1)}, bf16[128,2560]{1,0:T(8,128)(2,1)}, u32[]{:S(2)}, u32[]{:S(2)}) collective-permute-start(bf16[128,2560]{1,0:T(8,128)(2,1)} %collective-permute-done.21.refs_1_), channel_id=1, source_target_pairs={{0,24},{1,25},{2,26},{3,27},{4,28},{5,29},{6,30},{7,31},{8,16},{9,... | collective-permute-start | bytes 1966088 | tf_op jit(solution)/shard_map/ppermute | solution.py:78
  250.2 30.1 %collective-permute-start.51 = (bf16[640,1024]{1,0:T(8,128)(2,1)}, bf16[640,1024]{1,0:T(8,128)(2,1)}, u32[]{:S(2)}, u32[]{:S(2)}) collective-permute-start(bf16[640,1024]{1,0:T(8,128)(2,1)} %shard_map.198.refs_29_), channel_id=1, source_target_pairs={{0,1},{1,0},{2,3},{3,2},{4,5},{5,4},{6,7},{7,6},{8,9},{9,8},{10,11... | collective-permute-start | bytes 3932168 | tf_op jit(solution)/shard_map/ppermute | solution.py:78
  250.3 30.5 %collective-permute-start.32 = (bf16[256,2560]{1,0:T(8,128)(2,1)}, bf16[256,2560]{1,0:T(8,128)(2,1)}, u32[]{:S(2)}, u32[]{:S(2)}) collective-permute-start(bf16[256,2560]{1,0:T(8,128)(2,1)} %get-tuple-element.148), channel_id=1, source_target_pairs={{0,1},{1,0},{2,3},{3,2},{4,5},{5,4},{6,7},{7,6},{8,9},{9,8},{10,11... | collective-permute-start | bytes 3932168 | tf_op jit(solution)/shard_map/ppermute | solution.py:78
  250.8 21.0 %collective-permute-start.41 = (bf16[128,2560]{1,0:T(8,128)(2,1)}, bf16[128,2560]{1,0:T(8,128)(2,1)}, u32[]{:S(2)}, u32[]{:S(2)}) collective-permute-start(bf16[128,2560]{1,0:T(8,128)(2,1)} %collective-permute-done.31.refs_4_), channel_id=1, source_target_pairs={{0,1},{1,0},{2,3},{3,2},{4,5},{5,4},{6,7},{7,6},{8,9},{9,8},{10,11... | collective-permute-start | bytes 1966088 | tf_op jit(solution)/shard_map/ppermute | solution.py:78
  280.8 29.9 %collective-permute-start.37 = (bf16[128,2560]{1,0:T(8,128)(2,1)}, bf16[128,2560]{1,0:T(8,128)(2,1)}, u32[]{:S(2)}, u32[]{:S(2)}) collective-permute-start(bf16[128,2560]{1,0:T(8,128)(2,1)} %maximum_select_fusion.7), channel_id=1, source_target_pairs={{0,2},{1,3},{2,0},{3,1},{4,6},{5,7},{6,4},{7,5},{8,10},{9,11},{10,... | collective-permute-start | bytes 1966088 | tf_op jit(solution)/shard_map/ppermute | solution.py:78
  285.5 193.2 %collective-permute-start.64 = (bf16[640,256]{1,0:T(8,128)(2,1)}, bf16[640,256]{1,0:T(8,128)(2,1)}, u32[]{:S(2)}, u32[]{:S(2)}) collective-permute-start(bf16[640,256]{1,0:T(8,128)(2,1)} %get-tuple-element.251), channel_id=1, source_target_pairs={{0,4},{1,5},{2,6},{3,7},{4,0},{5,1},{6,2},{7,3},{8,12},{9,13},{10,... | collective-permute-start | bytes 983048 | tf_op jit(solution)/shard_map/ppermute | solution.py:78
  322.1 19.0 %collective-permute-start.52 = (f32[4,1280]{1,0:T(4,128)S(1)}, f32[4,1280]{1,0:T(4,128)S(1)}, u32[]{:S(2)}, u32[]{:S(2)}) collective-permute-start(f32[4,1280]{1,0:T(4,128)S(1)} %get-tuple-element.170), channel_id=1, source_target_pairs={{0,4},{1,5},{2,6},{3,7},{4,0},{5,1},{6,2},{7,3},{8,12},{9,13},{10,... | collective-permute-start | bytes 61448 | tf_op jit(solution)/shard_map/ppermute | solution.py:78
  335.3 101.6 %collective-permute-start.86 = (bf16[2,320,256]{2,1,0:T(8,128)(2,1)}, bf16[2,320,256]{2,1,0:T(8,128)(2,1)}, u32[]{:S(2)}, u32[]{:S(2)}) collective-permute-start(bf16[2,320,256]{2,1,0:T(8,128)(2,1)} %get-tuple-element.191), channel_id=1, source_target_pairs={{0,1},{1,0},{2,3},{3,2},{4,5},{5,4},{6,7},{7,6},{8,9},{9,8},{10,11... | collective-permute-start | bytes 983048 | tf_op jit(solution)/shard_map/ppermute | solution.py:78
  380.5 50.2 %collective-permute-start.80 = (bf16[2,4,80,512]{3,2,1,0:T(8,128)(2,1)S(1)}, bf16[2,4,80,512]{3,2,1,0:T(8,128)(2,1)}, u32[]{:S(2)}, u32[]{:S(2)}) collective-permute-start(bf16[2,4,80,512]{3,2,1,0:T(8,128)(2,1)S(1)} %fusion.43), channel_id=1, source_target_pairs={{0,1},{1,0},{2,3},{3,2},{4,5},{5,4},{6,7},{7,6},{8,9},{9,8},{10,11... | collective-permute-start | bytes 1966088 | tf_op jit(solution)/shard_map/ppermute | solution.py:78
  388.2 43.9 %collective-permute-start.56 = (bf16[128,2560]{1,0:T(8,128)(2,1)S(1)}, bf16[128,2560]{1,0:T(8,128)(2,1)S(1)}, u32[]{:S(2)}, u32[]{:S(2)}) collective-permute-start(bf16[128,2560]{1,0:T(8,128)(2,1)S(1)} %fusion), channel_id=1, source_target_pairs={{0,2},{1,3},{2,0},{3,1},{4,6},{5,7},{6,4},{7,5},{8,10},{9,11},{10,... | collective-permute-start | bytes 1966088 | tf_op jit(solution)/shard_map/ppermute | solution.py:78
  449.8 29.0 %collective-permute-start.65 = (bf16[640,256]{1,0:T(8,128)(2,1)S(1)}, bf16[640,256]{1,0:T(8,128)(2,1)S(1)}, u32[]{:S(2)}, u32[]{:S(2)}) collective-permute-start(bf16[640,256]{1,0:T(8,128)(2,1)S(1)} %copy-done.71), channel_id=1, source_target_pairs={{0,4},{1,5},{2,6},{3,7},{4,0},{5,1},{6,2},{7,3},{8,12},{9,13},{10,... | collective-permute-start | bytes 983048 | tf_op jit(solution)/shard_map/ppermute | solution.py:78
  451.4 30.8 %collective-permute-start.98 = (bf16[320,1152]{1,0:T(8,128)(2,1)S(1)}, bf16[320,1152]{1,0:T(8,128)(2,1)S(1)}, u32[]{:S(2)}, u32[]{:S(2)}) collective-permute-start(bf16[320,1152]{1,0:T(8,128)(2,1)S(1)} %copy-done.79), channel_id=1, source_target_pairs={{0,8},{1,9},{2,10},{3,11},{4,12},{5,13},{6,14},{7,15},{8,0},{9,1},... | collective-permute-start | bytes 2211848 | tf_op jit(solution)/shard_map/ppermute | solution.py:78
  455.8 26.2 %collective-permute-start.67 = (bf16[256,1280]{1,0:T(8,128)(2,1)S(1)}, bf16[256,1280]{1,0:T(8,128)(2,1)S(1)}, u32[]{:S(2)}, u32[]{:S(2)}) collective-permute-start(bf16[256,1280]{1,0:T(8,128)(2,1)S(1)} %bitcast.134), channel_id=1, source_target_pairs={{0,4},{1,5},{2,6},{3,7},{4,0},{5,1},{6,2},{7,3},{8,12},{9,13},{10,... | collective-permute-start | bytes 1966088 | tf_op jit(solution)/shard_map/ppermute | solution.py:78
  482.2 23.8 %collective-permute-start.57 = (bf16[128,2560]{1,0:T(8,128)(2,1)}, bf16[128,2560]{1,0:T(8,128)(2,1)}, u32[]{:S(2)}, u32[]{:S(2)}) collective-permute-start(bf16[128,2560]{1,0:T(8,128)(2,1)} %slice.427), channel_id=1, source_target_pairs={{0,2},{1,3},{2,0},{3,1},{4,6},{5,7},{6,4},{7,5},{8,10},{9,11},{10,... | collective-permute-start | bytes 1966088 | tf_op jit(solution)/shard_map/ppermute | solution.py:78
  492.4 62.5 %collective-permute-start.96 = (bf16[320,2304]{1,0:T(8,128)(2,1)}, bf16[320,2304]{1,0:T(8,128)(2,1)}, u32[]{:S(2)}, u32[]{:S(2)}) collective-permute-start(bf16[320,2304]{1,0:T(8,128)(2,1)} %get-tuple-element.193), channel_id=1, source_target_pairs={{0,8},{1,9},{2,10},{3,11},{4,12},{5,13},{6,14},{7,15},{8,0},{9,1},... | collective-permute-start | bytes 4423688 | tf_op jit(solution)/shard_map/ppermute | solution.py:78
  494.9 58.1 %collective-permute-start.90 = (bf16[256,2560]{1,0:T(8,128)(2,1)}, bf16[256,2560]{1,0:T(8,128)(2,1)}, u32[]{:S(2)}, u32[]{:S(2)}) collective-permute-start(bf16[256,2560]{1,0:T(8,128)(2,1)} %pad_maximum_fusion.6.refs_4_), channel_id=1, source_target_pairs={{0,4},{1,5},{2,6},{3,7},{4,0},{5,1},{6,2},{7,3},{8,12},{9,13},{10,... | collective-permute-start | bytes 3932168 | tf_op jit(solution)/shard_map/ppermute | solution.py:78
  506.0 49.4 %collective-permute-start.71 = (bf16[160,1280]{1,0:T(8,128)(2,1)}, bf16[160,1280]{1,0:T(8,128)(2,1)}, u32[]{:S(2)}, u32[]{:S(2)}) collective-permute-start(bf16[160,1280]{1,0:T(8,128)(2,1)} %get-tuple-element.228), channel_id=1, source_target_pairs={{0,24},{1,25},{2,26},{3,27},{4,28},{5,29},{6,30},{7,31},{8,0},{9,1... | collective-permute-start | bytes 1228808 | tf_op jit(solution)/shard_map/ppermute | solution.py:78
  509.3 50.9 %collective-permute-start.70 = (bf16[160,1280]{1,0:T(8,128)(2,1)}, bf16[160,1280]{1,0:T(8,128)(2,1)}, u32[]{:S(2)}, u32[]{:S(2)}) collective-permute-start(bf16[160,1280]{1,0:T(8,128)(2,1)} %get-tuple-element.229), channel_id=1, source_target_pairs={{0,16},{1,17},{2,18},{3,19},{4,20},{5,21},{6,22},{7,23},{8,24},{9,... | collective-permute-start | bytes 1228808 | tf_op jit(solution)/shard_map/ppermute | solution.py:78
  509.9 50.3 %collective-permute-start.69 = (bf16[160,1280]{1,0:T(8,128)(2,1)}, bf16[160,1280]{1,0:T(8,128)(2,1)}, u32[]{:S(2)}, u32[]{:S(2)}) collective-permute-start(bf16[160,1280]{1,0:T(8,128)(2,1)} %get-tuple-element.227), channel_id=1, source_target_pairs={{0,8},{1,9},{2,10},{3,11},{4,12},{5,13},{6,14},{7,15},{8,16},{9,17... | collective-permute-start | bytes 1228808 | tf_op jit(solution)/shard_map/ppermute | solution.py:78
  554.9 35.8 %collective-permute-start.77 = (bf16[160,1280]{1,0:T(8,128)(2,1)S(1)}, bf16[160,1280]{1,0:T(8,128)(2,1)S(1)}, u32[]{:S(2)}, u32[]{:S(2)}) collective-permute-start(bf16[160,1280]{1,0:T(8,128)(2,1)S(1)} %get-tuple-element.226), channel_id=1, source_target_pairs={{0,16},{1,17},{2,18},{3,19},{4,20},{5,21},{6,22},{7,23},{8,24},{9,... | collective-permute-start | bytes 1228808 | tf_op jit(solution)/shard_map/ppermute | solution.py:78
  555.4 35.3 %collective-permute-start.76 = (bf16[160,1280]{1,0:T(8,128)(2,1)S(1)}, bf16[160,1280]{1,0:T(8,128)(2,1)S(1)}, u32[]{:S(2)}, u32[]{:S(2)}) collective-permute-start(bf16[160,1280]{1,0:T(8,128)(2,1)S(1)} %get-tuple-element.224), channel_id=1, source_target_pairs={{0,8},{1,9},{2,10},{3,11},{4,12},{5,13},{6,14},{7,15},{8,16},{9,17... | collective-permute-start | bytes 1228808 | tf_op jit(solution)/shard_map/ppermute | solution.py:78
  560.2 50.8 %collective-permute-start.89 = (bf16[256,2560]{1,0:T(8,128)(2,1)}, bf16[256,2560]{1,0:T(8,128)(2,1)}, u32[]{:S(2)}, u32[]{:S(2)}) collective-permute-start(bf16[256,2560]{1,0:T(8,128)(2,1)} %pad_maximum_fusion.6.refs_4_), channel_id=1, source_target_pairs={{0,1},{1,0},{2,3},{3,2},{4,5},{5,4},{6,7},{7,6},{8,9},{9,8},{10,11... | collective-permute-start | bytes 3932168 | tf_op jit(solution)/shard_map/ppermute | solution.py:78
  560.3 46.7 %collective-permute-start.87 = (bf16[320,256]{1,0:T(8,128)(2,1)S(1)}, bf16[320,256]{1,0:T(8,128)(2,1)S(1)}, u32[]{:S(2)}, u32[]{:S(2)}) collective-permute-start(bf16[320,256]{1,0:T(8,128)(2,1)S(1)} %copy-done.72), channel_id=1, source_target_pairs={{0,4},{1,5},{2,6},{3,7},{4,0},{5,1},{6,2},{7,3},{8,12},{9,13},{10,... | collective-permute-start | bytes 491528 | tf_op jit(solution)/shard_map/ppermute | solution.py:78
  564.8 46.2 %collective-permute-start.91 = (bf16[256,2560]{1,0:T(8,128)(2,1)}, bf16[256,2560]{1,0:T(8,128)(2,1)}, u32[]{:S(2)}, u32[]{:S(2)}) collective-permute-start(bf16[256,2560]{1,0:T(8,128)(2,1)} %collective-permute-done.90.refs_6_), channel_id=1, source_target_pairs={{0,1},{1,0},{2,3},{3,2},{4,5},{5,4},{6,7},{7,6},{8,9},{9,8},{10,11... | collective-permute-start | bytes 3932168 | tf_op jit(solution)/shard_map/ppermute | solution.py:78
  590.8 37.1 %collective-permute-start.97 = (bf16[320,2304]{1,0:T(8,128)(2,1)}, bf16[320,2304]{1,0:T(8,128)(2,1)}, u32[]{:S(2)}, u32[]{:S(2)}) collective-permute-start(bf16[320,2304]{1,0:T(8,128)(2,1)} %get-tuple-element.198), channel_id=1, source_target_pairs={{0,8},{1,9},{2,10},{3,11},{4,12},{5,13},{6,14},{7,15},{8,0},{9,1},... | collective-permute-start | bytes 4423688 | tf_op jit(solution)/shard_map/ppermute | solution.py:78
  619.6 35.3 %collective-permute-start.93 = (bf16[80,2560]{1,0:T(8,128)(2,1)S(1)}, bf16[80,2560]{1,0:T(8,128)(2,1)S(1)}, u32[]{:S(2)}, u32[]{:S(2)}) collective-permute-start(bf16[80,2560]{1,0:T(8,128)(2,1)S(1)} %get-tuple-element.223), channel_id=1, source_target_pairs={{0,16},{1,17},{2,18},{3,19},{4,20},{5,21},{6,22},{7,23},{8,24},{9,... | collective-permute-start | bytes 1228808 | tf_op jit(solution)/shard_map/ppermute | solution.py:78
  622.1 32.8 %collective-permute-start.92 = (bf16[80,2560]{1,0:T(8,128)(2,1)S(1)}, bf16[80,2560]{1,0:T(8,128)(2,1)S(1)}, u32[]{:S(2)}, u32[]{:S(2)}) collective-permute-start(bf16[80,2560]{1,0:T(8,128)(2,1)S(1)} %get-tuple-element.221), channel_id=1, source_target_pairs={{0,8},{1,9},{2,10},{3,11},{4,12},{5,13},{6,14},{7,15},{8,16},{9,17... | collective-permute-start | bytes 1228808 | tf_op jit(solution)/shard_map/ppermute | solution.py:78
  656.1 27.9 %collective-permute-start.95 = (bf16[80,2560]{1,0:T(8,128)(2,1)S(1)}, bf16[80,2560]{1,0:T(8,128)(2,1)S(1)}, u32[]{:S(2)}, u32[]{:S(2)}) collective-permute-start(bf16[80,2560]{1,0:T(8,128)(2,1)S(1)} %fusion.36), channel_id=1, source_target_pairs={{0,0},{1,1},{2,16},{3,17},{4,8},{5,9},{6,24},{7,25},{8,2},{9,3},{1... | collective-permute-start | bytes 1228808 | tf_op jit(solution)/shard_map/ppermute | solution.py:78
  (132 other events, 1512.5 us)

commit v5 on v4

--- a/solution.py
+++ b/solution.py
@@ -18,7 +18,10 @@
 GELU_A = 0.044715
 VMEM_MAX = 60 * 1024 * 1024
 ANY = pl.BlockSpec(memory_space=pl.ANY)
-SMALL = pl.CostEstimate(flops=1, bytes_accessed=1, transcendentals=0)
+
+
+def work(us):
+    return pl.CostEstimate(flops=us, bytes_accessed=us, transcendentals=0)
 
 
 def norm_scale(values):
@@ -266,7 +269,7 @@
         out_specs=[spec(o.shape, False) for o in outs],
         out_shape=outs,
         compiler_params=pltpu.CompilerParams(vmem_limit_bytes=48 * 1024 * 1024),
-        cost_estimate=SMALL,
+        cost_estimate=work(7),
     )(*values)
 
 
@@ -300,7 +303,7 @@
         out_shape=jax.ShapeDtypeStruct((total, ff), F32),
         scratch_shapes=[pltpu.VMEM((total, width), BF16), pltpu.SemaphoreType.DMA((count,))],
         compiler_params=pltpu.CompilerParams(vmem_limit_bytes=VMEM_MAX),
-        cost_estimate=SMALL,
+        cost_estimate=work(5 + total // 64),
     )(*parts, w_down)
 
 
@@ -392,7 +395,7 @@
             pltpu.SemaphoreType.DMA((2, 3)),
         ],
         compiler_params=pltpu.CompilerParams(vmem_limit_bytes=VMEM_MAX),
-        cost_estimate=SMALL,
+        cost_estimate=work(23),
     )(*n2_parts, grad_hidden, w_gate, w_up)
 
 
@@ -423,11 +426,11 @@
         out_specs=[tall(rows), tall(rows), tall(total // 2), tall(total // 2)],
         out_shape=[shape(rows, F32), shape(rows, BF16), shape(total // 2, F32), shape(total // 2, BF16)],
         compiler_params=pltpu.CompilerParams(vmem_limit_bytes=VMEM_MAX),
-        cost_estimate=SMALL,
+        cost_estimate=work(19),
     )(hidden, grad_gate, grad_up, w_gate, w_up, w_down)
 
 
-def rows_of_tokens(parts, place, rows_out, each):
+def rows_of_tokens(place, parts, rows_out, each):
     tokens, width = parts[0].shape
     half = width // 2
     count = len(parts)
@@ -437,7 +440,7 @@
         for k in range(count):
             turned[...] = refs[k][...].T
             for i in range(rows_out // each):
-                at = pl.multiple_of((2 * i + place_ref[1]) * each, 16)
+                at = pl.multiple_of((2 * i + place_ref[2]) * each, 16)
                 out_ref[i * each : (i + 1) * each, k * tokens : (k + 1) * tokens] = turned[pl.ds(at, each), :]
 
     return pl.pallas_call(
@@ -445,18 +448,18 @@
         grid_spec=pltpu.PrefetchScalarGridSpec(
             num_scalar_prefetch=1,
             grid=(1,),
-            in_specs=[pl.BlockSpec((tokens, half), lambda i, place: (0, place[0]))] * count,
+            in_specs=[pl.BlockSpec((tokens, half), lambda i, place: (0, place[1]))] * count,
             out_specs=pl.BlockSpec((rows_out, count * tokens), lambda i, place: (0, 0)),
             scratch_shapes=[pltpu.VMEM((half, tokens), BF16)],
         ),
         out_shape=jax.ShapeDtypeStruct((rows_out, count * tokens), BF16),
         compiler_params=pltpu.CompilerParams(vmem_limit_bytes=VMEM_MAX),
-        cost_estimate=SMALL,
+        cost_estimate=work(5),
     )(place, *parts)
 
 
-def mlp_weight_grads(place, n2_parts, given, cot_parts, acts, n2_rows, cot_rows, weights, at, size, each):
-    groups, ready = (len(n2_parts), len(given))
+def mlp_weight_grads(place, n2_parts, first_hidden, cot_parts, acts, n2_rows, cot_rows, weights, at, size, each):
+    groups = len(n2_parts)
     per = len(n2_parts[0])
     tokens, width = n2_parts[0][0].shape
     group = per * tokens
@@ -464,52 +467,60 @@
     rows = n2_rows[0].shape[0]
     flat_n = [p for g in n2_parts for p in g]
     flat_c = [p for g in cot_parts for p in g]
-    lead = [len(flat_n), len(flat_c), ready]
+    total, total_c = (len(flat_n), len(flat_c))
 
     def body(place_ref, *refs):
-        n_refs, refs = (refs[: lead[0]], refs[lead[0] :])
-        c_refs, refs = (refs[: lead[1]], refs[lead[1] :])
-        h_refs, refs = (refs[: lead[2]], refs[lead[2] :])
-        wg_ref, wu_ref, wd_ref, hid_ref, gg_ref, gu_ref, nm, no, cm, co = refs[:10]
-        own_ref, rest_ref, n2_s, cot_s, gh_s, acc, sem = refs[10:]
+        n_refs, c_refs, refs = (refs[:total], refs[total : total + total_c], refs[total + total_c :])
+        gh_ref, wg_ref, wu_ref, wd_ref, hid_ref, gg_ref, gu_ref, nm, no, cm, co = refs[:11]
+        own_ref, rest_ref, n2_s, cot_s, acc, sem = refs[11:]
 
         def load(g, slot):
             found = []
             for i in range(per):
                 to = pl.ds(i * tokens, tokens)
                 found.append(pltpu.make_async_copy(n_refs[g * per + i], n2_s.at[slot, to], sem.at[slot, i]))
-                if g >= ready:
+                if g > 0:
                     found.append(pltpu.make_async_copy(
-                        c_refs[(g - ready) * per + i], cot_s.at[slot, to], sem.at[slot, per + i]))
-            if g < ready:
-                found.append(pltpu.make_async_copy(
-                    h_refs[g].at[:, pl.ds(at, size)], gh_s, sem.at[slot, per]))
+                        c_refs[(g - 1) * per + i], cot_s.at[slot, to], sem.at[slot, per + i]))
             return found
 
-        for copy in load(0, 0):
+        for copy in load(0, 0) + load(1, 1):
             copy.start()
 
         def add(g, act, fresh):
-            span = slice(g * both, (g + 1) * both)
+            start = g * both if isinstance(g, int) else pl.multiple_of(g * both, both)
             for i, (mine, other) in enumerate(((cm, co), (nm, no), (nm, no))):
-                part = dot(mine[:, span], act[i][:both]) + dot(other[:, span], act[i][both:])
+                part = dot(mine[:, pl.ds(start, both)], act[i][:both]) + dot(
+                    other[:, pl.ds(start, both)], act[i][both:])
                 if fresh:
                     acc[i] = part
                 else:
                     acc[i] += part
 
-        add(0, (hid_ref, gg_ref, gu_ref), True)
-        for g in range(groups):
-            slot = g % 2
-            if g + 1 < groups:
-                for copy in load(g + 1, 1 - slot):
-                    copy.start()
-            for copy in load(g, slot):
-                copy.wait()
+        def recompute(g, slot, gh):
             gelu, slope = gelu_pair(dot(n2_s[slot], wg_ref[...]))
             up = dot(n2_s[slot], wu_ref[...])
-            gh = gh_s[...] if g < ready else dot(cot_s[slot], wd_ref[...])
             add(g + 1, ((gelu * up).astype(BF16), (gh * up * slope).astype(BF16), (gh * gelu).astype(BF16)), False)
+
+        add(0, (hid_ref, gg_ref, gu_ref), True)
+        for copy in load(0, 0):
+            copy.wait()
+        recompute(0, 0, gh_ref[...])
+
+        def step(g, carry):
+            slot = lax.rem(g, 2)
+            for k in range(2, groups):
+                @pl.when(g + 1 == k)
+                def _():
+                    for copy in load(k, k % 2):
+                        copy.start()
+
+            for copy in load(1, slot):
+                copy.wait()
+            recompute(g, slot, dot(cot_s[slot], wd_ref[...]))
+            return carry
+
+        lax.fori_loop(1, groups, step, 0)
         for j in range(rows // each):
             start = pl.multiple_of((place_ref[0] ^ j) * each, 8)
             for i in range(3):
@@ -527,13 +538,13 @@
         grid_spec=pltpu.PrefetchScalarGridSpec(
             num_scalar_prefetch=1,
             grid=(1,),
-            in_specs=[ANY] * sum(lead) + [column(width)] * 3 + [column(group)] * 3 + [whole] * 4,
+            in_specs=[ANY] * (total + total_c) + [column(group)] + [column(width)] * 3 + [column(group)] * 3
+            + [whole] * 4,
             out_specs=[pl.BlockSpec((each, 3 * size), lambda j, place: (0, 0)),
                        pl.BlockSpec((rows - each, 3 * size), lambda j, place: (0, 0))],
             scratch_shapes=[
                 pltpu.VMEM((2, group, width), BF16),
                 pltpu.VMEM((2, group, width), BF16),
-                pltpu.VMEM((group, size), F32),
                 pltpu.VMEM((3, rows, size), F32),
                 pltpu.SemaphoreType.DMA((2, 2 * per)),
             ],
@@ -541,16 +552,19 @@
         out_shape=[jax.ShapeDtypeStruct((each, 3 * size), F32),
                    jax.ShapeDtypeStruct((rows - each, 3 * size), BF16)],
         compiler_params=pltpu.CompilerParams(vmem_limit_bytes=VMEM_MAX),
-        cost_estimate=SMALL,
-    )(place, *flat_n, *flat_c, *given, *weights, *acts, *n2_rows, *cot_rows)
+        cost_estimate=work(35 * size // 768),
+    )(place, *flat_n, *flat_c, first_hidden, *weights, *acts, *n2_rows, *cot_rows)
 
 
 def rows_by_device(place, parts, starts, block):
-    count = len(parts)
-    tokens, n = parts[0].shape
+    columns, count = (len(parts), len(parts[0]))
+    tokens, n = parts[0][0].shape
     rows = len(starts(0, 0)) * block
+    flat = [block_of for column in parts for block_of in column]
     if block % 16:
-        turned = jnp.concatenate(parts, axis=0).T
+        turned = [jnp.concatenate(column, axis=0).T for column in parts]
+        turned = turned[0] if columns == 1 else jnp.where(
+            place[2] == 0, jnp.concatenate(turned), jnp.concatenate(turned[::-1]))
 
         def taken(dc):
             return jnp.stack([
@@ -559,31 +573,80 @@
                     for start in starts(place[0] ^ dy, place[1] ^ dc)])
                 for dy in range(2)])
 
-        return taken(0), taken(1)
+        kept, sent = (taken(0), taken(1))
+        return kept[0], kept[1], sent[0], sent[1]
 
     def body(place_ref, *refs):
-        keep_ref, send_ref, turned = refs[count:]
-        for k in range(count):
-            turned[:, k * tokens : (k + 1) * tokens] = refs[k][...].T
-        for dy in range(2):
-            for dc, ref in ((0, keep_ref), (1, send_ref)):
-                for i, start in enumerate(starts(place_ref[0] ^ dy, place_ref[1] ^ dc)):
-                    ref[dy, i * block : (i + 1) * block, :] = turned[pl.ds(pl.multiple_of(start, 16), block), :]
-
-    shape = (2, rows, count * tokens)
+        keep_ref, keep_y_ref, send_ref, send_y_ref, turned = refs[len(flat):]
+        for h in range(columns):
+            base = 0 if columns == 1 else pl.multiple_of((place_ref[2] ^ h) * n, 16)
+            for k in range(count):
+                turned[pl.ds(base, n), k * tokens : (k + 1) * tokens] = refs[h * count + k][...].T
+        for dy, dc, ref in ((0, 0, keep_ref), (1, 0, keep_y_ref), (0, 1, send_ref), (1, 1, send_y_ref)):
+            for i, start in enumerate(starts(place_ref[0] ^ dy, place_ref[1] ^ dc)):
+                ref[i * block : (i + 1) * block, :] = turned[pl.ds(pl.multiple_of(start, 16), block), :]
+
+    shape = (rows, count * tokens)
     return pl.pallas_call(
         body,
         grid_spec=pltpu.PrefetchScalarGridSpec(
             num_scalar_prefetch=1,
             grid=(1,),
-            in_specs=[pl.BlockSpec((tokens, n), lambda i, place: (0, 0))] * count,
-            out_specs=[pl.BlockSpec(shape, lambda i, place: (0, 0, 0))] * 2,
-            scratch_shapes=[pltpu.VMEM((n, count * tokens), BF16)],
+            in_specs=[pl.BlockSpec((tokens, n), lambda i, place: (0, 0))] * len(flat),
+            out_specs=[pl.BlockSpec(shape, lambda i, place: (0, 0))] * 4,
+            scratch_shapes=[pltpu.VMEM((columns * n, count * tokens), BF16)],
         ),
-        out_shape=[jax.ShapeDtypeStruct(shape, BF16)] * 2,
+        out_shape=[jax.ShapeDtypeStruct(shape, BF16)] * 4,
         compiler_params=pltpu.CompilerParams(vmem_limit_bytes=VMEM_MAX),
-        cost_estimate=SMALL,
-    )(place, *parts)
+        cost_estimate=work(3),
+    )(place, *flat)
+
+
+def joined_columns(pairs):
+    rows = pairs[0][0].shape[0]
+    widths = [a.shape[1] // 3 for a, _ in pairs]
+    total = sum(widths)
+    step = rows // 4 if rows % 64 == 0 else rows
+    flat = [term for pair in pairs for term in pair]
+
+    def body(*refs):
+        for i in range(3):
+            at = 0
+            for k, n in enumerate(widths):
+                span = slice(i * n, (i + 1) * n)
+                refs[len(flat) + i][:, at : at + n] = refs[2 * k][:, span].astype(F32) + refs[
+                    2 * k + 1][:, span].astype(F32)
+                at += n
+
+    return pl.pallas_call(
+        body,
+        grid=(rows // step,),
+        in_specs=[pl.BlockSpec((step, term.shape[1]), lambda j: (j, 0)) for term in flat],
+        out_specs=[pl.BlockSpec((step, total), lambda j: (j, 0))] * 3,
+        out_shape=[jax.ShapeDtypeStruct((rows, total), F32)] * 3,
+        compiler_params=pltpu.CompilerParams(vmem_limit_bytes=VMEM_MAX),
+        cost_estimate=work(5),
+    )(*flat)
+
+
+def gate_weight_grad(conv, grad_in, grad_decay):
+    tokens, n = conv.shape
+
+    def body(conv_ref, in_ref, decay_ref, out_ref):
+        turned = conv_ref[...].T
+        out_ref[:, :BLK] = dot(turned, in_ref[...])
+        out_ref[:, BLK:] = dot(turned, decay_ref[...])
+
+    spec = pl.BlockSpec((tokens, BLK), lambda h: (0, h))
+    return pl.pallas_call(
+        body,
+        grid=(n // BLK,),
+        in_specs=[spec] * 3,
+        out_specs=pl.BlockSpec((BLK, 2 * BLK), lambda h: (h, 0)),
+        out_shape=jax.ShapeDtypeStruct((n, 2 * BLK), F32),
+        compiler_params=pltpu.CompilerParams(vmem_limit_bytes=VMEM_MAX),
+        cost_estimate=work(3),
+    )(conv, grad_in, grad_decay)
 
 
 def sum_of_dots(rows, values):
@@ -599,7 +662,7 @@
         body,
         out_shape=jax.ShapeDtypeStruct((rows[0].shape[0], values[0].shape[1]), BF16),
         compiler_params=pltpu.CompilerParams(vmem_limit_bytes=VMEM_MAX),
-        cost_estimate=SMALL,
+        cost_estimate=work(5),
     )(*rows, *values)
 
 
@@ -607,35 +670,41 @@
     return lax.optimization_barrier((value, others))[0]
 
 
-def entering(lay, summary, groups, backward):
+class Live:
+    def cut(self):
+        names = sorted(vars(self))
+        for name, value in zip(names, lax.optimization_barrier([getattr(self, n) for n in names])):
+            setattr(self, name, value)
+
+    def hold(self, **values):
+        for name, value in values.items():
+            setattr(self, name, value)
+        self.cut()
+
+
+def seq_bits(lay):
+    found, bit = ([], 1)
+    while bit < lay.seq:
+        found.append(bit)
+        bit *= 2
+    return found
+
+
+def scan_start(summary, groups):
     prod, state = (summary[:groups], summary[groups : 2 * groups])
-    before_p, before_s = (jnp.ones_like(prod), jnp.zeros_like(state))
-    mine = lax.axis_index("seq")
-    bit = 1
-    while bit < lay.seq:
-        other = lay.over_seq_bit(jnp.concatenate([prod, state], axis=0), bit)
-        other_p, other_s = (other[:groups], other[groups:])
-        is_later = (mine & bit) != 0
-        take = jnp.logical_not(is_later) if backward else is_later
-        before_s = jnp.where(take, before_p * other_s + before_s, before_s)
-        before_p = jnp.where(take, before_p * other_p, before_p)
-        state = jnp.where(take, prod * other_s + state, other_p * state + other_s)
-        prod = prod * other_p
-        bit *= 2
-    return before_s
-
-
-def owner_sum(lay, blocks, tie=None):
-    nz, z = (lay.nz, lay.z)
-
-    def pick(t):
-        return lax.dynamic_index_in_dim(blocks, t, 0, keepdims=False)
-
-    total = pick(z).astype(F32)
-    for step in range(1, nz):
-        come = lay.send(pick((z + step) % nz), lambda z, y, x, c: ((z + step) % nz, y, x, c))
-        total = total + come.astype(F32)
-    return total
+    return (prod, state, jnp.ones_like(prod), jnp.zeros_like(state))
+
+
+def scan_join(lay, held, other, bit, backward):
+    prod, state, before_p, before_s = held
+    groups = prod.shape[0]
+    other_p, other_s = (other[:groups], other[groups:])
+    is_later = (lay.seq_at & bit) != 0
+    take = jnp.logical_not(is_later) if backward else is_later
+    before_s = jnp.where(take, before_p * other_s + before_s, before_s)
+    before_p = jnp.where(take, before_p * other_p, before_p)
+    state = jnp.where(take, prod * other_s + state, other_p * state + other_s)
+    return (prod * other_p, state, before_p, before_s)
 
 
 def local(inputs, block_flags, decay_seed, vectors, in_y, in_x, gate_weight, out_proj,
@@ -643,228 +712,273 @@
     lay = Lay()
     nz, x, y, z, c = (lay.nz, lay.x, lay.y, lay.z, lay.c)
     tokens, width = inputs.shape[1:]
-    half = width // 2
-    quarter = width // 4
-    first = c == 0
+    half, quarter, two = (width // 2, width // 4, 2 * tokens)
+    each = width // lay.seq
+    own80 = each // 4
+    bits = seq_bits(lay)
+    place = jnp.stack([z % (nz // 2), lay.seq_at // nz, y]).astype(jnp.int32)
+    at_yc = jnp.stack([y, c, x]).astype(jnp.int32)
+    live = Live()
 
     def order_c(own, other, axis):
-        return jnp.where(first, jnp.concatenate([own, other], axis),
+        return jnp.where(c == 0, jnp.concatenate([own, other], axis),
                          jnp.concatenate([other, own], axis))
 
     def order_f(rel):
         b = rel.shape[-1] // 4
         p = [rel[..., i * b : (i + 1) * b] for i in range(4)]
-        by_c = jnp.where(first, rel, jnp.concatenate([p[1], p[0], p[3], p[2]], -1))
+        by_c = jnp.where(c == 0, rel, jnp.concatenate([p[1], p[0], p[3], p[2]], -1))
         return jnp.where(x == 0, by_c, jnp.concatenate([by_c[..., 2 * b :], by_c[..., : 2 * b]], -1))
 
+    def owner_parts(blocks):
+        pick = lambda t: lax.dynamic_index_in_dim(blocks, t, 0, keepdims=False)
+        come = [
+            lay.send(pick((z + step) % nz), lambda z, y, x, c: ((z + step) % nz, y, x, c))
+            for step in range(1, nz)
+        ]
+        return pick(z), come
+
+    def total_of(own, come):
+        total = own.astype(F32)
+        for part in come:
+            total = total + part.astype(F32)
+        return total.astype(BF16)
+
+    def half_of(value, which, n, axis):
+        return lax.dynamic_slice_in_dim(value, which * n, n, axis)
+
     cot = cotangent[0]
-    cot_y, cot_z = (lay.over_y(cot), lay.over_z(cot))
+    cut = tokens // 2
+    gate_away, inputs, gate_weight, out_proj, vectors, decay_seed, block_flags = lax.optimization_barrier(
+        (half_of(gate_weight, 1 - x, half, 0), inputs, gate_weight, out_proj, vectors, decay_seed, block_flags))
     halo_raw = lay.over_seq(inputs[0, tokens - 16 :], 1)
-    rows_theirs = lax.dynamic_slice_in_dim(gate_weight, (1 - x) * half, half, 0)
-    gate_x = lay.over_x(rows_theirs)
-    residual = after(inputs[0], rows_theirs).astype(F32)
-    scaled_one, inverse_one = norm_scale(residual)
-    normed_own = (scaled_one * vectors[0]).astype(BF16)
-    normed_x = lay.over_x(normed_own)
-    halo_own = (norm_scale(after(halo_raw, normed_own).astype(F32))[0] * vectors[0]).astype(BF16)
-    flag_row = jnp.pad(block_flags.astype(BF16), ((0, 0), (0, width - block_flags.shape[1])))
+    gate_x = lay.over_x(gate_away)
+    wx_c, wy_c = (lay.over_c(in_x), lay.over_c(in_y))
+    scaled_one, inverse_one = norm_scale(inputs[0].astype(F32))
+    live.hold(n1=(scaled_one * vectors[0]).astype(BF16), inv1=inverse_one, halo_raw=halo_raw,
+              params=(gate_weight, out_proj, vectors, decay_seed, block_flags))
+
+    gate_weight, out_proj, vectors, decay_seed, block_flags = live.params
+    n1_x = lay.over_x(live.n1)
+    halo_own = (norm_scale(live.halo_raw.astype(F32))[0] * vectors[0]).astype(BF16)
+    n_flags = block_flags.shape[1]
+    flag_row = jnp.pad(block_flags.astype(BF16), ((0, 0), (0, width - n_flags)))
     halo_x = lay.over_x(jnp.concatenate([flag_row, halo_own[1:]], axis=0))
-    n_flags = block_flags.shape[1]
-    flags = jnp.concatenate(
-        [block_flags.astype(F32), halo_x[:1, :n_flags].astype(F32)], axis=0)
-
-    wy, wx = (in_y, in_x)
-    wy_c, wx_c = (lay.over_c(in_y), lay.over_c(in_x))
-    out_later = after(out_proj, halo_own)
-    out_theirs = lax.dynamic_slice_in_dim(out_later, (1 - x) * half, half, 0)
-    out_x = lay.over_x(out_theirs)
-    out_mine = lax.dynamic_slice_in_dim(out_later, x * half, half, 0)
-    rows_mine = lax.dynamic_slice_in_dim(after(gate_weight, out_theirs), x * half, half, 0)
-    gate_c, gate_xc = (lay.over_c(rows_mine), lay.over_c(gate_x))
-    gates = order_f(jnp.concatenate([rows_mine, gate_c, gate_x, gate_xc], axis=1))
-    out_c, out_xc = (lay.over_c(out_mine), lay.over_c(out_x))
-    out_rel = jnp.concatenate([out_mine, out_c, out_x, out_xc], axis=1)
-    cot_x = lay.over_x(after(cot, out_theirs))
-
-    normed = jnp.concatenate([normed_own, normed_x, halo_own, halo_x], axis=0)
-    two = 2 * tokens
-    x_all = order_c(dot(normed, wx).astype(BF16), dot(normed, wx_c).astype(BF16), 1)
+    gate_own = half_of(gate_weight, x, half, 0)
+    gate_c = lay.over_c(gate_own)
+    cot_z = lay.over_z(after(cot, live.n1))
+    cot_y = lay.over_y(after(cot, live.n1))
+    base = -5.0 - decay_seed.astype(F32) + vectors[9]
+    del live.params, live.halo_raw
+    live.hold(
+        n1_x=n1_x, halo_x=halo_x, halo_own=halo_own, gate_x=gate_x, gate_c=gate_c, wx_c=wx_c, cot_y=cot_y,
+        flags=jnp.concatenate([block_flags.astype(F32), halo_x[:1, :n_flags].astype(F32)], axis=0),
+        gate_own=gate_own, out_away=half_of(out_proj, 2 * (1 - x) + y, quarter, 0),
+        out_mine=half_of(out_proj, x, half, 0), vec=half_of(vectors, x, half, 1), gain_two=vectors[1],
+        gain_one=vectors[0],
+        rates=half_of(jnp.stack([jax.nn.softplus(base), jax.nn.sigmoid(base)]), x, half, 1))
+
+    out_a = lay.over_x(live.out_away)
+    gates = order_f(jnp.concatenate(
+        [live.gate_own, live.gate_c, live.gate_x, lay.over_c(live.gate_x)], axis=1))
+    normed = jnp.concatenate([live.n1, live.n1_x, live.halo_own, live.halo_x], axis=0)
+    x_all = order_c(dot(normed, in_x).astype(BF16), dot(normed, live.wx_c).astype(BF16), 1)
     x_low = x_all[:two].reshape(2, tokens, half)
     halo = x_all[two:].reshape(2, 16, half)
-    vec_half = lax.dynamic_slice_in_dim(vectors, x * half, half, 1)
-    base = -5.0 - decay_seed.astype(F32) + vectors[9]
-    rates = lax.dynamic_slice_in_dim(
-        jnp.stack([jax.nn.softplus(base), jax.nn.sigmoid(base)]), x * half, half, 1)
     shape3 = lambda dt: jax.ShapeDtypeStruct((2, tokens, half), dt)
     summary_shape = jax.ShapeDtypeStruct((4, half), F32)
     conv_low, ig, dg, prods, local_state, summary = by_head(
-        mixer_forward, flags,
-        [(after(x_low, cot_y), False), (halo, False), (gates, True), (vec_half, False), (rates, False)],
+        mixer_forward, live.flags,
+        [(x_low, False), (halo, False), (gates, True), (live.vec, False), (live.rates, False)],
         [shape3(BF16), shape3(F32), shape3(F32), shape3(F32), shape3(F32), summary_shape])
-    state_in = entering(lay, summary, 2, False)
-    normed_two = after(normed[:two], summary)
-    y_pre = order_c(dot(normed_two, wy), dot(normed_two, wy_c), 1).reshape(2, tokens, half)
-    state_tied = after(state_in, cot_z)
-    cot_xy = lay.over_y(after(cot_x, state_in))
-    cot_xz = lay.over_z(after(cot_x, state_in))
-    cot_yz = lay.over_y(after(cot_z, state_in))
-    cot_xyz = lay.over_y(cot_xz)
-    cots = [[cot, cot_x], [cot_y, cot_xy], [cot_z, cot_xz], [cot_yz, cot_xyz]]
-    cots_c = [[lay.over_c(part) for part in group] for group in cots]
-    state = local_state + prods * state_tied[:, None, :]
-    mixed = (state * jax.nn.gelu(y_pre, approximate=True)).astype(BF16)
-    part_x_low = dot(mixed[1], out_rel).astype(BF16)
-    part_x = lay.over_x(part_x_low)
-    gh_main = grad_hidden_of(after(cots[0] + cots_c[0], part_x_low), mlp_down)
-    part_own = after(dot(after(mixed[0], part_x_low), out_rel), gh_main, cot_xy)
-    swapped = jnp.concatenate([part_x[:, half:], part_x[:, :half]], axis=1)
-    mid = residual + order_f(part_own + swapped.astype(F32))
-
+    out_c = lay.over_c(live.out_mine)
+    del live.gate_x, live.gate_own, live.gate_c, live.halo_own, live.halo_x
+    live.hold(x_low=x_low, halo=halo, gates=gates, conv_low=conv_low, ig=ig, dg=dg, prods=prods,
+              local_state=local_state, scan=scan_start(summary, 2), out_c=out_c, normed=normed[:two], wy_c=wy_c, out_a=out_a,
+              cot_z=cot_z)
+    del live.out_away
+
+    def n1_starts(at_y, at_c):
+        return [((2 * i + at_y) * 4 + 2 * j + at_c) * own80 for i in range(nz) for j in range(2)]
+
+    for bit in bits:
+        come = lay.over_seq_bit(jnp.concatenate(live.scan[:2], axis=0), bit)
+        live.scan = scan_join(lay, live.scan, come, bit, False)
+        if bit == 1:
+            live.cut()
+            out_b = lay.over_y(live.out_a)
+            cot_x = lay.over_x(after(cot, live.scan))
+    out_x = jnp.where(y == 0, jnp.concatenate([live.out_a, out_b], 0), jnp.concatenate([out_b, live.out_a], 0))
+    y_pre = order_c(dot(live.normed, in_y), dot(live.normed, live.wy_c), 1).reshape(2, tokens, half)
+    n1_own, n1_away, sent, sent_y = rows_by_device(at_yc, [[live.n1, live.n1_x]], n1_starts, own80)
+    state_in = live.scan[3]
+    del live.scan, live.out_a
+    live.hold(state_in=state_in, y_pre=y_pre, out_left=jnp.concatenate([live.out_mine, live.out_c], axis=1),
+              out_x=out_x, cot_x=cot_x, n1_own=n1_own, n1_away=n1_away, n1_c=lay.over_c(sent), n1_away_c=lay.over_c(sent_y))
+    del live.out_mine, live.out_c
+
+    n1_y = lay.over_y(live.n1_away)
+    state = live.local_state + live.prods * live.state_in[:, None, :]
+    mixed = (state * jax.nn.gelu(live.y_pre, approximate=True)).astype(BF16)
+    mixed_two = mixed.reshape(two, half)
+    out_right = jnp.concatenate([live.out_x, lay.over_c(live.out_x)], axis=1)
+    part = jnp.concatenate([dot(mixed_two, live.out_left), dot(mixed_two, out_right)], axis=1)
+    del live.out_x
+    live.hold(mixed=mixed, part_own=part[:tokens], part_x=part[tokens:].astype(BF16), out_right=out_right, n1_y=n1_y)
+
+    part_x = lay.over_x(live.part_x)
+    cot_xy = lay.over_y(live.cot_x)
+    gh_main = grad_hidden_of([cot, live.cot_x, lay.over_c(cot), lay.over_c(live.cot_x)], mlp_down)
+    live.hold(part_x=part_x, gh_main=gh_main, cot_xy=cot_xy)
+
+    swapped = jnp.concatenate([live.part_x[:, half:], live.part_x[:, :half]], axis=1)
+    mid = inputs[0].astype(F32) + order_f(live.part_own + swapped.astype(F32))
     scaled_two, inverse_two = norm_scale(mid)
-    n2 = (scaled_two * vectors[1]).astype(BF16)
-    n2_x = lay.over_x(n2)
-    n2_c, n2_xc = (lay.over_c(n2), lay.over_c(n2_x))
-    n2_z = lay.over_z(n2)
-    gh_y = grad_hidden_of(after(cots[1] + cots_c[1], n2), mlp_down)
-    place = jnp.stack([lay.seq_at // nz, y]).astype(jnp.int32)
-    each = width // lay.seq
-    cot_rows = rows_of_tokens(
-        after([p for group in cots for p in group], gh_y), place, half // 2, each)
-    n2_y = lay.over_y(after(n2, cot_xyz))
+    del live.part_x, live.part_own
+    live.hold(mid=mid, inv2=inverse_two, n2=(scaled_two * live.gain_two).astype(BF16))
+
+    n2_x = lay.over_x(live.n2)
+    n2_y = lay.over_y(live.n2)
+    n2_z_top = lay.over_z(live.n2[:cut])
+    n2_c = lay.over_c(live.n2)
+    pair = [live.cot_y, live.cot_xy]
+    gh_y = grad_hidden_of(pair + [lay.over_c(p) for p in pair], mlp_down)
+    live.hold(n2_x=n2_x, n2_c=n2_c, n2_y=n2_y, n2_z_top=n2_z_top, gh_y=gh_y)
+
+    live.hold(n2_xc=lay.over_c(live.n2_x))
+    cot_xz = lay.over_x(live.cot_z)
+    n2_xy = lay.over_y(live.n2_x)
+    n2_z_low = lay.over_z(live.n2[cut:])
     hidden, grad_gate, grad_up, far, far_c = mlp_forward(
-        after([n2, n2_x, n2_c, n2_xc], gh_y, cot_rows), gh_main, mlp_gate, mlp_up)
-    n2_xy = lay.over_x(after(n2_y, far))
-    n2_xz = lay.over_z(n2_x)
-    n2_yz = lay.over_y(n2_z)
-    n2_xyz = lay.over_y(n2_xz)
-    far_sum = (far + lay.over_c(far_c).astype(F32)).astype(BF16)
-    arriving = lay.over_x(far_sum)
-    near, near_c, out, out_c = mlp_rest(
-        after(hidden, far_sum, n2_y, n2_z), grad_gate, grad_up, mlp_gate, mlp_up, mlp_down, tokens)
-    near_sum = after(near + lay.over_c(near_c).astype(F32), n2_xz, n2_yz)
-    grad_n2 = near_sum + arriving.astype(F32)
-    out_sum = out + lay.over_c(out_c).astype(F32)
-    n2s = [[n2, n2_x], [n2_y, n2_xy], [n2_z, n2_xz], [n2_yz, n2_xyz]]
-    n2s_c = [[n2_c, n2_xc]] + [[lay.over_c(part) for part in group] for group in n2s[1:]]
-    acts = (hidden, grad_gate, grad_up)
-    low = (lay.z % (nz // 2)).astype(jnp.int32).reshape(1)
-    cot_row_pair = (cot_rows, lay.over_c(cot_rows))
-
-    def weight_piece(at, size, n2_row_pair, *ties):
-        own, rest = mlp_weight_grads(
-            low, [group + group_c for group, group_c in zip(n2s[1:], n2s_c[1:])], [gh_y],
-            [group + group_c for group, group_c in zip(cots[2:], cots_c[2:])],
-            after(acts, ties), n2_row_pair, cot_row_pair, (mlp_gate, mlp_up, mlp_down), at, size, each)
+        [live.n2, live.n2_x, live.n2_c, live.n2_xc], live.gh_main, mlp_gate, mlp_up)
+    del live.gh_main, live.n2_c
+    live.hold(acts=(hidden, grad_gate, grad_up), far=far, far_c=far_c, cot_xz=cot_xz, n2_xy=n2_xy,
+              n2_z_low=n2_z_low)
+    live.hold(far=(live.far + lay.over_c(live.far_c).astype(F32)).astype(BF16),
+              n2_z=jnp.concatenate([live.n2_z_top, live.n2_z_low], axis=0))
+
+    arriving = lay.over_x(live.far)
+    n2_yz = lay.over_y(live.n2_z)
+    n2_xz_top = lay.over_z(live.n2_x[:cut])
+    near, near_c, out, out_c = mlp_rest(*live.acts, mlp_gate, mlp_up, mlp_down, tokens)
+    del live.far, live.far_c, live.n2_z_top, live.n2_z_low
+    live.hold(arriving=arriving, near=near, near_c=near_c, out=out, out_c=lay.over_c(out_c), n2_yz=n2_yz, n2_xz_top=n2_xz_top)
+
+    grad_n2 = live.near + lay.over_c(live.near_c).astype(F32) + live.arriving.astype(F32)
+    grad_mid_norm, grad_gain_two = norm_back(grad_n2, live.mid * live.inv2, live.inv2, live.gain_two)
+    grad_mid = cot.astype(F32) + grad_mid_norm
+    branch = grad_mid.astype(BF16)
+    del live.near, live.near_c, live.arriving
+    live.hold(grad_gain_two=grad_gain_two, grad_mid=grad_mid, branch=branch, branch_rel=order_f(branch))
+
+    arriving = lay.over_x(live.branch_rel)
+    n2_xz_low = lay.over_z(live.n2_x[cut:])
+    cot_yz = lay.over_y(live.cot_z)
+    live.hold(arriving=arriving, n2_xz_low=n2_xz_low, cot_yz=cot_yz, out_sum=live.out + live.out_c.astype(F32),
+              n2_y_c=lay.over_c(live.n2_y),
+              n2_xy_c=lay.over_c(live.n2_xy))
+
+    n1_yc = lay.over_y(live.n1_away_c)
+    cot_z_c, cot_xz_c = (lay.over_c(live.cot_z), lay.over_c(live.cot_xz))
+    branch_x_rel = jnp.concatenate([live.arriving[:, half:], live.arriving[:, :half]], axis=1)
+    both_rel = jnp.concatenate([live.branch_rel, branch_x_rel], 0)
+    grad_mixed = dot_cols(both_rel[:, :half], live.out_left) + dot_cols(both_rel[:, half:], live.out_right)
+    gy, bprod, blocal, back_summary = by_head(
+        mixer_back_scan, live.flags,
+        [(grad_mixed.reshape(2, tokens, half), False), (live.y_pre, False), (live.dg, False),
+         (live.prods, False), (live.local_state, False), (live.state_in, False), (live.rates, False)],
+        [shape3(BF16), shape3(F32), shape3(F32), summary_shape])
+    del live.arriving, live.branch_rel, live.y_pre
+    live.hold(gy=gy.reshape(two, half), bprod=bprod, blocal=blocal, scan=scan_start(back_summary, 2),
+              branch_x_rel=branch_x_rel, n1_yc=n1_yc, cot_z_c=cot_z_c, cot_xz_c=cot_xz_c)
+
+    n2_xyz = lay.over_x(live.n2_yz)
+    own_cols = lambda value, which: half_of(value, which, quarter, 1)
+    part_y = dot_cols(own_cols(live.gy, c), in_y) + dot_cols(own_cols(live.gy, 1 - c), live.wy_c)
+    for bit in bits:
+        come = lay.over_seq_bit(jnp.concatenate(live.scan[:2], axis=0), bit)
+        live.scan = scan_join(lay, live.scan, come, bit, True)
+        if bit == 1:
+            live.cut()
+            cot_xyz = lay.over_y(live.cot_xz)
+            n2_z_c, n2_yz_c, cot_yz_c = (lay.over_c(live.n2_z), lay.over_c(live.n2_yz), lay.over_c(live.cot_yz))
+    back_in = live.scan[3]
+    del live.scan
+    live.hold(back_in=back_in, cot_xyz=cot_xyz, n2_xyz=n2_xyz, part_y=part_y, n2_z_c=n2_z_c, n2_yz_c=n2_yz_c,
+              cot_yz_c=cot_yz_c)
+
+    gip, gdp, gx_main, gx_tail, edge, vec_rows = by_head(
+        mixer_backward, live.flags,
+        [(live.bprod, False), (live.blocal, False), (live.back_in, False), (live.prods, False),
+         (live.local_state, False), (live.state_in, False), (live.ig, False), (live.dg, False),
+         (live.conv_low, False), (live.x_low, False), (live.halo, False), (live.gates, True),
+         (live.vec, False), (live.rates, False)],
+        [shape3(BF16), shape3(BF16), shape3(BF16), jax.ShapeDtypeStruct((2, 16, half), F32),
+         jax.ShapeDtypeStruct((2, 8, half), F32), jax.ShapeDtypeStruct((8, half), F32)])
+    for name in ("bprod", "blocal", "back_in", "prods", "local_state", "state_in", "ig", "dg", "x_low", "halo",
+                 "gates", "vec", "rates", "flags"):
+        delattr(live, name)
+    live.hold(gip=gip, gdp=gdp, gx_main=gx_main, gx_tail=gx_tail, edge=edge, vec_rows=vec_rows)
+
+    edge_next = lay.over_seq(live.edge, -1)
+    mixed_x = lay.over_x(jnp.concatenate([live.mixed[1], live.mixed[0]], axis=0))
+    n2_xz = jnp.concatenate([live.n2_xz_top, live.n2_xz_low], axis=0)
+    n2_xz_c, n2_xyz_c, cot_xyz_c = (lay.over_c(n2_xz), lay.over_c(live.n2_xyz), lay.over_c(live.cot_xyz))
+    live.n2s = [[live.n2, live.n2_x], [live.n2_y, live.n2_xy], [live.n2_z, n2_xz], [live.n2_yz, live.n2_xyz]]
+    live.cots = [cot, live.cot_x, live.cot_y, live.cot_xy, live.cot_z, live.cot_xz, live.cot_yz, live.cot_xyz]
+    n2_rows = rows_of_tokens(place, [p for group in live.n2s for p in group], half // 2, each)
+    cot_rows = rows_of_tokens(place, live.cots, half // 2, each)
+    del live.edge
+    live.hold(edge_next=edge_next, n2_rows=n2_rows, cot_rows=cot_rows,
+              n2s_c=[[live.n2_y_c, live.n2_xy_c], [live.n2_z_c, n2_xz_c], [live.n2_yz_c, n2_xyz_c]],
+              cots_c=[live.cot_z_c, live.cot_xz_c, live.cot_yz_c, cot_xyz_c], mixed_x=mixed_x)
+
+    gx_last = (live.gx_tail + jnp.pad(live.edge_next, ((0, 0), (8, 0), (0, 0)))).astype(BF16)
+    gx = jnp.concatenate([live.gx_main[:, : tokens - 16], gx_last], axis=1).reshape(two, half)
+    gx_o, gx_c = (own_cols(gx, c), own_cols(gx, 1 - c))
+    part_n1 = live.part_y + dot_cols(gx_o, in_x) + dot_cols(gx_c, live.wx_c)
+    del live.gx_main, live.gx_tail, live.edge_next, live.part_y
+    live.hold(gx=gx, n1_near=part_n1[:tokens], n1_far=part_n1[tokens:].astype(BF16),
+              n2_rows_c=lay.over_c(live.n2_rows), cot_rows_c=lay.over_c(live.cot_rows))
+
+    cuts = sections_of(mlp_gate.shape[1])
+    cuts = cuts[-1:] + cuts[:-1]
+
+    def weight_piece(at, size):
+        return mlp_weight_grads(
+            place, [a + b for a, b in zip(live.n2s[1:], live.n2s_c)], live.gh_y,
+            [live.cots[4:6] + live.cots_c[:2], live.cots[6:] + live.cots_c[2:]], live.acts,
+            (live.n2_rows, live.n2_rows_c), (live.cot_rows, live.cot_rows_c), (mlp_gate, mlp_up, mlp_down),
+            at, size, each)
+
+    def piece_sum(own, rest):
         blocks = [own] + [rest[j * each : (j + 1) * each] for j in range(nz // 2 - 1)]
         bit = nz // 4
         while bit >= 1:
             gone = blocks[bit] if bit == 1 else jnp.concatenate(
                 [b.astype(BF16) for b in blocks[bit : 2 * bit]], axis=0)
             come = lay.over_seq_bit(gone.astype(BF16), 2 * bit)
-            blocks = [blocks[j].astype(F32) + come[j * each : (j + 1) * each].astype(F32) for j in range(bit)]
+            blocks = [(blocks[j], come[j * each : (j + 1) * each]) for j in range(bit)]
+            if bit > 1:
+                blocks = [a.astype(F32) + b.astype(F32) for a, b in blocks]
             bit //= 2
-        return own, blocks[0]
-
-    grad_mid_norm, grad_gain_two = norm_back(grad_n2, scaled_two, inverse_two, vectors[1])
-    grad_mid = cot.astype(F32) + grad_mid_norm
-    branch = grad_mid.astype(BF16)
-    branch_rel = order_f(branch)
-    arriving = lay.over_x(branch_rel)
-    n2_rows = rows_of_tokens(
-        after([p for group in n2s for p in group], branch_rel), place, half // 2, each)
-    n2_row_pair = (n2_rows, lay.over_c(n2_rows))
-    cuts = sections_of(mlp_gate.shape[1])
-    cuts = cuts[-1:] + cuts[:-1]
-    first_own, first_piece = weight_piece(*cuts[0], n2_row_pair, branch_rel)
-    arriving = after(arriving, first_own)
-    branch_x_rel = jnp.concatenate([arriving[:, half:], arriving[:, :half]], axis=1)
-    branch_two = jnp.concatenate([branch, order_f(branch_x_rel)], 0)
-    grad_mixed = dot_cols(jnp.concatenate([branch_rel, branch_x_rel], 0), out_rel)
-    gy, bprod, blocal, back_summary = by_head(
-        mixer_back_scan, flags,
-        [(grad_mixed.reshape(2, tokens, half), False), (y_pre, False), (dg, False), (prods, False),
-         (local_state, False), (state_in, False), (rates, False)],
-        [shape3(BF16), shape3(F32), shape3(F32), summary_shape])
-    back_in = entering(lay, back_summary, 2, True)
-
-    own80 = each // 4
-    at_yc = jnp.stack([y, c]).astype(jnp.int32)
-
-    def spread(parts, starts):
-        keep, away = rows_by_device(at_yc, parts, starts, own80)
-        come = lay.over_c(away)
-        keep_y, come_y = (lay.over_y(keep[1]), lay.over_y(come[1]))
-        return [keep[0], come[0], keep_y, come_y]
-
-    def n1_starts(at_y, at_c):
-        return [((2 * i + at_y) * 4 + 2 * j + at_c) * own80 for i in range(nz) for j in range(2)]
-
-    def mixed_starts(at_y, at_c):
-        return [((at_y * nz + i) * 2 + at_c) * own80 for i in range(nz)]
-
-    def all_tokens(value, tie):
-        other_y = lay.over_y(after(value, tie))
-        return [value, lay.over_c(value), other_y, lay.over_c(other_y)]
-
-    n1_rows = spread([normed_own, normed_x], n1_starts)
-    mixed_rows = spread([after(mixed, back_summary)[i] for i in range(2)], mixed_starts)
-
-    gip, gdp, gx_main, gx_tail, edge, vec_rows = by_head(
-        mixer_backward, flags,
-        [(bprod, False), (blocal, False), (back_in, False), (prods, False), (local_state, False),
-         (state_in, False), (ig, False), (dg, False), (conv_low, False), (x_low, False),
-         (halo, False), (gates, True), (vec_half, False), (rates, False)],
-        [shape3(BF16), shape3(BF16), shape3(BF16), jax.ShapeDtypeStruct((2, 16, half), F32),
-         jax.ShapeDtypeStruct((2, 8, half), F32), jax.ShapeDtypeStruct((8, half), F32)])
-    edge_next = lay.over_seq(edge, -1)
-    gx_last = (gx_tail + jnp.pad(edge_next, ((0, 0), (8, 0), (0, 0)))).astype(BF16)
-    gx = jnp.concatenate([gx_main[:, : tokens - 16], gx_last], axis=1).reshape(two, half)
-    gy = gy.reshape(two, half)
-
-    def own_cols(value, which):
-        return lax.dynamic_slice_in_dim(value, which * quarter, quarter, 1)
-
-    gy_o, gy_c, gx_o, gx_c = (
-        own_cols(gy, c), own_cols(gy, 1 - c), own_cols(gx, c), own_cols(gx, 1 - c))
-
-    def grad_n1_of(rows):
-        return (dot_cols(gy_o[rows], wy) + dot_cols(gy_c[rows], wy_c)
-                + dot_cols(gx_o[rows], wx) + dot_cols(gx_c[rows], wx_c))
-
-    grad_n1_far = grad_n1_of(slice(tokens, two)).astype(BF16)
-    arriving = lay.over_x(grad_n1_far)
-    grad_n1_near = grad_n1_of(slice(0, tokens))
-    second_own, second_piece = weight_piece(*cuts[1], n2_row_pair, grad_n1_far)
-    grad_n1 = after(grad_n1_near, second_own) + arriving.astype(F32)
-    grad_in_norm, grad_gain_one = norm_back(grad_n1, scaled_one, inverse_one, vectors[0])
-    input_grad = (grad_mid + grad_in_norm).astype(BF16)[None]
-
-    branch_all = all_tokens(branch_two, edge)
-    out_part = sum_of_dots(mixed_rows, branch_all)
-    out_sum_z = owner_sum(lay, out_part.reshape(nz, own80, width))
-    in_y_part = sum_of_dots(n1_rows, all_tokens(gy, edge))
-    in_y_sum = owner_sum(lay, in_y_part.reshape(nz, 2 * own80, half)).astype(BF16)
-    heads = half // BLK
-    gate_part = jnp.einsum(
-        "thi,thj->hij", conv_low.reshape(two, heads, BLK),
-        jnp.concatenate([gip.reshape(two, heads, BLK), gdp.reshape(two, heads, BLK)], 2),
-        preferred_element_type=F32).reshape(2, nz, 2, own80, 2 * BLK)
-    keep = lax.dynamic_index_in_dim(gate_part, c, 2, keepdims=False)
-    away = lax.dynamic_index_in_dim(gate_part, 1 - c, 2, keepdims=False)
-    gate_part = keep + lay.over_c(away.astype(BF16)).astype(F32)
-    keep = lax.dynamic_index_in_dim(gate_part, y, 0, keepdims=False)
-    away = lax.dynamic_index_in_dim(gate_part, 1 - y, 0, keepdims=False)
-    gate_part = (keep + lay.over_y(away.astype(BF16)).astype(F32)).astype(BF16)
-    in_x_part = sum_of_dots(n1_rows, all_tokens(gx, edge))
-    in_x_sum = owner_sum(lay, in_x_part.reshape(nz, 2 * own80, half)).astype(BF16)
-    gate_sum = owner_sum(lay, gate_part).astype(BF16)
-
-    third_own, third_piece = weight_piece(*cuts[2], n2_row_pair, in_x_part)
-    pieces = [second_piece, third_piece, first_piece]
-    widths = [cuts[1][1], cuts[2][1], cuts[0][1]]
-    mlp_down_grad, mlp_gate_grad, mlp_up_grad = [
-        jnp.concatenate([p[:, i * n : (i + 1) * n] for p, n in zip(pieces, widths)], axis=1)
-        for i in range(3)]
+        return blocks[0]
+
+    arriving = lay.over_x(live.n1_far)
+    gy_y = lay.over_y(live.gy)
+    live.gy_c = lay.over_c(live.gy)
+    live.hold(piece_a=weight_piece(*cuts[0]), arriving=arriving, gy_y=gy_y)
+
+    grad_n1 = live.n1_near + live.arriving.astype(F32)
+    scaled_one = inputs[0].astype(F32) * live.inv1
+    grad_in_norm, grad_gain_one = norm_back(grad_n1, scaled_one, live.inv1, live.gain_one)
+    input_grad = (live.grad_mid + grad_in_norm).astype(BF16)[None]
+    rows_full = lax.dynamic_update_slice_in_dim(
+        jnp.zeros((8, width), F32), live.vec_rows, x * half, 1)
+    sums = jnp.concatenate([grad_gain_one[None], live.grad_gain_two[None], rows_full], axis=0)
+    sums = sums + lay.over_c(sums)
+    del live.n1_near, live.n1_far, live.arriving, live.vec_rows, live.grad_gain_two, live.grad_mid
+    live.hold(sums=sums, gy_yc=lay.over_c(live.gy_y))
 
     def over_columns(value):
         split = value.reshape(2, own80, half)
@@ -873,30 +987,81 @@
         return jnp.where(x == 0, jnp.concatenate([mine, theirs], -1),
                          jnp.concatenate([theirs, mine], -1)).astype(F32)
 
-    in_y_grad = over_columns(in_y_sum)
-    in_x_grad = over_columns(in_x_sum)
+    sums = live.sums + lay.over_x(live.sums)
+    sums = sums + lay.over_seq_bit(sums, 1)
+    n1_all = [live.n1_own, live.n1_c, live.n1_y, live.n1_yc]
+    in_y_part = sum_of_dots(n1_all, [live.gy, live.gy_c, live.gy_y, live.gy_yc])
+    branch_far = half_of(order_f(live.branch_x_rel), x, half, 1)
+    branch_near = half_of(live.branch, x, half, 1)
+    del live.gy, live.gy_c, live.gy_y, live.gy_yc, live.branch_x_rel
+    live.hold(in_y_part=in_y_part, sums=sums, branch_two=jnp.concatenate([branch_near, branch_far], axis=0))
+
+    sum_a = piece_sum(*live.piece_a)
+    in_y_own, in_y_come = owner_parts(live.in_y_part.reshape(nz, 2 * own80, half))
+    gx_y = lay.over_y(live.gx)
+    branch_two_y = lay.over_y(live.branch_two)
+    piece_b = weight_piece(*cuts[1])
+    del live.piece_a
+    live.hold(piece_b=piece_b, sum_a=sum_a, gx_y=gx_y, branch_two_y=branch_two_y, in_y_own=in_y_own,
+              in_y_come=in_y_come[:-1], in_y_part=live.in_y_part)
+
+    in_y_last = owner_parts(live.in_y_part.reshape(nz, 2 * own80, half))[1][-1:]
+    sum_b = piece_sum(*live.piece_b)
+    mixed_own, mixed_away, sent, sent_y = rows_by_device(
+        at_yc, [[live.mixed[0], live.mixed[1]], [live.mixed_x[:tokens], live.mixed_x[tokens:]]], n1_starts, own80)
+    in_x_part = sum_of_dots(n1_all, [live.gx, lay.over_c(live.gx), live.gx_y, lay.over_c(live.gx_y)])
+    gate_part = gate_weight_grad(
+        live.conv_low.reshape(two, half), live.gip.reshape(two, half), live.gdp.reshape(two, half)
+    ).reshape(2, nz, 2, own80, 2 * BLK)
+    pick = lambda value, at, axis: lax.dynamic_index_in_dim(value, at, axis, keepdims=False)
+    gate_part = pick(gate_part, c, 2) + lay.over_c(pick(gate_part, 1 - c, 2).astype(BF16)).astype(F32)
+    gate_y = lay.over_y(pick(gate_part, 1 - y, 0).astype(BF16))
+    del live.mixed, live.mixed_x, live.conv_low, live.gip, live.gdp, live.in_y_part, live.piece_b
+    live.hold(in_x_part=in_x_part, gate_keep=pick(gate_part, y, 0), gate_y=gate_y, sum_b=sum_b,
+              in_y_total=total_of(live.in_y_own, live.in_y_come + in_y_last),
+              mixed_own=mixed_own, mixed_away=mixed_away, mixed_c=lay.over_c(sent), mixed_away_c=lay.over_c(sent_y),
+              branch_c=lay.over_c(live.branch_two), branch_yc=lay.over_c(live.branch_two_y))
+    del live.in_y_own, live.in_y_come
+
+    mixed_y = (lay.over_y(live.mixed_away), lay.over_y(live.mixed_away_c))
+    in_y_grad = over_columns(live.in_y_total)
+    gate_part = (live.gate_keep + live.gate_y.astype(F32)).astype(BF16)
+    del live.gate_keep, live.gate_y, live.mixed_away, live.mixed_away_c, live.in_y_total
+    live.hold(in_x_part=jnp.concatenate(
+        [live.in_x_part.reshape(nz, 2 * own80, half), gate_part.reshape(nz, own80 * 2 * BLK // half, half)], axis=1),
+        mixed_y=mixed_y, in_y_grad=in_y_grad)
+
+    live.hold(out_part=sum_of_dots(
+        [live.mixed_own, live.mixed_c, *live.mixed_y],
+        [live.branch_two, live.branch_c, live.branch_two_y, live.branch_yc]))
+    del live.mixed_own, live.mixed_c, live.mixed_y
+
+    in_x_own, in_x_come = owner_parts(live.in_x_part)
+    out_arriving = lay.over_x(live.out_sum[tokens:].astype(BF16))
+    piece_c = weight_piece(*cuts[2])
+    del live.in_x_part
+    live.hold(piece_c=piece_c, in_x_own=in_x_own, in_x_come=in_x_come, out_arriving=out_arriving)
+
+    sum_c = piece_sum(*live.piece_c)
+    out_own, out_come = owner_parts(live.out_part.reshape(nz, 2 * own80, half))
+    live.hold(sum_c=sum_c, out_own=out_own, out_come=out_come,
+              in_x_total=total_of(live.in_x_own, live.in_x_come),
+              output=(live.mid + live.out_sum[:tokens] + live.out_arriving.astype(F32)).astype(BF16)[None])
+
+    sums = live.sums
+    for bit in bits[1:]:
+        sums = sums + lay.over_seq_bit(sums, bit)
+    mlp_down_grad, mlp_gate_grad, mlp_up_grad = joined_columns([live.sum_b, live.sum_c, live.sum_a])
 
     def final(z, y, x, c):
         at = ((x * 2 + y) * nz + z) * 2 + c
         s, f = (at // 4, at % 4)
         return (s // 2, s % 2, f // 2, f % 2)
 
-    out_grad = lay.send(out_sum_z.astype(BF16), final).astype(F32)
-    gate_grad = lay.send(gate_sum, final).astype(F32)
-    out_arriving = lay.over_x(after(out_sum[tokens:].astype(BF16), input_grad))
-    output = (mid + out_sum[:tokens] + out_arriving.astype(F32)).astype(BF16)[None]
-
-    rows_full = lax.dynamic_update_slice_in_dim(
-        jnp.zeros((8, width), F32), vec_rows, x * half, 1)
-    vec = jnp.concatenate([grad_gain_one[None], grad_gain_two[None], rows_full], axis=0)
-    vec = vec + lay.over_c(vec)
-    vec = vec + lay.over_x(vec)
-    bit = 1
-    while bit < lay.seq:
-        vec = vec + lay.over_seq_bit(vec, bit)
-        bit *= 2
-
-    return (output, input_grad, vec, in_y_grad, in_x_grad, gate_grad, out_grad,
+    in_x_grad = over_columns(live.in_x_total[: 2 * own80])
+    out_grad = over_columns(total_of(live.out_own, live.out_come))
+    gate_grad = lay.send(live.in_x_total[2 * own80 :].reshape(own80, 2 * BLK), final).astype(F32)
+    return (live.output, input_grad, sums, live.in_y_grad, in_x_grad, gate_grad, out_grad,
             mlp_gate_grad, mlp_up_grad, mlp_down_grad)
 
 

time: 692 us -> 633 us (0.915)
  waiting for transfers between devices: 233 us -> 160 us
  Pallas kernels: 214 us -> 231 us
  matrix products: 39.5 us -> 26.1 us
  other arithmetic: 42.6 us -> 50.9 us
    ppermute x99 -> x102, waiting for transfers between devices: 233 us -> 160 us  [send(): return lax.ppermute(value, ALL, self.pairs(target))]
    pallas_call x0 -> x2, Pallas kernels: none -> 12.4 us  [the longest x1 7.18 us: joined_columns(): pl.pallas_call(body, grid=(rows // step,), in_specs=[pl.BlockSpec((step,...]
    dot_general x9 -> x6, matrix products: 25.2 us -> 14.8 us  [dot_cols(): lax.dot_general(left, right, (((1,), (1,)), ((), ())), preferred_element_...]
    reshape x5 -> x2, local copies, waits for them, and re-layouts: 9.07 us -> 0.36 us  [the longest x1 0.28 us: local(): gate_part.reshape(nz, own80 * 2 * BLK // half, half)]
    slice x8 -> x18, local copies, waits for them, and re-layouts: 5.7 us -> 13.9 us  [the longest x1 2.22 us: local(): out_arriving = lay.over_x(live.out_sum[tokens:].astype(BF16))]
    unnamed x162 -> x189, local copies, waits for them, and re-layouts: 13.7 us -> 18.7 us
    ppermute x99 -> x102, starting transfers between devices: 103 us -> 102 us  [send(): return lax.ppermute(value, ALL, self.pairs(target))]
  transfers between devices with their start and end apart: 99 -> 102, of which waited for: 32 -> 36; matrix products, arithmetic and copies ran while one was open for 17% -> 14% of each run, Pallas kernels for 25% -> 31%
where the time goes in v5:
time: 633 us; the launch traced here: 625 us
  Pallas kernels  231 us (36%)
  waiting for transfers between devices  160 us (25%)
  starting transfers between devices  102 us (16%)
  local copies, waits for them, and re-layouts  52.4 us (8%)
  other arithmetic  50.9 us (8%)
  matrix products  26.1 us (4%)
    ppermute x102, waiting for transfers between devices, send(): return lax.ppermute(value, ALL, self.pairs(target))  160 us
    ppermute x102, starting transfers between devices, send(): return lax.ppermute(value, ALL, self.pairs(target))  102 us
    pallas_call x3, Pallas kernels, mlp_weight_grads(): pl.pallas_call(body, grid_spec=pltpu.PrefetchScalarGridSpec(num_scalar_pr...  98.5 us
    pallas_call x2, Pallas kernels, grad_hidden_of(): pl.pallas_call(body, grid=(pl.cdiv(ff, BLK),), in_specs=[ANY] * count + [...  25.7 us
    pallas_call x1, Pallas kernels, mlp_forward(): pl.pallas_call(body, in_specs=[ANY] * (count + 3), out_shape=[act, act, a...  23.4 us
    pallas_call x3, Pallas kernels, by_head(): pl.pallas_call(body, grid=(heads,), in_specs=in_specs, out_specs=[spec(o....  20.7 us
    pallas_call x1, Pallas kernels, mlp_rest(): pl.pallas_call(body, grid=(width // block,), in_specs=[whole] * 3 + [weig...  19 us
    unnamed x189, local copies, waits for them, and re-layouts  18.7 us
  transfers between devices with their start and end apart: 102, of which 36 were waited for; matrix products, arithmetic and copies ran while one was open for 14% of the time, Pallas kernels for 31%

profile of v5, /device:TPU:2, one launch (start us, length us, event | category | flops | bytes accessed | tf_op | source)
XLA Modules:
  0.0 624.5 jit_solution(12440053856174009514)
XLA Ops:
  3.5 3.5 collective-permute-start
  23.8 8.0 %collective-permute-done.1.refs_0_.refs_2_ = bf16[128,2560]{1,0:T(8,128)(2,1)S(1)} collective-permute-done((bf16[128,2560]{1,0:T(8,128)(2,1)}, bf16[128,2560]{1,0:T(8,128)(2,1)S(1)}, u32[]{:S(2)}, u32[]{:S(2)}) %collective-permute-start.1) | collective-permute-done | bytes 655392 | tf_op jit(solution)/shard_map/ppermute | solution.py:81
  34.0 3.2 convolution_convert_fusion
  43.8 7.4 %shard_map.195 = (bf16[2,128,1280]{2,1,0:T(8,128)(2,1)S(1)}, f32[2,128,1280]{2,1,0:T(8,128)S(1)}, f32[2,128,1280]{2,1,0:T(8,128)S(1)}, f32[2,128,1280]{2,1,0:T(8...) custom-call(f32[2,2]{1,0:T(2,128)S(1)} %pad_maximum_fusion.16.flags_ref, bf16[2,128,1280]{2,1,0:T(8,128)(2,1)S(1)} %bitcast.118, ...), custom_call_target="tpu_custom_call" | custom-call | flops 7 | bytes 7 | tf_op jit(solution)/shard_map/pallas_call | solution.py:265
  53.1 5.4 collective-permute-done.9
  67.1 3.4 shard_map.196
  72.5 3.5 fusion.74
  81.1 3.3 collective-permute-done.18
  94.6 3.6 collective-permute-done.19.refs_2_
  101.1 12.8 %shard_map.197.refs_4_ = f32[512,1920]{1,0:T(8,128)} custom-call(bf16[128,2560]{1,0:T(8,128)(2,1)} %bitcast.139, bf16[128,2560]{1,0:T(8,128)(2,1)} %collective-permute-done.13.refs_1_, bf16[128,2560]{1,0:T(8,128)(2,1)} %copy-done.74, bf16[128,2560]{1,0:T(8,128)(2,1)} %collective-permute-done.23.refs_3_, bf16[2560,1920]{1,0:T(8,128)(2,1)} %refs_23_.5), custom_call_target="tpu_custom_call" | custom-call | flops 13 | bytes 13 | tf_op jit(solution)/shard_map/pallas_call | solution.py:298
  129.0 12.9 %shard_map.198.refs_20_ = f32[512,1920]{1,0:T(8,128)} custom-call(bf16[128,2560]{1,0:T(8,128)(2,1)} %copy-done.58, bf16[128,2560]{1,0:T(8,128)(2,1)} %collective-permute-done.21.refs_1_.refs_3_, bf16[128,2560]{1,0:T(8,128)(2,1)} %copy-done.75, bf16[128,2560]{1,0:T(8,128)(2,1)} %collective-permute-done.26.refs_3_, bf16[2560,1920]{1,0:T(8,128)(2,1)} %refs_23_.5), custom_call_target="tpu_custom_call" | custom-call | flops 13 | bytes 13 | tf_op jit(solution)/shard_map/pallas_call | solution.py:298
  148.5 23.4 %shard_map.199 = (bf16[512,1920]{1,0:T(8,128)(2,1)}, bf16[512,1920]{1,0:T(8,128)(2,1)}, bf16[512,1920]{1,0:T(8,128)(2,1)}, f32[128,2560]{1,0:T(8,128)}, bf16[128,2560]{1,0:T(8,128)(2,1)}) custom-call(bf16[128,2560]{1,0:T(8,128)(2,1)} %multiply_convert_fusion.refs_0_, bf16[128,2560]{1,0:T(8,128)(2,1)} %collective-permute-done.28.refs_1_, ...), custom_call_target="tpu_custom_call" | custom-call | flops 23 | bytes 23 | tf_op jit(solution)/shard_map/pallas_call | solution.py:383
  175.3 19.0 %shard_map.200 = (f32[128,2560]{1,0:T(8,128)}, bf16[128,2560]{1,0:T(8,128)(2,1)}, f32[256,2560]{1,0:T(8,128)}, bf16[256,2560]{1,0:T(8,128)(2,1)}) custom-call(bf16[512,1920]{1,0:T(8,128)(2,1)} %get-tuple-element.2512.hid_ref.refs_24_, bf16[512,1920]{1,0:T(8,128)(2,1)} %get-tuple-element.2513.gg_ref.refs_25_, ...), custom_call_target="tpu_custom_call" | custom-call | flops 19 | bytes 19 | tf_op jit(solution)/shard_map/pallas_call | solution.py:422
  201.1 8.7 %collective-permute-done.37 = bf16[64,2560]{1,0:T(8,128)(2,1)S(1)} collective-permute-done((bf16[64,2560]{1,0:T(8,128)(2,1)S(1)}, bf16[64,2560]{1,0:T(8,128)(2,1)S(1)}, u32[]{:S(2)}, u32[]{:S(2)}) %collective-permute-start.37) | collective-permute-done | bytes 327712 | tf_op jit(solution)/shard_map/ppermute | solution.py:81
  227.9 7.4 %collective-permute-done.44 = bf16[64,2560]{1,0:T(8,128)(2,1)S(1)} collective-permute-done((bf16[64,2560]{1,0:T(8,128)(2,1)S(1)}, bf16[64,2560]{1,0:T(8,128)(2,1)S(1)}, u32[]{:S(2)}, u32[]{:S(2)}) %collective-permute-start.44) | collective-permute-done | bytes 327712 | tf_op jit(solution)/shard_map/ppermute | solution.py:81
  243.0 5.4 shard_map.201
  256.1 5.6 collective-permute-start.50
  263.5 3.1 collective-permute-start.51
  266.6 3.3 fusion.41
  271.1 2.8 convolution_add_fusion
  273.9 3.3 collective-permute-done.54.refs_7_.refs_9_
  277.3 7.2 %collective-permute-done.52.refs_7_.refs_17_ = bf16[128,2560]{1,0:T(8,128)(2,1)} collective-permute-done((bf16[128,2560]{1,0:T(8,128)(2,1)}, bf16[128,2560]{1,0:T(8,128)(2,1)}, u32[]{:S(2)}, u32[]{:S(2)}) %collective-permute-start.52) | collective-permute-done | bytes 655392 | tf_op jit(solution)/shard_map/ppermute | solution.py:81
  284.5 7.9 %shard_map.202 = (bf16[2,128,1280]{2,1,0:T(8,128)(2,1)S(1)}, bf16[2,128,1280]{2,1,0:T(8,128)(2,1)S(1)}, bf16[2,128,1280]{2,1,0:T(8,128)(2,1)S(1)}, f32[2,16,1280...) custom-call(f32[2,2]{1,0:T(2,128)S(1)} %pad_maximum_fusion.16.flags_ref, ...), custom_call_target="tpu_custom_call" | custom-call | flops 7 | bytes 7 | tf_op jit(solution)/shard_map/pallas_call | solution.py:265
  299.4 4.4 shard_map.204.refs_27_
  303.8 4.4 shard_map.203.refs_29_
  308.2 2.9 collective-permute-done.59
  311.7 3.4 fusion.39
  315.1 3.2 add_add_fusion
  321.5 24.3 %shard_map.205 = (f32[320,1152]{1,0:T(8,128)}, bf16[320,1152]{1,0:T(8,128)(2,1)}) custom-call(s32[3]{0:T(128)} %pad_add_fusion.1.place_ref, bf16[128,2560]{1,0:T(8,128)(2,1)} %collective-permute-done.29.refs_2_.refs_0_, bf16[128,2560]{1,0:T(8,128)(2,1)} %collective-permute-done.33.refs_3_.refs_1_, bf16[128,2560]{1,0:T(8,128)(2,1)} %copy-done.35, ...), custom_call_target="tpu_custom_call" | custom-call | flops 17 | bytes 17 | tf_op jit(solution)/shard_map/pallas_call | solution.py:536
  352.9 3.7 collective-permute-done.69
  359.2 5.2 shard_map.206
  371.8 36.9 %shard_map.207 = (f32[320,2304]{1,0:T(8,128)}, bf16[320,2304]{1,0:T(8,128)(2,1)}) custom-call(s32[3]{0:T(128)} %pad_add_fusion.1.place_ref, bf16[128,2560]{1,0:T(8,128)(2,1)} %collective-permute-done.29.refs_2_.refs_0_, bf16[128,2560]{1,0:T(8,128)(2,1)} %collective-permute-done.33.refs_3_.refs_1_, bf16[128,2560]{1,0:T(8,128)(2,1)} %copy-done.35, ...), custom_call_target="tpu_custom_call" | custom-call | flops 35 | bytes 35 | tf_op jit(solution)/shard_map/pallas_call | solution.py:536
  410.7 5.3 shard_map.208
  419.3 2.8 collective-permute-start.82
  423.6 3.4 shard_map.210
  434.9 5.3 shard_map.209
  443.0 20.9 %collective-permute-done.85.refs_1_ = bf16[320,2304]{1,0:T(8,128)(2,1)} collective-permute-done((bf16[320,2304]{1,0:T(8,128)(2,1)}, bf16[320,2304]{1,0:T(8,128)(2,1)}, u32[]{:S(2)}, u32[]{:S(2)}) %collective-permute-start.85) | collective-permute-done | bytes 1474592 | tf_op jit(solution)/shard_map/ppermute | solution.py:81
  468.7 2.8 pad_maximum_fusion.1
  472.5 5.0 collective-permute-done.87.refs_2_
  477.5 5.7 collective-permute-done.88.refs_3_
  483.9 5.1 shard_map.211
  489.0 2.8 dynamic-slice_bitcast_fusion.1
  502.5 37.3 %shard_map.212 = (f32[320,2304]{1,0:T(8,128)}, bf16[320,2304]{1,0:T(8,128)(2,1)}) custom-call(s32[3]{0:T(128)} %pad_add_fusion.1.place_ref, bf16[128,2560]{1,0:T(8,128)(2,1)} %collective-permute-done.29.refs_2_.refs_0_, bf16[128,2560]{1,0:T(8,128)(2,1)} %collective-permute-done.33.refs_3_.refs_1_, bf16[128,2560]{1,0:T(8,128)(2,1)} %copy-done.35, ...), custom_call_target="tpu_custom_call" | custom-call | flops 35 | bytes 35 | tf_op jit(solution)/shard_map/pallas_call | solution.py:536
  550.8 33.9 %collective-permute-done.93 = bf16[160,1280]{1,0:T(8,128)(2,1)S(1)} collective-permute-done((bf16[160,1280]{1,0:T(8,128)(2,1)S(1)}, bf16[160,1280]{1,0:T(8,128)(2,1)S(1)}, u32[]{:S(2)}, u32[]{:S(2)}) %collective-permute-start.93) | collective-permute-done | bytes 409632 | tf_op jit(solution)/shard_map/ppermute | solution.py:81
  584.7 7.3 %collective-permute-done.94 = bf16[160,1280]{1,0:T(8,128)(2,1)S(1)} collective-permute-done((bf16[160,1280]{1,0:T(8,128)(2,1)S(1)}, bf16[160,1280]{1,0:T(8,128)(2,1)S(1)}, u32[]{:S(2)}, u32[]{:S(2)}) %collective-permute-start.94) | collective-permute-done | bytes 409632 | tf_op jit(solution)/shard_map/ppermute | solution.py:81
  592.0 7.3 %collective-permute-done.95 = bf16[160,1280]{1,0:T(8,128)(2,1)S(1)} collective-permute-done((bf16[160,1280]{1,0:T(8,128)(2,1)S(1)}, bf16[160,1280]{1,0:T(8,128)(2,1)S(1)}, u32[]{:S(2)}, u32[]{:S(2)}) %collective-permute-start.95) | collective-permute-done | bytes 409632 | tf_op jit(solution)/shard_map/ppermute | solution.py:81
  602.1 6.8 %collective-permute-start.100 = (bf16[80,512]{1,0:T(8,128)(2,1)S(1)}, bf16[80,512]{1,0:T(8,128)(2,1)S(1)}, u32[]{:S(2)}, u32[]{:S(2)}) collective-permute-start(bf16[80,512]{1,0:T(8,128)(2,1)S(1)} %reshape.165), channel_id=1, source_target_pairs={{0,0},{1,1},{2,16},{3,17},{4,8},{5,9},{6,24},{7,25},{8,2},{9,3},{1... | collective-permute-start | bytes 245768 | tf_op jit(solution)/shard_map/ppermute | solution.py:81
  610.7 7.2 %shard_map.213 = (f32[320,1920]{1,0:T(8,128)}, f32[320,1920]{1,0:T(8,128)}, f32[320,1920]{1,0:T(8,128)}) custom-call(f32[320,2304]{1,0:T(8,128)} %get-tuple-element.2577.refs_0_, bf16[320,2304]{1,0:T(8,128)(2,1)} %collective-permute-done.85.refs_1_, f32[320,2304]{1,0:T(8,128)} %get-tuple-element.2579.refs_2_, bf16[320,2304]{1,0:T(8,128)(2,1)} %copy-done.64, ...), custom_call_target="tpu_custom_call" | custom-call | flops 5 | bytes 5 | tf_op jit(solution)/shard_map/pallas_call | solution.py:621
  (511 shorter events, 210.5 us)
Async XLA Ops:
  7.6 24.7 %collective-permute-start.6 = (bf16[2560,640]{1,0:T(8,128)(2,1)}, bf16[2560,640]{1,0:T(8,128)(2,1)}, u32[]{:S(2)}, u32[]{:S(2)}) collective-permute-start(bf16[2560,640]{1,0:T(8,128)(2,1)} %param.17), channel_id=1, source_target_pairs={{0,1},{1,0},{2,3},{3,2},{4,5},{5,4},{6,7},{7,6},{8,9},{9,8},{10,11... | collective-permute-start | bytes 9830408 | tf_op jit(solution)/shard_map/ppermute | solution.py:81
  14.5 17.8 %collective-permute-start.5 = (bf16[128,2560]{1,0:T(8,128)(2,1)}, bf16[128,2560]{1,0:T(8,128)(2,1)S(1)}, u32[]{:S(2)}, u32[]{:S(2)}) collective-permute-start(bf16[128,2560]{1,0:T(8,128)(2,1)} %fusion.20.refs_0_), channel_id=1, source_target_pairs={{0,2},{1,3},{2,0},{3,1},{4,6},{5,7},{6,4},{7,5},{8,10},{9,11},{10,... | collective-permute-start | bytes 1966088 | tf_op jit(solution)/shard_map/ppermute | solution.py:81
  15.0 16.8 %collective-permute-start.1 = (bf16[128,2560]{1,0:T(8,128)(2,1)}, bf16[128,2560]{1,0:T(8,128)(2,1)S(1)}, u32[]{:S(2)}, u32[]{:S(2)}) collective-permute-start(bf16[128,2560]{1,0:T(8,128)(2,1)} %bitcast.137), channel_id=1, source_target_pairs={{0,4},{1,5},{2,6},{3,7},{4,0},{5,1},{6,2},{7,3},{8,12},{9,13},{10,... | collective-permute-start | bytes 1966088 | tf_op jit(solution)/shard_map/ppermute | solution.py:81
  21.2 31.9 %collective-permute-start.11 = (bf16[2560,640]{1,0:T(8,128)(2,1)S(1)}, bf16[2560,640]{1,0:T(8,128)(2,1)}, u32[]{:S(2)}, u32[]{:S(2)}) collective-permute-start(bf16[2560,640]{1,0:T(8,128)(2,1)S(1)} %copy-done.53), channel_id=1, source_target_pairs={{0,1},{1,0},{2,3},{3,2},{4,5},{5,4},{6,7},{7,6},{8,9},{9,8},{10,11... | collective-permute-start | bytes 9830408 | tf_op jit(solution)/shard_map/ppermute | solution.py:81
  21.4 31.7 %collective-permute-start.8 = (bf16[128,2560]{1,0:T(8,128)(2,1)S(1)}, bf16[128,2560]{1,0:T(8,128)(2,1)}, u32[]{:S(2)}, u32[]{:S(2)}) collective-permute-start(bf16[128,2560]{1,0:T(8,128)(2,1)S(1)} %bitcast.141), channel_id=1, source_target_pairs={{0,24},{1,25},{2,26},{3,27},{4,28},{5,29},{6,30},{7,31},{8,16},{9,... | collective-permute-start | bytes 1966088 | tf_op jit(solution)/shard_map/ppermute | solution.py:81
  37.6 20.9 %collective-permute-start.10 = (bf16[1280,640]{1,0:T(8,128)(2,1)S(1)}, bf16[1280,640]{1,0:T(8,128)(2,1)S(1)}, u32[]{:S(2)}, u32[]{:S(2)}) collective-permute-start(bf16[1280,640]{1,0:T(8,128)(2,1)S(1)} %constant_dynamic-slice_fusion.2), channel_id=1, source_target_pairs={{0,1},{1,0},{2,3},{3,2},{4,5},{5,4},{6,7},{7,6},{8,9},{9,8},{10,11... | collective-permute-start | bytes 4915208 | tf_op jit(solution)/shard_map/ppermute | solution.py:81
  38.1 20.4 %collective-permute-start.9 = (bf16[640,640]{1,0:T(8,128)(2,1)}, bf16[640,640]{1,0:T(8,128)(2,1)S(1)}, u32[]{:S(2)}, u32[]{:S(2)}) collective-permute-start(bf16[640,640]{1,0:T(8,128)(2,1)} %constant_dynamic-slice_fusion.3), channel_id=1, source_target_pairs={{0,2},{1,3},{2,0},{3,1},{4,6},{5,7},{6,4},{7,5},{8,10},{9,11},{10,... | collective-permute-start | bytes 2457608 | tf_op jit(solution)/shard_map/ppermute | solution.py:81
  63.9 15.6 %collective-permute-start.17 = (f32[4,1280]{1,0:T(4,128)S(1)}, f32[4,1280]{1,0:T(4,128)S(1)}, u32[]{:S(2)}, u32[]{:S(2)}) collective-permute-start(f32[4,1280]{1,0:T(4,128)S(1)} %pad_maximum_fusion.11), channel_id=1, source_target_pairs={{0,8},{1,9},{2,10},{3,11},{4,12},{5,13},{6,14},{7,15},{8,0},{9,1},... | collective-permute-start | bytes 61448 | tf_op jit(solution)/shard_map/ppermute | solution.py:81
  65.5 19.0 %collective-permute-start.16 = (bf16[640,640]{1,0:T(8,128)(2,1)}, bf16[640,640]{1,0:T(8,128)(2,1)}, u32[]{:S(2)}, u32[]{:S(2)}) collective-permute-start(bf16[640,640]{1,0:T(8,128)(2,1)} %copy-done.71), channel_id=1, source_target_pairs={{0,4},{1,5},{2,6},{3,7},{4,0},{5,1},{6,2},{7,3},{8,12},{9,13},{10,... | collective-permute-start | bytes 2457608 | tf_op jit(solution)/shard_map/ppermute | solution.py:81
  70.5 16.0 %collective-permute-start.14 = (bf16[640,256]{1,0:T(8,128)(2,1)}, bf16[640,256]{1,0:T(8,128)(2,1)S(1)}, u32[]{:S(2)}, u32[]{:S(2)}) collective-permute-start(bf16[640,256]{1,0:T(8,128)(2,1)} %get-tuple-element.1385), channel_id=1, source_target_pairs={{0,1},{1,0},{2,3},{3,2},{4,5},{5,4},{6,7},{7,6},{8,9},{9,8},{10,11... | collective-permute-start | bytes 983048 | tf_op jit(solution)/shard_map/ppermute | solution.py:81
  70.5 16.0 %collective-permute-start.15 = (bf16[640,256]{1,0:T(8,128)(2,1)}, bf16[640,256]{1,0:T(8,128)(2,1)S(1)}, u32[]{:S(2)}, u32[]{:S(2)}) collective-permute-start(bf16[640,256]{1,0:T(8,128)(2,1)} %get-tuple-element.1386), channel_id=1, source_target_pairs={{0,1},{1,0},{2,3},{3,2},{4,5},{5,4},{6,7},{7,6},{8,9},{9,8},{10,11... | collective-permute-start | bytes 983048 | tf_op jit(solution)/shard_map/ppermute | solution.py:81
  71.0 17.0 %collective-permute-start.13 = (bf16[128,2560]{1,0:T(8,128)(2,1)}, bf16[128,2560]{1,0:T(8,128)(2,1)}, u32[]{:S(2)}, u32[]{:S(2)}) collective-permute-start(bf16[128,2560]{1,0:T(8,128)(2,1)} %bitcast.138), channel_id=1, source_target_pairs={{0,2},{1,3},{2,0},{3,1},{4,6},{5,7},{6,4},{7,5},{8,10},{9,11},{10,... | collective-permute-start | bytes 1966088 | tf_op jit(solution)/shard_map/ppermute | solution.py:81
  98.2 17.5 %collective-permute-start.21 = (bf16[128,2560]{1,0:T(8,128)(2,1)}, bf16[128,2560]{1,0:T(8,128)(2,1)}, u32[]{:S(2)}, u32[]{:S(2)}) collective-permute-start(bf16[128,2560]{1,0:T(8,128)(2,1)} %collective-permute-done.13.refs_1_), channel_id=1, source_target_pairs={{0,4},{1,5},{2,6},{3,7},{4,0},{5,1},{6,2},{7,3},{8,12},{9,13},{10,... | collective-permute-start | bytes 1966088 | tf_op jit(solution)/shard_map/ppermute | solution.py:81
  98.7 17.2 %collective-permute-start.24 = (bf16[128,2560]{1,0:T(8,128)(2,1)}, bf16[128,2560]{1,0:T(8,128)(2,1)}, u32[]{:S(2)}, u32[]{:S(2)}) collective-permute-start(bf16[128,2560]{1,0:T(8,128)(2,1)} %fusion.22), channel_id=1, source_target_pairs={{0,2},{1,3},{2,0},{3,1},{4,6},{5,7},{6,4},{7,5},{8,10},{9,11},{10,... | collective-permute-start | bytes 1966088 | tf_op jit(solution)/shard_map/ppermute | solution.py:81
  120.9 21.0 %collective-permute-start.27 = (bf16[128,2560]{1,0:T(8,128)(2,1)}, bf16[128,2560]{1,0:T(8,128)(2,1)}, u32[]{:S(2)}, u32[]{:S(2)}) collective-permute-start(bf16[128,2560]{1,0:T(8,128)(2,1)} %multiply_convert_fusion.refs_0_), channel_id=1, source_target_pairs={{0,1},{1,0},{2,3},{3,2},{4,5},{5,4},{6,7},{7,6},{8,9},{9,8},{10,11... | collective-permute-start | bytes 1966088 | tf_op jit(solution)/shard_map/ppermute | solution.py:81
  120.9 21.0 %collective-permute-start.28 = (bf16[128,2560]{1,0:T(8,128)(2,1)}, bf16[128,2560]{1,0:T(8,128)(2,1)}, u32[]{:S(2)}, u32[]{:S(2)}) collective-permute-start(bf16[128,2560]{1,0:T(8,128)(2,1)} %multiply_convert_fusion.refs_0_), channel_id=1, source_target_pairs={{0,2},{1,3},{2,0},{3,1},{4,6},{5,7},{6,4},{7,5},{8,10},{9,11},{10,... | collective-permute-start | bytes 1966088 | tf_op jit(solution)/shard_map/ppermute | solution.py:81
  122.4 19.5 %collective-permute-start.29 = (bf16[128,2560]{1,0:T(8,128)(2,1)}, bf16[128,2560]{1,0:T(8,128)(2,1)}, u32[]{:S(2)}, u32[]{:S(2)}) collective-permute-start(bf16[128,2560]{1,0:T(8,128)(2,1)} %multiply_convert_fusion.refs_0_), channel_id=1, source_target_pairs={{0,4},{1,5},{2,6},{3,7},{4,0},{5,1},{6,2},{7,3},{8,12},{9,13},{10,... | collective-permute-start | bytes 1966088 | tf_op jit(solution)/shard_map/ppermute | solution.py:81
  144.4 27.5 %collective-permute-start.32 = (bf16[128,2560]{1,0:T(8,128)(2,1)}, bf16[128,2560]{1,0:T(8,128)(2,1)}, u32[]{:S(2)}, u32[]{:S(2)}) collective-permute-start(bf16[128,2560]{1,0:T(8,128)(2,1)} %collective-permute-done.8.refs_4_.refs_12_), channel_id=1, source_target_pairs={{0,2},{1,3},{2,0},{3,1},{4,6},{5,7},{6,4},{7,5},{8,10},{9,11},{10,... | collective-permute-start | bytes 1966088 | tf_op jit(solution)/shard_map/ppermute | solution.py:81
  145.0 27.0 %collective-permute-start.33 = (bf16[128,2560]{1,0:T(8,128)(2,1)}, bf16[128,2560]{1,0:T(8,128)(2,1)}, u32[]{:S(2)}, u32[]{:S(2)}) collective-permute-start(bf16[128,2560]{1,0:T(8,128)(2,1)} %collective-permute-done.28.refs_1_), channel_id=1, source_target_pairs={{0,4},{1,5},{2,6},{3,7},{4,0},{5,1},{6,2},{7,3},{8,12},{9,13},{10,... | collective-permute-start | bytes 1966088 | tf_op jit(solution)/shard_map/ppermute | solution.py:81
  147.2 24.8 %collective-permute-start.34 = (bf16[64,2560]{1,0:T(8,128)(2,1)}, bf16[64,2560]{1,0:T(8,128)(2,1)}, u32[]{:S(2)}, u32[]{:S(2)}) collective-permute-start(bf16[64,2560]{1,0:T(8,128)(2,1)} %slice.239), channel_id=1, source_target_pairs={{0,24},{1,25},{2,26},{3,27},{4,28},{5,29},{6,30},{7,31},{8,16},{9,... | collective-permute-start | bytes 983048 | tf_op jit(solution)/shard_map/ppermute | solution.py:81
  194.3 18.7 %collective-permute-start.39 = (bf16[256,2560]{1,0:T(8,128)(2,1)}, bf16[256,2560]{1,0:T(8,128)(2,1)S(1)}, u32[]{:S(2)}, u32[]{:S(2)}) collective-permute-start(bf16[256,2560]{1,0:T(8,128)(2,1)} %get-tuple-element.1714), channel_id=1, source_target_pairs={{0,1},{1,0},{2,3},{3,2},{4,5},{5,4},{6,7},{7,6},{8,9},{9,8},{10,11... | collective-permute-start | bytes 3932168 | tf_op jit(solution)/shard_map/ppermute | solution.py:81
  194.6 17.1 %collective-permute-start.36 = (bf16[128,2560]{1,0:T(8,128)(2,1)}, bf16[128,2560]{1,0:T(8,128)(2,1)S(1)}, u32[]{:S(2)}, u32[]{:S(2)}) collective-permute-start(bf16[128,2560]{1,0:T(8,128)(2,1)} %add_convert_fusion.1), channel_id=1, source_target_pairs={{0,2},{1,3},{2,0},{3,1},{4,6},{5,7},{6,4},{7,5},{8,10},{9,11},{10,... | collective-permute-start | bytes 1966088 | tf_op jit(solution)/shard_map/ppermute | solution.py:81
  196.1 16.9 %collective-permute-start.38 = (bf16[128,2560]{1,0:T(8,128)(2,1)}, bf16[128,2560]{1,0:T(8,128)(2,1)}, u32[]{:S(2)}, u32[]{:S(2)}) collective-permute-start(bf16[128,2560]{1,0:T(8,128)(2,1)} %pad_maximum_fusion.4.refs_4_), channel_id=1, source_target_pairs={{0,4},{1,5},{2,6},{3,7},{4,0},{5,1},{6,2},{7,3},{8,12},{9,13},{10,... | collective-permute-start | bytes 1966088 | tf_op jit(solution)/shard_map/ppermute | solution.py:81
  220.1 16.8 %collective-permute-start.41 = (bf16[128,2560]{1,0:T(8,128)(2,1)S(1)}, bf16[128,2560]{1,0:T(8,128)(2,1)S(1)}, u32[]{:S(2)}, u32[]{:S(2)}) collective-permute-start(bf16[128,2560]{1,0:T(8,128)(2,1)S(1)} %maximum_select_fusion.8), channel_id=1, source_target_pairs={{0,2},{1,3},{2,0},{3,1},{4,6},{5,7},{6,4},{7,5},{8,10},{9,11},{10,... | collective-permute-start | bytes 1966088 | tf_op jit(solution)/shard_map/ppermute | solution.py:81
  220.7 16.7 %collective-permute-start.42 = (bf16[128,2560]{1,0:T(8,128)(2,1)}, bf16[128,2560]{1,0:T(8,128)(2,1)S(1)}, u32[]{:S(2)}, u32[]{:S(2)}) collective-permute-start(bf16[128,2560]{1,0:T(8,128)(2,1)} %collective-permute-done.8.refs_4_.refs_12_), channel_id=1, source_target_pairs={{0,4},{1,5},{2,6},{3,7},{4,0},{5,1},{6,2},{7,3},{8,12},{9,13},{10,... | collective-permute-start | bytes 1966088 | tf_op jit(solution)/shard_map/ppermute | solution.py:81
  261.7 15.6 %collective-permute-start.54 = (bf16[128,2560]{1,0:T(8,128)(2,1)}, bf16[128,2560]{1,0:T(8,128)(2,1)}, u32[]{:S(2)}, u32[]{:S(2)}) collective-permute-start(bf16[128,2560]{1,0:T(8,128)(2,1)} %collective-permute-done.38.refs_6_.refs_8_), channel_id=1, source_target_pairs={{0,2},{1,3},{2,0},{3,1},{4,6},{5,7},{6,4},{7,5},{8,10},{9,11},{10,... | collective-permute-start | bytes 1966088 | tf_op jit(solution)/shard_map/ppermute | solution.py:81
  292.6 15.6 %collective-permute-start.60 = (bf16[128,2560]{1,0:T(8,128)(2,1)S(1)}, bf16[128,2560]{1,0:T(8,128)(2,1)S(1)}, u32[]{:S(2)}, u32[]{:S(2)}) collective-permute-start(bf16[128,2560]{1,0:T(8,128)(2,1)S(1)} %constant_dynamic-update-slice_fusion.6.refs_5_), channel_id=1, source_target_pairs={{0,1},{1,0},{2,3},{3,2},{4,5},{5,4},{6,7},{7,6},{8,9},{9,8},{10,11... | collective-permute-start | bytes 1966088 | tf_op jit(solution)/shard_map/ppermute | solution.py:81
  295.0 16.0 %collective-permute-start.59 = (bf16[256,1280]{1,0:T(8,128)(2,1)}, bf16[256,1280]{1,0:T(8,128)(2,1)}, u32[]{:S(2)}, u32[]{:S(2)}) collective-permute-start(bf16[256,1280]{1,0:T(8,128)(2,1)} %pad_maximum_fusion.6), channel_id=1, source_target_pairs={{0,2},{1,3},{2,0},{3,1},{4,6},{5,7},{6,4},{7,5},{8,10},{9,11},{10,... | collective-permute-start | bytes 1966088 | tf_op jit(solution)/shard_map/ppermute | solution.py:81
  319.4 26.4 %collective-permute-start.64 = (bf16[128,2560]{1,0:T(8,128)(2,1)}, bf16[128,2560]{1,0:T(8,128)(2,1)}, u32[]{:S(2)}, u32[]{:S(2)}) collective-permute-start(bf16[128,2560]{1,0:T(8,128)(2,1)} %slice.363), channel_id=1, source_target_pairs={{0,2},{1,3},{2,0},{3,1},{4,6},{5,7},{6,4},{7,5},{8,10},{9,11},{10,... | collective-permute-start | bytes 1966088 | tf_op jit(solution)/shard_map/ppermute | solution.py:81
  320.9 24.9 %collective-permute-start.65 = (bf16[256,1280]{1,0:T(8,128)(2,1)S(1)}, bf16[256,1280]{1,0:T(8,128)(2,1)}, u32[]{:S(2)}, u32[]{:S(2)}) collective-permute-start(bf16[256,1280]{1,0:T(8,128)(2,1)S(1)} %bitcast.124), channel_id=1, source_target_pairs={{0,1},{1,0},{2,3},{3,2},{4,5},{5,4},{6,7},{7,6},{8,9},{9,8},{10,11... | collective-permute-start | bytes 1966088 | tf_op jit(solution)/shard_map/ppermute | solution.py:81
  321.0 24.9 %collective-permute-start.66 = (bf16[256,1280]{1,0:T(8,128)(2,1)S(1)}, bf16[256,1280]{1,0:T(8,128)(2,1)}, u32[]{:S(2)}, u32[]{:S(2)}) collective-permute-start(bf16[256,1280]{1,0:T(8,128)(2,1)S(1)} %bitcast.125), channel_id=1, source_target_pairs={{0,4},{1,5},{2,6},{3,7},{4,0},{5,1},{6,2},{7,3},{8,12},{9,13},{10,... | collective-permute-start | bytes 1966088 | tf_op jit(solution)/shard_map/ppermute | solution.py:81
  365.0 43.7 %collective-permute-start.75 = (bf16[320,1152]{1,0:T(8,128)(2,1)}, bf16[320,1152]{1,0:T(8,128)(2,1)}, u32[]{:S(2)}, u32[]{:S(2)}) collective-permute-start(bf16[320,1152]{1,0:T(8,128)(2,1)} %get-tuple-element.2366), channel_id=1, source_target_pairs={{0,8},{1,9},{2,10},{3,11},{4,12},{5,13},{6,14},{7,15},{8,0},{9,1},... | collective-permute-start | bytes 2211848 | tf_op jit(solution)/shard_map/ppermute | solution.py:81
  365.3 43.4 %collective-permute-start.71 = (bf16[256,1280]{1,0:T(8,128)(2,1)}, bf16[256,1280]{1,0:T(8,128)(2,1)}, u32[]{:S(2)}, u32[]{:S(2)}) collective-permute-start(bf16[256,1280]{1,0:T(8,128)(2,1)} %pad_maximum_fusion.8.refs_4_), channel_id=1, source_target_pairs={{0,4},{1,5},{2,6},{3,7},{4,0},{5,1},{6,2},{7,3},{8,12},{9,13},{10,... | collective-permute-start | bytes 1966088 | tf_op jit(solution)/shard_map/ppermute | solution.py:81
  365.8 42.9 %collective-permute-start.72 = (bf16[256,1280]{1,0:T(8,128)(2,1)S(1)}, bf16[256,1280]{1,0:T(8,128)(2,1)}, u32[]{:S(2)}, u32[]{:S(2)}) collective-permute-start(bf16[256,1280]{1,0:T(8,128)(2,1)S(1)} %bitcast.145), channel_id=1, source_target_pairs={{0,4},{1,5},{2,6},{3,7},{4,0},{5,1},{6,2},{7,3},{8,12},{9,13},{10,... | collective-permute-start | bytes 1966088 | tf_op jit(solution)/shard_map/ppermute | solution.py:81
  369.5 39.2 %collective-permute-start.73 = (bf16[160,1280]{1,0:T(8,128)(2,1)}, bf16[160,1280]{1,0:T(8,128)(2,1)}, u32[]{:S(2)}, u32[]{:S(2)}) collective-permute-start(bf16[160,1280]{1,0:T(8,128)(2,1)} %get-tuple-element.2607), channel_id=1, source_target_pairs={{0,8},{1,9},{2,10},{3,11},{4,12},{5,13},{6,14},{7,15},{8,16},{9,17... | collective-permute-start | bytes 1228808 | tf_op jit(solution)/shard_map/ppermute | solution.py:81
  371.5 37.3 %collective-permute-start.74 = (bf16[160,1280]{1,0:T(8,128)(2,1)S(1)}, bf16[160,1280]{1,0:T(8,128)(2,1)}, u32[]{:S(2)}, u32[]{:S(2)}) collective-permute-start(bf16[160,1280]{1,0:T(8,128)(2,1)S(1)} %get-tuple-element.2606), channel_id=1, source_target_pairs={{0,16},{1,17},{2,18},{3,19},{4,20},{5,21},{6,22},{7,23},{8,24},{9,... | collective-permute-start | bytes 1228808 | tf_op jit(solution)/shard_map/ppermute | solution.py:81
  422.7 41.2 %collective-permute-start.85 = (bf16[320,2304]{1,0:T(8,128)(2,1)}, bf16[320,2304]{1,0:T(8,128)(2,1)}, u32[]{:S(2)}, u32[]{:S(2)}) collective-permute-start(bf16[320,2304]{1,0:T(8,128)(2,1)} %get-tuple-element.2418), channel_id=1, source_target_pairs={{0,8},{1,9},{2,10},{3,11},{4,12},{5,13},{6,14},{7,15},{8,0},{9,1},... | collective-permute-start | bytes 4423688 | tf_op jit(solution)/shard_map/ppermute | solution.py:81
  467.2 16.0 %collective-permute-start.88 = (bf16[640,256]{1,0:T(8,128)(2,1)}, bf16[640,256]{1,0:T(8,128)(2,1)S(1)}, u32[]{:S(2)}, u32[]{:S(2)}) collective-permute-start(bf16[640,256]{1,0:T(8,128)(2,1)} %copy-done.89), channel_id=1, source_target_pairs={{0,4},{1,5},{2,6},{3,7},{4,0},{5,1},{6,2},{7,3},{8,12},{9,13},{10,... | collective-permute-start | bytes 983048 | tf_op jit(solution)/shard_map/ppermute | solution.py:81
  491.8 48.0 %collective-permute-start.89 = (bf16[192,1280]{1,0:T(8,128)(2,1)}, bf16[192,1280]{1,0:T(8,128)(2,1)}, u32[]{:S(2)}, u32[]{:S(2)}) collective-permute-start(bf16[192,1280]{1,0:T(8,128)(2,1)} %get-tuple-element.2600), channel_id=1, source_target_pairs={{0,8},{1,9},{2,10},{3,11},{4,12},{5,13},{6,14},{7,15},{8,16},{9,17... | collective-permute-start | bytes 1474568 | tf_op jit(solution)/shard_map/ppermute | solution.py:81
  493.5 46.3 %collective-permute-start.90 = (bf16[192,1280]{1,0:T(8,128)(2,1)}, bf16[192,1280]{1,0:T(8,128)(2,1)}, u32[]{:S(2)}, u32[]{:S(2)}) collective-permute-start(bf16[192,1280]{1,0:T(8,128)(2,1)} %get-tuple-element.2599), channel_id=1, source_target_pairs={{0,16},{1,17},{2,18},{3,19},{4,20},{5,21},{6,22},{7,23},{8,24},{9,... | collective-permute-start | bytes 1474568 | tf_op jit(solution)/shard_map/ppermute | solution.py:81
  496.2 43.6 %collective-permute-start.91 = (bf16[192,1280]{1,0:T(8,128)(2,1)}, bf16[192,1280]{1,0:T(8,128)(2,1)}, u32[]{:S(2)}, u32[]{:S(2)}) collective-permute-start(bf16[192,1280]{1,0:T(8,128)(2,1)} %get-tuple-element.2598), channel_id=1, source_target_pairs={{0,24},{1,25},{2,26},{3,27},{4,28},{5,29},{6,30},{7,31},{8,0},{9,1... | collective-permute-start | bytes 1474568 | tf_op jit(solution)/shard_map/ppermute | solution.py:81
  499.4 40.4 %collective-permute-start.92 = (bf16[128,2560]{1,0:T(8,128)(2,1)}, bf16[128,2560]{1,0:T(8,128)(2,1)}, u32[]{:S(2)}, u32[]{:S(2)}) collective-permute-start(bf16[128,2560]{1,0:T(8,128)(2,1)} %slice.362), channel_id=1, source_target_pairs={{0,2},{1,3},{2,0},{3,1},{4,6},{5,7},{6,4},{7,5},{8,10},{9,11},{10,... | collective-permute-start | bytes 1966088 | tf_op jit(solution)/shard_map/ppermute | solution.py:81
  539.8 59.4 %collective-permute-start.96 = (bf16[320,2304]{1,0:T(8,128)(2,1)}, bf16[320,2304]{1,0:T(8,128)(2,1)S(1)}, u32[]{:S(2)}, u32[]{:S(2)}) collective-permute-start(bf16[320,2304]{1,0:T(8,128)(2,1)} %get-tuple-element.2561), channel_id=1, source_target_pairs={{0,8},{1,9},{2,10},{3,11},{4,12},{5,13},{6,14},{7,15},{8,0},{9,1},... | collective-permute-start | bytes 4423688 | tf_op jit(solution)/shard_map/ppermute | solution.py:81
  543.1 41.6 %collective-permute-start.93 = (bf16[160,1280]{1,0:T(8,128)(2,1)S(1)}, bf16[160,1280]{1,0:T(8,128)(2,1)S(1)}, u32[]{:S(2)}, u32[]{:S(2)}) collective-permute-start(bf16[160,1280]{1,0:T(8,128)(2,1)S(1)} %get-tuple-element.2604), channel_id=1, source_target_pairs={{0,8},{1,9},{2,10},{3,11},{4,12},{5,13},{6,14},{7,15},{8,16},{9,17... | collective-permute-start | bytes 1228808 | tf_op jit(solution)/shard_map/ppermute | solution.py:81
  543.6 48.4 %collective-permute-start.94 = (bf16[160,1280]{1,0:T(8,128)(2,1)S(1)}, bf16[160,1280]{1,0:T(8,128)(2,1)S(1)}, u32[]{:S(2)}, u32[]{:S(2)}) collective-permute-start(bf16[160,1280]{1,0:T(8,128)(2,1)S(1)} %get-tuple-element.2603), channel_id=1, source_target_pairs={{0,16},{1,17},{2,18},{3,19},{4,20},{5,21},{6,22},{7,23},{8,24},{9,... | collective-permute-start | bytes 1228808 | tf_op jit(solution)/shard_map/ppermute | solution.py:81
  544.6 54.6 %collective-permute-start.95 = (bf16[160,1280]{1,0:T(8,128)(2,1)S(1)}, bf16[160,1280]{1,0:T(8,128)(2,1)S(1)}, u32[]{:S(2)}, u32[]{:S(2)}) collective-permute-start(bf16[160,1280]{1,0:T(8,128)(2,1)S(1)} %get-tuple-element.2602), channel_id=1, source_target_pairs={{0,24},{1,25},{2,26},{3,27},{4,28},{5,29},{6,30},{7,31},{8,0},{9,1... | collective-permute-start | bytes 1228808 | tf_op jit(solution)/shard_map/ppermute | solution.py:81
  600.6 19.7 %collective-permute-start.101 = (bf16[80,1280]{1,0:T(8,128)(2,1)}, bf16[80,1280]{1,0:T(8,128)(2,1)}, u32[]{:S(2)}, u32[]{:S(2)}) collective-permute-start(bf16[80,1280]{1,0:T(8,128)(2,1)} %get-tuple-element.2639), channel_id=1, source_target_pairs={{0,2},{1,3},{2,0},{3,1},{4,6},{5,7},{6,4},{7,5},{8,10},{9,11},{10,... | collective-permute-start | bytes 614408 | tf_op jit(solution)/shard_map/ppermute | solution.py:81
  602.1 15.8 %collective-permute-start.100 = (bf16[80,512]{1,0:T(8,128)(2,1)S(1)}, bf16[80,512]{1,0:T(8,128)(2,1)S(1)}, u32[]{:S(2)}, u32[]{:S(2)}) collective-permute-start(bf16[80,512]{1,0:T(8,128)(2,1)S(1)} %reshape.165), channel_id=1, source_target_pairs={{0,0},{1,1},{2,16},{3,17},{4,8},{5,9},{6,24},{7,25},{8,2},{9,3},{1... | collective-permute-start | bytes 245768 | tf_op jit(solution)/shard_map/ppermute | solution.py:81
  (146 other events, 1392.0 us)

commit v6 on v5

--- a/solution.py
+++ b/solution.py
@@ -21,7 +21,8 @@
 
 
 def work(us):
-    return pl.CostEstimate(flops=us, bytes_accessed=us, transcendentals=0)
+    scale = 1000 if us >= 10 else 0
+    return pl.CostEstimate(flops=1 + us * scale * 900000, bytes_accessed=1 + us * scale * 2000, transcendentals=0)
 
 
 def norm_scale(values):
@@ -574,17 +575,17 @@
                 for dy in range(2)])
 
         kept, sent = (taken(0), taken(1))
-        return kept[0], kept[1], sent[0], sent[1]
+        return kept[0], sent[0], jnp.concatenate([kept[1], sent[1]], axis=0)
 
     def body(place_ref, *refs):
-        keep_ref, keep_y_ref, send_ref, send_y_ref, turned = refs[len(flat):]
+        keep_ref, send_ref, y_ref, turned = refs[len(flat):]
         for h in range(columns):
             base = 0 if columns == 1 else pl.multiple_of((place_ref[2] ^ h) * n, 16)
             for k in range(count):
                 turned[pl.ds(base, n), k * tokens : (k + 1) * tokens] = refs[h * count + k][...].T
-        for dy, dc, ref in ((0, 0, keep_ref), (1, 0, keep_y_ref), (0, 1, send_ref), (1, 1, send_y_ref)):
+        for dy, dc, ref, at in ((0, 0, keep_ref, 0), (0, 1, send_ref, 0), (1, 0, y_ref, 0), (1, 1, y_ref, rows)):
             for i, start in enumerate(starts(place_ref[0] ^ dy, place_ref[1] ^ dc)):
-                ref[i * block : (i + 1) * block, :] = turned[pl.ds(pl.multiple_of(start, 16), block), :]
+                ref[at + i * block : at + (i + 1) * block, :] = turned[pl.ds(pl.multiple_of(start, 16), block), :]
 
     shape = (rows, count * tokens)
     return pl.pallas_call(
@@ -593,10 +594,10 @@
             num_scalar_prefetch=1,
             grid=(1,),
             in_specs=[pl.BlockSpec((tokens, n), lambda i, place: (0, 0))] * len(flat),
-            out_specs=[pl.BlockSpec(shape, lambda i, place: (0, 0))] * 4,
+            out_specs=[pl.BlockSpec((n_rows, shape[1]), lambda i, place: (0, 0)) for n_rows in (rows, rows, 2 * rows)],
             scratch_shapes=[pltpu.VMEM((columns * n, count * tokens), BF16)],
         ),
-        out_shape=[jax.ShapeDtypeStruct(shape, BF16)] * 4,
+        out_shape=[jax.ShapeDtypeStruct((n_rows, shape[1]), BF16) for n_rows in (rows, rows, 2 * rows)],
         compiler_params=pltpu.CompilerParams(vmem_limit_bytes=VMEM_MAX),
         cost_estimate=work(3),
     )(place, *flat)
@@ -810,14 +811,14 @@
             cot_x = lay.over_x(after(cot, live.scan))
     out_x = jnp.where(y == 0, jnp.concatenate([live.out_a, out_b], 0), jnp.concatenate([out_b, live.out_a], 0))
     y_pre = order_c(dot(live.normed, in_y), dot(live.normed, live.wy_c), 1).reshape(2, tokens, half)
-    n1_own, n1_away, sent, sent_y = rows_by_device(at_yc, [[live.n1, live.n1_x]], n1_starts, own80)
+    n1_own, sent, n1_away = rows_by_device(at_yc, [[live.n1, live.n1_x]], n1_starts, own80)
     state_in = live.scan[3]
     del live.scan, live.out_a
     live.hold(state_in=state_in, y_pre=y_pre, out_left=jnp.concatenate([live.out_mine, live.out_c], axis=1),
-              out_x=out_x, cot_x=cot_x, n1_own=n1_own, n1_away=n1_away, n1_c=lay.over_c(sent), n1_away_c=lay.over_c(sent_y))
+              out_x=out_x, cot_x=cot_x, n1_own=n1_own, n1_away=n1_away, n1_c=lay.over_c(sent))
     del live.out_mine, live.out_c
 
-    n1_y = lay.over_y(live.n1_away)
+    n1_y = lay.over_y(live.n1_away[: live.n1_own.shape[0]])
     state = live.local_state + live.prods * live.state_in[:, None, :]
     mixed = (state * jax.nn.gelu(live.y_pre, approximate=True)).astype(BF16)
     mixed_two = mixed.reshape(two, half)
@@ -845,10 +846,10 @@
     gh_y = grad_hidden_of(pair + [lay.over_c(p) for p in pair], mlp_down)
     live.hold(n2_x=n2_x, n2_c=n2_c, n2_y=n2_y, n2_z_top=n2_z_top, gh_y=gh_y)
 
-    live.hold(n2_xc=lay.over_c(live.n2_x))
+    live.hold(n2_xc=lay.over_c(live.n2_x), n2_low=live.n2[cut:], n2_x_top=live.n2_x[:cut], n2_x_low=live.n2_x[cut:])
     cot_xz = lay.over_x(live.cot_z)
     n2_xy = lay.over_y(live.n2_x)
-    n2_z_low = lay.over_z(live.n2[cut:])
+    n2_z_low = lay.over_z(live.n2_low)
     hidden, grad_gate, grad_up, far, far_c = mlp_forward(
         [live.n2, live.n2_x, live.n2_c, live.n2_xc], live.gh_main, mlp_gate, mlp_up)
     del live.gh_main, live.n2_c
@@ -859,26 +860,29 @@
 
     arriving = lay.over_x(live.far)
     n2_yz = lay.over_y(live.n2_z)
-    n2_xz_top = lay.over_z(live.n2_x[:cut])
+    n2_xz_top = lay.over_z(live.n2_x_top)
     near, near_c, out, out_c = mlp_rest(*live.acts, mlp_gate, mlp_up, mlp_down, tokens)
     del live.far, live.far_c, live.n2_z_top, live.n2_z_low
-    live.hold(arriving=arriving, near=near, near_c=near_c, out=out, out_c=lay.over_c(out_c), n2_yz=n2_yz, n2_xz_top=n2_xz_top)
-
+    live.hold(arriving=arriving, near=near, near_c=near_c, out=out, out_c=out_c, n2_yz=n2_yz, n2_xz_top=n2_xz_top)
+
+    out_c = lay.over_c(live.out_c)
     grad_n2 = live.near + lay.over_c(live.near_c).astype(F32) + live.arriving.astype(F32)
     grad_mid_norm, grad_gain_two = norm_back(grad_n2, live.mid * live.inv2, live.inv2, live.gain_two)
     grad_mid = cot.astype(F32) + grad_mid_norm
     branch = grad_mid.astype(BF16)
+    live.out_c = out_c
     del live.near, live.near_c, live.arriving
     live.hold(grad_gain_two=grad_gain_two, grad_mid=grad_mid, branch=branch, branch_rel=order_f(branch))
 
     arriving = lay.over_x(live.branch_rel)
-    n2_xz_low = lay.over_z(live.n2_x[cut:])
+    n2_xz_low = lay.over_z(live.n2_x_low)
     cot_yz = lay.over_y(live.cot_z)
     live.hold(arriving=arriving, n2_xz_low=n2_xz_low, cot_yz=cot_yz, out_sum=live.out + live.out_c.astype(F32),
               n2_y_c=lay.over_c(live.n2_y),
               n2_xy_c=lay.over_c(live.n2_xy))
 
-    n1_yc = lay.over_y(live.n1_away_c)
+    rows_each = live.n1_own.shape[0]
+    n1_yc = lay.over_y(live.n1_away[rows_each:])
     cot_z_c, cot_xz_c = (lay.over_c(live.cot_z), lay.over_c(live.cot_xz))
     branch_x_rel = jnp.concatenate([live.arriving[:, half:], live.arriving[:, :half]], axis=1)
     both_rel = jnp.concatenate([live.branch_rel, branch_x_rel], 0)
@@ -904,6 +908,7 @@
             n2_z_c, n2_yz_c, cot_yz_c = (lay.over_c(live.n2_z), lay.over_c(live.n2_yz), lay.over_c(live.cot_yz))
     back_in = live.scan[3]
     del live.scan
+    live.n1_yc = lay.over_c(live.n1_yc)
     live.hold(back_in=back_in, cot_xyz=cot_xyz, n2_xyz=n2_xyz, part_y=part_y, n2_z_c=n2_z_c, n2_yz_c=n2_yz_c,
               cot_yz_c=cot_yz_c)
 
@@ -978,7 +983,10 @@
     sums = jnp.concatenate([grad_gain_one[None], live.grad_gain_two[None], rows_full], axis=0)
     sums = sums + lay.over_c(sums)
     del live.n1_near, live.n1_far, live.arriving, live.vec_rows, live.grad_gain_two, live.grad_mid
-    live.hold(sums=sums, gy_yc=lay.over_c(live.gy_y))
+    branch_far = half_of(order_f(live.branch_x_rel), x, half, 1)
+    branch_near = half_of(live.branch, x, half, 1)
+    del live.branch_x_rel
+    live.hold(sums=sums, gy_yc=lay.over_c(live.gy_y), branch_two=jnp.concatenate([branch_near, branch_far], axis=0))
 
     def over_columns(value):
         split = value.reshape(2, own80, half)
@@ -989,79 +997,74 @@
 
     sums = live.sums + lay.over_x(live.sums)
     sums = sums + lay.over_seq_bit(sums, 1)
+    branch_two_y = lay.over_y(live.branch_two)
+    sum_a = piece_sum(*live.piece_a)
     n1_all = [live.n1_own, live.n1_c, live.n1_y, live.n1_yc]
     in_y_part = sum_of_dots(n1_all, [live.gy, live.gy_c, live.gy_y, live.gy_yc])
-    branch_far = half_of(order_f(live.branch_x_rel), x, half, 1)
-    branch_near = half_of(live.branch, x, half, 1)
-    del live.gy, live.gy_c, live.gy_y, live.gy_yc, live.branch_x_rel
-    live.hold(in_y_part=in_y_part, sums=sums, branch_two=jnp.concatenate([branch_near, branch_far], axis=0))
-
-    sum_a = piece_sum(*live.piece_a)
-    in_y_own, in_y_come = owner_parts(live.in_y_part.reshape(nz, 2 * own80, half))
-    gx_y = lay.over_y(live.gx)
-    branch_two_y = lay.over_y(live.branch_two)
-    piece_b = weight_piece(*cuts[1])
-    del live.piece_a
-    live.hold(piece_b=piece_b, sum_a=sum_a, gx_y=gx_y, branch_two_y=branch_two_y, in_y_own=in_y_own,
-              in_y_come=in_y_come[:-1], in_y_part=live.in_y_part)
-
-    in_y_last = owner_parts(live.in_y_part.reshape(nz, 2 * own80, half))[1][-1:]
-    sum_b = piece_sum(*live.piece_b)
-    mixed_own, mixed_away, sent, sent_y = rows_by_device(
-        at_yc, [[live.mixed[0], live.mixed[1]], [live.mixed_x[:tokens], live.mixed_x[tokens:]]], n1_starts, own80)
-    in_x_part = sum_of_dots(n1_all, [live.gx, lay.over_c(live.gx), live.gx_y, lay.over_c(live.gx_y)])
     gate_part = gate_weight_grad(
         live.conv_low.reshape(two, half), live.gip.reshape(two, half), live.gdp.reshape(two, half)
     ).reshape(2, nz, 2, own80, 2 * BLK)
     pick = lambda value, at, axis: lax.dynamic_index_in_dim(value, at, axis, keepdims=False)
     gate_part = pick(gate_part, c, 2) + lay.over_c(pick(gate_part, 1 - c, 2).astype(BF16)).astype(F32)
     gate_y = lay.over_y(pick(gate_part, 1 - y, 0).astype(BF16))
-    del live.mixed, live.mixed_x, live.conv_low, live.gip, live.gdp, live.in_y_part, live.piece_b
-    live.hold(in_x_part=in_x_part, gate_keep=pick(gate_part, y, 0), gate_y=gate_y, sum_b=sum_b,
-              in_y_total=total_of(live.in_y_own, live.in_y_come + in_y_last),
-              mixed_own=mixed_own, mixed_away=mixed_away, mixed_c=lay.over_c(sent), mixed_away_c=lay.over_c(sent_y),
-              branch_c=lay.over_c(live.branch_two), branch_yc=lay.over_c(live.branch_two_y))
+    mixed_own, sent, mixed_away = rows_by_device(
+        at_yc, [[live.mixed[0], live.mixed[1]], [live.mixed_x[:tokens], live.mixed_x[tokens:]]], n1_starts, own80)
+    del live.gy, live.gy_c, live.gy_y, live.gy_yc, live.mixed, live.mixed_x, live.conv_low, live.gip, live.gdp
+    live.hold(in_y_part=in_y_part, sums=sums, sum_a=sum_a, branch_two_y=branch_two_y, gate_keep=pick(gate_part, y, 0), gate_y=gate_y,
+              mixed_own=mixed_own, mixed_away=mixed_away, mixed_c=lay.over_c(sent),
+              gx_c=lay.over_c(live.gx), branch_c=lay.over_c(live.branch_two))
+
+    in_y_own, in_y_come = owner_parts(live.in_y_part.reshape(nz, 2 * own80, half))
+    gx_y = lay.over_y(live.gx)
+    mixed_y = lay.over_y(live.mixed_away)
+    piece_b = weight_piece(*cuts[1])
+    del live.piece_a, live.mixed_away
+    del live.in_y_part
+    live.hold(piece_b=piece_b, gx_y=gx_y, mixed_y=mixed_y, in_y_own=in_y_own, in_y_come=in_y_come)
+
+    sum_b = piece_sum(*live.piece_b)
+    in_x_part = sum_of_dots(n1_all, [live.gx, live.gx_c, live.gx_y, lay.over_c(live.gx_y)])
+    out_part = sum_of_dots(
+        [live.mixed_own, live.mixed_c, live.mixed_y[:rows_each], lay.over_c(live.mixed_y[rows_each:])],
+        [live.branch_two, live.branch_c, live.branch_two_y, lay.over_c(live.branch_two_y)])
+    gate_part = (live.gate_keep + live.gate_y.astype(F32)).astype(BF16)
+    del live.piece_b, live.gate_keep, live.gate_y, live.mixed_own, live.mixed_c, live.mixed_y
+    live.hold(in_x_part=jnp.concatenate(
+        [in_x_part.reshape(nz, 2 * own80, half), gate_part.reshape(nz, own80 * 2 * BLK // half, half)], axis=1),
+        out_part=out_part, sum_b=sum_b, in_y_total=total_of(live.in_y_own, live.in_y_come),
+        out_far=live.out_sum[tokens:].astype(BF16))
     del live.in_y_own, live.in_y_come
 
-    mixed_y = (lay.over_y(live.mixed_away), lay.over_y(live.mixed_away_c))
-    in_y_grad = over_columns(live.in_y_total)
-    gate_part = (live.gate_keep + live.gate_y.astype(F32)).astype(BF16)
-    del live.gate_keep, live.gate_y, live.mixed_away, live.mixed_away_c, live.in_y_total
-    live.hold(in_x_part=jnp.concatenate(
-        [live.in_x_part.reshape(nz, 2 * own80, half), gate_part.reshape(nz, own80 * 2 * BLK // half, half)], axis=1),
-        mixed_y=mixed_y, in_y_grad=in_y_grad)
-
-    live.hold(out_part=sum_of_dots(
-        [live.mixed_own, live.mixed_c, *live.mixed_y],
-        [live.branch_two, live.branch_c, live.branch_two_y, live.branch_yc]))
-    del live.mixed_own, live.mixed_c, live.mixed_y
-
     in_x_own, in_x_come = owner_parts(live.in_x_part)
-    out_arriving = lay.over_x(live.out_sum[tokens:].astype(BF16))
+    out_arriving = lay.over_x(live.out_far)
+    sums = live.sums
+    sums_z = lay.over_seq_bit(sums, 2)
     piece_c = weight_piece(*cuts[2])
     del live.in_x_part
-    live.hold(piece_c=piece_c, in_x_own=in_x_own, in_x_come=in_x_come, out_arriving=out_arriving)
+    live.hold(piece_c=piece_c, in_x_own=in_x_own, in_x_come=in_x_come, out_arriving=out_arriving, sums=sums + sums_z)
 
     sum_c = piece_sum(*live.piece_c)
+    sums = live.sums
+    for bit in bits[2:]:
+        sums = sums + lay.over_seq_bit(sums, bit)
+    in_y_grad = over_columns(live.in_y_total)
+    live.hold(sum_c=sum_c, sums=sums, in_x_total=total_of(live.in_x_own, live.in_x_come), in_y_grad=in_y_grad,
+              output=(live.mid + live.out_sum[:tokens] + live.out_arriving.astype(F32)).astype(BF16)[None])
+
     out_own, out_come = owner_parts(live.out_part.reshape(nz, 2 * own80, half))
-    live.hold(sum_c=sum_c, out_own=out_own, out_come=out_come,
-              in_x_total=total_of(live.in_x_own, live.in_x_come),
-              output=(live.mid + live.out_sum[:tokens] + live.out_arriving.astype(F32)).astype(BF16)[None])
-
-    sums = live.sums
-    for bit in bits[1:]:
-        sums = sums + lay.over_seq_bit(sums, bit)
-    mlp_down_grad, mlp_gate_grad, mlp_up_grad = joined_columns([live.sum_b, live.sum_c, live.sum_a])
+    in_x_grad = over_columns(live.in_x_total[: 2 * own80])
+    mlp_grads = joined_columns([live.sum_b, live.sum_c, live.sum_a])
+    live.hold(out_own=out_own, out_come=out_come, mlp_grads=mlp_grads, in_x_grad=in_x_grad)
+    mlp_down_grad, mlp_gate_grad, mlp_up_grad = live.mlp_grads
 
     def final(z, y, x, c):
         at = ((x * 2 + y) * nz + z) * 2 + c
         s, f = (at // 4, at % 4)
         return (s // 2, s % 2, f // 2, f % 2)
 
-    in_x_grad = over_columns(live.in_x_total[: 2 * own80])
     out_grad = over_columns(total_of(live.out_own, live.out_come))
     gate_grad = lay.send(live.in_x_total[2 * own80 :].reshape(own80, 2 * BLK), final).astype(F32)
-    return (live.output, input_grad, sums, live.in_y_grad, in_x_grad, gate_grad, out_grad,
+    return (live.output, input_grad, live.sums, live.in_y_grad, live.in_x_grad, gate_grad, out_grad,
             mlp_gate_grad, mlp_up_grad, mlp_down_grad)
 
 

time: 633 us -> 599 us (0.946)
  waiting for transfers between devices: 160 us -> 126 us
  starting transfers between devices: 102 us -> 113 us
  other arithmetic: 50.9 us -> 42.3 us
    ppermute x102 -> x101, waiting for transfers between devices: 160 us -> 126 us  [send(): return lax.ppermute(value, ALL, self.pairs(target))]
    ppermute x102 -> x101, starting transfers between devices: 102 us -> 113 us  [send(): return lax.ppermute(value, ALL, self.pairs(target))]
    unnamed x189 -> x211, local copies, waits for them, and re-layouts: 18.7 us -> 21.6 us
  transfers between devices with their start and end apart: 102 -> 101, of which waited for: 36 -> 26; matrix products, arithmetic and copies ran while one was open for 14% -> 15% of each run, Pallas kernels for 31% -> 38%
where the time goes in v6:
time: 599 us; the launch traced here: 593 us
  Pallas kernels  231 us (39%)
  waiting for transfers between devices  126 us (21%)
  starting transfers between devices  113 us (19%)
  local copies, waits for them, and re-layouts  49.4 us (8%)
  other arithmetic  42.3 us (7%)
  matrix products  29.2 us (5%)
    ppermute x101, waiting for transfers between devices, send(): return lax.ppermute(value, ALL, self.pairs(target))  126 us
    ppermute x101, starting transfers between devices, send(): return lax.ppermute(value, ALL, self.pairs(target))  113 us
    pallas_call x3, Pallas kernels, mlp_weight_grads(): pl.pallas_call(body, grid_spec=pltpu.PrefetchScalarGridSpec(num_scalar_pr...  98.3 us
    pallas_call x2, Pallas kernels, grad_hidden_of(): pl.pallas_call(body, grid=(pl.cdiv(ff, BLK),), in_specs=[ANY] * count + [...  25.7 us
    pallas_call x1, Pallas kernels, mlp_forward(): pl.pallas_call(body, in_specs=[ANY] * (count + 3), out_shape=[act, act, a...  23.4 us
    unnamed x211, local copies, waits for them, and re-layouts  21.6 us
    pallas_call x3, Pallas kernels, by_head(): pl.pallas_call(body, grid=(heads,), in_specs=in_specs, out_specs=[spec(o....  20.7 us
    pallas_call x1, Pallas kernels, mlp_rest(): pl.pallas_call(body, grid=(width // block,), in_specs=[whole] * 3 + [weig...  19 us
  transfers between devices with their start and end apart: 101, of which 26 were waited for; matrix products, arithmetic and copies ran while one was open for 15% of the time, Pallas kernels for 38%

profile of v6, /device:TPU:2, one launch (start us, length us, event | category | flops | bytes accessed | tf_op | source)
XLA Modules:
  0.0 592.9 jit_solution(3578005414592513469)
XLA Ops:
  3.5 3.6 collective-permute-start
  18.3 14.0 %collective-permute-done.2 = bf16[16,2560]{1,0:T(8,128)(2,1)S(1)} collective-permute-done((bf16[16,2560]{1,0:T(8,128)(2,1)S(1)}, bf16[16,2560]{1,0:T(8,128)(2,1)S(1)}, u32[]{:S(2)}, u32[]{:S(2)}) %collective-permute-start.2) | collective-permute-done | bytes 81952 | tf_op jit(solution)/shard_map/ppermute | solution.py:82
  33.9 3.6 collective-permute-start.8
  39.7 3.2 convolution_convert_fusion
  48.3 7.4 %shard_map.195 = (bf16[2,128,1280]{2,1,0:T(8,128)(2,1)S(1)}, f32[2,128,1280]{2,1,0:T(8,128)S(1)}, f32[2,128,1280]{2,1,0:T(8,128)S(1)}, f32[2,128,1280]{2,1,0:T(8...) custom-call(f32[2,2]{1,0:T(2,128)S(1)} %pad_maximum_fusion.16.flags_ref, bf16[2,128,1280]{2,1,0:T(8,128)(2,1)S(1)} %bitcast.117, ...), custom_call_target="tpu_custom_call" | custom-call | flops 1 | bytes 1 | tf_op jit(solution)/shard_map/pallas_call | solution.py:266
  57.6 6.4 %collective-permute-done.9 = bf16[640,640]{1,0:T(8,128)(2,1)S(1)} collective-permute-done((bf16[640,640]{1,0:T(8,128)(2,1)S(1)}, bf16[640,640]{1,0:T(8,128)(2,1)S(1)}, u32[]{:S(2)}, u32[]{:S(2)}) %collective-permute-start.9) | collective-permute-done | bytes 819232 | tf_op jit(solution)/shard_map/ppermute | solution.py:82
  66.2 3.1 collective-permute-done.12
  70.0 3.4 shard_map.196
  73.5 4.0 collective-permute-start.16
  77.4 3.5 fusion.75
  82.3 4.3 fusion.76
  87.8 3.5 collective-permute-done.17
  91.4 2.8 collective-permute-done.15
  101.5 3.8 collective-permute-done.18.refs_2_
  107.9 12.8 %shard_map.197.refs_4_ = f32[512,1920]{1,0:T(8,128)} custom-call(bf16[128,2560]{1,0:T(8,128)(2,1)} %bitcast.144, bf16[128,2560]{1,0:T(8,128)(2,1)} %collective-permute-done.13.refs_1_, bf16[128,2560]{1,0:T(8,128)(2,1)} %copy-done.100, bf16[128,2560]{1,0:T(8,128)(2,1)} %collective-permute-done.22.refs_3_, bf16[2560,1920]{1,0:T(8,128)(2,1)} %refs_23_.5), custom_call_target="tpu_custom_call" | custom-call | flops 11699999744 | bytes 26000000 | tf_op jit(solution)/shard_map/pallas_call | solution.py:299
  133.7 12.9 %shard_map.198.refs_20_ = f32[512,1920]{1,0:T(8,128)} custom-call(bf16[128,2560]{1,0:T(8,128)(2,1)} %copy-done.80, bf16[128,2560]{1,0:T(8,128)(2,1)} %collective-permute-done.20.refs_1_.refs_3_, bf16[128,2560]{1,0:T(8,128)(2,1)} %copy-done.101, bf16[128,2560]{1,0:T(8,128)(2,1)} %collective-permute-done.25.refs_3_, bf16[2560,1920]{1,0:T(8,128)(2,1)} %refs_23_.5), custom_call_target="tpu_custom_call" | custom-call | flops 11699999744 | bytes 26000000 | tf_op jit(solution)/shard_map/pallas_call | solution.py:299
  155.4 23.4 %shard_map.199 = (bf16[512,1920]{1,0:T(8,128)(2,1)}, bf16[512,1920]{1,0:T(8,128)(2,1)}, bf16[512,1920]{1,0:T(8,128)(2,1)}, f32[128,2560]{1,0:T(8,128)}, bf16[128,2560]{1,0:T(8,128)(2,1)}) custom-call(bf16[128,2560]{1,0:T(8,128)(2,1)} %multiply_convert_fusion.refs_0_, bf16[128,2560]{1,0:T(8,128)(2,1)} %collective-permute-done.27.refs_1_, ...), custom_call_target="tpu_custom_call" | custom-call | flops 20700000256 | bytes 46000000 | tf_op jit(solution)/shard_map/pallas_call | solution.py:384
  185.9 19.0 %shard_map.200 = (f32[128,2560]{1,0:T(8,128)}, bf16[128,2560]{1,0:T(8,128)(2,1)}, f32[256,2560]{1,0:T(8,128)}, bf16[256,2560]{1,0:T(8,128)(2,1)}) custom-call(bf16[512,1920]{1,0:T(8,128)(2,1)} %get-tuple-element.2334.hid_ref.refs_24_, bf16[512,1920]{1,0:T(8,128)(2,1)} %get-tuple-element.2335.gg_ref.refs_25_, ...), custom_call_target="tpu_custom_call" | custom-call | flops 17100000256 | bytes 38000000 | tf_op jit(solution)/shard_map/pallas_call | solution.py:423
  209.5 2.8 fusion.59
  219.9 7.6 %collective-permute-done.43 = bf16[64,2560]{1,0:T(8,128)(2,1)S(1)} collective-permute-done((bf16[64,2560]{1,0:T(8,128)(2,1)S(1)}, bf16[64,2560]{1,0:T(8,128)(2,1)S(1)}, u32[]{:S(2)}, u32[]{:S(2)}) %collective-permute-start.43) | collective-permute-done | bytes 327712 | tf_op jit(solution)/shard_map/ppermute | solution.py:82
  236.7 5.4 shard_map.201
  249.1 4.5 collective-permute-start.49
  258.0 3.3 fusion.41
  263.5 2.8 convolution_add_fusion
  266.4 3.2 collective-permute-done.54.refs_7_.refs_9_
  269.6 6.8 %collective-permute-done.51.refs_7_.refs_17_ = bf16[128,2560]{1,0:T(8,128)(2,1)} collective-permute-done((bf16[128,2560]{1,0:T(8,128)(2,1)}, bf16[128,2560]{1,0:T(8,128)(2,1)}, u32[]{:S(2)}, u32[]{:S(2)}) %collective-permute-start.51) | collective-permute-done | bytes 655392 | tf_op jit(solution)/shard_map/ppermute | solution.py:82
  276.5 7.9 %shard_map.202 = (bf16[2,128,1280]{2,1,0:T(8,128)(2,1)S(1)}, bf16[2,128,1280]{2,1,0:T(8,128)(2,1)S(1)}, bf16[2,128,1280]{2,1,0:T(8,128)(2,1)S(1)}, f32[2,16,1280...) custom-call(f32[2,2]{1,0:T(2,128)S(1)} %pad_maximum_fusion.16.flags_ref, ...), custom_call_target="tpu_custom_call" | custom-call | flops 1 | bytes 1 | tf_op jit(solution)/shard_map/pallas_call | solution.py:266
  291.1 4.4 shard_map.203.refs_29_
  295.5 4.4 shard_map.204.refs_27_
  299.9 3.0 collective-permute-done.59
  303.6 3.4 fusion.39
  307.0 3.2 add_add_fusion
  314.3 24.4 %shard_map.205 = (f32[320,1152]{1,0:T(8,128)}, bf16[320,1152]{1,0:T(8,128)(2,1)}) custom-call(s32[3]{0:T(128)} %pad_add_fusion.1.place_ref, bf16[128,2560]{1,0:T(8,128)(2,1)} %collective-permute-done.28.refs_2_.refs_0_, bf16[128,2560]{1,0:T(8,128)(2,1)} %collective-permute-done.32.refs_3_.refs_1_, bf16[128,2560]{1,0:T(8,128)(2,1)} %copy-done.73, ...), custom_call_target="tpu_custom_call" | custom-call | flops 15299999744 | bytes 34000000 | tf_op jit(solution)/shard_map/pallas_call | solution.py:537
  343.7 5.3 shard_map.206
  355.0 3.0 collective-permute-done.76
  360.7 3.4 shard_map.208
  368.5 5.2 shard_map.207
  384.2 37.0 %shard_map.209 = (f32[320,2304]{1,0:T(8,128)}, bf16[320,2304]{1,0:T(8,128)(2,1)}) custom-call(s32[3]{0:T(128)} %pad_add_fusion.1.place_ref, bf16[128,2560]{1,0:T(8,128)(2,1)} %collective-permute-done.28.refs_2_.refs_0_, bf16[128,2560]{1,0:T(8,128)(2,1)} %collective-permute-done.32.refs_3_.refs_1_, bf16[128,2560]{1,0:T(8,128)(2,1)} %copy-done.73, ...), custom_call_target="tpu_custom_call" | custom-call | flops 31499999232 | bytes 70000000 | tf_op jit(solution)/shard_map/pallas_call | solution.py:537
  429.1 5.1 shard_map.210
  435.0 5.2 shard_map.211
  441.7 12.9 %collective-permute-done.86.refs_1_ = bf16[320,2304]{1,0:T(8,128)(2,1)} collective-permute-done((bf16[320,2304]{1,0:T(8,128)(2,1)}, bf16[320,2304]{1,0:T(8,128)(2,1)}, u32[]{:S(2)}, u32[]{:S(2)}) %collective-permute-start.86) | collective-permute-done | bytes 1474592 | tf_op jit(solution)/shard_map/ppermute | solution.py:82
  457.9 13.7 %collective-permute-start.89 = (bf16[192,1280]{1,0:T(8,128)(2,1)}, bf16[192,1280]{1,0:T(8,128)(2,1)}, u32[]{:S(2)}, u32[]{:S(2)}) collective-permute-start(bf16[192,1280]{1,0:T(8,128)(2,1)} %get-tuple-element.2430), channel_id=1, source_target_pairs={{0,24},{1,25},{2,26},{3,27},{4,28},{5,29},{6,30},{7,31},{8,0},{9,1... | collective-permute-start | bytes 1474568 | tf_op jit(solution)/shard_map/ppermute | solution.py:82
  472.7 37.0 %shard_map.212 = (f32[320,2304]{1,0:T(8,128)}, bf16[320,2304]{1,0:T(8,128)(2,1)}) custom-call(s32[3]{0:T(128)} %pad_add_fusion.1.place_ref, bf16[128,2560]{1,0:T(8,128)(2,1)} %collective-permute-done.28.refs_2_.refs_0_, bf16[128,2560]{1,0:T(8,128)(2,1)} %collective-permute-done.32.refs_3_.refs_1_, bf16[128,2560]{1,0:T(8,128)(2,1)} %copy-done.73, ...), custom_call_target="tpu_custom_call" | custom-call | flops 31499999232 | bytes 70000000 | tf_op jit(solution)/shard_map/pallas_call | solution.py:537
  517.7 26.9 %collective-permute-done.94 = f32[10,2560]{1,0:T(8,128)S(1)} collective-permute-done((f32[10,2560]{1,0:T(8,128)S(1)}, f32[10,2560]{1,0:T(8,128)S(1)}, u32[]{:S(2)}, u32[]{:S(2)}) %collective-permute-start.94) | collective-permute-done | bytes 102432 | tf_op jit(solution)/shard_map/ppermute | solution.py:82
  550.8 2.9 collective-permute-start.98
  553.7 7.2 %shard_map.213 = (f32[320,1920]{1,0:T(8,128)}, f32[320,1920]{1,0:T(8,128)}, f32[320,1920]{1,0:T(8,128)}) custom-call(f32[320,2304]{1,0:T(8,128)} %get-tuple-element.2393.refs_0_, bf16[320,2304]{1,0:T(8,128)(2,1)} %collective-permute-done.86.refs_1_, f32[320,2304]{1,0:T(8,128)} %get-tuple-element.2395.refs_2_, bf16[320,2304]{1,0:T(8,128)(2,1)} %copy-done.59, ...), custom_call_target="tpu_custom_call" | custom-call | flops 1 | bytes 1 | tf_op jit(solution)/shard_map/pallas_call | solution.py:622
  561.9 11.4 %collective-permute-done.97 = bf16[160,1280]{1,0:T(8,128)(2,1)S(1)} collective-permute-done((bf16[160,1280]{1,0:T(8,128)(2,1)S(1)}, bf16[160,1280]{1,0:T(8,128)(2,1)S(1)}, u32[]{:S(2)}, u32[]{:S(2)}) %collective-permute-start.97) | collective-permute-done | bytes 409632 | tf_op jit(solution)/shard_map/ppermute | solution.py:82
  573.4 10.9 %collective-permute-start.99 = (bf16[80,512]{1,0:T(8,128)(2,1)S(1)}, bf16[80,512]{1,0:T(8,128)(2,1)S(1)}, u32[]{:S(2)}, u32[]{:S(2)}) collective-permute-start(bf16[80,512]{1,0:T(8,128)(2,1)S(1)} %reshape.161), channel_id=1, source_target_pairs={{0,0},{1,1},{2,16},{3,17},{4,8},{5,9},{6,24},{7,25},{8,2},{9,3},{1... | collective-permute-start | bytes 245768 | tf_op jit(solution)/shard_map/ppermute | solution.py:82
  (532 shorter events, 181.2 us)
Async XLA Ops:
  7.0 25.3 %collective-permute-start.4 = (bf16[1280,128]{1,0:T(8,128)(2,1)}, bf16[1280,128]{1,0:T(8,128)(2,1)}, u32[]{:S(2)}, u32[]{:S(2)}) collective-permute-start(bf16[1280,128]{1,0:T(8,128)(2,1)} %constant_dynamic-slice_fusion.5), channel_id=1, source_target_pairs={{0,2},{1,3},{2,0},{3,1},{4,6},{5,7},{6,4},{7,5},{8,10},{9,11},{10,... | collective-permute-start | bytes 983048 | tf_op jit(solution)/shard_map/ppermute | solution.py:82
  7.6 29.9 %collective-permute-start.6 = (bf16[2560,640]{1,0:T(8,128)(2,1)}, bf16[2560,640]{1,0:T(8,128)(2,1)}, u32[]{:S(2)}, u32[]{:S(2)}) collective-permute-start(bf16[2560,640]{1,0:T(8,128)(2,1)} %param.17), channel_id=1, source_target_pairs={{0,1},{1,0},{2,3},{3,2},{4,5},{5,4},{6,7},{7,6},{8,9},{9,8},{10,11... | collective-permute-start | bytes 9830408 | tf_op jit(solution)/shard_map/ppermute | solution.py:82
  11.0 26.6 %collective-permute-start.5 = (bf16[128,2560]{1,0:T(8,128)(2,1)}, bf16[128,2560]{1,0:T(8,128)(2,1)S(1)}, u32[]{:S(2)}, u32[]{:S(2)}) collective-permute-start(bf16[128,2560]{1,0:T(8,128)(2,1)} %fusion.20.refs_0_), channel_id=1, source_target_pairs={{0,2},{1,3},{2,0},{3,1},{4,6},{5,7},{6,4},{7,5},{8,10},{9,11},{10,... | collective-permute-start | bytes 1966088 | tf_op jit(solution)/shard_map/ppermute | solution.py:82
  12.4 25.1 %collective-permute-start.1 = (bf16[128,2560]{1,0:T(8,128)(2,1)}, bf16[128,2560]{1,0:T(8,128)(2,1)S(1)}, u32[]{:S(2)}, u32[]{:S(2)}) collective-permute-start(bf16[128,2560]{1,0:T(8,128)(2,1)} %bitcast.142), channel_id=1, source_target_pairs={{0,4},{1,5},{2,6},{3,7},{4,0},{5,1},{6,2},{7,3},{8,12},{9,13},{10,... | collective-permute-start | bytes 1966088 | tf_op jit(solution)/shard_map/ppermute | solution.py:82
  15.3 16.9 %collective-permute-start.2 = (bf16[16,2560]{1,0:T(8,128)(2,1)S(1)}, bf16[16,2560]{1,0:T(8,128)(2,1)S(1)}, u32[]{:S(2)}, u32[]{:S(2)}) collective-permute-start(bf16[16,2560]{1,0:T(8,128)(2,1)S(1)} %fusion.48), channel_id=1, source_target_pairs={{0,2},{1,3},{2,0},{3,1},{4,6},{5,7},{6,4},{7,5},{8,10},{9,11},{10,... | collective-permute-start | bytes 245768 | tf_op jit(solution)/shard_map/ppermute | solution.py:82
  32.3 25.3 %collective-permute-start.11 = (bf16[2560,640]{1,0:T(8,128)(2,1)S(1)}, bf16[2560,640]{1,0:T(8,128)(2,1)}, u32[]{:S(2)}, u32[]{:S(2)}) collective-permute-start(bf16[2560,640]{1,0:T(8,128)(2,1)S(1)} %copy-done.45), channel_id=1, source_target_pairs={{0,1},{1,0},{2,3},{3,2},{4,5},{5,4},{6,7},{7,6},{8,9},{9,8},{10,11... | collective-permute-start | bytes 9830408 | tf_op jit(solution)/shard_map/ppermute | solution.py:82
  33.9 23.7 %collective-permute-start.8 = (bf16[128,2560]{1,0:T(8,128)(2,1)S(1)}, bf16[128,2560]{1,0:T(8,128)(2,1)}, u32[]{:S(2)}, u32[]{:S(2)}) collective-permute-start(bf16[128,2560]{1,0:T(8,128)(2,1)S(1)} %bitcast.146), channel_id=1, source_target_pairs={{0,24},{1,25},{2,26},{3,27},{4,28},{5,29},{6,30},{7,31},{8,16},{9,... | collective-permute-start | bytes 1966088 | tf_op jit(solution)/shard_map/ppermute | solution.py:82
  43.3 20.7 %collective-permute-start.9 = (bf16[640,640]{1,0:T(8,128)(2,1)S(1)}, bf16[640,640]{1,0:T(8,128)(2,1)S(1)}, u32[]{:S(2)}, u32[]{:S(2)}) collective-permute-start(bf16[640,640]{1,0:T(8,128)(2,1)S(1)} %constant_dynamic-slice_fusion.3), channel_id=1, source_target_pairs={{0,2},{1,3},{2,0},{3,1},{4,6},{5,7},{6,4},{7,5},{8,10},{9,11},{10,... | collective-permute-start | bytes 2457608 | tf_op jit(solution)/shard_map/ppermute | solution.py:82
  43.9 20.1 %collective-permute-start.10 = (bf16[1280,640]{1,0:T(8,128)(2,1)S(1)}, bf16[1280,640]{1,0:T(8,128)(2,1)S(1)}, u32[]{:S(2)}, u32[]{:S(2)}) collective-permute-start(bf16[1280,640]{1,0:T(8,128)(2,1)S(1)} %constant_dynamic-slice_fusion.2), channel_id=1, source_target_pairs={{0,1},{1,0},{2,3},{3,2},{4,5},{5,4},{6,7},{7,6},{8,9},{9,8},{10,11... | collective-permute-start | bytes 4915208 | tf_op jit(solution)/shard_map/ppermute | solution.py:82
  69.4 25.5 %collective-permute-start.13 = (bf16[128,2560]{1,0:T(8,128)(2,1)}, bf16[128,2560]{1,0:T(8,128)(2,1)}, u32[]{:S(2)}, u32[]{:S(2)}) collective-permute-start(bf16[128,2560]{1,0:T(8,128)(2,1)} %bitcast.143), channel_id=1, source_target_pairs={{0,2},{1,3},{2,0},{3,1},{4,6},{5,7},{6,4},{7,5},{8,10},{9,11},{10,... | collective-permute-start | bytes 1966088 | tf_op jit(solution)/shard_map/ppermute | solution.py:82
  73.4 21.5 %collective-permute-start.14 = (bf16[640,256]{1,0:T(8,128)(2,1)}, bf16[640,256]{1,0:T(8,128)(2,1)S(1)}, u32[]{:S(2)}, u32[]{:S(2)}) collective-permute-start(bf16[640,256]{1,0:T(8,128)(2,1)} %get-tuple-element.1301), channel_id=1, source_target_pairs={{0,1},{1,0},{2,3},{3,2},{4,5},{5,4},{6,7},{7,6},{8,9},{9,8},{10,11... | collective-permute-start | bytes 983048 | tf_op jit(solution)/shard_map/ppermute | solution.py:82
  73.4 20.9 %collective-permute-start.15 = (bf16[640,640]{1,0:T(8,128)(2,1)}, bf16[640,640]{1,0:T(8,128)(2,1)S(1)}, u32[]{:S(2)}, u32[]{:S(2)}) collective-permute-start(bf16[640,640]{1,0:T(8,128)(2,1)} %copy-done.70), channel_id=1, source_target_pairs={{0,4},{1,5},{2,6},{3,7},{4,0},{5,1},{6,2},{7,3},{8,12},{9,13},{10,... | collective-permute-start | bytes 2457608 | tf_op jit(solution)/shard_map/ppermute | solution.py:82
  105.3 17.5 %collective-permute-start.20 = (bf16[128,2560]{1,0:T(8,128)(2,1)}, bf16[128,2560]{1,0:T(8,128)(2,1)}, u32[]{:S(2)}, u32[]{:S(2)}) collective-permute-start(bf16[128,2560]{1,0:T(8,128)(2,1)} %collective-permute-done.13.refs_1_), channel_id=1, source_target_pairs={{0,4},{1,5},{2,6},{3,7},{4,0},{5,1},{6,2},{7,3},{8,12},{9,13},{10,... | collective-permute-start | bytes 1966088 | tf_op jit(solution)/shard_map/ppermute | solution.py:82
  105.5 17.2 %collective-permute-start.23 = (bf16[128,2560]{1,0:T(8,128)(2,1)}, bf16[128,2560]{1,0:T(8,128)(2,1)}, u32[]{:S(2)}, u32[]{:S(2)}) collective-permute-start(bf16[128,2560]{1,0:T(8,128)(2,1)} %fusion.22), channel_id=1, source_target_pairs={{0,2},{1,3},{2,0},{3,1},{4,6},{5,7},{6,4},{7,5},{8,10},{9,11},{10,... | collective-permute-start | bytes 1966088 | tf_op jit(solution)/shard_map/ppermute | solution.py:82
  127.7 19.0 %collective-permute-start.26 = (bf16[128,2560]{1,0:T(8,128)(2,1)}, bf16[128,2560]{1,0:T(8,128)(2,1)}, u32[]{:S(2)}, u32[]{:S(2)}) collective-permute-start(bf16[128,2560]{1,0:T(8,128)(2,1)} %multiply_convert_fusion.refs_0_), channel_id=1, source_target_pairs={{0,1},{1,0},{2,3},{3,2},{4,5},{5,4},{6,7},{7,6},{8,9},{9,8},{10,11... | collective-permute-start | bytes 1966088 | tf_op jit(solution)/shard_map/ppermute | solution.py:82
  127.7 19.0 %collective-permute-start.27 = (bf16[128,2560]{1,0:T(8,128)(2,1)}, bf16[128,2560]{1,0:T(8,128)(2,1)}, u32[]{:S(2)}, u32[]{:S(2)}) collective-permute-start(bf16[128,2560]{1,0:T(8,128)(2,1)} %multiply_convert_fusion.refs_0_), channel_id=1, source_target_pairs={{0,2},{1,3},{2,0},{3,1},{4,6},{5,7},{6,4},{7,5},{8,10},{9,11},{10,... | collective-permute-start | bytes 1966088 | tf_op jit(solution)/shard_map/ppermute | solution.py:82
  129.2 17.5 %collective-permute-start.28 = (bf16[128,2560]{1,0:T(8,128)(2,1)}, bf16[128,2560]{1,0:T(8,128)(2,1)}, u32[]{:S(2)}, u32[]{:S(2)}) collective-permute-start(bf16[128,2560]{1,0:T(8,128)(2,1)} %multiply_convert_fusion.refs_0_), channel_id=1, source_target_pairs={{0,4},{1,5},{2,6},{3,7},{4,0},{5,1},{6,2},{7,3},{8,12},{9,13},{10,... | collective-permute-start | bytes 1966088 | tf_op jit(solution)/shard_map/ppermute | solution.py:82
  151.0 27.9 %collective-permute-start.31 = (bf16[128,2560]{1,0:T(8,128)(2,1)}, bf16[128,2560]{1,0:T(8,128)(2,1)}, u32[]{:S(2)}, u32[]{:S(2)}) collective-permute-start(bf16[128,2560]{1,0:T(8,128)(2,1)} %collective-permute-done.8.refs_4_.refs_12_), channel_id=1, source_target_pairs={{0,2},{1,3},{2,0},{3,1},{4,6},{5,7},{6,4},{7,5},{8,10},{9,11},{10,... | collective-permute-start | bytes 1966088 | tf_op jit(solution)/shard_map/ppermute | solution.py:82
  151.5 27.3 %collective-permute-start.32 = (bf16[128,2560]{1,0:T(8,128)(2,1)}, bf16[128,2560]{1,0:T(8,128)(2,1)}, u32[]{:S(2)}, u32[]{:S(2)}) collective-permute-start(bf16[128,2560]{1,0:T(8,128)(2,1)} %collective-permute-done.27.refs_1_), channel_id=1, source_target_pairs={{0,4},{1,5},{2,6},{3,7},{4,0},{5,1},{6,2},{7,3},{8,12},{9,13},{10,... | collective-permute-start | bytes 1966088 | tf_op jit(solution)/shard_map/ppermute | solution.py:82
  153.0 25.8 %collective-permute-start.33 = (bf16[64,2560]{1,0:T(8,128)(2,1)}, bf16[64,2560]{1,0:T(8,128)(2,1)}, u32[]{:S(2)}, u32[]{:S(2)}) collective-permute-start(bf16[64,2560]{1,0:T(8,128)(2,1)} %slice.252), channel_id=1, source_target_pairs={{0,24},{1,25},{2,26},{3,27},{4,28},{5,29},{6,30},{7,31},{8,16},{9,... | collective-permute-start | bytes 983048 | tf_op jit(solution)/shard_map/ppermute | solution.py:82
  182.4 22.4 %collective-permute-start.35 = (bf16[128,2560]{1,0:T(8,128)(2,1)}, bf16[128,2560]{1,0:T(8,128)(2,1)}, u32[]{:S(2)}, u32[]{:S(2)}) collective-permute-start(bf16[128,2560]{1,0:T(8,128)(2,1)} %add_convert_fusion.1), channel_id=1, source_target_pairs={{0,2},{1,3},{2,0},{3,1},{4,6},{5,7},{6,4},{7,5},{8,10},{9,11},{10,... | collective-permute-start | bytes 1966088 | tf_op jit(solution)/shard_map/ppermute | solution.py:82
  183.9 21.0 %collective-permute-start.36 = (bf16[64,2560]{1,0:T(8,128)(2,1)}, bf16[64,2560]{1,0:T(8,128)(2,1)}, u32[]{:S(2)}, u32[]{:S(2)}) collective-permute-start(bf16[64,2560]{1,0:T(8,128)(2,1)} %get-tuple-element.1621), channel_id=1, source_target_pairs={{0,24},{1,25},{2,26},{3,27},{4,28},{5,29},{6,30},{7,31},{8,16},{9,... | collective-permute-start | bytes 983048 | tf_op jit(solution)/shard_map/ppermute | solution.py:82
  185.3 19.5 %collective-permute-start.37 = (bf16[128,2560]{1,0:T(8,128)(2,1)}, bf16[128,2560]{1,0:T(8,128)(2,1)}, u32[]{:S(2)}, u32[]{:S(2)}) collective-permute-start(bf16[128,2560]{1,0:T(8,128)(2,1)} %pad_maximum_fusion.4.refs_4_), channel_id=1, source_target_pairs={{0,4},{1,5},{2,6},{3,7},{4,0},{5,1},{6,2},{7,3},{8,12},{9,13},{10,... | collective-permute-start | bytes 1966088 | tf_op jit(solution)/shard_map/ppermute | solution.py:82
  213.3 16.8 %collective-permute-start.40 = (bf16[128,2560]{1,0:T(8,128)(2,1)S(1)}, bf16[128,2560]{1,0:T(8,128)(2,1)S(1)}, u32[]{:S(2)}, u32[]{:S(2)}) collective-permute-start(bf16[128,2560]{1,0:T(8,128)(2,1)S(1)} %maximum_select_fusion.8), channel_id=1, source_target_pairs={{0,2},{1,3},{2,0},{3,1},{4,6},{5,7},{6,4},{7,5},{8,10},{9,11},{10,... | collective-permute-start | bytes 1966088 | tf_op jit(solution)/shard_map/ppermute | solution.py:82
  213.9 16.7 %collective-permute-start.41 = (bf16[128,2560]{1,0:T(8,128)(2,1)}, bf16[128,2560]{1,0:T(8,128)(2,1)S(1)}, u32[]{:S(2)}, u32[]{:S(2)}) collective-permute-start(bf16[128,2560]{1,0:T(8,128)(2,1)} %collective-permute-done.8.refs_4_.refs_12_), channel_id=1, source_target_pairs={{0,4},{1,5},{2,6},{3,7},{4,0},{5,1},{6,2},{7,3},{8,12},{9,13},{10,... | collective-permute-start | bytes 1966088 | tf_op jit(solution)/shard_map/ppermute | solution.py:82
  285.7 17.2 %collective-permute-start.59 = (bf16[256,1280]{1,0:T(8,128)(2,1)}, bf16[256,1280]{1,0:T(8,128)(2,1)}, u32[]{:S(2)}, u32[]{:S(2)}) collective-permute-start(bf16[256,1280]{1,0:T(8,128)(2,1)} %pad_maximum_fusion.6), channel_id=1, source_target_pairs={{0,2},{1,3},{2,0},{3,1},{4,6},{5,7},{6,4},{7,5},{8,10},{9,11},{10,... | collective-permute-start | bytes 1966088 | tf_op jit(solution)/shard_map/ppermute | solution.py:82
  311.3 27.4 %collective-permute-start.65 = (bf16[256,1280]{1,0:T(8,128)(2,1)S(1)}, bf16[256,1280]{1,0:T(8,128)(2,1)}, u32[]{:S(2)}, u32[]{:S(2)}) collective-permute-start(bf16[256,1280]{1,0:T(8,128)(2,1)S(1)} %bitcast.123), channel_id=1, source_target_pairs={{0,1},{1,0},{2,3},{3,2},{4,5},{5,4},{6,7},{7,6},{8,9},{9,8},{10,11... | collective-permute-start | bytes 1966088 | tf_op jit(solution)/shard_map/ppermute | solution.py:82
  311.4 27.3 %collective-permute-start.66 = (bf16[256,1280]{1,0:T(8,128)(2,1)S(1)}, bf16[256,1280]{1,0:T(8,128)(2,1)}, u32[]{:S(2)}, u32[]{:S(2)}) collective-permute-start(bf16[256,1280]{1,0:T(8,128)(2,1)S(1)} %bitcast.124), channel_id=1, source_target_pairs={{0,4},{1,5},{2,6},{3,7},{4,0},{5,1},{6,2},{7,3},{8,12},{9,13},{10,... | collective-permute-start | bytes 1966088 | tf_op jit(solution)/shard_map/ppermute | solution.py:82
  312.9 25.7 %collective-permute-start.64 = (bf16[128,2560]{1,0:T(8,128)(2,1)}, bf16[128,2560]{1,0:T(8,128)(2,1)S(1)}, u32[]{:S(2)}, u32[]{:S(2)}) collective-permute-start(bf16[128,2560]{1,0:T(8,128)(2,1)} %slice.379), channel_id=1, source_target_pairs={{0,2},{1,3},{2,0},{3,1},{4,6},{5,7},{6,4},{7,5},{8,10},{9,11},{10,... | collective-permute-start | bytes 1966088 | tf_op jit(solution)/shard_map/ppermute | solution.py:82
  342.2 32.4 %collective-permute-start.69 = (bf16[256,1280]{1,0:T(8,128)(2,1)}, bf16[256,1280]{1,0:T(8,128)(2,1)}, u32[]{:S(2)}, u32[]{:S(2)}) collective-permute-start(bf16[256,1280]{1,0:T(8,128)(2,1)} %pad_maximum_fusion.8.refs_4_), channel_id=1, source_target_pairs={{0,1},{1,0},{2,3},{3,2},{4,5},{5,4},{6,7},{7,6},{8,9},{9,8},{10,11... | collective-permute-start | bytes 1966088 | tf_op jit(solution)/shard_map/ppermute | solution.py:82
  342.4 32.3 %collective-permute-start.70 = (bf16[256,1280]{1,0:T(8,128)(2,1)}, bf16[256,1280]{1,0:T(8,128)(2,1)}, u32[]{:S(2)}, u32[]{:S(2)}) collective-permute-start(bf16[256,1280]{1,0:T(8,128)(2,1)} %pad_maximum_fusion.8.refs_4_), channel_id=1, source_target_pairs={{0,4},{1,5},{2,6},{3,7},{4,0},{5,1},{6,2},{7,3},{8,12},{9,13},{10,... | collective-permute-start | bytes 1966088 | tf_op jit(solution)/shard_map/ppermute | solution.py:82
  353.0 21.7 %collective-permute-start.75 = (bf16[320,1152]{1,0:T(8,128)(2,1)}, bf16[320,1152]{1,0:T(8,128)(2,1)}, u32[]{:S(2)}, u32[]{:S(2)}) collective-permute-start(bf16[320,1152]{1,0:T(8,128)(2,1)} %get-tuple-element.2235), channel_id=1, source_target_pairs={{0,8},{1,9},{2,10},{3,11},{4,12},{5,13},{6,14},{7,15},{8,0},{9,1},... | collective-permute-start | bytes 2211848 | tf_op jit(solution)/shard_map/ppermute | solution.py:82
  376.9 44.4 %collective-permute-start.78 = (bf16[256,1280]{1,0:T(8,128)(2,1)S(1)}, bf16[256,1280]{1,0:T(8,128)(2,1)S(1)}, u32[]{:S(2)}, u32[]{:S(2)}) collective-permute-start(bf16[256,1280]{1,0:T(8,128)(2,1)S(1)} %bitcast.139), channel_id=1, source_target_pairs={{0,4},{1,5},{2,6},{3,7},{4,0},{5,1},{6,2},{7,3},{8,12},{9,13},{10,... | collective-permute-start | bytes 1966088 | tf_op jit(solution)/shard_map/ppermute | solution.py:82
  379.1 42.1 %collective-permute-start.79 = (bf16[160,1280]{1,0:T(8,128)(2,1)S(1)}, bf16[160,1280]{1,0:T(8,128)(2,1)S(1)}, u32[]{:S(2)}, u32[]{:S(2)}) collective-permute-start(bf16[160,1280]{1,0:T(8,128)(2,1)S(1)} %get-tuple-element.2440), channel_id=1, source_target_pairs={{0,8},{1,9},{2,10},{3,11},{4,12},{5,13},{6,14},{7,15},{8,16},{9,17... | collective-permute-start | bytes 1228808 | tf_op jit(solution)/shard_map/ppermute | solution.py:82
  380.2 41.0 %collective-permute-start.80 = (bf16[160,1280]{1,0:T(8,128)(2,1)S(1)}, bf16[160,1280]{1,0:T(8,128)(2,1)S(1)}, u32[]{:S(2)}, u32[]{:S(2)}) collective-permute-start(bf16[160,1280]{1,0:T(8,128)(2,1)S(1)} %get-tuple-element.2439), channel_id=1, source_target_pairs={{0,16},{1,17},{2,18},{3,19},{4,20},{5,21},{6,22},{7,23},{8,24},{9,... | collective-permute-start | bytes 1228808 | tf_op jit(solution)/shard_map/ppermute | solution.py:82
  380.7 40.5 %collective-permute-start.81 = (bf16[160,1280]{1,0:T(8,128)(2,1)S(1)}, bf16[160,1280]{1,0:T(8,128)(2,1)S(1)}, u32[]{:S(2)}, u32[]{:S(2)}) collective-permute-start(bf16[160,1280]{1,0:T(8,128)(2,1)S(1)} %get-tuple-element.2438), channel_id=1, source_target_pairs={{0,24},{1,25},{2,26},{3,27},{4,28},{5,29},{6,30},{7,31},{8,0},{9,1... | collective-permute-start | bytes 1228808 | tf_op jit(solution)/shard_map/ppermute | solution.py:82
  383.1 39.1 %collective-permute-start.82 = (bf16[1280,256]{1,0:T(8,128)(2,1)}, bf16[1280,256]{1,0:T(8,128)(2,1)}, u32[]{:S(2)}, u32[]{:S(2)}) collective-permute-start(bf16[1280,256]{1,0:T(8,128)(2,1)} %get-tuple-element.2263), channel_id=1, source_target_pairs={{0,4},{1,5},{2,6},{3,7},{4,0},{5,1},{6,2},{7,3},{8,12},{9,13},{10,... | collective-permute-start | bytes 1966088 | tf_op jit(solution)/shard_map/ppermute | solution.py:82
  422.2 32.5 %collective-permute-start.86 = (bf16[320,2304]{1,0:T(8,128)(2,1)}, bf16[320,2304]{1,0:T(8,128)(2,1)}, u32[]{:S(2)}, u32[]{:S(2)}) collective-permute-start(bf16[320,2304]{1,0:T(8,128)(2,1)} %get-tuple-element.2332), channel_id=1, source_target_pairs={{0,8},{1,9},{2,10},{3,11},{4,12},{5,13},{6,14},{7,15},{8,0},{9,1},... | collective-permute-start | bytes 4423688 | tf_op jit(solution)/shard_map/ppermute | solution.py:82
  455.8 53.9 %collective-permute-start.87 = (bf16[192,1280]{1,0:T(8,128)(2,1)}, bf16[192,1280]{1,0:T(8,128)(2,1)}, u32[]{:S(2)}, u32[]{:S(2)}) collective-permute-start(bf16[192,1280]{1,0:T(8,128)(2,1)} %get-tuple-element.2432), channel_id=1, source_target_pairs={{0,8},{1,9},{2,10},{3,11},{4,12},{5,13},{6,14},{7,15},{8,16},{9,17... | collective-permute-start | bytes 1474568 | tf_op jit(solution)/shard_map/ppermute | solution.py:82
  456.5 53.3 %collective-permute-start.88 = (bf16[192,1280]{1,0:T(8,128)(2,1)}, bf16[192,1280]{1,0:T(8,128)(2,1)}, u32[]{:S(2)}, u32[]{:S(2)}) collective-permute-start(bf16[192,1280]{1,0:T(8,128)(2,1)} %get-tuple-element.2431), channel_id=1, source_target_pairs={{0,16},{1,17},{2,18},{3,19},{4,20},{5,21},{6,22},{7,23},{8,24},{9,... | collective-permute-start | bytes 1474568 | tf_op jit(solution)/shard_map/ppermute | solution.py:82
  457.9 51.9 %collective-permute-start.89 = (bf16[192,1280]{1,0:T(8,128)(2,1)}, bf16[192,1280]{1,0:T(8,128)(2,1)}, u32[]{:S(2)}, u32[]{:S(2)}) collective-permute-start(bf16[192,1280]{1,0:T(8,128)(2,1)} %get-tuple-element.2430), channel_id=1, source_target_pairs={{0,24},{1,25},{2,26},{3,27},{4,28},{5,29},{6,30},{7,31},{8,0},{9,1... | collective-permute-start | bytes 1474568 | tf_op jit(solution)/shard_map/ppermute | solution.py:82
  471.6 38.2 %collective-permute-start.90 = (bf16[128,2560]{1,0:T(8,128)(2,1)}, bf16[128,2560]{1,0:T(8,128)(2,1)}, u32[]{:S(2)}, u32[]{:S(2)}) collective-permute-start(bf16[128,2560]{1,0:T(8,128)(2,1)} %slice.378), channel_id=1, source_target_pairs={{0,2},{1,3},{2,0},{3,1},{4,6},{5,7},{6,4},{7,5},{8,10},{9,11},{10,... | collective-permute-start | bytes 1966088 | tf_op jit(solution)/shard_map/ppermute | solution.py:82
  472.2 37.5 %collective-permute-start.91 = (f32[10,2560]{1,0:T(8,128)S(1)}, f32[10,2560]{1,0:T(8,128)S(1)}, u32[]{:S(2)}, u32[]{:S(2)}) collective-permute-start(f32[10,2560]{1,0:T(8,128)S(1)} %add.370), channel_id=1, source_target_pairs={{0,8},{1,9},{2,10},{3,11},{4,12},{5,13},{6,14},{7,15},{8,0},{9,1},... | collective-permute-start | bytes 307208 | tf_op jit(solution)/shard_map/ppermute | solution.py:82
  509.8 35.5 %collective-permute-start.92 = (bf16[80,1280]{1,0:T(8,128)(2,1)S(1)}, bf16[80,1280]{1,0:T(8,128)(2,1)S(1)}, u32[]{:S(2)}, u32[]{:S(2)}) collective-permute-start(bf16[80,1280]{1,0:T(8,128)(2,1)S(1)} %get-tuple-element.2480), channel_id=1, source_target_pairs={{0,2},{1,3},{2,0},{3,1},{4,6},{5,7},{6,4},{7,5},{8,10},{9,11},{10,... | collective-permute-start | bytes 614408 | tf_op jit(solution)/shard_map/ppermute | solution.py:82
  510.8 35.5 %collective-permute-start.93 = (bf16[320,2304]{1,0:T(8,128)(2,1)}, bf16[320,2304]{1,0:T(8,128)(2,1)S(1)}, u32[]{:S(2)}, u32[]{:S(2)}) collective-permute-start(bf16[320,2304]{1,0:T(8,128)(2,1)} %get-tuple-element.2384), channel_id=1, source_target_pairs={{0,8},{1,9},{2,10},{3,11},{4,12},{5,13},{6,14},{7,15},{8,0},{9,1},... | collective-permute-start | bytes 4423688 | tf_op jit(solution)/shard_map/ppermute | solution.py:82
  512.8 31.8 %collective-permute-start.94 = (f32[10,2560]{1,0:T(8,128)S(1)}, f32[10,2560]{1,0:T(8,128)S(1)}, u32[]{:S(2)}, u32[]{:S(2)}) collective-permute-start(f32[10,2560]{1,0:T(8,128)S(1)} %add.385), channel_id=1, source_target_pairs={{0,16},{1,17},{2,18},{3,19},{4,20},{5,21},{6,22},{7,23},{8,24},{9,... | collective-permute-start | bytes 307208 | tf_op jit(solution)/shard_map/ppermute | solution.py:82
  548.7 24.5 %collective-permute-start.97 = (bf16[160,1280]{1,0:T(8,128)(2,1)S(1)}, bf16[160,1280]{1,0:T(8,128)(2,1)S(1)}, u32[]{:S(2)}, u32[]{:S(2)}) collective-permute-start(bf16[160,1280]{1,0:T(8,128)(2,1)S(1)} %get-tuple-element.2435), channel_id=1, source_target_pairs={{0,16},{1,17},{2,18},{3,19},{4,20},{5,21},{6,22},{7,23},{8,24},{9,... | collective-permute-start | bytes 1228808 | tf_op jit(solution)/shard_map/ppermute | solution.py:82
  550.8 22.5 %collective-permute-start.98 = (bf16[160,1280]{1,0:T(8,128)(2,1)S(1)}, bf16[160,1280]{1,0:T(8,128)(2,1)S(1)}, u32[]{:S(2)}, u32[]{:S(2)}) collective-permute-start(bf16[160,1280]{1,0:T(8,128)(2,1)S(1)} %get-tuple-element.2434), channel_id=1, source_target_pairs={{0,24},{1,25},{2,26},{3,27},{4,28},{5,29},{6,30},{7,31},{8,0},{9,1... | collective-permute-start | bytes 1228808 | tf_op jit(solution)/shard_map/ppermute | solution.py:82
  (156 other events, 1587.9 us)

commit v7 on v6

--- a/solution.py
+++ b/solution.py
@@ -472,8 +472,9 @@
 
     def body(place_ref, *refs):
         n_refs, c_refs, refs = (refs[:total], refs[total : total + total_c], refs[total + total_c :])
-        gh_ref, wg_ref, wu_ref, wd_ref, hid_ref, gg_ref, gu_ref, nm, no, cm, co = refs[:11]
-        own_ref, rest_ref, n2_s, cot_s, acc, sem = refs[11:]
+        gh_ref, wg_ref, wu_ref, wd_ref, hid_ref, gg_ref, gu_ref = refs[:7]
+        n_rows, c_rows = (refs[7:11], refs[11:15])
+        own_ref, rest_ref, n2_s, cot_s, acc, sem = refs[15:]
 
         def load(g, slot):
             found = []
@@ -489,8 +490,10 @@
             copy.start()
 
         def add(g, act, fresh):
-            start = g * both if isinstance(g, int) else pl.multiple_of(g * both, both)
-            for i, (mine, other) in enumerate(((cm, co), (nm, no), (nm, no))):
+            fixed = isinstance(g, int)
+            start = g * both if fixed else pl.multiple_of((g - 2) * both, both)
+            for i, four in enumerate((c_rows, n_rows, n_rows)):
+                mine, other = four[:2] if fixed else four[2:]
                 part = dot(mine[:, pl.ds(start, both)], act[i][:both]) + dot(
                     other[:, pl.ds(start, both)], act[i][both:])
                 if fresh:
@@ -540,7 +543,7 @@
             num_scalar_prefetch=1,
             grid=(1,),
             in_specs=[ANY] * (total + total_c) + [column(group)] + [column(width)] * 3 + [column(group)] * 3
-            + [whole] * 4,
+            + [whole] * 8,
             out_specs=[pl.BlockSpec((each, 3 * size), lambda j, place: (0, 0)),
                        pl.BlockSpec((rows - each, 3 * size), lambda j, place: (0, 0))],
             scratch_shapes=[
@@ -630,24 +633,46 @@
     )(*flat)
 
 
-def gate_weight_grad(conv, grad_in, grad_decay):
+def gate_weight_grad(place, conv, grad_in, grad_decay, block):
     tokens, n = conv.shape
-
-    def body(conv_ref, in_ref, decay_ref, out_ref):
-        turned = conv_ref[...].T
-        out_ref[:, :BLK] = dot(turned, in_ref[...])
-        out_ref[:, BLK:] = dot(turned, decay_ref[...])
-
-    spec = pl.BlockSpec((tokens, BLK), lambda h: (0, h))
+    count = n // block // 2
+    if block % 16:
+        by_head = lambda v: v.reshape(tokens, n // BLK, BLK)
+        blocks = jnp.einsum(
+            "thi,thj->hij", by_head(conv), jnp.concatenate([by_head(grad_in), by_head(grad_decay)], 2),
+            preferred_element_type=F32).reshape(count, 2, block, 2 * BLK)
+        mine, theirs = [
+            lax.dynamic_index_in_dim(blocks, core, 1, keepdims=False).reshape(n // 2, 2 * BLK)
+            for core in (place[1], 1 - place[1])]
+        return mine, theirs.astype(BF16)
+
+    def body(place_ref, conv_ref, in_ref, decay_ref, keep_ref, away_ref, whole):
+        for h in range(n // BLK):
+            cols = slice(h * BLK, (h + 1) * BLK)
+            turned = conv_ref[:, cols].T
+            whole[cols, :BLK] = dot(turned, in_ref[:, cols])
+            whole[cols, BLK:] = dot(turned, decay_ref[:, cols])
+        for i in range(count):
+            at = pl.multiple_of((2 * i + place_ref[1]) * block, 16)
+            keep_ref[i * block : (i + 1) * block, :] = whole[pl.ds(at, block), :]
+            at = pl.multiple_of((2 * i + 1 - place_ref[1]) * block, 16)
+            away_ref[i * block : (i + 1) * block, :] = whole[pl.ds(at, block), :].astype(BF16)
+
+    spec = pl.BlockSpec((tokens, n), lambda h, place: (0, 0))
+    out = pl.BlockSpec((n // 2, 2 * BLK), lambda h, place: (0, 0))
     return pl.pallas_call(
         body,
-        grid=(n // BLK,),
-        in_specs=[spec] * 3,
-        out_specs=pl.BlockSpec((BLK, 2 * BLK), lambda h: (h, 0)),
-        out_shape=jax.ShapeDtypeStruct((n, 2 * BLK), F32),
+        grid_spec=pltpu.PrefetchScalarGridSpec(
+            num_scalar_prefetch=1,
+            grid=(1,),
+            in_specs=[spec] * 3,
+            out_specs=[out, out],
+            scratch_shapes=[pltpu.VMEM((n, 2 * BLK), F32)],
+        ),
+        out_shape=[jax.ShapeDtypeStruct((n // 2, 2 * BLK), F32), jax.ShapeDtypeStruct((n // 2, 2 * BLK), BF16)],
         compiler_params=pltpu.CompilerParams(vmem_limit_bytes=VMEM_MAX),
         cost_estimate=work(3),
-    )(conv, grad_in, grad_decay)
+    )(place, conv, grad_in, grad_decay)
 
 
 def sum_of_dots(rows, values):
@@ -754,9 +779,10 @@
         (half_of(gate_weight, 1 - x, half, 0), inputs, gate_weight, out_proj, vectors, decay_seed, block_flags))
     halo_raw = lay.over_seq(inputs[0, tokens - 16 :], 1)
     gate_x = lay.over_x(gate_away)
-    wx_c, wy_c = (lay.over_c(in_x), lay.over_c(in_y))
+    wx_c = lay.over_c(in_x)
     scaled_one, inverse_one = norm_scale(inputs[0].astype(F32))
-    live.hold(n1=(scaled_one * vectors[0]).astype(BF16), inv1=inverse_one, halo_raw=halo_raw,
+    live.hold(n1=(scaled_one * vectors[0]).astype(BF16), inv1=inverse_one, halo_raw=halo_raw, cot_top=cot[:cut],
+              cot_low=cot[cut:], wx_c=wx_c,
               params=(gate_weight, out_proj, vectors, decay_seed, block_flags))
 
     gate_weight, out_proj, vectors, decay_seed, block_flags = live.params
@@ -767,12 +793,11 @@
     halo_x = lay.over_x(jnp.concatenate([flag_row, halo_own[1:]], axis=0))
     gate_own = half_of(gate_weight, x, half, 0)
     gate_c = lay.over_c(gate_own)
-    cot_z = lay.over_z(after(cot, live.n1))
-    cot_y = lay.over_y(after(cot, live.n1))
+    cot_z_top = lay.over_z(live.cot_top)
     base = -5.0 - decay_seed.astype(F32) + vectors[9]
-    del live.params, live.halo_raw
+    del live.params, live.halo_raw, live.cot_top
     live.hold(
-        n1_x=n1_x, halo_x=halo_x, halo_own=halo_own, gate_x=gate_x, gate_c=gate_c, wx_c=wx_c, cot_y=cot_y,
+        n1_x=n1_x, halo_x=halo_x, halo_own=halo_own, gate_x=gate_x, gate_c=gate_c, cot_z_top=cot_z_top,
         flags=jnp.concatenate([block_flags.astype(F32), halo_x[:1, :n_flags].astype(F32)], axis=0),
         gate_own=gate_own, out_away=half_of(out_proj, 2 * (1 - x) + y, quarter, 0),
         out_mine=half_of(out_proj, x, half, 0), vec=half_of(vectors, x, half, 1), gain_two=vectors[1],
@@ -780,6 +805,8 @@
         rates=half_of(jnp.stack([jax.nn.softplus(base), jax.nn.sigmoid(base)]), x, half, 1))
 
     out_a = lay.over_x(live.out_away)
+    cot_z_low, cot_y = (lay.over_z(live.cot_low), lay.over_y(after(cot, live.n1_x)))
+    wy_c = lay.over_c(after(in_y, live.n1_x))
     gates = order_f(jnp.concatenate(
         [live.gate_own, live.gate_c, live.gate_x, lay.over_c(live.gate_x)], axis=1))
     normed = jnp.concatenate([live.n1, live.n1_x, live.halo_own, live.halo_x], axis=0)
@@ -792,11 +819,11 @@
         mixer_forward, live.flags,
         [(x_low, False), (halo, False), (gates, True), (live.vec, False), (live.rates, False)],
         [shape3(BF16), shape3(F32), shape3(F32), shape3(F32), shape3(F32), summary_shape])
-    out_c = lay.over_c(live.out_mine)
     del live.gate_x, live.gate_own, live.gate_c, live.halo_own, live.halo_x
     live.hold(x_low=x_low, halo=halo, gates=gates, conv_low=conv_low, ig=ig, dg=dg, prods=prods,
-              local_state=local_state, scan=scan_start(summary, 2), out_c=out_c, normed=normed[:two], wy_c=wy_c, out_a=out_a,
-              cot_z=cot_z)
+              local_state=local_state, scan=scan_start(summary, 2), cot_y=cot_y, normed=normed[:two], wy_c=wy_c, out_a=out_a,
+              cot_z_low=cot_z_low)
+    del live.cot_low
     del live.out_away
 
     def n1_starts(at_y, at_c):
@@ -808,15 +835,17 @@
         if bit == 1:
             live.cut()
             out_b = lay.over_y(live.out_a)
+            out_c = lay.over_c(live.out_mine)
             cot_x = lay.over_x(after(cot, live.scan))
     out_x = jnp.where(y == 0, jnp.concatenate([live.out_a, out_b], 0), jnp.concatenate([out_b, live.out_a], 0))
     y_pre = order_c(dot(live.normed, in_y), dot(live.normed, live.wy_c), 1).reshape(2, tokens, half)
     n1_own, sent, n1_away = rows_by_device(at_yc, [[live.n1, live.n1_x]], n1_starts, own80)
     state_in = live.scan[3]
     del live.scan, live.out_a
-    live.hold(state_in=state_in, y_pre=y_pre, out_left=jnp.concatenate([live.out_mine, live.out_c], axis=1),
+    live.hold(state_in=state_in, y_pre=y_pre, out_left=jnp.concatenate([live.out_mine, out_c], axis=1),
+              cot_z=jnp.concatenate([live.cot_z_top, live.cot_z_low], axis=0),
               out_x=out_x, cot_x=cot_x, n1_own=n1_own, n1_away=n1_away, n1_c=lay.over_c(sent))
-    del live.out_mine, live.out_c
+    del live.out_mine, live.cot_z_top, live.cot_z_low
 
     n1_y = lay.over_y(live.n1_away[: live.n1_own.shape[0]])
     state = live.local_state + live.prods * live.state_in[:, None, :]
@@ -859,11 +888,11 @@
               n2_z=jnp.concatenate([live.n2_z_top, live.n2_z_low], axis=0))
 
     arriving = lay.over_x(live.far)
-    n2_yz = lay.over_y(live.n2_z)
+    n2_yz, n2_y_c, n2_xy_c = (lay.over_y(live.n2_z), lay.over_c(live.n2_y), lay.over_c(live.n2_xy))
     n2_xz_top = lay.over_z(live.n2_x_top)
     near, near_c, out, out_c = mlp_rest(*live.acts, mlp_gate, mlp_up, mlp_down, tokens)
     del live.far, live.far_c, live.n2_z_top, live.n2_z_low
-    live.hold(arriving=arriving, near=near, near_c=near_c, out=out, out_c=out_c, n2_yz=n2_yz, n2_xz_top=n2_xz_top)
+    live.hold(arriving=arriving, near=near, near_c=near_c, out=out, out_c=out_c, n2_yz=n2_yz, n2_y_c=n2_y_c, n2_xy_c=n2_xy_c, n2_xz_top=n2_xz_top)
 
     out_c = lay.over_c(live.out_c)
     grad_n2 = live.near + lay.over_c(live.near_c).astype(F32) + live.arriving.astype(F32)
@@ -878,12 +907,14 @@
     n2_xz_low = lay.over_z(live.n2_x_low)
     cot_yz = lay.over_y(live.cot_z)
     live.hold(arriving=arriving, n2_xz_low=n2_xz_low, cot_yz=cot_yz, out_sum=live.out + live.out_c.astype(F32),
-              n2_y_c=lay.over_c(live.n2_y),
-              n2_xy_c=lay.over_c(live.n2_xy))
+              n2_z_c=lay.over_c(live.n2_z), cot_z_c=lay.over_c(live.cot_z),
+              n2_rows_ahead=rows_of_tokens(place, [live.n2, live.n2_x, live.n2_y, live.n2_xy], half // 2, each),
+              cot_rows_ahead=rows_of_tokens(place, [cot, live.cot_x, live.cot_y, live.cot_xy], half // 2, each))
 
     rows_each = live.n1_own.shape[0]
     n1_yc = lay.over_y(live.n1_away[rows_each:])
-    cot_z_c, cot_xz_c = (lay.over_c(live.cot_z), lay.over_c(live.cot_xz))
+    cot_xz_c, n2_yz_c = (lay.over_c(live.cot_xz), lay.over_c(live.n2_yz))
+    mixed_xa = lay.over_x(live.mixed[1])
     branch_x_rel = jnp.concatenate([live.arriving[:, half:], live.arriving[:, :half]], axis=1)
     both_rel = jnp.concatenate([live.branch_rel, branch_x_rel], 0)
     grad_mixed = dot_cols(both_rel[:, :half], live.out_left) + dot_cols(both_rel[:, half:], live.out_right)
@@ -894,7 +925,8 @@
         [shape3(BF16), shape3(F32), shape3(F32), summary_shape])
     del live.arriving, live.branch_rel, live.y_pre
     live.hold(gy=gy.reshape(two, half), bprod=bprod, blocal=blocal, scan=scan_start(back_summary, 2),
-              branch_x_rel=branch_x_rel, n1_yc=n1_yc, cot_z_c=cot_z_c, cot_xz_c=cot_xz_c)
+              branch_x_rel=branch_x_rel, n1_yc=n1_yc, cot_xz_c=cot_xz_c, n2_yz_c=n2_yz_c,
+              mixed_xa=mixed_xa, mixed_b=live.mixed[0])
 
     n2_xyz = lay.over_x(live.n2_yz)
     own_cols = lambda value, which: half_of(value, which, quarter, 1)
@@ -905,13 +937,13 @@
         if bit == 1:
             live.cut()
             cot_xyz = lay.over_y(live.cot_xz)
-            n2_z_c, n2_yz_c, cot_yz_c = (lay.over_c(live.n2_z), lay.over_c(live.n2_yz), lay.over_c(live.cot_yz))
+            cot_yz_c = lay.over_c(live.cot_yz)
     back_in = live.scan[3]
     del live.scan
+    live.hold(back_in=back_in, cot_xyz=cot_xyz, n2_xyz=n2_xyz, part_y=part_y, cot_yz_c=cot_yz_c)
+
+    live.ahead_c = (lay.over_c(live.n2_rows_ahead), lay.over_c(live.cot_rows_ahead))
     live.n1_yc = lay.over_c(live.n1_yc)
-    live.hold(back_in=back_in, cot_xyz=cot_xyz, n2_xyz=n2_xyz, part_y=part_y, n2_z_c=n2_z_c, n2_yz_c=n2_yz_c,
-              cot_yz_c=cot_yz_c)
-
     gip, gdp, gx_main, gx_tail, edge, vec_rows = by_head(
         mixer_backward, live.flags,
         [(live.bprod, False), (live.blocal, False), (live.back_in, False), (live.prods, False),
@@ -926,17 +958,17 @@
     live.hold(gip=gip, gdp=gdp, gx_main=gx_main, gx_tail=gx_tail, edge=edge, vec_rows=vec_rows)
 
     edge_next = lay.over_seq(live.edge, -1)
-    mixed_x = lay.over_x(jnp.concatenate([live.mixed[1], live.mixed[0]], axis=0))
+    mixed_xb = lay.over_x(live.mixed_b)
     n2_xz = jnp.concatenate([live.n2_xz_top, live.n2_xz_low], axis=0)
     n2_xz_c, n2_xyz_c, cot_xyz_c = (lay.over_c(n2_xz), lay.over_c(live.n2_xyz), lay.over_c(live.cot_xyz))
     live.n2s = [[live.n2, live.n2_x], [live.n2_y, live.n2_xy], [live.n2_z, n2_xz], [live.n2_yz, live.n2_xyz]]
     live.cots = [cot, live.cot_x, live.cot_y, live.cot_xy, live.cot_z, live.cot_xz, live.cot_yz, live.cot_xyz]
-    n2_rows = rows_of_tokens(place, [p for group in live.n2s for p in group], half // 2, each)
-    cot_rows = rows_of_tokens(place, live.cots, half // 2, each)
+    n2_rows = rows_of_tokens(place, [p for group in live.n2s[2:] for p in group], half // 2, each)
+    cot_rows = rows_of_tokens(place, live.cots[4:], half // 2, each)
     del live.edge
     live.hold(edge_next=edge_next, n2_rows=n2_rows, cot_rows=cot_rows,
               n2s_c=[[live.n2_y_c, live.n2_xy_c], [live.n2_z_c, n2_xz_c], [live.n2_yz_c, n2_xyz_c]],
-              cots_c=[live.cot_z_c, live.cot_xz_c, live.cot_yz_c, cot_xyz_c], mixed_x=mixed_x)
+              cots_c=[live.cot_z_c, live.cot_xz_c, live.cot_yz_c, cot_xyz_c], mixed_xb=mixed_xb)
 
     gx_last = (live.gx_tail + jnp.pad(live.edge_next, ((0, 0), (8, 0), (0, 0)))).astype(BF16)
     gx = jnp.concatenate([live.gx_main[:, : tokens - 16], gx_last], axis=1).reshape(two, half)
@@ -953,8 +985,9 @@
         return mlp_weight_grads(
             place, [a + b for a, b in zip(live.n2s[1:], live.n2s_c)], live.gh_y,
             [live.cots[4:6] + live.cots_c[:2], live.cots[6:] + live.cots_c[2:]], live.acts,
-            (live.n2_rows, live.n2_rows_c), (live.cot_rows, live.cot_rows_c), (mlp_gate, mlp_up, mlp_down),
-            at, size, each)
+            (live.n2_rows_ahead, live.ahead_c[0], live.n2_rows, live.n2_rows_c),
+            (live.cot_rows_ahead, live.ahead_c[1], live.cot_rows, live.cot_rows_c),
+            (mlp_gate, mlp_up, mlp_down), at, size, each)
 
     def piece_sum(own, rest):
         blocks = [own] + [rest[j * each : (j + 1) * each] for j in range(nz // 2 - 1)]
@@ -996,20 +1029,18 @@
                          jnp.concatenate([theirs, mine], -1)).astype(F32)
 
     sums = live.sums + lay.over_x(live.sums)
-    sums = sums + lay.over_seq_bit(sums, 1)
     branch_two_y = lay.over_y(live.branch_two)
     sum_a = piece_sum(*live.piece_a)
     n1_all = [live.n1_own, live.n1_c, live.n1_y, live.n1_yc]
     in_y_part = sum_of_dots(n1_all, [live.gy, live.gy_c, live.gy_y, live.gy_yc])
-    gate_part = gate_weight_grad(
-        live.conv_low.reshape(two, half), live.gip.reshape(two, half), live.gdp.reshape(two, half)
-    ).reshape(2, nz, 2, own80, 2 * BLK)
+    gate_part, gate_away = gate_weight_grad(
+        at_yc, live.conv_low.reshape(two, half), live.gip.reshape(two, half), live.gdp.reshape(two, half), own80)
+    gate_part = (gate_part + lay.over_c(gate_away).astype(F32)).reshape(2, nz, own80, 2 * BLK)
     pick = lambda value, at, axis: lax.dynamic_index_in_dim(value, at, axis, keepdims=False)
-    gate_part = pick(gate_part, c, 2) + lay.over_c(pick(gate_part, 1 - c, 2).astype(BF16)).astype(F32)
     gate_y = lay.over_y(pick(gate_part, 1 - y, 0).astype(BF16))
     mixed_own, sent, mixed_away = rows_by_device(
-        at_yc, [[live.mixed[0], live.mixed[1]], [live.mixed_x[:tokens], live.mixed_x[tokens:]]], n1_starts, own80)
-    del live.gy, live.gy_c, live.gy_y, live.gy_yc, live.mixed, live.mixed_x, live.conv_low, live.gip, live.gdp
+        at_yc, [[live.mixed[0], live.mixed[1]], [live.mixed_xa, live.mixed_xb]], n1_starts, own80)
+    del live.gy, live.gy_c, live.gy_y, live.gy_yc, live.mixed, live.mixed_xa, live.mixed_xb, live.conv_low, live.gip, live.gdp
     live.hold(in_y_part=in_y_part, sums=sums, sum_a=sum_a, branch_two_y=branch_two_y, gate_keep=pick(gate_part, y, 0), gate_y=gate_y,
               mixed_own=mixed_own, mixed_away=mixed_away, mixed_c=lay.over_c(sent),
               gx_c=lay.over_c(live.gx), branch_c=lay.over_c(live.branch_two))
@@ -1023,6 +1054,9 @@
     live.hold(piece_b=piece_b, gx_y=gx_y, mixed_y=mixed_y, in_y_own=in_y_own, in_y_come=in_y_come)
 
     sum_b = piece_sum(*live.piece_b)
+    sums = live.sums
+    for bit in bits[:1]:
+        sums = sums + lay.over_seq_bit(sums, bit)
     in_x_part = sum_of_dots(n1_all, [live.gx, live.gx_c, live.gx_y, lay.over_c(live.gx_y)])
     out_part = sum_of_dots(
         [live.mixed_own, live.mixed_c, live.mixed_y[:rows_each], lay.over_c(live.mixed_y[rows_each:])],
@@ -1031,40 +1065,42 @@
     del live.piece_b, live.gate_keep, live.gate_y, live.mixed_own, live.mixed_c, live.mixed_y
     live.hold(in_x_part=jnp.concatenate(
         [in_x_part.reshape(nz, 2 * own80, half), gate_part.reshape(nz, own80 * 2 * BLK // half, half)], axis=1),
-        out_part=out_part, sum_b=sum_b, in_y_total=total_of(live.in_y_own, live.in_y_come),
+        out_part=out_part, sum_b=sum_b, sums=sums, in_y_total=total_of(live.in_y_own, live.in_y_come),
         out_far=live.out_sum[tokens:].astype(BF16))
     del live.in_y_own, live.in_y_come
 
     in_x_own, in_x_come = owner_parts(live.in_x_part)
+    out_own, out_come = owner_parts(live.out_part.reshape(nz, 2 * own80, half))
     out_arriving = lay.over_x(live.out_far)
-    sums = live.sums
-    sums_z = lay.over_seq_bit(sums, 2)
     piece_c = weight_piece(*cuts[2])
     del live.in_x_part
-    live.hold(piece_c=piece_c, in_x_own=in_x_own, in_x_come=in_x_come, out_arriving=out_arriving, sums=sums + sums_z)
+    live.hold(piece_c=piece_c, in_x_own=in_x_own, in_x_come=in_x_come, out_arriving=out_arriving,
+              out_come=out_come[:1])
 
     sum_c = piece_sum(*live.piece_c)
-    sums = live.sums
+    out_own, out_come = owner_parts(live.out_part.reshape(nz, 2 * own80, half))
+    in_x_own, in_x_come, in_y_total = after((live.in_x_own, live.in_x_come, live.in_y_total), out_come[1])
+    in_x_total = total_of(in_x_own, in_x_come)
+    sums_z = lay.over_seq_bit(live.sums, 2)
+    live.hold(sum_c=sum_c, sums_z=sums_z, out_total=total_of(out_own, live.out_come + out_come[1:]),
+              in_y_grad=over_columns(in_y_total), in_x_grad=over_columns(in_x_total[: 2 * own80]),
+              gate_total=in_x_total[2 * own80 :].reshape(own80, 2 * BLK),
+              output=(live.mid + after(live.out_sum, out_come[1])[:tokens] + live.out_arriving.astype(F32)
+                      ).astype(BF16)[None])
+
+    sums = live.sums + live.sums_z
     for bit in bits[2:]:
         sums = sums + lay.over_seq_bit(sums, bit)
-    in_y_grad = over_columns(live.in_y_total)
-    live.hold(sum_c=sum_c, sums=sums, in_x_total=total_of(live.in_x_own, live.in_x_come), in_y_grad=in_y_grad,
-              output=(live.mid + live.out_sum[:tokens] + live.out_arriving.astype(F32)).astype(BF16)[None])
-
-    out_own, out_come = owner_parts(live.out_part.reshape(nz, 2 * own80, half))
-    in_x_grad = over_columns(live.in_x_total[: 2 * own80])
-    mlp_grads = joined_columns([live.sum_b, live.sum_c, live.sum_a])
-    live.hold(out_own=out_own, out_come=out_come, mlp_grads=mlp_grads, in_x_grad=in_x_grad)
-    mlp_down_grad, mlp_gate_grad, mlp_up_grad = live.mlp_grads
+    mlp_down_grad, mlp_gate_grad, mlp_up_grad = joined_columns([live.sum_b, live.sum_c, live.sum_a])
 
     def final(z, y, x, c):
         at = ((x * 2 + y) * nz + z) * 2 + c
         s, f = (at // 4, at % 4)
         return (s // 2, s % 2, f // 2, f % 2)
 
-    out_grad = over_columns(total_of(live.out_own, live.out_come))
-    gate_grad = lay.send(live.in_x_total[2 * own80 :].reshape(own80, 2 * BLK), final).astype(F32)
-    return (live.output, input_grad, live.sums, live.in_y_grad, live.in_x_grad, gate_grad, out_grad,
+    out_grad = over_columns(live.out_total)
+    gate_grad = lay.send(live.gate_total, final).astype(F32)
+    return (live.output, input_grad, sums, live.in_y_grad, live.in_x_grad, gate_grad, out_grad,
             mlp_gate_grad, mlp_up_grad, mlp_down_grad)
 
 

time: 599 us -> 589 us (0.983)
  starting transfers between devices: 113 us -> 96.5 us
    ppermute x101 -> x105, starting transfers between devices: 113 us -> 96.5 us  [send(): return lax.ppermute(value, ALL, self.pairs(target))]
    pallas_call x2 -> x4, Pallas kernels: 8.82 us -> 13.1 us  [rows_of_tokens(): pl.pallas_call(body, grid_spec=pltpu.PrefetchScalarGridSpec(num_scalar_pr...]
    ppermute x101 -> x105, waiting for transfers between devices: 126 us -> 122 us  [send(): return lax.ppermute(value, ALL, self.pairs(target))]
    unnamed x211 -> x199, local copies, waits for them, and re-layouts: 21.6 us -> 22.2 us
  transfers between devices with their start and end apart: 101 -> 105, of which waited for: 26 -> 28; matrix products, arithmetic and copies ran while one was open for 15% -> 16% of each run, Pallas kernels for 38% -> 40%
where the time goes in v7:
time: 589 us; the launch traced here: 580 us
  Pallas kernels  234 us (40%)
  waiting for transfers between devices  122 us (21%)
  starting transfers between devices  96.5 us (16%)
  local copies, waits for them, and re-layouts  52.6 us (9%)
  other arithmetic  45.5 us (8%)
  matrix products  26.4 us (4%)
    ppermute x105, waiting for transfers between devices, send(): return lax.ppermute(value, ALL, self.pairs(target))  122 us
    pallas_call x3, Pallas kernels, mlp_weight_grads(): pl.pallas_call(body, grid_spec=pltpu.PrefetchScalarGridSpec(num_scalar_pr...  98.7 us
    ppermute x105, starting transfers between devices, send(): return lax.ppermute(value, ALL, self.pairs(target))  96.5 us
    pallas_call x2, Pallas kernels, grad_hidden_of(): pl.pallas_call(body, grid=(pl.cdiv(ff, BLK),), in_specs=[ANY] * count + [...  25.9 us
    pallas_call x1, Pallas kernels, mlp_forward(): pl.pallas_call(body, in_specs=[ANY] * (count + 3), out_shape=[act, act, a...  23.3 us
    unnamed x199, local copies, waits for them, and re-layouts  22.2 us
    pallas_call x3, Pallas kernels, by_head(): pl.pallas_call(body, grid=(heads,), in_specs=in_specs, out_specs=[spec(o....  19.9 us
    pallas_call x1, Pallas kernels, mlp_rest(): pl.pallas_call(body, grid=(width // block,), in_specs=[whole] * 3 + [weig...  19.1 us
  transfers between devices with their start and end apart: 105, of which 28 were waited for; matrix products, arithmetic and copies ran while one was open for 16% of the time, Pallas kernels for 40%

profile of v7, /device:TPU:2, one launch (start us, length us, event | category | flops | bytes accessed | tf_op | source)
XLA Modules:
  0.0 580.3 jit_solution(4601420038711241001)
XLA Ops:
  3.6 3.4 collective-permute-start
  11.8 3.7 collective-permute-start.2
  23.6 13.9 %collective-permute-done.6.refs_1_ = bf16[128,2560]{1,0:T(8,128)(2,1)S(1)} collective-permute-done((bf16[128,2560]{1,0:T(8,128)(2,1)S(1)}, bf16[128,2560]{1,0:T(8,128)(2,1)S(1)}, u32[]{:S(2)}, u32[]{:S(2)}) %collective-permute-start.6) | collective-permute-done | bytes 655392 | tf_op jit(solution)/shard_map/ppermute | solution.py:82
  39.1 3.3 convolution_convert_fusion
  49.9 7.1 %shard_map.195 = (bf16[2,128,1280]{2,1,0:T(8,128)(2,1)S(1)}, f32[2,128,1280]{2,1,0:T(8,128)S(1)}, f32[2,128,1280]{2,1,0:T(8,128)S(1)}, f32[2,128,1280]{2,1,0:T(8...) custom-call(f32[2,2]{1,0:T(2,128)S(1)} %pad_maximum_fusion.16.flags_ref, bf16[2,128,1280]{2,1,0:T(8,128)(2,1)S(1)} %bitcast.119, ...), custom_call_target="tpu_custom_call" | custom-call | flops 1 | bytes 1 | tf_op jit(solution)/shard_map/pallas_call | solution.py:266
  60.6 4.9 collective-permute-done.10
  72.0 3.4 shard_map.196
  76.5 3.8 fusion.76
  82.5 3.9 collective-permute-start.18
  88.1 8.2 %collective-permute-done.16 = bf16[640,640]{1,0:T(8,128)(2,1)S(1)} collective-permute-done((bf16[640,640]{1,0:T(8,128)(2,1)}, bf16[640,640]{1,0:T(8,128)(2,1)S(1)}, u32[]{:S(2)}, u32[]{:S(2)}) %collective-permute-start.16) | collective-permute-done | bytes 819232 | tf_op jit(solution)/shard_map/ppermute | solution.py:82
  104.5 3.7 collective-permute-done.19.refs_2_
  111.1 12.9 %shard_map.197.refs_4_ = f32[512,1920]{1,0:T(8,128)} custom-call(bf16[128,2560]{1,0:T(8,128)(2,1)} %bitcast.143, bf16[128,2560]{1,0:T(8,128)(2,1)} %collective-permute-done.13.refs_1_, bf16[128,2560]{1,0:T(8,128)(2,1)} %copy-done.94, bf16[128,2560]{1,0:T(8,128)(2,1)} %collective-permute-done.23.refs_3_, bf16[2560,1920]{1,0:T(8,128)(2,1)} %refs_23_.5), custom_call_target="tpu_custom_call" | custom-call | flops 11699999744 | bytes 26000000 | tf_op jit(solution)/shard_map/pallas_call | solution.py:299
  138.9 13.0 %shard_map.198.refs_20_ = f32[512,1920]{1,0:T(8,128)} custom-call(bf16[128,2560]{1,0:T(8,128)(2,1)} %copy-done.75, bf16[128,2560]{1,0:T(8,128)(2,1)} %collective-permute-done.21.refs_1_.refs_3_, bf16[128,2560]{1,0:T(8,128)(2,1)} %copy-done.95, bf16[128,2560]{1,0:T(8,128)(2,1)} %collective-permute-done.26.refs_3_, bf16[2560,1920]{1,0:T(8,128)(2,1)} %refs_23_.5), custom_call_target="tpu_custom_call" | custom-call | flops 11699999744 | bytes 26000000 | tf_op jit(solution)/shard_map/pallas_call | solution.py:299
  158.8 23.3 %shard_map.199 = (bf16[512,1920]{1,0:T(8,128)(2,1)}, bf16[512,1920]{1,0:T(8,128)(2,1)}, bf16[512,1920]{1,0:T(8,128)(2,1)}, f32[128,2560]{1,0:T(8,128)}, bf16[128,2560]{1,0:T(8,128)(2,1)}) custom-call(bf16[128,2560]{1,0:T(8,128)(2,1)} %multiply_convert_fusion.refs_0_, bf16[128,2560]{1,0:T(8,128)(2,1)} %collective-permute-done.28.refs_1_, ...), custom_call_target="tpu_custom_call" | custom-call | flops 20700000256 | bytes 46000000 | tf_op jit(solution)/shard_map/pallas_call | solution.py:384
  187.4 3.5 collective-permute-start.38
  191.5 19.1 %shard_map.200 = (f32[128,2560]{1,0:T(8,128)}, bf16[128,2560]{1,0:T(8,128)(2,1)}, f32[256,2560]{1,0:T(8,128)}, bf16[256,2560]{1,0:T(8,128)(2,1)}) custom-call(bf16[512,1920]{1,0:T(8,128)(2,1)} %get-tuple-element.2399.hid_ref.refs_24_, bf16[512,1920]{1,0:T(8,128)(2,1)} %get-tuple-element.2400.gg_ref.refs_25_, ...), custom_call_target="tpu_custom_call" | custom-call | flops 17100000256 | bytes 38000000 | tf_op jit(solution)/shard_map/pallas_call | solution.py:423
  215.5 3.0 fusion.61
  224.0 3.2 shard_map.201.refs_31_
  227.2 3.3 shard_map.202.refs_27_
  230.5 3.3 collective-permute-done.46
  233.8 4.8 collective-permute-done.43
  246.2 5.4 shard_map.203
  258.8 3.3 fusion.43
  264.8 2.8 convolution_add_fusion
  268.6 3.8 collective-permute-done.57.refs_3_.refs_9_
  272.3 5.8 %collective-permute-done.55.refs_3_.refs_17_ = bf16[128,2560]{1,0:T(8,128)(2,1)} collective-permute-done((bf16[128,2560]{1,0:T(8,128)(2,1)}, bf16[128,2560]{1,0:T(8,128)(2,1)}, u32[]{:S(2)}, u32[]{:S(2)}) %collective-permute-start.55) | collective-permute-done | bytes 655392 | tf_op jit(solution)/shard_map/ppermute | solution.py:82
  279.5 7.4 %shard_map.204 = (bf16[2,128,1280]{2,1,0:T(8,128)(2,1)S(1)}, bf16[2,128,1280]{2,1,0:T(8,128)(2,1)S(1)}, bf16[2,128,1280]{2,1,0:T(8,128)(2,1)S(1)}, f32[2,16,1280...) custom-call(f32[2,2]{1,0:T(2,128)S(1)} %pad_maximum_fusion.16.flags_ref, ...), custom_call_target="tpu_custom_call" | custom-call | flops 1 | bytes 1 | tf_op jit(solution)/shard_map/pallas_call | solution.py:266
  293.6 3.2 shard_map.206.refs_29_
  296.9 3.4 shard_map.205.refs_33_
  301.5 3.4 fusion.41
  304.9 3.2 add_add_fusion
  313.1 24.3 %shard_map.207 = (f32[320,1152]{1,0:T(8,128)}, bf16[320,1152]{1,0:T(8,128)(2,1)}) custom-call(s32[3]{0:T(128)} %pad_add_fusion.1.place_ref, bf16[128,2560]{1,0:T(8,128)(2,1)} %collective-permute-done.29.refs_2_.refs_0_, bf16[128,2560]{1,0:T(8,128)(2,1)} %collective-permute-done.33.refs_3_.refs_1_, bf16[128,2560]{1,0:T(8,128)(2,1)} %collective-permute-done.39.refs_2_, ...), custom_call_target="tpu_custom_call" | custom-call | flops 15299999744 | bytes 34000000 | tf_op jit(solution)/shard_map/pallas_call | solution.py:540
  341.6 4.2 shard_map.208
  349.4 3.4 shard_map.210
  360.0 5.3 shard_map.209
  365.4 7.5 %collective-permute-done.79.refs_5_ = bf16[320,1152]{1,0:T(8,128)(2,1)} collective-permute-done((bf16[320,1152]{1,0:T(8,128)(2,1)}, bf16[320,1152]{1,0:T(8,128)(2,1)}, u32[]{:S(2)}, u32[]{:S(2)}) %collective-permute-start.79) | collective-permute-done | bytes 737312 | tf_op jit(solution)/shard_map/ppermute | solution.py:82
  381.8 37.0 %shard_map.211 = (f32[320,2304]{1,0:T(8,128)}, bf16[320,2304]{1,0:T(8,128)(2,1)}) custom-call(s32[3]{0:T(128)} %pad_add_fusion.1.place_ref, bf16[128,2560]{1,0:T(8,128)(2,1)} %collective-permute-done.29.refs_2_.refs_0_, bf16[128,2560]{1,0:T(8,128)(2,1)} %collective-permute-done.33.refs_3_.refs_1_, bf16[128,2560]{1,0:T(8,128)(2,1)} %collective-permute-done.39.refs_2_, ...), custom_call_target="tpu_custom_call" | custom-call | flops 31499999232 | bytes 70000000 | tf_op jit(solution)/shard_map/pallas_call | solution.py:540
  428.1 5.1 shard_map.212
  434.1 5.2 shard_map.213
  439.5 12.3 %collective-permute-done.89.refs_1_ = bf16[320,2304]{1,0:T(8,128)(2,1)} collective-permute-done((bf16[320,2304]{1,0:T(8,128)(2,1)}, bf16[320,2304]{1,0:T(8,128)(2,1)}, u32[]{:S(2)}, u32[]{:S(2)}) %collective-permute-start.89) | collective-permute-done | bytes 1474592 | tf_op jit(solution)/shard_map/ppermute | solution.py:82
  459.9 37.4 %shard_map.214 = (f32[320,2304]{1,0:T(8,128)}, bf16[320,2304]{1,0:T(8,128)(2,1)}) custom-call(s32[3]{0:T(128)} %pad_add_fusion.1.place_ref, bf16[128,2560]{1,0:T(8,128)(2,1)} %collective-permute-done.29.refs_2_.refs_0_, bf16[128,2560]{1,0:T(8,128)(2,1)} %collective-permute-done.33.refs_3_.refs_1_, bf16[128,2560]{1,0:T(8,128)(2,1)} %collective-permute-done.39.refs_2_, ...), custom_call_target="tpu_custom_call" | custom-call | flops 31499999232 | bytes 70000000 | tf_op jit(solution)/shard_map/pallas_call | solution.py:540
  498.2 7.5 %collective-permute-start.96 = (bf16[160,1280]{1,0:T(8,128)(2,1)S(1)}, bf16[160,1280]{1,0:T(8,128)(2,1)S(1)}, u32[]{:S(2)}, u32[]{:S(2)}) collective-permute-start(bf16[160,1280]{1,0:T(8,128)(2,1)S(1)} %get-tuple-element.2500), channel_id=1, source_target_pairs={{0,16},{1,17},{2,18},{3,19},{4,20},{5,21},{6,22},{7,23},{8,24},{9,... | collective-permute-start | bytes 1228808 | tf_op jit(solution)/shard_map/ppermute | solution.py:82
  505.7 3.4 collective-permute-start.99
  511.1 13.8 %collective-permute-done.96 = bf16[160,1280]{1,0:T(8,128)(2,1)S(1)} collective-permute-done((bf16[160,1280]{1,0:T(8,128)(2,1)S(1)}, bf16[160,1280]{1,0:T(8,128)(2,1)S(1)}, u32[]{:S(2)}, u32[]{:S(2)}) %collective-permute-start.96) | collective-permute-done | bytes 409632 | tf_op jit(solution)/shard_map/ppermute | solution.py:82
  537.1 21.5 %collective-permute-done.101 = f32[10,2560]{1,0:T(8,128)} collective-permute-done((f32[10,2560]{1,0:T(8,128)S(1)}, f32[10,2560]{1,0:T(8,128)}, u32[]{:S(2)}, u32[]{:S(2)}) %collective-permute-start.101) | collective-permute-done | bytes 102432 | tf_op jit(solution)/shard_map/ppermute | solution.py:82
  559.6 3.8 collective-permute-start.102
  563.4 3.0 collective-permute-start.103
  568.5 7.3 %shard_map.215 = (f32[320,1920]{1,0:T(8,128)}, f32[320,1920]{1,0:T(8,128)}, f32[320,1920]{1,0:T(8,128)}) custom-call(f32[320,2304]{1,0:T(8,128)} %get-tuple-element.2475.refs_0_, bf16[320,2304]{1,0:T(8,128)(2,1)} %collective-permute-done.89.refs_1_, f32[320,2304]{1,0:T(8,128)} %get-tuple-element.2477.refs_2_, ...), custom_call_target="tpu_custom_call" | custom-call | flops 1 | bytes 1 | tf_op jit(solution)/shard_map/pallas_call | solution.py:625
  (530 shorter events, 185.1 us)
Async XLA Ops:
  20.4 17.1 %collective-permute-start.6 = (bf16[128,2560]{1,0:T(8,128)(2,1)S(1)}, bf16[128,2560]{1,0:T(8,128)(2,1)S(1)}, u32[]{:S(2)}, u32[]{:S(2)}) collective-permute-start(bf16[128,2560]{1,0:T(8,128)(2,1)S(1)} %copy-done.23), channel_id=1, source_target_pairs={{0,2},{1,3},{2,0},{3,1},{4,6},{5,7},{6,4},{7,5},{8,10},{9,11},{10,... | collective-permute-start | bytes 1966088 | tf_op jit(solution)/shard_map/ppermute | solution.py:82
  37.6 27.9 %collective-permute-start.11 = (bf16[2560,640]{1,0:T(8,128)(2,1)S(1)}, bf16[2560,640]{1,0:T(8,128)(2,1)S(1)}, u32[]{:S(2)}, u32[]{:S(2)}) collective-permute-start(bf16[2560,640]{1,0:T(8,128)(2,1)S(1)} %copy-done.46), channel_id=1, source_target_pairs={{0,1},{1,0},{2,3},{3,2},{4,5},{5,4},{6,7},{7,6},{8,9},{9,8},{10,11... | collective-permute-start | bytes 9830408 | tf_op jit(solution)/shard_map/ppermute | solution.py:82
  43.5 17.1 %collective-permute-start.8 = (bf16[128,2560]{1,0:T(8,128)(2,1)S(1)}, bf16[128,2560]{1,0:T(8,128)(2,1)S(1)}, u32[]{:S(2)}, u32[]{:S(2)}) collective-permute-start(bf16[128,2560]{1,0:T(8,128)(2,1)S(1)} %bitcast.145), channel_id=1, source_target_pairs={{0,4},{1,5},{2,6},{3,7},{4,0},{5,1},{6,2},{7,3},{8,12},{9,13},{10,... | collective-permute-start | bytes 1966088 | tf_op jit(solution)/shard_map/ppermute | solution.py:82
  45.2 20.3 %collective-permute-start.10 = (bf16[640,640]{1,0:T(8,128)(2,1)}, bf16[640,640]{1,0:T(8,128)(2,1)S(1)}, u32[]{:S(2)}, u32[]{:S(2)}) collective-permute-start(bf16[640,640]{1,0:T(8,128)(2,1)} %constant_dynamic-slice_fusion.3), channel_id=1, source_target_pairs={{0,2},{1,3},{2,0},{3,1},{4,6},{5,7},{6,4},{7,5},{8,10},{9,11},{10,... | collective-permute-start | bytes 2457608 | tf_op jit(solution)/shard_map/ppermute | solution.py:82
  71.4 25.9 %collective-permute-start.13 = (bf16[128,2560]{1,0:T(8,128)(2,1)}, bf16[128,2560]{1,0:T(8,128)(2,1)}, u32[]{:S(2)}, u32[]{:S(2)}) collective-permute-start(bf16[128,2560]{1,0:T(8,128)(2,1)} %bitcast.142), channel_id=1, source_target_pairs={{0,2},{1,3},{2,0},{3,1},{4,6},{5,7},{6,4},{7,5},{8,10},{9,11},{10,... | collective-permute-start | bytes 1966088 | tf_op jit(solution)/shard_map/ppermute | solution.py:82
  75.4 21.8 %collective-permute-start.14 = (bf16[640,256]{1,0:T(8,128)(2,1)}, bf16[640,256]{1,0:T(8,128)(2,1)S(1)}, u32[]{:S(2)}, u32[]{:S(2)}) collective-permute-start(bf16[640,256]{1,0:T(8,128)(2,1)} %get-tuple-element.1340), channel_id=1, source_target_pairs={{0,1},{1,0},{2,3},{3,2},{4,5},{5,4},{6,7},{7,6},{8,9},{9,8},{10,11... | collective-permute-start | bytes 983048 | tf_op jit(solution)/shard_map/ppermute | solution.py:82
  75.4 21.5 %collective-permute-start.15 = (bf16[1280,640]{1,0:T(8,128)(2,1)}, bf16[1280,640]{1,0:T(8,128)(2,1)S(1)}, u32[]{:S(2)}, u32[]{:S(2)}) collective-permute-start(bf16[1280,640]{1,0:T(8,128)(2,1)} %constant_dynamic-slice_fusion.2), channel_id=1, source_target_pairs={{0,1},{1,0},{2,3},{3,2},{4,5},{5,4},{6,7},{7,6},{8,9},{9,8},{10,11... | collective-permute-start | bytes 4915208 | tf_op jit(solution)/shard_map/ppermute | solution.py:82
  75.9 20.4 %collective-permute-start.16 = (bf16[640,640]{1,0:T(8,128)(2,1)}, bf16[640,640]{1,0:T(8,128)(2,1)S(1)}, u32[]{:S(2)}, u32[]{:S(2)}) collective-permute-start(bf16[640,640]{1,0:T(8,128)(2,1)} %copy-done.66), channel_id=1, source_target_pairs={{0,4},{1,5},{2,6},{3,7},{4,0},{5,1},{6,2},{7,3},{8,12},{9,13},{10,... | collective-permute-start | bytes 2457608 | tf_op jit(solution)/shard_map/ppermute | solution.py:82
  108.2 17.5 %collective-permute-start.21 = (bf16[128,2560]{1,0:T(8,128)(2,1)}, bf16[128,2560]{1,0:T(8,128)(2,1)}, u32[]{:S(2)}, u32[]{:S(2)}) collective-permute-start(bf16[128,2560]{1,0:T(8,128)(2,1)} %collective-permute-done.13.refs_1_), channel_id=1, source_target_pairs={{0,4},{1,5},{2,6},{3,7},{4,0},{5,1},{6,2},{7,3},{8,12},{9,13},{10,... | collective-permute-start | bytes 1966088 | tf_op jit(solution)/shard_map/ppermute | solution.py:82
  108.8 17.2 %collective-permute-start.24 = (bf16[128,2560]{1,0:T(8,128)(2,1)}, bf16[128,2560]{1,0:T(8,128)(2,1)}, u32[]{:S(2)}, u32[]{:S(2)}) collective-permute-start(bf16[128,2560]{1,0:T(8,128)(2,1)} %fusion.22), channel_id=1, source_target_pairs={{0,2},{1,3},{2,0},{3,1},{4,6},{5,7},{6,4},{7,5},{8,10},{9,11},{10,... | collective-permute-start | bytes 1966088 | tf_op jit(solution)/shard_map/ppermute | solution.py:82
  130.9 21.0 %collective-permute-start.27 = (bf16[128,2560]{1,0:T(8,128)(2,1)}, bf16[128,2560]{1,0:T(8,128)(2,1)}, u32[]{:S(2)}, u32[]{:S(2)}) collective-permute-start(bf16[128,2560]{1,0:T(8,128)(2,1)} %multiply_convert_fusion.refs_0_), channel_id=1, source_target_pairs={{0,1},{1,0},{2,3},{3,2},{4,5},{5,4},{6,7},{7,6},{8,9},{9,8},{10,11... | collective-permute-start | bytes 1966088 | tf_op jit(solution)/shard_map/ppermute | solution.py:82
  131.0 21.0 %collective-permute-start.28 = (bf16[128,2560]{1,0:T(8,128)(2,1)}, bf16[128,2560]{1,0:T(8,128)(2,1)}, u32[]{:S(2)}, u32[]{:S(2)}) collective-permute-start(bf16[128,2560]{1,0:T(8,128)(2,1)} %multiply_convert_fusion.refs_0_), channel_id=1, source_target_pairs={{0,2},{1,3},{2,0},{3,1},{4,6},{5,7},{6,4},{7,5},{8,10},{9,11},{10,... | collective-permute-start | bytes 1966088 | tf_op jit(solution)/shard_map/ppermute | solution.py:82
  132.4 19.6 %collective-permute-start.29 = (bf16[128,2560]{1,0:T(8,128)(2,1)}, bf16[128,2560]{1,0:T(8,128)(2,1)}, u32[]{:S(2)}, u32[]{:S(2)}) collective-permute-start(bf16[128,2560]{1,0:T(8,128)(2,1)} %multiply_convert_fusion.refs_0_), channel_id=1, source_target_pairs={{0,4},{1,5},{2,6},{3,7},{4,0},{5,1},{6,2},{7,3},{8,12},{9,13},{10,... | collective-permute-start | bytes 1966088 | tf_op jit(solution)/shard_map/ppermute | solution.py:82
  156.3 25.9 %collective-permute-start.32 = (bf16[128,2560]{1,0:T(8,128)(2,1)}, bf16[128,2560]{1,0:T(8,128)(2,1)}, u32[]{:S(2)}, u32[]{:S(2)}) collective-permute-start(bf16[128,2560]{1,0:T(8,128)(2,1)} %pad_maximum_fusion.4.refs_0_.refs_12_), channel_id=1, source_target_pairs={{0,2},{1,3},{2,0},{3,1},{4,6},{5,7},{6,4},{7,5},{8,10},{9,11},{10,... | collective-permute-start | bytes 1966088 | tf_op jit(solution)/shard_map/ppermute | solution.py:82
  156.8 25.3 %collective-permute-start.33 = (bf16[128,2560]{1,0:T(8,128)(2,1)}, bf16[128,2560]{1,0:T(8,128)(2,1)}, u32[]{:S(2)}, u32[]{:S(2)}) collective-permute-start(bf16[128,2560]{1,0:T(8,128)(2,1)} %collective-permute-done.28.refs_1_), channel_id=1, source_target_pairs={{0,4},{1,5},{2,6},{3,7},{4,0},{5,1},{6,2},{7,3},{8,12},{9,13},{10,... | collective-permute-start | bytes 1966088 | tf_op jit(solution)/shard_map/ppermute | solution.py:82
  158.5 23.6 %collective-permute-start.34 = (bf16[64,2560]{1,0:T(8,128)(2,1)}, bf16[64,2560]{1,0:T(8,128)(2,1)}, u32[]{:S(2)}, u32[]{:S(2)}) collective-permute-start(bf16[64,2560]{1,0:T(8,128)(2,1)} %slice.262), channel_id=1, source_target_pairs={{0,24},{1,25},{2,26},{3,27},{4,28},{5,29},{6,30},{7,31},{8,16},{9,... | collective-permute-start | bytes 983048 | tf_op jit(solution)/shard_map/ppermute | solution.py:82
  185.9 24.7 %collective-permute-start.36 = (bf16[128,2560]{1,0:T(8,128)(2,1)}, bf16[128,2560]{1,0:T(8,128)(2,1)}, u32[]{:S(2)}, u32[]{:S(2)}) collective-permute-start(bf16[128,2560]{1,0:T(8,128)(2,1)} %add_convert_fusion.1), channel_id=1, source_target_pairs={{0,2},{1,3},{2,0},{3,1},{4,6},{5,7},{6,4},{7,5},{8,10},{9,11},{10,... | collective-permute-start | bytes 1966088 | tf_op jit(solution)/shard_map/ppermute | solution.py:82
  187.4 23.2 %collective-permute-start.37 = (bf16[128,2560]{1,0:T(8,128)(2,1)}, bf16[128,2560]{1,0:T(8,128)(2,1)}, u32[]{:S(2)}, u32[]{:S(2)}) collective-permute-start(bf16[128,2560]{1,0:T(8,128)(2,1)} %collective-permute-done.33.refs_3_.refs_1_), channel_id=1, source_target_pairs={{0,1},{1,0},{2,3},{3,2},{4,5},{5,4},{6,7},{7,6},{8,9},{9,8},{10,11... | collective-permute-start | bytes 1966088 | tf_op jit(solution)/shard_map/ppermute | solution.py:82
  187.4 23.2 %collective-permute-start.38 = (bf16[64,2560]{1,0:T(8,128)(2,1)S(1)}, bf16[64,2560]{1,0:T(8,128)(2,1)}, u32[]{:S(2)}, u32[]{:S(2)}) collective-permute-start(bf16[64,2560]{1,0:T(8,128)(2,1)S(1)} %get-tuple-element.1659), channel_id=1, source_target_pairs={{0,24},{1,25},{2,26},{3,27},{4,28},{5,29},{6,30},{7,31},{8,16},{9,... | collective-permute-start | bytes 983048 | tf_op jit(solution)/shard_map/ppermute | solution.py:82
  190.9 19.7 %collective-permute-start.39 = (bf16[128,2560]{1,0:T(8,128)(2,1)}, bf16[128,2560]{1,0:T(8,128)(2,1)}, u32[]{:S(2)}, u32[]{:S(2)}) collective-permute-start(bf16[128,2560]{1,0:T(8,128)(2,1)} %collective-permute-done.29.refs_2_.refs_0_), channel_id=1, source_target_pairs={{0,1},{1,0},{2,3},{3,2},{4,5},{5,4},{6,7},{7,6},{8,9},{9,8},{10,11... | collective-permute-start | bytes 1966088 | tf_op jit(solution)/shard_map/ppermute | solution.py:82
  191.1 19.5 %collective-permute-start.40 = (bf16[128,2560]{1,0:T(8,128)(2,1)}, bf16[128,2560]{1,0:T(8,128)(2,1)}, u32[]{:S(2)}, u32[]{:S(2)}) collective-permute-start(bf16[128,2560]{1,0:T(8,128)(2,1)} %pad_maximum_fusion.5.refs_0_.refs_4_), channel_id=1, source_target_pairs={{0,4},{1,5},{2,6},{3,7},{4,0},{5,1},{6,2},{7,3},{8,12},{9,13},{10,... | collective-permute-start | bytes 1966088 | tf_op jit(solution)/shard_map/ppermute | solution.py:82
  219.6 19.0 %collective-permute-start.44 = (bf16[128,2560]{1,0:T(8,128)(2,1)}, bf16[128,2560]{1,0:T(8,128)(2,1)S(1)}, u32[]{:S(2)}, u32[]{:S(2)}) collective-permute-start(bf16[128,2560]{1,0:T(8,128)(2,1)} %pad_maximum_fusion.4.refs_0_.refs_12_), channel_id=1, source_target_pairs={{0,4},{1,5},{2,6},{3,7},{4,0},{5,1},{6,2},{7,3},{8,12},{9,13},{10,... | collective-permute-start | bytes 1966088 | tf_op jit(solution)/shard_map/ppermute | solution.py:82
  221.3 17.3 %collective-permute-start.45 = (bf16[128,2560]{1,0:T(8,128)(2,1)}, bf16[128,2560]{1,0:T(8,128)(2,1)}, u32[]{:S(2)}, u32[]{:S(2)}) collective-permute-start(bf16[128,2560]{1,0:T(8,128)(2,1)} %pad_maximum_fusion.4.refs_0_.refs_12_), channel_id=1, source_target_pairs={{0,1},{1,0},{2,3},{3,2},{4,5},{5,4},{6,7},{7,6},{8,9},{9,8},{10,11... | collective-permute-start | bytes 1966088 | tf_op jit(solution)/shard_map/ppermute | solution.py:82
  221.3 17.3 %collective-permute-start.43 = (bf16[128,2560]{1,0:T(8,128)(2,1)S(1)}, bf16[128,2560]{1,0:T(8,128)(2,1)}, u32[]{:S(2)}, u32[]{:S(2)}) collective-permute-start(bf16[128,2560]{1,0:T(8,128)(2,1)S(1)} %maximum_select_fusion.8), channel_id=1, source_target_pairs={{0,2},{1,3},{2,0},{3,1},{4,6},{5,7},{6,4},{7,5},{8,10},{9,11},{10,... | collective-permute-start | bytes 1966088 | tf_op jit(solution)/shard_map/ppermute | solution.py:82
  255.2 17.1 %collective-permute-start.57 = (bf16[128,2560]{1,0:T(8,128)(2,1)}, bf16[128,2560]{1,0:T(8,128)(2,1)}, u32[]{:S(2)}, u32[]{:S(2)}) collective-permute-start(bf16[128,2560]{1,0:T(8,128)(2,1)} %collective-permute-done.40.refs_2_.refs_8_), channel_id=1, source_target_pairs={{0,2},{1,3},{2,0},{3,1},{4,6},{5,7},{6,4},{7,5},{8,10},{9,11},{10,... | collective-permute-start | bytes 1966088 | tf_op jit(solution)/shard_map/ppermute | solution.py:82
  310.2 27.2 %collective-permute-start.69 = (bf16[256,1280]{1,0:T(8,128)(2,1)S(1)}, bf16[256,1280]{1,0:T(8,128)(2,1)}, u32[]{:S(2)}, u32[]{:S(2)}) collective-permute-start(bf16[256,1280]{1,0:T(8,128)(2,1)S(1)} %bitcast.125), channel_id=1, source_target_pairs={{0,1},{1,0},{2,3},{3,2},{4,5},{5,4},{6,7},{7,6},{8,9},{9,8},{10,11... | collective-permute-start | bytes 1966088 | tf_op jit(solution)/shard_map/ppermute | solution.py:82
  310.3 27.1 %collective-permute-start.70 = (bf16[256,1280]{1,0:T(8,128)(2,1)S(1)}, bf16[256,1280]{1,0:T(8,128)(2,1)}, u32[]{:S(2)}, u32[]{:S(2)}) collective-permute-start(bf16[256,1280]{1,0:T(8,128)(2,1)S(1)} %bitcast.126), channel_id=1, source_target_pairs={{0,4},{1,5},{2,6},{3,7},{4,0},{5,1},{6,2},{7,3},{8,12},{9,13},{10,... | collective-permute-start | bytes 1966088 | tf_op jit(solution)/shard_map/ppermute | solution.py:82
  312.6 24.8 %collective-permute-start.68 = (bf16[128,2560]{1,0:T(8,128)(2,1)}, bf16[128,2560]{1,0:T(8,128)(2,1)S(1)}, u32[]{:S(2)}, u32[]{:S(2)}) collective-permute-start(bf16[128,2560]{1,0:T(8,128)(2,1)} %slice.391), channel_id=1, source_target_pairs={{0,2},{1,3},{2,0},{3,1},{4,6},{5,7},{6,4},{7,5},{8,10},{9,11},{10,... | collective-permute-start | bytes 1966088 | tf_op jit(solution)/shard_map/ppermute | solution.py:82
  346.0 19.4 %collective-permute-start.73 = (bf16[256,1280]{1,0:T(8,128)(2,1)}, bf16[256,1280]{1,0:T(8,128)(2,1)}, u32[]{:S(2)}, u32[]{:S(2)}) collective-permute-start(bf16[256,1280]{1,0:T(8,128)(2,1)} %pad_maximum_fusion.8.refs_4_), channel_id=1, source_target_pairs={{0,1},{1,0},{2,3},{3,2},{4,5},{5,4},{6,7},{7,6},{8,9},{9,8},{10,11... | collective-permute-start | bytes 1966088 | tf_op jit(solution)/shard_map/ppermute | solution.py:82
  346.3 19.2 %collective-permute-start.74 = (bf16[256,1280]{1,0:T(8,128)(2,1)}, bf16[256,1280]{1,0:T(8,128)(2,1)}, u32[]{:S(2)}, u32[]{:S(2)}) collective-permute-start(bf16[256,1280]{1,0:T(8,128)(2,1)} %pad_maximum_fusion.8.refs_4_), channel_id=1, source_target_pairs={{0,4},{1,5},{2,6},{3,7},{4,0},{5,1},{6,2},{7,3},{8,12},{9,13},{10,... | collective-permute-start | bytes 1966088 | tf_op jit(solution)/shard_map/ppermute | solution.py:82
  347.1 18.4 %collective-permute-start.77 = (bf16[256,1280]{1,0:T(8,128)(2,1)S(1)}, bf16[256,1280]{1,0:T(8,128)(2,1)}, u32[]{:S(2)}, u32[]{:S(2)}) collective-permute-start(bf16[256,1280]{1,0:T(8,128)(2,1)S(1)} %bitcast.139), channel_id=1, source_target_pairs={{0,1},{1,0},{2,3},{3,2},{4,5},{5,4},{6,7},{7,6},{8,9},{9,8},{10,11... | collective-permute-start | bytes 1966088 | tf_op jit(solution)/shard_map/ppermute | solution.py:82
  353.7 19.3 %collective-permute-start.79 = (bf16[320,1152]{1,0:T(8,128)(2,1)}, bf16[320,1152]{1,0:T(8,128)(2,1)}, u32[]{:S(2)}, u32[]{:S(2)}) collective-permute-start(bf16[320,1152]{1,0:T(8,128)(2,1)} %get-tuple-element.2292), channel_id=1, source_target_pairs={{0,8},{1,9},{2,10},{3,11},{4,12},{5,13},{6,14},{7,15},{8,0},{9,1},... | collective-permute-start | bytes 2211848 | tf_op jit(solution)/shard_map/ppermute | solution.py:82
  373.0 45.9 %collective-permute-start.81 = (bf16[256,1280]{1,0:T(8,128)(2,1)S(1)}, bf16[256,1280]{1,0:T(8,128)(2,1)}, u32[]{:S(2)}, u32[]{:S(2)}) collective-permute-start(bf16[256,1280]{1,0:T(8,128)(2,1)S(1)} %bitcast.140), channel_id=1, source_target_pairs={{0,4},{1,5},{2,6},{3,7},{4,0},{5,1},{6,2},{7,3},{8,12},{9,13},{10,... | collective-permute-start | bytes 1966088 | tf_op jit(solution)/shard_map/ppermute | solution.py:82
  375.3 43.6 %collective-permute-start.82 = (bf16[160,1280]{1,0:T(8,128)(2,1)}, bf16[160,1280]{1,0:T(8,128)(2,1)S(1)}, u32[]{:S(2)}, u32[]{:S(2)}) collective-permute-start(bf16[160,1280]{1,0:T(8,128)(2,1)} %get-tuple-element.2504), channel_id=1, source_target_pairs={{0,8},{1,9},{2,10},{3,11},{4,12},{5,13},{6,14},{7,15},{8,16},{9,17... | collective-permute-start | bytes 1228808 | tf_op jit(solution)/shard_map/ppermute | solution.py:82
  377.0 41.9 %collective-permute-start.83 = (bf16[160,1280]{1,0:T(8,128)(2,1)}, bf16[160,1280]{1,0:T(8,128)(2,1)}, u32[]{:S(2)}, u32[]{:S(2)}) collective-permute-start(bf16[160,1280]{1,0:T(8,128)(2,1)} %get-tuple-element.2503), channel_id=1, source_target_pairs={{0,16},{1,17},{2,18},{3,19},{4,20},{5,21},{6,22},{7,23},{8,24},{9,... | collective-permute-start | bytes 1228808 | tf_op jit(solution)/shard_map/ppermute | solution.py:82
  378.0 40.9 %collective-permute-start.84 = (bf16[160,1280]{1,0:T(8,128)(2,1)}, bf16[160,1280]{1,0:T(8,128)(2,1)}, u32[]{:S(2)}, u32[]{:S(2)}) collective-permute-start(bf16[160,1280]{1,0:T(8,128)(2,1)} %get-tuple-element.2502), channel_id=1, source_target_pairs={{0,24},{1,25},{2,26},{3,27},{4,28},{5,29},{6,30},{7,31},{8,0},{9,1... | collective-permute-start | bytes 1228808 | tf_op jit(solution)/shard_map/ppermute | solution.py:82
  380.5 38.4 %collective-permute-start.85 = (bf16[1280,256]{1,0:T(8,128)(2,1)}, bf16[1280,256]{1,0:T(8,128)(2,1)S(1)}, u32[]{:S(2)}, u32[]{:S(2)}) collective-permute-start(bf16[1280,256]{1,0:T(8,128)(2,1)} %get-tuple-element.2323), channel_id=1, source_target_pairs={{0,4},{1,5},{2,6},{3,7},{4,0},{5,1},{6,2},{7,3},{8,12},{9,13},{10,... | collective-permute-start | bytes 1966088 | tf_op jit(solution)/shard_map/ppermute | solution.py:82
  418.9 32.9 %collective-permute-start.89 = (bf16[320,2304]{1,0:T(8,128)(2,1)}, bf16[320,2304]{1,0:T(8,128)(2,1)}, u32[]{:S(2)}, u32[]{:S(2)}) collective-permute-start(bf16[320,2304]{1,0:T(8,128)(2,1)} %get-tuple-element.2397), channel_id=1, source_target_pairs={{0,8},{1,9},{2,10},{3,11},{4,12},{5,13},{6,14},{7,15},{8,0},{9,1},... | collective-permute-start | bytes 4423688 | tf_op jit(solution)/shard_map/ppermute | solution.py:82
  452.9 44.4 %collective-permute-start.91 = (bf16[192,1280]{1,0:T(8,128)(2,1)}, bf16[192,1280]{1,0:T(8,128)(2,1)}, u32[]{:S(2)}, u32[]{:S(2)}) collective-permute-start(bf16[192,1280]{1,0:T(8,128)(2,1)} %get-tuple-element.2498), channel_id=1, source_target_pairs={{0,8},{1,9},{2,10},{3,11},{4,12},{5,13},{6,14},{7,15},{8,16},{9,17... | collective-permute-start | bytes 1474568 | tf_op jit(solution)/shard_map/ppermute | solution.py:82
  453.2 44.2 %collective-permute-start.92 = (bf16[192,1280]{1,0:T(8,128)(2,1)}, bf16[192,1280]{1,0:T(8,128)(2,1)}, u32[]{:S(2)}, u32[]{:S(2)}) collective-permute-start(bf16[192,1280]{1,0:T(8,128)(2,1)} %get-tuple-element.2497), channel_id=1, source_target_pairs={{0,16},{1,17},{2,18},{3,19},{4,20},{5,21},{6,22},{7,23},{8,24},{9,... | collective-permute-start | bytes 1474568 | tf_op jit(solution)/shard_map/ppermute | solution.py:82
  454.3 43.0 %collective-permute-start.93 = (bf16[192,1280]{1,0:T(8,128)(2,1)}, bf16[192,1280]{1,0:T(8,128)(2,1)}, u32[]{:S(2)}, u32[]{:S(2)}) collective-permute-start(bf16[192,1280]{1,0:T(8,128)(2,1)} %get-tuple-element.2496), channel_id=1, source_target_pairs={{0,24},{1,25},{2,26},{3,27},{4,28},{5,29},{6,30},{7,31},{8,0},{9,1... | collective-permute-start | bytes 1474568 | tf_op jit(solution)/shard_map/ppermute | solution.py:82
  456.9 40.5 %collective-permute-start.94 = (bf16[128,2560]{1,0:T(8,128)(2,1)S(1)}, bf16[128,2560]{1,0:T(8,128)(2,1)}, u32[]{:S(2)}, u32[]{:S(2)}) collective-permute-start(bf16[128,2560]{1,0:T(8,128)(2,1)S(1)} %slice.390), channel_id=1, source_target_pairs={{0,2},{1,3},{2,0},{3,1},{4,6},{5,7},{6,4},{7,5},{8,10},{9,11},{10,... | collective-permute-start | bytes 1966088 | tf_op jit(solution)/shard_map/ppermute | solution.py:82
  459.2 38.1 %collective-permute-start.95 = (bf16[160,1280]{1,0:T(8,128)(2,1)}, bf16[160,1280]{1,0:T(8,128)(2,1)}, u32[]{:S(2)}, u32[]{:S(2)}) collective-permute-start(bf16[160,1280]{1,0:T(8,128)(2,1)} %dynamic-slice_bitcast_fusion.7), channel_id=1, source_target_pairs={{0,8},{1,9},{2,10},{3,11},{4,12},{5,13},{6,14},{7,15},{8,16},{9,17... | collective-permute-start | bytes 1228808 | tf_op jit(solution)/shard_map/ppermute | solution.py:82
  498.2 26.7 %collective-permute-start.96 = (bf16[160,1280]{1,0:T(8,128)(2,1)S(1)}, bf16[160,1280]{1,0:T(8,128)(2,1)S(1)}, u32[]{:S(2)}, u32[]{:S(2)}) collective-permute-start(bf16[160,1280]{1,0:T(8,128)(2,1)S(1)} %get-tuple-element.2500), channel_id=1, source_target_pairs={{0,16},{1,17},{2,18},{3,19},{4,20},{5,21},{6,22},{7,23},{8,24},{9,... | collective-permute-start | bytes 1228808 | tf_op jit(solution)/shard_map/ppermute | solution.py:82
  505.7 26.5 %collective-permute-start.99 = (bf16[160,1280]{1,0:T(8,128)(2,1)}, bf16[160,1280]{1,0:T(8,128)(2,1)}, u32[]{:S(2)}, u32[]{:S(2)}) collective-permute-start(bf16[160,1280]{1,0:T(8,128)(2,1)} %get-tuple-element.2499), channel_id=1, source_target_pairs={{0,24},{1,25},{2,26},{3,27},{4,28},{5,29},{6,30},{7,31},{8,0},{9,1... | collective-permute-start | bytes 1228808 | tf_op jit(solution)/shard_map/ppermute | solution.py:82
  509.1 49.6 %collective-permute-start.100 = (bf16[320,2304]{1,0:T(8,128)(2,1)}, bf16[320,2304]{1,0:T(8,128)(2,1)}, u32[]{:S(2)}, u32[]{:S(2)}) collective-permute-start(bf16[320,2304]{1,0:T(8,128)(2,1)} %get-tuple-element.2460), channel_id=1, source_target_pairs={{0,8},{1,9},{2,10},{3,11},{4,12},{5,13},{6,14},{7,15},{8,0},{9,1},... | collective-permute-start | bytes 4423688 | tf_op jit(solution)/shard_map/ppermute | solution.py:82
  509.1 49.6 %collective-permute-start.101 = (f32[10,2560]{1,0:T(8,128)S(1)}, f32[10,2560]{1,0:T(8,128)}, u32[]{:S(2)}, u32[]{:S(2)}) collective-permute-start(f32[10,2560]{1,0:T(8,128)S(1)} %add.374), channel_id=1, source_target_pairs={{0,8},{1,9},{2,10},{3,11},{4,12},{5,13},{6,14},{7,15},{8,0},{9,1},... | collective-permute-start | bytes 307208 | tf_op jit(solution)/shard_map/ppermute | solution.py:82
  559.6 17.9 %collective-permute-start.102 = (f32[10,2560]{1,0:T(8,128)S(1)}, f32[10,2560]{1,0:T(8,128)}, u32[]{:S(2)}, u32[]{:S(2)}) collective-permute-start(f32[10,2560]{1,0:T(8,128)S(1)} %add.386), channel_id=1, source_target_pairs={{0,16},{1,17},{2,18},{3,19},{4,20},{5,21},{6,22},{7,23},{8,24},{9,... | collective-permute-start | bytes 307208 | tf_op jit(solution)/shard_map/ppermute | solution.py:82
  (154 other events, 1402.5 us)

commit v8 on v7

--- a/solution.py
+++ b/solution.py
@@ -979,7 +979,6 @@
               n2_rows_c=lay.over_c(live.n2_rows), cot_rows_c=lay.over_c(live.cot_rows))
 
     cuts = sections_of(mlp_gate.shape[1])
-    cuts = cuts[-1:] + cuts[:-1]
 
     def weight_piece(at, size):
         return mlp_weight_grads(
@@ -1070,28 +1069,27 @@
     del live.in_y_own, live.in_y_come
 
     in_x_own, in_x_come = owner_parts(live.in_x_part)
-    out_own, out_come = owner_parts(live.out_part.reshape(nz, 2 * own80, half))
     out_arriving = lay.over_x(live.out_far)
+    sums_z = lay.over_seq_bit(live.sums, 2)
     piece_c = weight_piece(*cuts[2])
     del live.in_x_part
     live.hold(piece_c=piece_c, in_x_own=in_x_own, in_x_come=in_x_come, out_arriving=out_arriving,
-              out_come=out_come[:1])
+              sums=live.sums + sums_z)
 
     sum_c = piece_sum(*live.piece_c)
     out_own, out_come = owner_parts(live.out_part.reshape(nz, 2 * own80, half))
     in_x_own, in_x_come, in_y_total = after((live.in_x_own, live.in_x_come, live.in_y_total), out_come[1])
     in_x_total = total_of(in_x_own, in_x_come)
-    sums_z = lay.over_seq_bit(live.sums, 2)
-    live.hold(sum_c=sum_c, sums_z=sums_z, out_total=total_of(out_own, live.out_come + out_come[1:]),
+    live.hold(sum_c=sum_c, out_total=total_of(out_own, out_come),
               in_y_grad=over_columns(in_y_total), in_x_grad=over_columns(in_x_total[: 2 * own80]),
               gate_total=in_x_total[2 * own80 :].reshape(own80, 2 * BLK),
               output=(live.mid + after(live.out_sum, out_come[1])[:tokens] + live.out_arriving.astype(F32)
                       ).astype(BF16)[None])
 
-    sums = live.sums + live.sums_z
+    sums = live.sums
     for bit in bits[2:]:
         sums = sums + lay.over_seq_bit(sums, bit)
-    mlp_down_grad, mlp_gate_grad, mlp_up_grad = joined_columns([live.sum_b, live.sum_c, live.sum_a])
+    mlp_down_grad, mlp_gate_grad, mlp_up_grad = joined_columns([live.sum_a, live.sum_b, live.sum_c])
 
     def final(z, y, x, c):
         at = ((x * 2 + y) * nz + z) * 2 + c

time: 589 us -> 585 us (level)
    unnamed x199 -> x207, local copies, waits for them, and re-layouts: 22.2 us -> 22.1 us
  transfers between devices with their start and end apart: 105 -> 105, of which waited for: 28 -> 30; matrix products, arithmetic and copies ran while one was open for 16% -> 16% of each run, Pallas kernels for 40% -> 41%
where the time goes in v8:
time: 585 us; the launch traced here: 576 us
  Pallas kernels  233 us (40%)
  waiting for transfers between devices  122 us (21%)
  starting transfers between devices  93.2 us (16%)
  local copies, waits for them, and re-layouts  51.8 us (9%)
  other arithmetic  46.3 us (8%)
  matrix products  26.3 us (4%)
    ppermute x105, waiting for transfers between devices, send(): return lax.ppermute(value, ALL, self.pairs(target))  122 us
    pallas_call x3, Pallas kernels, mlp_weight_grads(): pl.pallas_call(body, grid_spec=pltpu.PrefetchScalarGridSpec(num_scalar_pr...  98.3 us
    ppermute x105, starting transfers between devices, send(): return lax.ppermute(value, ALL, self.pairs(target))  93.2 us
    pallas_call x2, Pallas kernels, grad_hidden_of(): pl.pallas_call(body, grid=(pl.cdiv(ff, BLK),), in_specs=[ANY] * count + [...  25.7 us
    pallas_call x1, Pallas kernels, mlp_forward(): pl.pallas_call(body, in_specs=[ANY] * (count + 3), out_shape=[act, act, a...  23.3 us
    unnamed x207, local copies, waits for them, and re-layouts  22.1 us
    pallas_call x3, Pallas kernels, by_head(): pl.pallas_call(body, grid=(heads,), in_specs=in_specs, out_specs=[spec(o....  19.9 us
    pallas_call x1, Pallas kernels, mlp_rest(): pl.pallas_call(body, grid=(width // block,), in_specs=[whole] * 3 + [weig...  19 us
  transfers between devices with their start and end apart: 105, of which 30 were waited for; matrix products, arithmetic and copies ran while one was open for 16% of the time, Pallas kernels for 41%

profile of v8, /device:TPU:2, one launch (start us, length us, event | category | flops | bytes accessed | tf_op | source)
XLA Modules:
  0.0 576.0 jit_solution(2801153438763327628)
XLA Ops:
  3.6 3.4 collective-permute-start
  12.3 3.7 collective-permute-start.2
  24.1 13.9 %collective-permute-done.6.refs_1_ = bf16[128,2560]{1,0:T(8,128)(2,1)S(1)} collective-permute-done((bf16[128,2560]{1,0:T(8,128)(2,1)S(1)}, bf16[128,2560]{1,0:T(8,128)(2,1)S(1)}, u32[]{:S(2)}, u32[]{:S(2)}) %collective-permute-start.6) | collective-permute-done | bytes 655392 | tf_op jit(solution)/shard_map/ppermute | solution.py:82
  39.6 3.3 convolution_convert_fusion
  50.5 7.1 %shard_map.195 = (bf16[2,128,1280]{2,1,0:T(8,128)(2,1)S(1)}, f32[2,128,1280]{2,1,0:T(8,128)S(1)}, f32[2,128,1280]{2,1,0:T(8,128)S(1)}, f32[2,128,1280]{2,1,0:T(8...) custom-call(f32[2,2]{1,0:T(2,128)S(1)} %pad_maximum_fusion.16.flags_ref, bf16[2,128,1280]{2,1,0:T(8,128)(2,1)S(1)} %bitcast.118, ...), custom_call_target="tpu_custom_call" | custom-call | flops 1 | bytes 1 | tf_op jit(solution)/shard_map/pallas_call | solution.py:266
  61.1 4.9 collective-permute-done.10
  72.5 3.4 shard_map.196
  77.0 3.8 fusion.76
  83.0 3.9 collective-permute-start.18
  88.7 8.2 %collective-permute-done.16 = bf16[640,640]{1,0:T(8,128)(2,1)S(1)} collective-permute-done((bf16[640,640]{1,0:T(8,128)(2,1)}, bf16[640,640]{1,0:T(8,128)(2,1)S(1)}, u32[]{:S(2)}, u32[]{:S(2)}) %collective-permute-start.16) | collective-permute-done | bytes 819232 | tf_op jit(solution)/shard_map/ppermute | solution.py:82
  105.0 3.8 collective-permute-done.19.refs_2_
  111.7 12.8 %shard_map.197.refs_4_ = f32[512,1920]{1,0:T(8,128)} custom-call(bf16[128,2560]{1,0:T(8,128)(2,1)} %bitcast.141, bf16[128,2560]{1,0:T(8,128)(2,1)} %collective-permute-done.13.refs_1_, bf16[128,2560]{1,0:T(8,128)(2,1)} %copy-done.98, bf16[128,2560]{1,0:T(8,128)(2,1)} %collective-permute-done.23.refs_3_, bf16[2560,1920]{1,0:T(8,128)(2,1)} %refs_23_.5), custom_call_target="tpu_custom_call" | custom-call | flops 11699999744 | bytes 26000000 | tf_op jit(solution)/shard_map/pallas_call | solution.py:299
  139.5 13.0 %shard_map.198.refs_20_ = f32[512,1920]{1,0:T(8,128)} custom-call(bf16[128,2560]{1,0:T(8,128)(2,1)} %copy-done.75, bf16[128,2560]{1,0:T(8,128)(2,1)} %collective-permute-done.21.refs_1_.refs_3_, bf16[128,2560]{1,0:T(8,128)(2,1)} %copy-done.99, bf16[128,2560]{1,0:T(8,128)(2,1)} %collective-permute-done.26.refs_3_, bf16[2560,1920]{1,0:T(8,128)(2,1)} %refs_23_.5), custom_call_target="tpu_custom_call" | custom-call | flops 11699999744 | bytes 26000000 | tf_op jit(solution)/shard_map/pallas_call | solution.py:299
  159.2 23.3 %shard_map.199 = (bf16[512,1920]{1,0:T(8,128)(2,1)}, bf16[512,1920]{1,0:T(8,128)(2,1)}, bf16[512,1920]{1,0:T(8,128)(2,1)}, f32[128,2560]{1,0:T(8,128)}, bf16[128,2560]{1,0:T(8,128)(2,1)}) custom-call(bf16[128,2560]{1,0:T(8,128)(2,1)} %multiply_convert_fusion.refs_0_, bf16[128,2560]{1,0:T(8,128)(2,1)} %collective-permute-done.28.refs_1_, ...), custom_call_target="tpu_custom_call" | custom-call | flops 20700000256 | bytes 46000000 | tf_op jit(solution)/shard_map/pallas_call | solution.py:384
  187.8 3.5 collective-permute-start.38
  192.0 19.0 %shard_map.200 = (f32[128,2560]{1,0:T(8,128)}, bf16[128,2560]{1,0:T(8,128)(2,1)}, f32[256,2560]{1,0:T(8,128)}, bf16[256,2560]{1,0:T(8,128)(2,1)}) custom-call(bf16[512,1920]{1,0:T(8,128)(2,1)} %get-tuple-element.2397.hid_ref.refs_24_, bf16[512,1920]{1,0:T(8,128)(2,1)} %get-tuple-element.2398.gg_ref.refs_25_, ...), custom_call_target="tpu_custom_call" | custom-call | flops 17100000256 | bytes 38000000 | tf_op jit(solution)/shard_map/pallas_call | solution.py:423
  224.4 3.2 shard_map.201.refs_31_
  227.7 3.2 shard_map.202.refs_27_
  230.9 3.3 collective-permute-done.46
  234.2 4.8 collective-permute-done.43
  246.6 5.4 shard_map.203
  259.1 3.3 fusion.43
  268.9 3.8 collective-permute-done.57.refs_3_.refs_9_
  272.7 5.8 %collective-permute-done.55.refs_3_.refs_17_ = bf16[128,2560]{1,0:T(8,128)(2,1)} collective-permute-done((bf16[128,2560]{1,0:T(8,128)(2,1)}, bf16[128,2560]{1,0:T(8,128)(2,1)}, u32[]{:S(2)}, u32[]{:S(2)}) %collective-permute-start.55) | collective-permute-done | bytes 655392 | tf_op jit(solution)/shard_map/ppermute | solution.py:82
  279.9 7.4 %shard_map.204 = (bf16[2,128,1280]{2,1,0:T(8,128)(2,1)S(1)}, bf16[2,128,1280]{2,1,0:T(8,128)(2,1)S(1)}, bf16[2,128,1280]{2,1,0:T(8,128)(2,1)S(1)}, f32[2,16,1280...) custom-call(f32[2,2]{1,0:T(2,128)S(1)} %pad_maximum_fusion.16.flags_ref, ...), custom_call_target="tpu_custom_call" | custom-call | flops 1 | bytes 1 | tf_op jit(solution)/shard_map/pallas_call | solution.py:266
  293.9 3.2 shard_map.206.refs_29_
  297.2 3.4 shard_map.205.refs_33_
  301.8 3.4 fusion.41
  305.3 3.2 add_add_fusion
  313.4 37.2 %shard_map.207 = (f32[320,2304]{1,0:T(8,128)}, bf16[320,2304]{1,0:T(8,128)(2,1)}) custom-call(s32[3]{0:T(128)} %pad_add_fusion.1.place_ref, bf16[128,2560]{1,0:T(8,128)(2,1)} %collective-permute-done.29.refs_2_.refs_0_, bf16[128,2560]{1,0:T(8,128)(2,1)} %collective-permute-done.33.refs_3_.refs_1_, bf16[128,2560]{1,0:T(8,128)(2,1)} %collective-permute-done.39.refs_2_, ...), custom_call_target="tpu_custom_call" | custom-call | flops 31499999232 | bytes 70000000 | tf_op jit(solution)/shard_map/pallas_call | solution.py:540
  356.6 4.0 shard_map.208
  364.3 3.4 shard_map.210
  372.9 5.3 shard_map.209
  379.1 6.0 %collective-permute-done.76 = bf16[4,80,512]{2,1,0:T(8,128)(2,1)S(1)} collective-permute-done((bf16[4,80,512]{2,1,0:T(8,128)(2,1)}, bf16[4,80,512]{2,1,0:T(8,128)(2,1)S(1)}, u32[]{:S(2)}, u32[]{:S(2)}) %collective-permute-start.76) | collective-permute-done | bytes 327712 | tf_op jit(solution)/shard_map/ppermute | solution.py:82
  385.0 4.6 collective-permute-done.79.refs_1_
  398.0 37.0 %shard_map.211 = (f32[320,2304]{1,0:T(8,128)}, bf16[320,2304]{1,0:T(8,128)(2,1)}) custom-call(s32[3]{0:T(128)} %pad_add_fusion.1.place_ref, bf16[128,2560]{1,0:T(8,128)(2,1)} %collective-permute-done.29.refs_2_.refs_0_, bf16[128,2560]{1,0:T(8,128)(2,1)} %collective-permute-done.33.refs_3_.refs_1_, bf16[128,2560]{1,0:T(8,128)(2,1)} %collective-permute-done.39.refs_2_, ...), custom_call_target="tpu_custom_call" | custom-call | flops 31499999232 | bytes 70000000 | tf_op jit(solution)/shard_map/pallas_call | solution.py:540
  444.3 5.2 shard_map.212
  450.4 5.2 shard_map.213
  455.8 12.0 %collective-permute-done.89.refs_3_ = bf16[320,2304]{1,0:T(8,128)(2,1)} collective-permute-done((bf16[320,2304]{1,0:T(8,128)(2,1)}, bf16[320,2304]{1,0:T(8,128)(2,1)}, u32[]{:S(2)}, u32[]{:S(2)}) %collective-permute-start.89) | collective-permute-done | bytes 1474592 | tf_op jit(solution)/shard_map/ppermute | solution.py:82
  475.1 24.2 %shard_map.214 = (f32[320,1152]{1,0:T(8,128)}, bf16[320,1152]{1,0:T(8,128)(2,1)}) custom-call(s32[3]{0:T(128)} %pad_add_fusion.1.place_ref, bf16[128,2560]{1,0:T(8,128)(2,1)} %collective-permute-done.29.refs_2_.refs_0_, bf16[128,2560]{1,0:T(8,128)(2,1)} %collective-permute-done.33.refs_3_.refs_1_, bf16[128,2560]{1,0:T(8,128)(2,1)} %collective-permute-done.39.refs_2_, ...), custom_call_target="tpu_custom_call" | custom-call | flops 15299999744 | bytes 34000000 | tf_op jit(solution)/shard_map/pallas_call | solution.py:540
  499.3 6.1 %collective-permute-done.95 = f32[10,2560]{1,0:T(8,128)} collective-permute-done((f32[10,2560]{1,0:T(8,128)S(1)}, f32[10,2560]{1,0:T(8,128)}, u32[]{:S(2)}, u32[]{:S(2)}) %collective-permute-start.95) | collective-permute-done | bytes 102432 | tf_op jit(solution)/shard_map/ppermute | solution.py:82
  507.4 5.6 collective-permute-start.96
  513.0 3.4 collective-permute-start.100
  516.6 15.5 %collective-permute-done.96 = bf16[160,1280]{1,0:T(8,128)(2,1)S(1)} collective-permute-done((bf16[160,1280]{1,0:T(8,128)(2,1)S(1)}, bf16[160,1280]{1,0:T(8,128)(2,1)S(1)}, u32[]{:S(2)}, u32[]{:S(2)}) %collective-permute-start.96) | collective-permute-done | bytes 409632 | tf_op jit(solution)/shard_map/ppermute | solution.py:82
  539.5 5.0 collective-permute-done.99
  547.9 7.5 %collective-permute-done.101.refs_5_ = bf16[320,1152]{1,0:T(8,128)(2,1)} collective-permute-done((bf16[320,1152]{1,0:T(8,128)(2,1)}, bf16[320,1152]{1,0:T(8,128)(2,1)}, u32[]{:S(2)}, u32[]{:S(2)}) %collective-permute-start.101) | collective-permute-done | bytes 737312 | tf_op jit(solution)/shard_map/ppermute | solution.py:82
  555.4 3.7 collective-permute-start.102
  564.2 7.3 %shard_map.215 = (f32[320,1920]{1,0:T(8,128)}, f32[320,1920]{1,0:T(8,128)}, f32[320,1920]{1,0:T(8,128)}) custom-call(f32[320,2304]{1,0:T(8,128)} %get-tuple-element.2471.refs_0_, bf16[320,2304]{1,0:T(8,128)(2,1)} %collective-permute-done.79.refs_1_, f32[320,2304]{1,0:T(8,128)} %get-tuple-element.2473.refs_2_, ...), custom_call_target="tpu_custom_call" | custom-call | flops 1 | bytes 1 | tf_op jit(solution)/shard_map/pallas_call | solution.py:625
  (537 shorter events, 190.5 us)
Async XLA Ops:
  7.0 17.0 %collective-permute-start.5 = (bf16[1280,128]{1,0:T(8,128)(2,1)}, bf16[1280,128]{1,0:T(8,128)(2,1)}, u32[]{:S(2)}, u32[]{:S(2)}) collective-permute-start(bf16[1280,128]{1,0:T(8,128)(2,1)} %constant_dynamic-slice_fusion.5), channel_id=1, source_target_pairs={{0,2},{1,3},{2,0},{3,1},{4,6},{5,7},{6,4},{7,5},{8,10},{9,11},{10,... | collective-permute-start | bytes 983048 | tf_op jit(solution)/shard_map/ppermute | solution.py:82
  20.9 17.1 %collective-permute-start.6 = (bf16[128,2560]{1,0:T(8,128)(2,1)S(1)}, bf16[128,2560]{1,0:T(8,128)(2,1)S(1)}, u32[]{:S(2)}, u32[]{:S(2)}) collective-permute-start(bf16[128,2560]{1,0:T(8,128)(2,1)S(1)} %copy-done.23), channel_id=1, source_target_pairs={{0,2},{1,3},{2,0},{3,1},{4,6},{5,7},{6,4},{7,5},{8,10},{9,11},{10,... | collective-permute-start | bytes 1966088 | tf_op jit(solution)/shard_map/ppermute | solution.py:82
  38.1 27.9 %collective-permute-start.11 = (bf16[2560,640]{1,0:T(8,128)(2,1)S(1)}, bf16[2560,640]{1,0:T(8,128)(2,1)S(1)}, u32[]{:S(2)}, u32[]{:S(2)}) collective-permute-start(bf16[2560,640]{1,0:T(8,128)(2,1)S(1)} %copy-done.46), channel_id=1, source_target_pairs={{0,1},{1,0},{2,3},{3,2},{4,5},{5,4},{6,7},{7,6},{8,9},{9,8},{10,11... | collective-permute-start | bytes 9830408 | tf_op jit(solution)/shard_map/ppermute | solution.py:82
  44.0 17.1 %collective-permute-start.8 = (bf16[128,2560]{1,0:T(8,128)(2,1)S(1)}, bf16[128,2560]{1,0:T(8,128)(2,1)S(1)}, u32[]{:S(2)}, u32[]{:S(2)}) collective-permute-start(bf16[128,2560]{1,0:T(8,128)(2,1)S(1)} %bitcast.143), channel_id=1, source_target_pairs={{0,4},{1,5},{2,6},{3,7},{4,0},{5,1},{6,2},{7,3},{8,12},{9,13},{10,... | collective-permute-start | bytes 1966088 | tf_op jit(solution)/shard_map/ppermute | solution.py:82
  45.7 20.3 %collective-permute-start.10 = (bf16[640,640]{1,0:T(8,128)(2,1)}, bf16[640,640]{1,0:T(8,128)(2,1)S(1)}, u32[]{:S(2)}, u32[]{:S(2)}) collective-permute-start(bf16[640,640]{1,0:T(8,128)(2,1)} %constant_dynamic-slice_fusion.3), channel_id=1, source_target_pairs={{0,2},{1,3},{2,0},{3,1},{4,6},{5,7},{6,4},{7,5},{8,10},{9,11},{10,... | collective-permute-start | bytes 2457608 | tf_op jit(solution)/shard_map/ppermute | solution.py:82
  71.9 25.9 %collective-permute-start.13 = (bf16[128,2560]{1,0:T(8,128)(2,1)}, bf16[128,2560]{1,0:T(8,128)(2,1)}, u32[]{:S(2)}, u32[]{:S(2)}) collective-permute-start(bf16[128,2560]{1,0:T(8,128)(2,1)} %bitcast.140), channel_id=1, source_target_pairs={{0,2},{1,3},{2,0},{3,1},{4,6},{5,7},{6,4},{7,5},{8,10},{9,11},{10,... | collective-permute-start | bytes 1966088 | tf_op jit(solution)/shard_map/ppermute | solution.py:82
  75.9 21.8 %collective-permute-start.14 = (bf16[640,256]{1,0:T(8,128)(2,1)}, bf16[640,256]{1,0:T(8,128)(2,1)S(1)}, u32[]{:S(2)}, u32[]{:S(2)}) collective-permute-start(bf16[640,256]{1,0:T(8,128)(2,1)} %get-tuple-element.1338), channel_id=1, source_target_pairs={{0,1},{1,0},{2,3},{3,2},{4,5},{5,4},{6,7},{7,6},{8,9},{9,8},{10,11... | collective-permute-start | bytes 983048 | tf_op jit(solution)/shard_map/ppermute | solution.py:82
  75.9 21.5 %collective-permute-start.15 = (bf16[1280,640]{1,0:T(8,128)(2,1)}, bf16[1280,640]{1,0:T(8,128)(2,1)S(1)}, u32[]{:S(2)}, u32[]{:S(2)}) collective-permute-start(bf16[1280,640]{1,0:T(8,128)(2,1)} %constant_dynamic-slice_fusion.2), channel_id=1, source_target_pairs={{0,1},{1,0},{2,3},{3,2},{4,5},{5,4},{6,7},{7,6},{8,9},{9,8},{10,11... | collective-permute-start | bytes 4915208 | tf_op jit(solution)/shard_map/ppermute | solution.py:82
  76.4 20.4 %collective-permute-start.16 = (bf16[640,640]{1,0:T(8,128)(2,1)}, bf16[640,640]{1,0:T(8,128)(2,1)S(1)}, u32[]{:S(2)}, u32[]{:S(2)}) collective-permute-start(bf16[640,640]{1,0:T(8,128)(2,1)} %copy-done.66), channel_id=1, source_target_pairs={{0,4},{1,5},{2,6},{3,7},{4,0},{5,1},{6,2},{7,3},{8,12},{9,13},{10,... | collective-permute-start | bytes 2457608 | tf_op jit(solution)/shard_map/ppermute | solution.py:82
  108.8 17.5 %collective-permute-start.21 = (bf16[128,2560]{1,0:T(8,128)(2,1)}, bf16[128,2560]{1,0:T(8,128)(2,1)}, u32[]{:S(2)}, u32[]{:S(2)}) collective-permute-start(bf16[128,2560]{1,0:T(8,128)(2,1)} %collective-permute-done.13.refs_1_), channel_id=1, source_target_pairs={{0,4},{1,5},{2,6},{3,7},{4,0},{5,1},{6,2},{7,3},{8,12},{9,13},{10,... | collective-permute-start | bytes 1966088 | tf_op jit(solution)/shard_map/ppermute | solution.py:82
  109.3 17.2 %collective-permute-start.24 = (bf16[128,2560]{1,0:T(8,128)(2,1)}, bf16[128,2560]{1,0:T(8,128)(2,1)}, u32[]{:S(2)}, u32[]{:S(2)}) collective-permute-start(bf16[128,2560]{1,0:T(8,128)(2,1)} %fusion.22), channel_id=1, source_target_pairs={{0,2},{1,3},{2,0},{3,1},{4,6},{5,7},{6,4},{7,5},{8,10},{9,11},{10,... | collective-permute-start | bytes 1966088 | tf_op jit(solution)/shard_map/ppermute | solution.py:82
  131.5 21.0 %collective-permute-start.27 = (bf16[128,2560]{1,0:T(8,128)(2,1)}, bf16[128,2560]{1,0:T(8,128)(2,1)}, u32[]{:S(2)}, u32[]{:S(2)}) collective-permute-start(bf16[128,2560]{1,0:T(8,128)(2,1)} %multiply_convert_fusion.refs_0_), channel_id=1, source_target_pairs={{0,1},{1,0},{2,3},{3,2},{4,5},{5,4},{6,7},{7,6},{8,9},{9,8},{10,11... | collective-permute-start | bytes 1966088 | tf_op jit(solution)/shard_map/ppermute | solution.py:82
  131.5 21.0 %collective-permute-start.28 = (bf16[128,2560]{1,0:T(8,128)(2,1)}, bf16[128,2560]{1,0:T(8,128)(2,1)}, u32[]{:S(2)}, u32[]{:S(2)}) collective-permute-start(bf16[128,2560]{1,0:T(8,128)(2,1)} %multiply_convert_fusion.refs_0_), channel_id=1, source_target_pairs={{0,2},{1,3},{2,0},{3,1},{4,6},{5,7},{6,4},{7,5},{8,10},{9,11},{10,... | collective-permute-start | bytes 1966088 | tf_op jit(solution)/shard_map/ppermute | solution.py:82
  133.0 19.5 %collective-permute-start.29 = (bf16[128,2560]{1,0:T(8,128)(2,1)}, bf16[128,2560]{1,0:T(8,128)(2,1)}, u32[]{:S(2)}, u32[]{:S(2)}) collective-permute-start(bf16[128,2560]{1,0:T(8,128)(2,1)} %multiply_convert_fusion.refs_0_), channel_id=1, source_target_pairs={{0,4},{1,5},{2,6},{3,7},{4,0},{5,1},{6,2},{7,3},{8,12},{9,13},{10,... | collective-permute-start | bytes 1966088 | tf_op jit(solution)/shard_map/ppermute | solution.py:82
  156.8 25.9 %collective-permute-start.32 = (bf16[128,2560]{1,0:T(8,128)(2,1)}, bf16[128,2560]{1,0:T(8,128)(2,1)}, u32[]{:S(2)}, u32[]{:S(2)}) collective-permute-start(bf16[128,2560]{1,0:T(8,128)(2,1)} %pad_maximum_fusion.4.refs_0_.refs_12_), channel_id=1, source_target_pairs={{0,2},{1,3},{2,0},{3,1},{4,6},{5,7},{6,4},{7,5},{8,10},{9,11},{10,... | collective-permute-start | bytes 1966088 | tf_op jit(solution)/shard_map/ppermute | solution.py:82
  157.3 25.3 %collective-permute-start.33 = (bf16[128,2560]{1,0:T(8,128)(2,1)}, bf16[128,2560]{1,0:T(8,128)(2,1)}, u32[]{:S(2)}, u32[]{:S(2)}) collective-permute-start(bf16[128,2560]{1,0:T(8,128)(2,1)} %collective-permute-done.28.refs_1_), channel_id=1, source_target_pairs={{0,4},{1,5},{2,6},{3,7},{4,0},{5,1},{6,2},{7,3},{8,12},{9,13},{10,... | collective-permute-start | bytes 1966088 | tf_op jit(solution)/shard_map/ppermute | solution.py:82
  159.0 23.6 %collective-permute-start.34 = (bf16[64,2560]{1,0:T(8,128)(2,1)}, bf16[64,2560]{1,0:T(8,128)(2,1)}, u32[]{:S(2)}, u32[]{:S(2)}) collective-permute-start(bf16[64,2560]{1,0:T(8,128)(2,1)} %slice.262), channel_id=1, source_target_pairs={{0,24},{1,25},{2,26},{3,27},{4,28},{5,29},{6,30},{7,31},{8,16},{9,... | collective-permute-start | bytes 983048 | tf_op jit(solution)/shard_map/ppermute | solution.py:82
  186.4 24.6 %collective-permute-start.36 = (bf16[128,2560]{1,0:T(8,128)(2,1)}, bf16[128,2560]{1,0:T(8,128)(2,1)}, u32[]{:S(2)}, u32[]{:S(2)}) collective-permute-start(bf16[128,2560]{1,0:T(8,128)(2,1)} %add_convert_fusion.1), channel_id=1, source_target_pairs={{0,2},{1,3},{2,0},{3,1},{4,6},{5,7},{6,4},{7,5},{8,10},{9,11},{10,... | collective-permute-start | bytes 1966088 | tf_op jit(solution)/shard_map/ppermute | solution.py:82
  187.8 23.1 %collective-permute-start.37 = (bf16[128,2560]{1,0:T(8,128)(2,1)}, bf16[128,2560]{1,0:T(8,128)(2,1)}, u32[]{:S(2)}, u32[]{:S(2)}) collective-permute-start(bf16[128,2560]{1,0:T(8,128)(2,1)} %collective-permute-done.33.refs_3_.refs_1_), channel_id=1, source_target_pairs={{0,1},{1,0},{2,3},{3,2},{4,5},{5,4},{6,7},{7,6},{8,9},{9,8},{10,11... | collective-permute-start | bytes 1966088 | tf_op jit(solution)/shard_map/ppermute | solution.py:82
  187.8 23.1 %collective-permute-start.38 = (bf16[64,2560]{1,0:T(8,128)(2,1)S(1)}, bf16[64,2560]{1,0:T(8,128)(2,1)}, u32[]{:S(2)}, u32[]{:S(2)}) collective-permute-start(bf16[64,2560]{1,0:T(8,128)(2,1)S(1)} %get-tuple-element.1657), channel_id=1, source_target_pairs={{0,24},{1,25},{2,26},{3,27},{4,28},{5,29},{6,30},{7,31},{8,16},{9,... | collective-permute-start | bytes 983048 | tf_op jit(solution)/shard_map/ppermute | solution.py:82
  191.4 19.6 %collective-permute-start.39 = (bf16[128,2560]{1,0:T(8,128)(2,1)}, bf16[128,2560]{1,0:T(8,128)(2,1)}, u32[]{:S(2)}, u32[]{:S(2)}) collective-permute-start(bf16[128,2560]{1,0:T(8,128)(2,1)} %collective-permute-done.29.refs_2_.refs_0_), channel_id=1, source_target_pairs={{0,1},{1,0},{2,3},{3,2},{4,5},{5,4},{6,7},{7,6},{8,9},{9,8},{10,11... | collective-permute-start | bytes 1966088 | tf_op jit(solution)/shard_map/ppermute | solution.py:82
  191.6 19.4 %collective-permute-start.40 = (bf16[128,2560]{1,0:T(8,128)(2,1)}, bf16[128,2560]{1,0:T(8,128)(2,1)}, u32[]{:S(2)}, u32[]{:S(2)}) collective-permute-start(bf16[128,2560]{1,0:T(8,128)(2,1)} %pad_maximum_fusion.5.refs_0_.refs_4_), channel_id=1, source_target_pairs={{0,4},{1,5},{2,6},{3,7},{4,0},{5,1},{6,2},{7,3},{8,12},{9,13},{10,... | collective-permute-start | bytes 1966088 | tf_op jit(solution)/shard_map/ppermute | solution.py:82
  220.0 19.0 %collective-permute-start.44 = (bf16[128,2560]{1,0:T(8,128)(2,1)}, bf16[128,2560]{1,0:T(8,128)(2,1)S(1)}, u32[]{:S(2)}, u32[]{:S(2)}) collective-permute-start(bf16[128,2560]{1,0:T(8,128)(2,1)} %pad_maximum_fusion.4.refs_0_.refs_12_), channel_id=1, source_target_pairs={{0,4},{1,5},{2,6},{3,7},{4,0},{5,1},{6,2},{7,3},{8,12},{9,13},{10,... | collective-permute-start | bytes 1966088 | tf_op jit(solution)/shard_map/ppermute | solution.py:82
  221.7 17.3 %collective-permute-start.45 = (bf16[128,2560]{1,0:T(8,128)(2,1)}, bf16[128,2560]{1,0:T(8,128)(2,1)}, u32[]{:S(2)}, u32[]{:S(2)}) collective-permute-start(bf16[128,2560]{1,0:T(8,128)(2,1)} %pad_maximum_fusion.4.refs_0_.refs_12_), channel_id=1, source_target_pairs={{0,1},{1,0},{2,3},{3,2},{4,5},{5,4},{6,7},{7,6},{8,9},{9,8},{10,11... | collective-permute-start | bytes 1966088 | tf_op jit(solution)/shard_map/ppermute | solution.py:82
  221.7 17.3 %collective-permute-start.43 = (bf16[128,2560]{1,0:T(8,128)(2,1)S(1)}, bf16[128,2560]{1,0:T(8,128)(2,1)}, u32[]{:S(2)}, u32[]{:S(2)}) collective-permute-start(bf16[128,2560]{1,0:T(8,128)(2,1)S(1)} %maximum_select_fusion.8), channel_id=1, source_target_pairs={{0,2},{1,3},{2,0},{3,1},{4,6},{5,7},{6,4},{7,5},{8,10},{9,11},{10,... | collective-permute-start | bytes 1966088 | tf_op jit(solution)/shard_map/ppermute | solution.py:82
  255.5 17.1 %collective-permute-start.57 = (bf16[128,2560]{1,0:T(8,128)(2,1)}, bf16[128,2560]{1,0:T(8,128)(2,1)}, u32[]{:S(2)}, u32[]{:S(2)}) collective-permute-start(bf16[128,2560]{1,0:T(8,128)(2,1)} %collective-permute-done.40.refs_2_.refs_8_), channel_id=1, source_target_pairs={{0,2},{1,3},{2,0},{3,1},{4,6},{5,7},{6,4},{7,5},{8,10},{9,11},{10,... | collective-permute-start | bytes 1966088 | tf_op jit(solution)/shard_map/ppermute | solution.py:82
  310.5 40.1 %collective-permute-start.69 = (bf16[256,1280]{1,0:T(8,128)(2,1)S(1)}, bf16[256,1280]{1,0:T(8,128)(2,1)}, u32[]{:S(2)}, u32[]{:S(2)}) collective-permute-start(bf16[256,1280]{1,0:T(8,128)(2,1)S(1)} %bitcast.124), channel_id=1, source_target_pairs={{0,1},{1,0},{2,3},{3,2},{4,5},{5,4},{6,7},{7,6},{8,9},{9,8},{10,11... | collective-permute-start | bytes 1966088 | tf_op jit(solution)/shard_map/ppermute | solution.py:82
  310.6 40.0 %collective-permute-start.70 = (bf16[256,1280]{1,0:T(8,128)(2,1)S(1)}, bf16[256,1280]{1,0:T(8,128)(2,1)}, u32[]{:S(2)}, u32[]{:S(2)}) collective-permute-start(bf16[256,1280]{1,0:T(8,128)(2,1)S(1)} %bitcast.125), channel_id=1, source_target_pairs={{0,4},{1,5},{2,6},{3,7},{4,0},{5,1},{6,2},{7,3},{8,12},{9,13},{10,... | collective-permute-start | bytes 1966088 | tf_op jit(solution)/shard_map/ppermute | solution.py:82
  312.9 37.7 %collective-permute-start.68 = (bf16[128,2560]{1,0:T(8,128)(2,1)}, bf16[128,2560]{1,0:T(8,128)(2,1)S(1)}, u32[]{:S(2)}, u32[]{:S(2)}) collective-permute-start(bf16[128,2560]{1,0:T(8,128)(2,1)} %slice.391), channel_id=1, source_target_pairs={{0,2},{1,3},{2,0},{3,1},{4,6},{5,7},{6,4},{7,5},{8,10},{9,11},{10,... | collective-permute-start | bytes 1966088 | tf_op jit(solution)/shard_map/ppermute | solution.py:82
  354.8 34.9 %collective-permute-start.79 = (bf16[320,2304]{1,0:T(8,128)(2,1)}, bf16[320,2304]{1,0:T(8,128)(2,1)}, u32[]{:S(2)}, u32[]{:S(2)}) collective-permute-start(bf16[320,2304]{1,0:T(8,128)(2,1)} %get-tuple-element.2290), channel_id=1, source_target_pairs={{0,8},{1,9},{2,10},{3,11},{4,12},{5,13},{6,14},{7,15},{8,0},{9,1},... | collective-permute-start | bytes 4423688 | tf_op jit(solution)/shard_map/ppermute | solution.py:82
  360.7 17.6 %collective-permute-start.73 = (bf16[256,1280]{1,0:T(8,128)(2,1)}, bf16[256,1280]{1,0:T(8,128)(2,1)}, u32[]{:S(2)}, u32[]{:S(2)}) collective-permute-start(bf16[256,1280]{1,0:T(8,128)(2,1)} %pad_maximum_fusion.8.refs_4_), channel_id=1, source_target_pairs={{0,1},{1,0},{2,3},{3,2},{4,5},{5,4},{6,7},{7,6},{8,9},{9,8},{10,11... | collective-permute-start | bytes 1966088 | tf_op jit(solution)/shard_map/ppermute | solution.py:82
  361.1 17.9 %collective-permute-start.74 = (bf16[256,1280]{1,0:T(8,128)(2,1)}, bf16[256,1280]{1,0:T(8,128)(2,1)}, u32[]{:S(2)}, u32[]{:S(2)}) collective-permute-start(bf16[256,1280]{1,0:T(8,128)(2,1)} %pad_maximum_fusion.8.refs_4_), channel_id=1, source_target_pairs={{0,4},{1,5},{2,6},{3,7},{4,0},{5,1},{6,2},{7,3},{8,12},{9,13},{10,... | collective-permute-start | bytes 1966088 | tf_op jit(solution)/shard_map/ppermute | solution.py:82
  389.7 45.4 %collective-permute-start.81 = (bf16[256,1280]{1,0:T(8,128)(2,1)S(1)}, bf16[256,1280]{1,0:T(8,128)(2,1)}, u32[]{:S(2)}, u32[]{:S(2)}) collective-permute-start(bf16[256,1280]{1,0:T(8,128)(2,1)S(1)} %bitcast.138), channel_id=1, source_target_pairs={{0,4},{1,5},{2,6},{3,7},{4,0},{5,1},{6,2},{7,3},{8,12},{9,13},{10,... | collective-permute-start | bytes 1966088 | tf_op jit(solution)/shard_map/ppermute | solution.py:82
  391.6 43.4 %collective-permute-start.82 = (bf16[160,1280]{1,0:T(8,128)(2,1)}, bf16[160,1280]{1,0:T(8,128)(2,1)S(1)}, u32[]{:S(2)}, u32[]{:S(2)}) collective-permute-start(bf16[160,1280]{1,0:T(8,128)(2,1)} %get-tuple-element.2501), channel_id=1, source_target_pairs={{0,8},{1,9},{2,10},{3,11},{4,12},{5,13},{6,14},{7,15},{8,16},{9,17... | collective-permute-start | bytes 1228808 | tf_op jit(solution)/shard_map/ppermute | solution.py:82
  393.4 41.7 %collective-permute-start.83 = (bf16[160,1280]{1,0:T(8,128)(2,1)}, bf16[160,1280]{1,0:T(8,128)(2,1)}, u32[]{:S(2)}, u32[]{:S(2)}) collective-permute-start(bf16[160,1280]{1,0:T(8,128)(2,1)} %get-tuple-element.2500), channel_id=1, source_target_pairs={{0,16},{1,17},{2,18},{3,19},{4,20},{5,21},{6,22},{7,23},{8,24},{9,... | collective-permute-start | bytes 1228808 | tf_op jit(solution)/shard_map/ppermute | solution.py:82
  394.7 40.4 %collective-permute-start.84 = (bf16[160,1280]{1,0:T(8,128)(2,1)}, bf16[160,1280]{1,0:T(8,128)(2,1)}, u32[]{:S(2)}, u32[]{:S(2)}) collective-permute-start(bf16[160,1280]{1,0:T(8,128)(2,1)} %get-tuple-element.2499), channel_id=1, source_target_pairs={{0,24},{1,25},{2,26},{3,27},{4,28},{5,29},{6,30},{7,31},{8,0},{9,1... | collective-permute-start | bytes 1228808 | tf_op jit(solution)/shard_map/ppermute | solution.py:82
  397.3 37.8 %collective-permute-start.85 = (bf16[1280,256]{1,0:T(8,128)(2,1)}, bf16[1280,256]{1,0:T(8,128)(2,1)S(1)}, u32[]{:S(2)}, u32[]{:S(2)}) collective-permute-start(bf16[1280,256]{1,0:T(8,128)(2,1)} %get-tuple-element.2321), channel_id=1, source_target_pairs={{0,4},{1,5},{2,6},{3,7},{4,0},{5,1},{6,2},{7,3},{8,12},{9,13},{10,... | collective-permute-start | bytes 1966088 | tf_op jit(solution)/shard_map/ppermute | solution.py:82
  435.1 32.7 %collective-permute-start.89 = (bf16[320,2304]{1,0:T(8,128)(2,1)}, bf16[320,2304]{1,0:T(8,128)(2,1)}, u32[]{:S(2)}, u32[]{:S(2)}) collective-permute-start(bf16[320,2304]{1,0:T(8,128)(2,1)} %get-tuple-element.2395), channel_id=1, source_target_pairs={{0,8},{1,9},{2,10},{3,11},{4,12},{5,13},{6,14},{7,15},{8,0},{9,1},... | collective-permute-start | bytes 4423688 | tf_op jit(solution)/shard_map/ppermute | solution.py:82
  469.0 37.4 %collective-permute-start.91 = (bf16[192,1280]{1,0:T(8,128)(2,1)}, bf16[192,1280]{1,0:T(8,128)(2,1)}, u32[]{:S(2)}, u32[]{:S(2)}) collective-permute-start(bf16[192,1280]{1,0:T(8,128)(2,1)} %get-tuple-element.2494), channel_id=1, source_target_pairs={{0,8},{1,9},{2,10},{3,11},{4,12},{5,13},{6,14},{7,15},{8,16},{9,17... | collective-permute-start | bytes 1474568 | tf_op jit(solution)/shard_map/ppermute | solution.py:82
  469.2 37.1 %collective-permute-start.92 = (bf16[192,1280]{1,0:T(8,128)(2,1)}, bf16[192,1280]{1,0:T(8,128)(2,1)}, u32[]{:S(2)}, u32[]{:S(2)}) collective-permute-start(bf16[192,1280]{1,0:T(8,128)(2,1)} %get-tuple-element.2493), channel_id=1, source_target_pairs={{0,16},{1,17},{2,18},{3,19},{4,20},{5,21},{6,22},{7,23},{8,24},{9,... | collective-permute-start | bytes 1474568 | tf_op jit(solution)/shard_map/ppermute | solution.py:82
  470.8 35.6 %collective-permute-start.93 = (bf16[192,1280]{1,0:T(8,128)(2,1)}, bf16[192,1280]{1,0:T(8,128)(2,1)}, u32[]{:S(2)}, u32[]{:S(2)}) collective-permute-start(bf16[192,1280]{1,0:T(8,128)(2,1)} %get-tuple-element.2492), channel_id=1, source_target_pairs={{0,24},{1,25},{2,26},{3,27},{4,28},{5,29},{6,30},{7,31},{8,0},{9,1... | collective-permute-start | bytes 1474568 | tf_op jit(solution)/shard_map/ppermute | solution.py:82
  473.1 33.3 %collective-permute-start.94 = (bf16[128,2560]{1,0:T(8,128)(2,1)S(1)}, bf16[128,2560]{1,0:T(8,128)(2,1)}, u32[]{:S(2)}, u32[]{:S(2)}) collective-permute-start(bf16[128,2560]{1,0:T(8,128)(2,1)S(1)} %slice.390), channel_id=1, source_target_pairs={{0,2},{1,3},{2,0},{3,1},{4,6},{5,7},{6,4},{7,5},{8,10},{9,11},{10,... | collective-permute-start | bytes 1966088 | tf_op jit(solution)/shard_map/ppermute | solution.py:82
  474.6 30.8 %collective-permute-start.95 = (f32[10,2560]{1,0:T(8,128)S(1)}, f32[10,2560]{1,0:T(8,128)}, u32[]{:S(2)}, u32[]{:S(2)}) collective-permute-start(f32[10,2560]{1,0:T(8,128)S(1)} %add.374), channel_id=1, source_target_pairs={{0,8},{1,9},{2,10},{3,11},{4,12},{5,13},{6,14},{7,15},{8,0},{9,1},... | collective-permute-start | bytes 307208 | tf_op jit(solution)/shard_map/ppermute | solution.py:82
  507.4 24.8 %collective-permute-start.96 = (bf16[160,1280]{1,0:T(8,128)(2,1)S(1)}, bf16[160,1280]{1,0:T(8,128)(2,1)S(1)}, u32[]{:S(2)}, u32[]{:S(2)}) collective-permute-start(bf16[160,1280]{1,0:T(8,128)(2,1)S(1)} %get-tuple-element.2497), channel_id=1, source_target_pairs={{0,16},{1,17},{2,18},{3,19},{4,20},{5,21},{6,22},{7,23},{8,24},{9,... | collective-permute-start | bytes 1228808 | tf_op jit(solution)/shard_map/ppermute | solution.py:82
  513.0 26.5 %collective-permute-start.100 = (bf16[160,1280]{1,0:T(8,128)(2,1)}, bf16[160,1280]{1,0:T(8,128)(2,1)}, u32[]{:S(2)}, u32[]{:S(2)}) collective-permute-start(bf16[160,1280]{1,0:T(8,128)(2,1)} %get-tuple-element.2496), channel_id=1, source_target_pairs={{0,24},{1,25},{2,26},{3,27},{4,28},{5,29},{6,30},{7,31},{8,0},{9,1... | collective-permute-start | bytes 1228808 | tf_op jit(solution)/shard_map/ppermute | solution.py:82
  516.4 28.1 %collective-permute-start.99 = (bf16[160,1280]{1,0:T(8,128)(2,1)}, bf16[160,1280]{1,0:T(8,128)(2,1)}, u32[]{:S(2)}, u32[]{:S(2)}) collective-permute-start(bf16[160,1280]{1,0:T(8,128)(2,1)} %get-tuple-element.2495), channel_id=1, source_target_pairs={{0,8},{1,9},{2,10},{3,11},{4,12},{5,13},{6,14},{7,15},{8,16},{9,17... | collective-permute-start | bytes 1228808 | tf_op jit(solution)/shard_map/ppermute | solution.py:82
  516.4 39.0 %collective-permute-start.101 = (bf16[320,1152]{1,0:T(8,128)(2,1)}, bf16[320,1152]{1,0:T(8,128)(2,1)}, u32[]{:S(2)}, u32[]{:S(2)}) collective-permute-start(bf16[320,1152]{1,0:T(8,128)(2,1)} %get-tuple-element.2457), channel_id=1, source_target_pairs={{0,8},{1,9},{2,10},{3,11},{4,12},{5,13},{6,14},{7,15},{8,0},{9,1},... | collective-permute-start | bytes 2211848 | tf_op jit(solution)/shard_map/ppermute | solution.py:82
  555.4 17.7 %collective-permute-start.102 = (f32[10,2560]{1,0:T(8,128)S(1)}, f32[10,2560]{1,0:T(8,128)S(1)}, u32[]{:S(2)}, u32[]{:S(2)}) collective-permute-start(f32[10,2560]{1,0:T(8,128)S(1)} %add.375), channel_id=1, source_target_pairs={{0,16},{1,17},{2,18},{3,19},{4,20},{5,21},{6,22},{7,23},{8,24},{9,... | collective-permute-start | bytes 307208 | tf_op jit(solution)/shard_map/ppermute | solution.py:82
  (158 other events, 1450.3 us)

commit v9 on v8

--- a/solution.py
+++ b/solution.py
@@ -606,31 +606,35 @@
     )(place, *flat)
 
 
-def joined_columns(pairs):
+def joined_columns(pairs, total, before=None):
     rows = pairs[0][0].shape[0]
     widths = [a.shape[1] // 3 for a, _ in pairs]
-    total = sum(widths)
+    span = sum(widths)
     step = rows // 4 if rows % 64 == 0 else rows
     flat = [term for pair in pairs for term in pair]
+    kept = [] if before is None else list(before)
+    index = 0 if before is None else total // span - 1
 
     def body(*refs):
+        refs = refs[len(kept) :]
         for i in range(3):
             at = 0
             for k, n in enumerate(widths):
-                span = slice(i * n, (i + 1) * n)
-                refs[len(flat) + i][:, at : at + n] = refs[2 * k][:, span].astype(F32) + refs[
-                    2 * k + 1][:, span].astype(F32)
+                cols = slice(i * n, (i + 1) * n)
+                refs[len(flat) + i][:, at : at + n] = refs[2 * k][:, cols].astype(F32) + refs[
+                    2 * k + 1][:, cols].astype(F32)
                 at += n
 
     return pl.pallas_call(
         body,
         grid=(rows // step,),
-        in_specs=[pl.BlockSpec((step, term.shape[1]), lambda j: (j, 0)) for term in flat],
-        out_specs=[pl.BlockSpec((step, total), lambda j: (j, 0))] * 3,
+        in_specs=[ANY] * len(kept) + [pl.BlockSpec((step, term.shape[1]), lambda j: (j, 0)) for term in flat],
+        out_specs=[pl.BlockSpec((step, span), lambda j: (j, index))] * 3,
         out_shape=[jax.ShapeDtypeStruct((rows, total), F32)] * 3,
+        input_output_aliases={i: i for i in range(len(kept))},
         compiler_params=pltpu.CompilerParams(vmem_limit_bytes=VMEM_MAX),
-        cost_estimate=work(5),
-    )(*flat)
+        cost_estimate=work(5 if kept else 10),
+    )(*kept, *flat)
 
 
 def gate_weight_grad(place, conv, grad_in, grad_decay, block):
@@ -1080,7 +1084,8 @@
     out_own, out_come = owner_parts(live.out_part.reshape(nz, 2 * own80, half))
     in_x_own, in_x_come, in_y_total = after((live.in_x_own, live.in_x_come, live.in_y_total), out_come[1])
     in_x_total = total_of(in_x_own, in_x_come)
-    live.hold(sum_c=sum_c, out_total=total_of(out_own, out_come),
+    mlp_grads = joined_columns([live.sum_a, live.sum_b], mlp_gate.shape[1])
+    live.hold(sum_c=sum_c, mlp_grads=mlp_grads, out_total=total_of(out_own, out_come),
               in_y_grad=over_columns(in_y_total), in_x_grad=over_columns(in_x_total[: 2 * own80]),
               gate_total=in_x_total[2 * own80 :].reshape(own80, 2 * BLK),
               output=(live.mid + after(live.out_sum, out_come[1])[:tokens] + live.out_arriving.astype(F32)
@@ -1089,7 +1094,8 @@
     sums = live.sums
     for bit in bits[2:]:
         sums = sums + lay.over_seq_bit(sums, bit)
-    mlp_down_grad, mlp_gate_grad, mlp_up_grad = joined_columns([live.sum_a, live.sum_b, live.sum_c])
+    mlp_down_grad, mlp_gate_grad, mlp_up_grad = joined_columns(
+        [live.sum_c], mlp_gate.shape[1], live.mlp_grads)
 
     def final(z, y, x, c):
         at = ((x * 2 + y) * nz + z) * 2 + c

time: 585 us -> 583 us (level)
  transfers between devices with their start and end apart: 105 -> 105, of which waited for: 30 -> 31; matrix products, arithmetic and copies ran while one was open for 16% -> 16% of each run, Pallas kernels for 41% -> 41%
where the time goes in v9:
time: 583 us; the launch traced here: 576 us
  Pallas kernels  237 us (41%)
  waiting for transfers between devices  119 us (20%)
  starting transfers between devices  93.4 us (16%)
  local copies, waits for them, and re-layouts  51.9 us (9%)
  other arithmetic  46.3 us (8%)
  matrix products  26.4 us (5%)
    ppermute x105, waiting for transfers between devices, send(): return lax.ppermute(value, ALL, self.pairs(target))  119 us
    pallas_call x3, Pallas kernels, mlp_weight_grads(): pl.pallas_call(body, grid_spec=pltpu.PrefetchScalarGridSpec(num_scalar_pr...  98.9 us
    ppermute x105, starting transfers between devices, send(): return lax.ppermute(value, ALL, self.pairs(target))  93.4 us
    pallas_call x2, Pallas kernels, grad_hidden_of(): pl.pallas_call(body, grid=(pl.cdiv(ff, BLK),), in_specs=[ANY] * count + [...  25.8 us
    pallas_call x1, Pallas kernels, mlp_forward(): pl.pallas_call(body, in_specs=[ANY] * (count + 3), out_shape=[act, act, a...  23.4 us
    unnamed x207, local copies, waits for them, and re-layouts  22.1 us
    pallas_call x3, Pallas kernels, by_head(): pl.pallas_call(body, grid=(heads,), in_specs=in_specs, out_specs=[spec(o....  19.9 us
    pallas_call x1, Pallas kernels, mlp_rest(): pl.pallas_call(body, grid=(width // block,), in_specs=[whole] * 3 + [weig...  19 us
  transfers between devices with their start and end apart: 105, of which 31 were waited for; matrix products, arithmetic and copies ran while one was open for 16% of the time, Pallas kernels for 41%

profile of v9, /device:TPU:2, one launch (start us, length us, event | category | flops | bytes accessed | tf_op | source)
XLA Modules:
  0.0 576.2 jit_solution(1573974533726808772)
XLA Ops:
  3.6 3.4 collective-permute-start
  12.3 3.7 collective-permute-start.2
  24.1 13.9 %collective-permute-done.6.refs_1_ = bf16[128,2560]{1,0:T(8,128)(2,1)S(1)} collective-permute-done((bf16[128,2560]{1,0:T(8,128)(2,1)S(1)}, bf16[128,2560]{1,0:T(8,128)(2,1)S(1)}, u32[]{:S(2)}, u32[]{:S(2)}) %collective-permute-start.6) | collective-permute-done | bytes 655392 | tf_op jit(solution)/shard_map/ppermute | solution.py:82
  39.6 3.3 convolution_convert_fusion
  50.5 7.0 %shard_map.195 = (bf16[2,128,1280]{2,1,0:T(8,128)(2,1)S(1)}, f32[2,128,1280]{2,1,0:T(8,128)S(1)}, f32[2,128,1280]{2,1,0:T(8,128)S(1)}, f32[2,128,1280]{2,1,0:T(8...) custom-call(f32[2,2]{1,0:T(2,128)S(1)} %pad_maximum_fusion.16.flags_ref, bf16[2,128,1280]{2,1,0:T(8,128)(2,1)S(1)} %bitcast.118, ...), custom_call_target="tpu_custom_call" | custom-call | flops 1 | bytes 1 | tf_op jit(solution)/shard_map/pallas_call | solution.py:266
  61.1 4.9 collective-permute-done.10
  72.5 3.4 shard_map.196
  77.0 3.8 fusion.76
  83.0 3.9 collective-permute-start.18
  88.7 8.2 %collective-permute-done.16 = bf16[640,640]{1,0:T(8,128)(2,1)S(1)} collective-permute-done((bf16[640,640]{1,0:T(8,128)(2,1)}, bf16[640,640]{1,0:T(8,128)(2,1)S(1)}, u32[]{:S(2)}, u32[]{:S(2)}) %collective-permute-start.16) | collective-permute-done | bytes 819232 | tf_op jit(solution)/shard_map/ppermute | solution.py:82
  105.0 3.8 collective-permute-done.19.refs_2_
  111.7 12.8 %shard_map.197.refs_4_ = f32[512,1920]{1,0:T(8,128)} custom-call(bf16[128,2560]{1,0:T(8,128)(2,1)} %bitcast.141, bf16[128,2560]{1,0:T(8,128)(2,1)} %collective-permute-done.13.refs_1_, bf16[128,2560]{1,0:T(8,128)(2,1)} %copy-done.98, bf16[128,2560]{1,0:T(8,128)(2,1)} %collective-permute-done.23.refs_3_, bf16[2560,1920]{1,0:T(8,128)(2,1)} %refs_23_.5), custom_call_target="tpu_custom_call" | custom-call | flops 11699999744 | bytes 26000000 | tf_op jit(solution)/shard_map/pallas_call | solution.py:299
  139.5 13.0 %shard_map.198.refs_20_ = f32[512,1920]{1,0:T(8,128)} custom-call(bf16[128,2560]{1,0:T(8,128)(2,1)} %copy-done.75, bf16[128,2560]{1,0:T(8,128)(2,1)} %collective-permute-done.21.refs_1_.refs_3_, bf16[128,2560]{1,0:T(8,128)(2,1)} %copy-done.99, bf16[128,2560]{1,0:T(8,128)(2,1)} %collective-permute-done.26.refs_3_, bf16[2560,1920]{1,0:T(8,128)(2,1)} %refs_23_.5), custom_call_target="tpu_custom_call" | custom-call | flops 11699999744 | bytes 26000000 | tf_op jit(solution)/shard_map/pallas_call | solution.py:299
  159.3 23.4 %shard_map.199 = (bf16[512,1920]{1,0:T(8,128)(2,1)}, bf16[512,1920]{1,0:T(8,128)(2,1)}, bf16[512,1920]{1,0:T(8,128)(2,1)}, f32[128,2560]{1,0:T(8,128)}, bf16[128,2560]{1,0:T(8,128)(2,1)}) custom-call(bf16[128,2560]{1,0:T(8,128)(2,1)} %multiply_convert_fusion.refs_0_, bf16[128,2560]{1,0:T(8,128)(2,1)} %collective-permute-done.28.refs_1_, ...), custom_call_target="tpu_custom_call" | custom-call | flops 20700000256 | bytes 46000000 | tf_op jit(solution)/shard_map/pallas_call | solution.py:384
  187.9 3.5 collective-permute-start.38
  192.0 19.0 %shard_map.200 = (f32[128,2560]{1,0:T(8,128)}, bf16[128,2560]{1,0:T(8,128)(2,1)}, f32[256,2560]{1,0:T(8,128)}, bf16[256,2560]{1,0:T(8,128)(2,1)}) custom-call(bf16[512,1920]{1,0:T(8,128)(2,1)} %get-tuple-element.2399.hid_ref.refs_24_, bf16[512,1920]{1,0:T(8,128)(2,1)} %get-tuple-element.2400.gg_ref.refs_25_, ...), custom_call_target="tpu_custom_call" | custom-call | flops 17100000256 | bytes 38000000 | tf_op jit(solution)/shard_map/pallas_call | solution.py:423
  224.4 3.2 shard_map.201.refs_31_
  227.7 3.2 shard_map.202.refs_27_
  230.9 3.3 collective-permute-done.46
  234.2 4.8 collective-permute-done.43
  246.7 5.4 shard_map.203
  259.2 3.3 fusion.43
  269.0 3.8 collective-permute-done.57.refs_3_.refs_9_
  272.7 5.8 %collective-permute-done.55.refs_3_.refs_17_ = bf16[128,2560]{1,0:T(8,128)(2,1)} collective-permute-done((bf16[128,2560]{1,0:T(8,128)(2,1)}, bf16[128,2560]{1,0:T(8,128)(2,1)}, u32[]{:S(2)}, u32[]{:S(2)}) %collective-permute-start.55) | collective-permute-done | bytes 655392 | tf_op jit(solution)/shard_map/ppermute | solution.py:82
  280.0 7.4 %shard_map.204 = (bf16[2,128,1280]{2,1,0:T(8,128)(2,1)S(1)}, bf16[2,128,1280]{2,1,0:T(8,128)(2,1)S(1)}, bf16[2,128,1280]{2,1,0:T(8,128)(2,1)S(1)}, f32[2,16,1280...) custom-call(f32[2,2]{1,0:T(2,128)S(1)} %pad_maximum_fusion.16.flags_ref, ...), custom_call_target="tpu_custom_call" | custom-call | flops 1 | bytes 1 | tf_op jit(solution)/shard_map/pallas_call | solution.py:266
  294.1 3.3 shard_map.206.refs_29_
  297.3 3.4 shard_map.205.refs_33_
  302.0 3.4 fusion.41
  313.6 37.4 %shard_map.207 = (f32[320,2304]{1,0:T(8,128)}, bf16[320,2304]{1,0:T(8,128)(2,1)}) custom-call(s32[3]{0:T(128)} %pad_add_fusion.1.place_ref, bf16[128,2560]{1,0:T(8,128)(2,1)} %collective-permute-done.29.refs_2_.refs_0_, bf16[128,2560]{1,0:T(8,128)(2,1)} %collective-permute-done.33.refs_3_.refs_1_, bf16[128,2560]{1,0:T(8,128)(2,1)} %collective-permute-done.39.refs_2_, ...), custom_call_target="tpu_custom_call" | custom-call | flops 31499999232 | bytes 70000000 | tf_op jit(solution)/shard_map/pallas_call | solution.py:540
  357.0 4.0 shard_map.208
  364.7 3.4 shard_map.210
  373.3 5.3 shard_map.209
  379.5 6.0 %collective-permute-done.76 = bf16[4,80,512]{2,1,0:T(8,128)(2,1)S(1)} collective-permute-done((bf16[4,80,512]{2,1,0:T(8,128)(2,1)}, bf16[4,80,512]{2,1,0:T(8,128)(2,1)S(1)}, u32[]{:S(2)}, u32[]{:S(2)}) %collective-permute-start.76) | collective-permute-done | bytes 327712 | tf_op jit(solution)/shard_map/ppermute | solution.py:82
  385.5 4.7 collective-permute-done.79.refs_1_
  398.5 37.3 %shard_map.211 = (f32[320,2304]{1,0:T(8,128)}, bf16[320,2304]{1,0:T(8,128)(2,1)}) custom-call(s32[3]{0:T(128)} %pad_add_fusion.1.place_ref, bf16[128,2560]{1,0:T(8,128)(2,1)} %collective-permute-done.29.refs_2_.refs_0_, bf16[128,2560]{1,0:T(8,128)(2,1)} %collective-permute-done.33.refs_3_.refs_1_, bf16[128,2560]{1,0:T(8,128)(2,1)} %collective-permute-done.39.refs_2_, ...), custom_call_target="tpu_custom_call" | custom-call | flops 31499999232 | bytes 70000000 | tf_op jit(solution)/shard_map/pallas_call | solution.py:540
  445.1 5.2 shard_map.212
  451.2 5.2 shard_map.213
  456.5 12.0 %collective-permute-done.89.refs_3_ = bf16[320,2304]{1,0:T(8,128)(2,1)} collective-permute-done((bf16[320,2304]{1,0:T(8,128)(2,1)}, bf16[320,2304]{1,0:T(8,128)(2,1)}, u32[]{:S(2)}, u32[]{:S(2)}) %collective-permute-start.89) | collective-permute-done | bytes 1474592 | tf_op jit(solution)/shard_map/ppermute | solution.py:82
  475.8 24.2 %shard_map.214 = (f32[320,1152]{1,0:T(8,128)}, bf16[320,1152]{1,0:T(8,128)(2,1)}) custom-call(s32[3]{0:T(128)} %pad_add_fusion.1.place_ref, bf16[128,2560]{1,0:T(8,128)(2,1)} %collective-permute-done.29.refs_2_.refs_0_, bf16[128,2560]{1,0:T(8,128)(2,1)} %collective-permute-done.33.refs_3_.refs_1_, bf16[128,2560]{1,0:T(8,128)(2,1)} %collective-permute-done.39.refs_2_, ...), custom_call_target="tpu_custom_call" | custom-call | flops 15299999744 | bytes 34000000 | tf_op jit(solution)/shard_map/pallas_call | solution.py:540
  500.0 6.0 %collective-permute-done.95 = f32[10,2560]{1,0:T(8,128)} collective-permute-done((f32[10,2560]{1,0:T(8,128)S(1)}, f32[10,2560]{1,0:T(8,128)}, u32[]{:S(2)}, u32[]{:S(2)}) %collective-permute-start.95) | collective-permute-done | bytes 102432 | tf_op jit(solution)/shard_map/ppermute | solution.py:82
  508.0 5.6 collective-permute-start.96
  513.6 3.4 collective-permute-start.100
  517.3 6.2 %shard_map.215 = (f32[320,1920]{1,0:T(8,128)}, f32[320,1920]{1,0:T(8,128)}, f32[320,1920]{1,0:T(8,128)}) custom-call(f32[320,2304]{1,0:T(8,128)} %get-tuple-element.2456.refs_0_, bf16[320,2304]{1,0:T(8,128)(2,1)} %collective-permute-done.79.refs_1_, f32[320,2304]{1,0:T(8,128)} %get-tuple-element.2458.refs_2_, bf16[320,2304]{1,0:T(8,128)(2,1)} %collective-permute-done.89.refs_3_), custom_call_target="tpu_custom_call" | custom-call | flops 9000000512 | bytes 20000000 | tf_op jit(solution)/shard_map/pallas_call | solution.py:628
  523.5 9.3 %collective-permute-done.96 = bf16[160,1280]{1,0:T(8,128)(2,1)S(1)} collective-permute-done((bf16[160,1280]{1,0:T(8,128)(2,1)S(1)}, bf16[160,1280]{1,0:T(8,128)(2,1)S(1)}, u32[]{:S(2)}, u32[]{:S(2)}) %collective-permute-start.96) | collective-permute-done | bytes 409632 | tf_op jit(solution)/shard_map/ppermute | solution.py:82
  540.1 5.0 collective-permute-done.99
  548.5 7.5 %collective-permute-done.101.refs_4_ = bf16[320,1152]{1,0:T(8,128)(2,1)} collective-permute-done((bf16[320,1152]{1,0:T(8,128)(2,1)}, bf16[320,1152]{1,0:T(8,128)(2,1)}, u32[]{:S(2)}, u32[]{:S(2)}) %collective-permute-start.101) | collective-permute-done | bytes 737312 | tf_op jit(solution)/shard_map/ppermute | solution.py:82
  556.0 3.7 collective-permute-start.102
  564.9 3.8 shard_map.216
  (538 shorter events, 197.0 us)
Async XLA Ops:
  7.0 17.0 %collective-permute-start.5 = (bf16[1280,128]{1,0:T(8,128)(2,1)}, bf16[1280,128]{1,0:T(8,128)(2,1)}, u32[]{:S(2)}, u32[]{:S(2)}) collective-permute-start(bf16[1280,128]{1,0:T(8,128)(2,1)} %constant_dynamic-slice_fusion.5), channel_id=1, source_target_pairs={{0,2},{1,3},{2,0},{3,1},{4,6},{5,7},{6,4},{7,5},{8,10},{9,11},{10,... | collective-permute-start | bytes 983048 | tf_op jit(solution)/shard_map/ppermute | solution.py:82
  20.9 17.1 %collective-permute-start.6 = (bf16[128,2560]{1,0:T(8,128)(2,1)S(1)}, bf16[128,2560]{1,0:T(8,128)(2,1)S(1)}, u32[]{:S(2)}, u32[]{:S(2)}) collective-permute-start(bf16[128,2560]{1,0:T(8,128)(2,1)S(1)} %copy-done.23), channel_id=1, source_target_pairs={{0,2},{1,3},{2,0},{3,1},{4,6},{5,7},{6,4},{7,5},{8,10},{9,11},{10,... | collective-permute-start | bytes 1966088 | tf_op jit(solution)/shard_map/ppermute | solution.py:82
  38.1 27.9 %collective-permute-start.11 = (bf16[2560,640]{1,0:T(8,128)(2,1)S(1)}, bf16[2560,640]{1,0:T(8,128)(2,1)S(1)}, u32[]{:S(2)}, u32[]{:S(2)}) collective-permute-start(bf16[2560,640]{1,0:T(8,128)(2,1)S(1)} %copy-done.46), channel_id=1, source_target_pairs={{0,1},{1,0},{2,3},{3,2},{4,5},{5,4},{6,7},{7,6},{8,9},{9,8},{10,11... | collective-permute-start | bytes 9830408 | tf_op jit(solution)/shard_map/ppermute | solution.py:82
  44.0 17.1 %collective-permute-start.8 = (bf16[128,2560]{1,0:T(8,128)(2,1)S(1)}, bf16[128,2560]{1,0:T(8,128)(2,1)S(1)}, u32[]{:S(2)}, u32[]{:S(2)}) collective-permute-start(bf16[128,2560]{1,0:T(8,128)(2,1)S(1)} %bitcast.143), channel_id=1, source_target_pairs={{0,4},{1,5},{2,6},{3,7},{4,0},{5,1},{6,2},{7,3},{8,12},{9,13},{10,... | collective-permute-start | bytes 1966088 | tf_op jit(solution)/shard_map/ppermute | solution.py:82
  45.7 20.3 %collective-permute-start.10 = (bf16[640,640]{1,0:T(8,128)(2,1)}, bf16[640,640]{1,0:T(8,128)(2,1)S(1)}, u32[]{:S(2)}, u32[]{:S(2)}) collective-permute-start(bf16[640,640]{1,0:T(8,128)(2,1)} %constant_dynamic-slice_fusion.3), channel_id=1, source_target_pairs={{0,2},{1,3},{2,0},{3,1},{4,6},{5,7},{6,4},{7,5},{8,10},{9,11},{10,... | collective-permute-start | bytes 2457608 | tf_op jit(solution)/shard_map/ppermute | solution.py:82
  71.9 25.9 %collective-permute-start.13 = (bf16[128,2560]{1,0:T(8,128)(2,1)}, bf16[128,2560]{1,0:T(8,128)(2,1)}, u32[]{:S(2)}, u32[]{:S(2)}) collective-permute-start(bf16[128,2560]{1,0:T(8,128)(2,1)} %bitcast.140), channel_id=1, source_target_pairs={{0,2},{1,3},{2,0},{3,1},{4,6},{5,7},{6,4},{7,5},{8,10},{9,11},{10,... | collective-permute-start | bytes 1966088 | tf_op jit(solution)/shard_map/ppermute | solution.py:82
  75.9 21.8 %collective-permute-start.14 = (bf16[640,256]{1,0:T(8,128)(2,1)}, bf16[640,256]{1,0:T(8,128)(2,1)S(1)}, u32[]{:S(2)}, u32[]{:S(2)}) collective-permute-start(bf16[640,256]{1,0:T(8,128)(2,1)} %get-tuple-element.1340), channel_id=1, source_target_pairs={{0,1},{1,0},{2,3},{3,2},{4,5},{5,4},{6,7},{7,6},{8,9},{9,8},{10,11... | collective-permute-start | bytes 983048 | tf_op jit(solution)/shard_map/ppermute | solution.py:82
  75.9 21.5 %collective-permute-start.15 = (bf16[1280,640]{1,0:T(8,128)(2,1)}, bf16[1280,640]{1,0:T(8,128)(2,1)S(1)}, u32[]{:S(2)}, u32[]{:S(2)}) collective-permute-start(bf16[1280,640]{1,0:T(8,128)(2,1)} %constant_dynamic-slice_fusion.2), channel_id=1, source_target_pairs={{0,1},{1,0},{2,3},{3,2},{4,5},{5,4},{6,7},{7,6},{8,9},{9,8},{10,11... | collective-permute-start | bytes 4915208 | tf_op jit(solution)/shard_map/ppermute | solution.py:82
  76.4 20.4 %collective-permute-start.16 = (bf16[640,640]{1,0:T(8,128)(2,1)}, bf16[640,640]{1,0:T(8,128)(2,1)S(1)}, u32[]{:S(2)}, u32[]{:S(2)}) collective-permute-start(bf16[640,640]{1,0:T(8,128)(2,1)} %copy-done.66), channel_id=1, source_target_pairs={{0,4},{1,5},{2,6},{3,7},{4,0},{5,1},{6,2},{7,3},{8,12},{9,13},{10,... | collective-permute-start | bytes 2457608 | tf_op jit(solution)/shard_map/ppermute | solution.py:82
  108.8 17.5 %collective-permute-start.21 = (bf16[128,2560]{1,0:T(8,128)(2,1)}, bf16[128,2560]{1,0:T(8,128)(2,1)}, u32[]{:S(2)}, u32[]{:S(2)}) collective-permute-start(bf16[128,2560]{1,0:T(8,128)(2,1)} %collective-permute-done.13.refs_1_), channel_id=1, source_target_pairs={{0,4},{1,5},{2,6},{3,7},{4,0},{5,1},{6,2},{7,3},{8,12},{9,13},{10,... | collective-permute-start | bytes 1966088 | tf_op jit(solution)/shard_map/ppermute | solution.py:82
  109.3 17.2 %collective-permute-start.24 = (bf16[128,2560]{1,0:T(8,128)(2,1)}, bf16[128,2560]{1,0:T(8,128)(2,1)}, u32[]{:S(2)}, u32[]{:S(2)}) collective-permute-start(bf16[128,2560]{1,0:T(8,128)(2,1)} %fusion.22), channel_id=1, source_target_pairs={{0,2},{1,3},{2,0},{3,1},{4,6},{5,7},{6,4},{7,5},{8,10},{9,11},{10,... | collective-permute-start | bytes 1966088 | tf_op jit(solution)/shard_map/ppermute | solution.py:82
  131.5 21.0 %collective-permute-start.27 = (bf16[128,2560]{1,0:T(8,128)(2,1)}, bf16[128,2560]{1,0:T(8,128)(2,1)}, u32[]{:S(2)}, u32[]{:S(2)}) collective-permute-start(bf16[128,2560]{1,0:T(8,128)(2,1)} %multiply_convert_fusion.refs_0_), channel_id=1, source_target_pairs={{0,1},{1,0},{2,3},{3,2},{4,5},{5,4},{6,7},{7,6},{8,9},{9,8},{10,11... | collective-permute-start | bytes 1966088 | tf_op jit(solution)/shard_map/ppermute | solution.py:82
  131.5 21.0 %collective-permute-start.28 = (bf16[128,2560]{1,0:T(8,128)(2,1)}, bf16[128,2560]{1,0:T(8,128)(2,1)}, u32[]{:S(2)}, u32[]{:S(2)}) collective-permute-start(bf16[128,2560]{1,0:T(8,128)(2,1)} %multiply_convert_fusion.refs_0_), channel_id=1, source_target_pairs={{0,2},{1,3},{2,0},{3,1},{4,6},{5,7},{6,4},{7,5},{8,10},{9,11},{10,... | collective-permute-start | bytes 1966088 | tf_op jit(solution)/shard_map/ppermute | solution.py:82
  133.0 19.5 %collective-permute-start.29 = (bf16[128,2560]{1,0:T(8,128)(2,1)}, bf16[128,2560]{1,0:T(8,128)(2,1)}, u32[]{:S(2)}, u32[]{:S(2)}) collective-permute-start(bf16[128,2560]{1,0:T(8,128)(2,1)} %multiply_convert_fusion.refs_0_), channel_id=1, source_target_pairs={{0,4},{1,5},{2,6},{3,7},{4,0},{5,1},{6,2},{7,3},{8,12},{9,13},{10,... | collective-permute-start | bytes 1966088 | tf_op jit(solution)/shard_map/ppermute | solution.py:82
  156.8 25.9 %collective-permute-start.32 = (bf16[128,2560]{1,0:T(8,128)(2,1)}, bf16[128,2560]{1,0:T(8,128)(2,1)}, u32[]{:S(2)}, u32[]{:S(2)}) collective-permute-start(bf16[128,2560]{1,0:T(8,128)(2,1)} %pad_maximum_fusion.4.refs_0_.refs_12_), channel_id=1, source_target_pairs={{0,2},{1,3},{2,0},{3,1},{4,6},{5,7},{6,4},{7,5},{8,10},{9,11},{10,... | collective-permute-start | bytes 1966088 | tf_op jit(solution)/shard_map/ppermute | solution.py:82
  157.3 25.4 %collective-permute-start.33 = (bf16[128,2560]{1,0:T(8,128)(2,1)}, bf16[128,2560]{1,0:T(8,128)(2,1)}, u32[]{:S(2)}, u32[]{:S(2)}) collective-permute-start(bf16[128,2560]{1,0:T(8,128)(2,1)} %collective-permute-done.28.refs_1_), channel_id=1, source_target_pairs={{0,4},{1,5},{2,6},{3,7},{4,0},{5,1},{6,2},{7,3},{8,12},{9,13},{10,... | collective-permute-start | bytes 1966088 | tf_op jit(solution)/shard_map/ppermute | solution.py:82
  159.0 23.7 %collective-permute-start.34 = (bf16[64,2560]{1,0:T(8,128)(2,1)}, bf16[64,2560]{1,0:T(8,128)(2,1)}, u32[]{:S(2)}, u32[]{:S(2)}) collective-permute-start(bf16[64,2560]{1,0:T(8,128)(2,1)} %slice.262), channel_id=1, source_target_pairs={{0,24},{1,25},{2,26},{3,27},{4,28},{5,29},{6,30},{7,31},{8,16},{9,... | collective-permute-start | bytes 983048 | tf_op jit(solution)/shard_map/ppermute | solution.py:82
  186.4 24.6 %collective-permute-start.36 = (bf16[128,2560]{1,0:T(8,128)(2,1)}, bf16[128,2560]{1,0:T(8,128)(2,1)}, u32[]{:S(2)}, u32[]{:S(2)}) collective-permute-start(bf16[128,2560]{1,0:T(8,128)(2,1)} %add_convert_fusion.1), channel_id=1, source_target_pairs={{0,2},{1,3},{2,0},{3,1},{4,6},{5,7},{6,4},{7,5},{8,10},{9,11},{10,... | collective-permute-start | bytes 1966088 | tf_op jit(solution)/shard_map/ppermute | solution.py:82
  187.9 23.1 %collective-permute-start.37 = (bf16[128,2560]{1,0:T(8,128)(2,1)}, bf16[128,2560]{1,0:T(8,128)(2,1)}, u32[]{:S(2)}, u32[]{:S(2)}) collective-permute-start(bf16[128,2560]{1,0:T(8,128)(2,1)} %collective-permute-done.33.refs_3_.refs_1_), channel_id=1, source_target_pairs={{0,1},{1,0},{2,3},{3,2},{4,5},{5,4},{6,7},{7,6},{8,9},{9,8},{10,11... | collective-permute-start | bytes 1966088 | tf_op jit(solution)/shard_map/ppermute | solution.py:82
  187.9 23.1 %collective-permute-start.38 = (bf16[64,2560]{1,0:T(8,128)(2,1)S(1)}, bf16[64,2560]{1,0:T(8,128)(2,1)}, u32[]{:S(2)}, u32[]{:S(2)}) collective-permute-start(bf16[64,2560]{1,0:T(8,128)(2,1)S(1)} %get-tuple-element.1659), channel_id=1, source_target_pairs={{0,24},{1,25},{2,26},{3,27},{4,28},{5,29},{6,30},{7,31},{8,16},{9,... | collective-permute-start | bytes 983048 | tf_op jit(solution)/shard_map/ppermute | solution.py:82
  191.4 19.6 %collective-permute-start.39 = (bf16[128,2560]{1,0:T(8,128)(2,1)}, bf16[128,2560]{1,0:T(8,128)(2,1)}, u32[]{:S(2)}, u32[]{:S(2)}) collective-permute-start(bf16[128,2560]{1,0:T(8,128)(2,1)} %collective-permute-done.29.refs_2_.refs_0_), channel_id=1, source_target_pairs={{0,1},{1,0},{2,3},{3,2},{4,5},{5,4},{6,7},{7,6},{8,9},{9,8},{10,11... | collective-permute-start | bytes 1966088 | tf_op jit(solution)/shard_map/ppermute | solution.py:82
  191.7 19.4 %collective-permute-start.40 = (bf16[128,2560]{1,0:T(8,128)(2,1)}, bf16[128,2560]{1,0:T(8,128)(2,1)}, u32[]{:S(2)}, u32[]{:S(2)}) collective-permute-start(bf16[128,2560]{1,0:T(8,128)(2,1)} %pad_maximum_fusion.5.refs_0_.refs_4_), channel_id=1, source_target_pairs={{0,4},{1,5},{2,6},{3,7},{4,0},{5,1},{6,2},{7,3},{8,12},{9,13},{10,... | collective-permute-start | bytes 1966088 | tf_op jit(solution)/shard_map/ppermute | solution.py:82
  220.0 19.0 %collective-permute-start.44 = (bf16[128,2560]{1,0:T(8,128)(2,1)}, bf16[128,2560]{1,0:T(8,128)(2,1)S(1)}, u32[]{:S(2)}, u32[]{:S(2)}) collective-permute-start(bf16[128,2560]{1,0:T(8,128)(2,1)} %pad_maximum_fusion.4.refs_0_.refs_12_), channel_id=1, source_target_pairs={{0,4},{1,5},{2,6},{3,7},{4,0},{5,1},{6,2},{7,3},{8,12},{9,13},{10,... | collective-permute-start | bytes 1966088 | tf_op jit(solution)/shard_map/ppermute | solution.py:82
  221.7 17.3 %collective-permute-start.45 = (bf16[128,2560]{1,0:T(8,128)(2,1)}, bf16[128,2560]{1,0:T(8,128)(2,1)}, u32[]{:S(2)}, u32[]{:S(2)}) collective-permute-start(bf16[128,2560]{1,0:T(8,128)(2,1)} %pad_maximum_fusion.4.refs_0_.refs_12_), channel_id=1, source_target_pairs={{0,1},{1,0},{2,3},{3,2},{4,5},{5,4},{6,7},{7,6},{8,9},{9,8},{10,11... | collective-permute-start | bytes 1966088 | tf_op jit(solution)/shard_map/ppermute | solution.py:82
  221.8 17.3 %collective-permute-start.43 = (bf16[128,2560]{1,0:T(8,128)(2,1)S(1)}, bf16[128,2560]{1,0:T(8,128)(2,1)}, u32[]{:S(2)}, u32[]{:S(2)}) collective-permute-start(bf16[128,2560]{1,0:T(8,128)(2,1)S(1)} %maximum_select_fusion.8), channel_id=1, source_target_pairs={{0,2},{1,3},{2,0},{3,1},{4,6},{5,7},{6,4},{7,5},{8,10},{9,11},{10,... | collective-permute-start | bytes 1966088 | tf_op jit(solution)/shard_map/ppermute | solution.py:82
  255.6 17.1 %collective-permute-start.57 = (bf16[128,2560]{1,0:T(8,128)(2,1)}, bf16[128,2560]{1,0:T(8,128)(2,1)}, u32[]{:S(2)}, u32[]{:S(2)}) collective-permute-start(bf16[128,2560]{1,0:T(8,128)(2,1)} %collective-permute-done.40.refs_2_.refs_8_), channel_id=1, source_target_pairs={{0,2},{1,3},{2,0},{3,1},{4,6},{5,7},{6,4},{7,5},{8,10},{9,11},{10,... | collective-permute-start | bytes 1966088 | tf_op jit(solution)/shard_map/ppermute | solution.py:82
  310.7 40.4 %collective-permute-start.69 = (bf16[256,1280]{1,0:T(8,128)(2,1)S(1)}, bf16[256,1280]{1,0:T(8,128)(2,1)}, u32[]{:S(2)}, u32[]{:S(2)}) collective-permute-start(bf16[256,1280]{1,0:T(8,128)(2,1)S(1)} %bitcast.124), channel_id=1, source_target_pairs={{0,1},{1,0},{2,3},{3,2},{4,5},{5,4},{6,7},{7,6},{8,9},{9,8},{10,11... | collective-permute-start | bytes 1966088 | tf_op jit(solution)/shard_map/ppermute | solution.py:82
  310.8 40.3 %collective-permute-start.70 = (bf16[256,1280]{1,0:T(8,128)(2,1)S(1)}, bf16[256,1280]{1,0:T(8,128)(2,1)}, u32[]{:S(2)}, u32[]{:S(2)}) collective-permute-start(bf16[256,1280]{1,0:T(8,128)(2,1)S(1)} %bitcast.125), channel_id=1, source_target_pairs={{0,4},{1,5},{2,6},{3,7},{4,0},{5,1},{6,2},{7,3},{8,12},{9,13},{10,... | collective-permute-start | bytes 1966088 | tf_op jit(solution)/shard_map/ppermute | solution.py:82
  313.1 38.0 %collective-permute-start.68 = (bf16[128,2560]{1,0:T(8,128)(2,1)}, bf16[128,2560]{1,0:T(8,128)(2,1)S(1)}, u32[]{:S(2)}, u32[]{:S(2)}) collective-permute-start(bf16[128,2560]{1,0:T(8,128)(2,1)} %slice.391), channel_id=1, source_target_pairs={{0,2},{1,3},{2,0},{3,1},{4,6},{5,7},{6,4},{7,5},{8,10},{9,11},{10,... | collective-permute-start | bytes 1966088 | tf_op jit(solution)/shard_map/ppermute | solution.py:82
  355.3 34.9 %collective-permute-start.79 = (bf16[320,2304]{1,0:T(8,128)(2,1)}, bf16[320,2304]{1,0:T(8,128)(2,1)}, u32[]{:S(2)}, u32[]{:S(2)}) collective-permute-start(bf16[320,2304]{1,0:T(8,128)(2,1)} %get-tuple-element.2292), channel_id=1, source_target_pairs={{0,8},{1,9},{2,10},{3,11},{4,12},{5,13},{6,14},{7,15},{8,0},{9,1},... | collective-permute-start | bytes 4423688 | tf_op jit(solution)/shard_map/ppermute | solution.py:82
  361.1 17.6 %collective-permute-start.73 = (bf16[256,1280]{1,0:T(8,128)(2,1)}, bf16[256,1280]{1,0:T(8,128)(2,1)}, u32[]{:S(2)}, u32[]{:S(2)}) collective-permute-start(bf16[256,1280]{1,0:T(8,128)(2,1)} %pad_maximum_fusion.8.refs_4_), channel_id=1, source_target_pairs={{0,1},{1,0},{2,3},{3,2},{4,5},{5,4},{6,7},{7,6},{8,9},{9,8},{10,11... | collective-permute-start | bytes 1966088 | tf_op jit(solution)/shard_map/ppermute | solution.py:82
  361.6 17.9 %collective-permute-start.74 = (bf16[256,1280]{1,0:T(8,128)(2,1)}, bf16[256,1280]{1,0:T(8,128)(2,1)}, u32[]{:S(2)}, u32[]{:S(2)}) collective-permute-start(bf16[256,1280]{1,0:T(8,128)(2,1)} %pad_maximum_fusion.8.refs_4_), channel_id=1, source_target_pairs={{0,4},{1,5},{2,6},{3,7},{4,0},{5,1},{6,2},{7,3},{8,12},{9,13},{10,... | collective-permute-start | bytes 1966088 | tf_op jit(solution)/shard_map/ppermute | solution.py:82
  390.1 45.7 %collective-permute-start.81 = (bf16[256,1280]{1,0:T(8,128)(2,1)S(1)}, bf16[256,1280]{1,0:T(8,128)(2,1)}, u32[]{:S(2)}, u32[]{:S(2)}) collective-permute-start(bf16[256,1280]{1,0:T(8,128)(2,1)S(1)} %bitcast.138), channel_id=1, source_target_pairs={{0,4},{1,5},{2,6},{3,7},{4,0},{5,1},{6,2},{7,3},{8,12},{9,13},{10,... | collective-permute-start | bytes 1966088 | tf_op jit(solution)/shard_map/ppermute | solution.py:82
  392.1 43.7 %collective-permute-start.82 = (bf16[160,1280]{1,0:T(8,128)(2,1)}, bf16[160,1280]{1,0:T(8,128)(2,1)S(1)}, u32[]{:S(2)}, u32[]{:S(2)}) collective-permute-start(bf16[160,1280]{1,0:T(8,128)(2,1)} %get-tuple-element.2505), channel_id=1, source_target_pairs={{0,8},{1,9},{2,10},{3,11},{4,12},{5,13},{6,14},{7,15},{8,16},{9,17... | collective-permute-start | bytes 1228808 | tf_op jit(solution)/shard_map/ppermute | solution.py:82
  393.8 42.0 %collective-permute-start.83 = (bf16[160,1280]{1,0:T(8,128)(2,1)}, bf16[160,1280]{1,0:T(8,128)(2,1)}, u32[]{:S(2)}, u32[]{:S(2)}) collective-permute-start(bf16[160,1280]{1,0:T(8,128)(2,1)} %get-tuple-element.2504), channel_id=1, source_target_pairs={{0,16},{1,17},{2,18},{3,19},{4,20},{5,21},{6,22},{7,23},{8,24},{9,... | collective-permute-start | bytes 1228808 | tf_op jit(solution)/shard_map/ppermute | solution.py:82
  395.1 40.7 %collective-permute-start.84 = (bf16[160,1280]{1,0:T(8,128)(2,1)}, bf16[160,1280]{1,0:T(8,128)(2,1)}, u32[]{:S(2)}, u32[]{:S(2)}) collective-permute-start(bf16[160,1280]{1,0:T(8,128)(2,1)} %get-tuple-element.2503), channel_id=1, source_target_pairs={{0,24},{1,25},{2,26},{3,27},{4,28},{5,29},{6,30},{7,31},{8,0},{9,1... | collective-permute-start | bytes 1228808 | tf_op jit(solution)/shard_map/ppermute | solution.py:82
  397.8 38.0 %collective-permute-start.85 = (bf16[1280,256]{1,0:T(8,128)(2,1)}, bf16[1280,256]{1,0:T(8,128)(2,1)S(1)}, u32[]{:S(2)}, u32[]{:S(2)}) collective-permute-start(bf16[1280,256]{1,0:T(8,128)(2,1)} %get-tuple-element.2323), channel_id=1, source_target_pairs={{0,4},{1,5},{2,6},{3,7},{4,0},{5,1},{6,2},{7,3},{8,12},{9,13},{10,... | collective-permute-start | bytes 1966088 | tf_op jit(solution)/shard_map/ppermute | solution.py:82
  435.8 32.6 %collective-permute-start.89 = (bf16[320,2304]{1,0:T(8,128)(2,1)}, bf16[320,2304]{1,0:T(8,128)(2,1)}, u32[]{:S(2)}, u32[]{:S(2)}) collective-permute-start(bf16[320,2304]{1,0:T(8,128)(2,1)} %get-tuple-element.2397), channel_id=1, source_target_pairs={{0,8},{1,9},{2,10},{3,11},{4,12},{5,13},{6,14},{7,15},{8,0},{9,1},... | collective-permute-start | bytes 4423688 | tf_op jit(solution)/shard_map/ppermute | solution.py:82
  469.6 37.4 %collective-permute-start.91 = (bf16[192,1280]{1,0:T(8,128)(2,1)}, bf16[192,1280]{1,0:T(8,128)(2,1)}, u32[]{:S(2)}, u32[]{:S(2)}) collective-permute-start(bf16[192,1280]{1,0:T(8,128)(2,1)} %get-tuple-element.2498), channel_id=1, source_target_pairs={{0,8},{1,9},{2,10},{3,11},{4,12},{5,13},{6,14},{7,15},{8,16},{9,17... | collective-permute-start | bytes 1474568 | tf_op jit(solution)/shard_map/ppermute | solution.py:82
  469.9 37.1 %collective-permute-start.92 = (bf16[192,1280]{1,0:T(8,128)(2,1)}, bf16[192,1280]{1,0:T(8,128)(2,1)}, u32[]{:S(2)}, u32[]{:S(2)}) collective-permute-start(bf16[192,1280]{1,0:T(8,128)(2,1)} %get-tuple-element.2497), channel_id=1, source_target_pairs={{0,16},{1,17},{2,18},{3,19},{4,20},{5,21},{6,22},{7,23},{8,24},{9,... | collective-permute-start | bytes 1474568 | tf_op jit(solution)/shard_map/ppermute | solution.py:82
  471.5 35.6 %collective-permute-start.93 = (bf16[192,1280]{1,0:T(8,128)(2,1)}, bf16[192,1280]{1,0:T(8,128)(2,1)}, u32[]{:S(2)}, u32[]{:S(2)}) collective-permute-start(bf16[192,1280]{1,0:T(8,128)(2,1)} %get-tuple-element.2496), channel_id=1, source_target_pairs={{0,24},{1,25},{2,26},{3,27},{4,28},{5,29},{6,30},{7,31},{8,0},{9,1... | collective-permute-start | bytes 1474568 | tf_op jit(solution)/shard_map/ppermute | solution.py:82
  473.8 33.3 %collective-permute-start.94 = (bf16[128,2560]{1,0:T(8,128)(2,1)S(1)}, bf16[128,2560]{1,0:T(8,128)(2,1)}, u32[]{:S(2)}, u32[]{:S(2)}) collective-permute-start(bf16[128,2560]{1,0:T(8,128)(2,1)S(1)} %slice.390), channel_id=1, source_target_pairs={{0,2},{1,3},{2,0},{3,1},{4,6},{5,7},{6,4},{7,5},{8,10},{9,11},{10,... | collective-permute-start | bytes 1966088 | tf_op jit(solution)/shard_map/ppermute | solution.py:82
  475.3 30.7 %collective-permute-start.95 = (f32[10,2560]{1,0:T(8,128)S(1)}, f32[10,2560]{1,0:T(8,128)}, u32[]{:S(2)}, u32[]{:S(2)}) collective-permute-start(f32[10,2560]{1,0:T(8,128)S(1)} %add.374), channel_id=1, source_target_pairs={{0,8},{1,9},{2,10},{3,11},{4,12},{5,13},{6,14},{7,15},{8,0},{9,1},... | collective-permute-start | bytes 307208 | tf_op jit(solution)/shard_map/ppermute | solution.py:82
  508.0 24.8 %collective-permute-start.96 = (bf16[160,1280]{1,0:T(8,128)(2,1)S(1)}, bf16[160,1280]{1,0:T(8,128)(2,1)S(1)}, u32[]{:S(2)}, u32[]{:S(2)}) collective-permute-start(bf16[160,1280]{1,0:T(8,128)(2,1)S(1)} %get-tuple-element.2501), channel_id=1, source_target_pairs={{0,16},{1,17},{2,18},{3,19},{4,20},{5,21},{6,22},{7,23},{8,24},{9,... | collective-permute-start | bytes 1228808 | tf_op jit(solution)/shard_map/ppermute | solution.py:82
  513.6 26.5 %collective-permute-start.100 = (bf16[160,1280]{1,0:T(8,128)(2,1)}, bf16[160,1280]{1,0:T(8,128)(2,1)}, u32[]{:S(2)}, u32[]{:S(2)}) collective-permute-start(bf16[160,1280]{1,0:T(8,128)(2,1)} %get-tuple-element.2500), channel_id=1, source_target_pairs={{0,24},{1,25},{2,26},{3,27},{4,28},{5,29},{6,30},{7,31},{8,0},{9,1... | collective-permute-start | bytes 1228808 | tf_op jit(solution)/shard_map/ppermute | solution.py:82
  517.0 28.1 %collective-permute-start.99 = (bf16[160,1280]{1,0:T(8,128)(2,1)}, bf16[160,1280]{1,0:T(8,128)(2,1)}, u32[]{:S(2)}, u32[]{:S(2)}) collective-permute-start(bf16[160,1280]{1,0:T(8,128)(2,1)} %get-tuple-element.2499), channel_id=1, source_target_pairs={{0,8},{1,9},{2,10},{3,11},{4,12},{5,13},{6,14},{7,15},{8,16},{9,17... | collective-permute-start | bytes 1228808 | tf_op jit(solution)/shard_map/ppermute | solution.py:82
  517.0 39.0 %collective-permute-start.101 = (bf16[320,1152]{1,0:T(8,128)(2,1)}, bf16[320,1152]{1,0:T(8,128)(2,1)}, u32[]{:S(2)}, u32[]{:S(2)}) collective-permute-start(bf16[320,1152]{1,0:T(8,128)(2,1)} %get-tuple-element.2466), channel_id=1, source_target_pairs={{0,8},{1,9},{2,10},{3,11},{4,12},{5,13},{6,14},{7,15},{8,0},{9,1},... | collective-permute-start | bytes 2211848 | tf_op jit(solution)/shard_map/ppermute | solution.py:82
  556.0 17.2 %collective-permute-start.102 = (f32[10,2560]{1,0:T(8,128)S(1)}, f32[10,2560]{1,0:T(8,128)S(1)}, u32[]{:S(2)}, u32[]{:S(2)}) collective-permute-start(f32[10,2560]{1,0:T(8,128)S(1)} %add.375), channel_id=1, source_target_pairs={{0,16},{1,17},{2,18},{3,19},{4,20},{5,21},{6,22},{7,23},{8,24},{9,... | collective-permute-start | bytes 307208 | tf_op jit(solution)/shard_map/ppermute | solution.py:82
  (158 other events, 1450.5 us)

commit v10 on v9

--- a/solution.py
+++ b/solution.py
@@ -843,7 +843,8 @@
             cot_x = lay.over_x(after(cot, live.scan))
     out_x = jnp.where(y == 0, jnp.concatenate([live.out_a, out_b], 0), jnp.concatenate([out_b, live.out_a], 0))
     y_pre = order_c(dot(live.normed, in_y), dot(live.normed, live.wy_c), 1).reshape(2, tokens, half)
-    n1_own, sent, n1_away = rows_by_device(at_yc, [[live.n1, live.n1_x]], n1_starts, own80)
+    n1_own, sent, n1_away = rows_by_device(
+        at_yc, [after([live.n1, live.n1_x], live.scan[3])], n1_starts, own80)
     state_in = live.scan[3]
     del live.scan, live.out_a
     live.hold(state_in=state_in, y_pre=y_pre, out_left=jnp.concatenate([live.out_mine, out_c], axis=1),

time: 583 us -> 584 us (level)
    unnamed x207 -> x205, local copies, waits for them, and re-layouts: 22.1 us -> 21.6 us
where the time goes in v10:
time: 584 us; the launch traced here: 577 us
  Pallas kernels  236 us (40%)
  waiting for transfers between devices  120 us (21%)
  starting transfers between devices  90.6 us (16%)
  local copies, waits for them, and re-layouts  51.3 us (9%)
  other arithmetic  49.4 us (8%)
  matrix products  26.3 us (5%)
    ppermute x105, waiting for transfers between devices, send(): return lax.ppermute(value, ALL, self.pairs(target))  120 us
    pallas_call x3, Pallas kernels, mlp_weight_grads(): pl.pallas_call(body, grid_spec=pltpu.PrefetchScalarGridSpec(num_scalar_pr...  98.7 us
    ppermute x105, starting transfers between devices, send(): return lax.ppermute(value, ALL, self.pairs(target))  90.6 us
    pallas_call x2, Pallas kernels, grad_hidden_of(): pl.pallas_call(body, grid=(pl.cdiv(ff, BLK),), in_specs=[ANY] * count + [...  25.7 us
    pallas_call x1, Pallas kernels, mlp_forward(): pl.pallas_call(body, in_specs=[ANY] * (count + 3), out_shape=[act, act, a...  23.4 us
    unnamed x205, local copies, waits for them, and re-layouts  21.6 us
    pallas_call x3, Pallas kernels, by_head(): pl.pallas_call(body, grid=(heads,), in_specs=in_specs, out_specs=[spec(o....  19.9 us
    pallas_call x1, Pallas kernels, mlp_rest(): pl.pallas_call(body, grid=(width // block,), in_specs=[whole] * 3 + [weig...  18.9 us
  transfers between devices with their start and end apart: 105, of which 31 were waited for; matrix products, arithmetic and copies ran while one was open for 16% of the time, Pallas kernels for 41%

profile of v10, /device:TPU:2, one launch (start us, length us, event | category | flops | bytes accessed | tf_op | source)
XLA Modules:
  0.0 577.1 jit_solution(2813520174296720535)
XLA Ops:
  3.6 3.4 collective-permute-start
  12.3 3.7 collective-permute-start.2
  24.1 13.9 %collective-permute-done.6.refs_1_ = bf16[128,2560]{1,0:T(8,128)(2,1)S(1)} collective-permute-done((bf16[128,2560]{1,0:T(8,128)(2,1)S(1)}, bf16[128,2560]{1,0:T(8,128)(2,1)S(1)}, u32[]{:S(2)}, u32[]{:S(2)}) %collective-permute-start.6) | collective-permute-done | bytes 655392 | tf_op jit(solution)/shard_map/ppermute | solution.py:82
  39.6 3.3 convolution_convert_fusion
  50.5 7.1 %shard_map.195 = (bf16[2,128,1280]{2,1,0:T(8,128)(2,1)S(1)}, f32[2,128,1280]{2,1,0:T(8,128)S(1)}, f32[2,128,1280]{2,1,0:T(8,128)S(1)}, f32[2,128,1280]{2,1,0:T(8...) custom-call(f32[2,2]{1,0:T(2,128)S(1)} %pad_maximum_fusion.16.flags_ref, bf16[2,128,1280]{2,1,0:T(8,128)(2,1)S(1)} %bitcast.118, ...), custom_call_target="tpu_custom_call" | custom-call | flops 1 | bytes 1 | tf_op jit(solution)/shard_map/pallas_call | solution.py:266
  61.1 4.9 collective-permute-done.10
  73.1 3.7 fusion.76
  79.0 4.0 collective-permute-start.15
  84.8 3.4 shard_map.196
  88.2 5.3 collective-permute-done.18
  110.9 12.7 %shard_map.197.refs_4_ = f32[512,1920]{1,0:T(8,128)} custom-call(bf16[128,2560]{1,0:T(8,128)(2,1)} %bitcast.141, bf16[128,2560]{1,0:T(8,128)(2,1)} %collective-permute-done.13.refs_1_, bf16[128,2560]{1,0:T(8,128)(2,1)} %copy-done.97, bf16[128,2560]{1,0:T(8,128)(2,1)} %collective-permute-done.23.refs_3_, bf16[2560,1920]{1,0:T(8,128)(2,1)} %refs_23_.5), custom_call_target="tpu_custom_call" | custom-call | flops 11699999744 | bytes 26000000 | tf_op jit(solution)/shard_map/pallas_call | solution.py:299
  138.7 12.9 %shard_map.198.refs_20_ = f32[512,1920]{1,0:T(8,128)} custom-call(bf16[128,2560]{1,0:T(8,128)(2,1)} %copy-done.74, bf16[128,2560]{1,0:T(8,128)(2,1)} %collective-permute-done.21.refs_1_.refs_3_, bf16[128,2560]{1,0:T(8,128)(2,1)} %copy-done.98, bf16[128,2560]{1,0:T(8,128)(2,1)} %collective-permute-done.26.refs_3_, bf16[2560,1920]{1,0:T(8,128)(2,1)} %refs_23_.5), custom_call_target="tpu_custom_call" | custom-call | flops 11699999744 | bytes 26000000 | tf_op jit(solution)/shard_map/pallas_call | solution.py:299
  158.5 23.4 %shard_map.199 = (bf16[512,1920]{1,0:T(8,128)(2,1)}, bf16[512,1920]{1,0:T(8,128)(2,1)}, bf16[512,1920]{1,0:T(8,128)(2,1)}, f32[128,2560]{1,0:T(8,128)}, bf16[128,2560]{1,0:T(8,128)(2,1)}) custom-call(bf16[128,2560]{1,0:T(8,128)(2,1)} %multiply_convert_fusion.refs_0_, bf16[128,2560]{1,0:T(8,128)(2,1)} %collective-permute-done.28.refs_1_, ...), custom_call_target="tpu_custom_call" | custom-call | flops 20700000256 | bytes 46000000 | tf_op jit(solution)/shard_map/pallas_call | solution.py:384
  187.2 3.5 collective-permute-start.38
  191.3 18.9 %shard_map.200 = (f32[128,2560]{1,0:T(8,128)}, bf16[128,2560]{1,0:T(8,128)(2,1)}, f32[256,2560]{1,0:T(8,128)}, bf16[256,2560]{1,0:T(8,128)(2,1)}) custom-call(bf16[512,1920]{1,0:T(8,128)(2,1)} %get-tuple-element.2403.hid_ref.refs_24_, bf16[512,1920]{1,0:T(8,128)(2,1)} %get-tuple-element.2404.gg_ref.refs_25_, ...), custom_call_target="tpu_custom_call" | custom-call | flops 17100000256 | bytes 38000000 | tf_op jit(solution)/shard_map/pallas_call | solution.py:423
  223.7 3.2 shard_map.201.refs_31_
  226.9 3.2 shard_map.202.refs_27_
  230.2 3.3 collective-permute-done.46
  233.5 4.8 collective-permute-done.43
  245.9 5.4 shard_map.203
  258.3 3.3 collective-permute-start.53
  261.6 3.3 fusion.43
  272.0 8.7 %collective-permute-done.55.refs_3_.refs_17_ = bf16[128,2560]{1,0:T(8,128)(2,1)} collective-permute-done((bf16[128,2560]{1,0:T(8,128)(2,1)}, bf16[128,2560]{1,0:T(8,128)(2,1)}, u32[]{:S(2)}, u32[]{:S(2)}) %collective-permute-start.55) | collective-permute-done | bytes 655392 | tf_op jit(solution)/shard_map/ppermute | solution.py:82
  282.1 7.4 %shard_map.204 = (bf16[2,128,1280]{2,1,0:T(8,128)(2,1)S(1)}, bf16[2,128,1280]{2,1,0:T(8,128)(2,1)S(1)}, bf16[2,128,1280]{2,1,0:T(8,128)(2,1)S(1)}, f32[2,16,1280...) custom-call(f32[2,2]{1,0:T(2,128)S(1)} %pad_maximum_fusion.16.flags_ref, ...), custom_call_target="tpu_custom_call" | custom-call | flops 1 | bytes 1 | tf_op jit(solution)/shard_map/pallas_call | solution.py:266
  295.3 3.2 shard_map.206.refs_29_
  298.5 3.4 shard_map.205.refs_33_
  304.1 3.4 fusion.41
  315.7 37.3 %shard_map.207 = (f32[320,2304]{1,0:T(8,128)}, bf16[320,2304]{1,0:T(8,128)(2,1)}) custom-call(s32[3]{0:T(128)} %pad_add_fusion.1.place_ref, bf16[128,2560]{1,0:T(8,128)(2,1)} %collective-permute-done.29.refs_2_.refs_0_, bf16[128,2560]{1,0:T(8,128)(2,1)} %collective-permute-done.33.refs_3_.refs_1_, bf16[128,2560]{1,0:T(8,128)(2,1)} %collective-permute-done.39.refs_2_, ...), custom_call_target="tpu_custom_call" | custom-call | flops 31499999232 | bytes 70000000 | tf_op jit(solution)/shard_map/pallas_call | solution.py:540
  358.1 4.1 shard_map.208
  365.4 3.4 shard_map.210
  374.4 5.3 shard_map.209
  380.5 6.0 %collective-permute-done.76 = bf16[4,80,512]{2,1,0:T(8,128)(2,1)S(1)} collective-permute-done((bf16[4,80,512]{2,1,0:T(8,128)(2,1)}, bf16[4,80,512]{2,1,0:T(8,128)(2,1)S(1)}, u32[]{:S(2)}, u32[]{:S(2)}) %collective-permute-start.76) | collective-permute-done | bytes 327712 | tf_op jit(solution)/shard_map/ppermute | solution.py:82
  386.5 5.6 collective-permute-done.79.refs_1_
  399.5 37.1 %shard_map.211 = (f32[320,2304]{1,0:T(8,128)}, bf16[320,2304]{1,0:T(8,128)(2,1)}) custom-call(s32[3]{0:T(128)} %pad_add_fusion.1.place_ref, bf16[128,2560]{1,0:T(8,128)(2,1)} %collective-permute-done.29.refs_2_.refs_0_, bf16[128,2560]{1,0:T(8,128)(2,1)} %collective-permute-done.33.refs_3_.refs_1_, bf16[128,2560]{1,0:T(8,128)(2,1)} %collective-permute-done.39.refs_2_, ...), custom_call_target="tpu_custom_call" | custom-call | flops 31499999232 | bytes 70000000 | tf_op jit(solution)/shard_map/pallas_call | solution.py:540
  446.5 5.2 shard_map.212
  452.6 5.2 shard_map.213
  458.0 11.7 %collective-permute-done.89.refs_3_ = bf16[320,2304]{1,0:T(8,128)(2,1)} collective-permute-done((bf16[320,2304]{1,0:T(8,128)(2,1)}, bf16[320,2304]{1,0:T(8,128)(2,1)}, u32[]{:S(2)}, u32[]{:S(2)}) %collective-permute-start.89) | collective-permute-done | bytes 1474592 | tf_op jit(solution)/shard_map/ppermute | solution.py:82
  476.2 24.2 %shard_map.214 = (f32[320,1152]{1,0:T(8,128)}, bf16[320,1152]{1,0:T(8,128)(2,1)}) custom-call(s32[3]{0:T(128)} %pad_add_fusion.1.place_ref, bf16[128,2560]{1,0:T(8,128)(2,1)} %collective-permute-done.29.refs_2_.refs_0_, bf16[128,2560]{1,0:T(8,128)(2,1)} %collective-permute-done.33.refs_3_.refs_1_, bf16[128,2560]{1,0:T(8,128)(2,1)} %collective-permute-done.39.refs_2_, ...), custom_call_target="tpu_custom_call" | custom-call | flops 15299999744 | bytes 34000000 | tf_op jit(solution)/shard_map/pallas_call | solution.py:540
  500.4 7.1 %collective-permute-done.95 = f32[10,2560]{1,0:T(8,128)} collective-permute-done((f32[10,2560]{1,0:T(8,128)S(1)}, f32[10,2560]{1,0:T(8,128)}, u32[]{:S(2)}, u32[]{:S(2)}) %collective-permute-start.95) | collective-permute-done | bytes 102432 | tf_op jit(solution)/shard_map/ppermute | solution.py:82
  509.6 5.6 collective-permute-start.96
  515.2 3.4 collective-permute-start.100
  519.3 6.2 %shard_map.215 = (f32[320,1920]{1,0:T(8,128)}, f32[320,1920]{1,0:T(8,128)}, f32[320,1920]{1,0:T(8,128)}) custom-call(f32[320,2304]{1,0:T(8,128)} %get-tuple-element.2460.refs_0_, bf16[320,2304]{1,0:T(8,128)(2,1)} %collective-permute-done.79.refs_1_, f32[320,2304]{1,0:T(8,128)} %get-tuple-element.2462.refs_2_, bf16[320,2304]{1,0:T(8,128)(2,1)} %collective-permute-done.89.refs_3_), custom_call_target="tpu_custom_call" | custom-call | flops 9000000512 | bytes 20000000 | tf_op jit(solution)/shard_map/pallas_call | solution.py:628
  525.5 8.8 %collective-permute-done.96 = bf16[160,1280]{1,0:T(8,128)(2,1)S(1)} collective-permute-done((bf16[160,1280]{1,0:T(8,128)(2,1)S(1)}, bf16[160,1280]{1,0:T(8,128)(2,1)S(1)}, u32[]{:S(2)}, u32[]{:S(2)}) %collective-permute-start.96) | collective-permute-done | bytes 409632 | tf_op jit(solution)/shard_map/ppermute | solution.py:82
  541.6 5.0 collective-permute-done.99
  550.1 7.5 %collective-permute-done.101.refs_4_ = bf16[320,1152]{1,0:T(8,128)(2,1)} collective-permute-done((bf16[320,1152]{1,0:T(8,128)(2,1)}, bf16[320,1152]{1,0:T(8,128)(2,1)}, u32[]{:S(2)}, u32[]{:S(2)}) %collective-permute-start.101) | collective-permute-done | bytes 737312 | tf_op jit(solution)/shard_map/ppermute | solution.py:82
  557.6 3.7 collective-permute-start.102
  565.6 3.8 shard_map.216
  569.4 3.3 collective-permute-done.103
  (536 shorter events, 197.7 us)
Async XLA Ops:
  7.0 17.0 %collective-permute-start.5 = (bf16[1280,128]{1,0:T(8,128)(2,1)}, bf16[1280,128]{1,0:T(8,128)(2,1)}, u32[]{:S(2)}, u32[]{:S(2)}) collective-permute-start(bf16[1280,128]{1,0:T(8,128)(2,1)} %constant_dynamic-slice_fusion.5), channel_id=1, source_target_pairs={{0,2},{1,3},{2,0},{3,1},{4,6},{5,7},{6,4},{7,5},{8,10},{9,11},{10,... | collective-permute-start | bytes 983048 | tf_op jit(solution)/shard_map/ppermute | solution.py:82
  20.9 17.1 %collective-permute-start.6 = (bf16[128,2560]{1,0:T(8,128)(2,1)S(1)}, bf16[128,2560]{1,0:T(8,128)(2,1)S(1)}, u32[]{:S(2)}, u32[]{:S(2)}) collective-permute-start(bf16[128,2560]{1,0:T(8,128)(2,1)S(1)} %copy-done.23), channel_id=1, source_target_pairs={{0,2},{1,3},{2,0},{3,1},{4,6},{5,7},{6,4},{7,5},{8,10},{9,11},{10,... | collective-permute-start | bytes 1966088 | tf_op jit(solution)/shard_map/ppermute | solution.py:82
  38.1 27.9 %collective-permute-start.11 = (bf16[2560,640]{1,0:T(8,128)(2,1)S(1)}, bf16[2560,640]{1,0:T(8,128)(2,1)S(1)}, u32[]{:S(2)}, u32[]{:S(2)}) collective-permute-start(bf16[2560,640]{1,0:T(8,128)(2,1)S(1)} %copy-done.46), channel_id=1, source_target_pairs={{0,1},{1,0},{2,3},{3,2},{4,5},{5,4},{6,7},{7,6},{8,9},{9,8},{10,11... | collective-permute-start | bytes 9830408 | tf_op jit(solution)/shard_map/ppermute | solution.py:82
  44.0 17.1 %collective-permute-start.8 = (bf16[128,2560]{1,0:T(8,128)(2,1)S(1)}, bf16[128,2560]{1,0:T(8,128)(2,1)S(1)}, u32[]{:S(2)}, u32[]{:S(2)}) collective-permute-start(bf16[128,2560]{1,0:T(8,128)(2,1)S(1)} %bitcast.143), channel_id=1, source_target_pairs={{0,4},{1,5},{2,6},{3,7},{4,0},{5,1},{6,2},{7,3},{8,12},{9,13},{10,... | collective-permute-start | bytes 1966088 | tf_op jit(solution)/shard_map/ppermute | solution.py:82
  45.7 20.3 %collective-permute-start.10 = (bf16[640,640]{1,0:T(8,128)(2,1)}, bf16[640,640]{1,0:T(8,128)(2,1)S(1)}, u32[]{:S(2)}, u32[]{:S(2)}) collective-permute-start(bf16[640,640]{1,0:T(8,128)(2,1)} %constant_dynamic-slice_fusion.3), channel_id=1, source_target_pairs={{0,2},{1,3},{2,0},{3,1},{4,6},{5,7},{6,4},{7,5},{8,10},{9,11},{10,... | collective-permute-start | bytes 2457608 | tf_op jit(solution)/shard_map/ppermute | solution.py:82
  71.9 25.7 %collective-permute-start.13 = (bf16[128,2560]{1,0:T(8,128)(2,1)}, bf16[128,2560]{1,0:T(8,128)(2,1)}, u32[]{:S(2)}, u32[]{:S(2)}) collective-permute-start(bf16[128,2560]{1,0:T(8,128)(2,1)} %bitcast.140), channel_id=1, source_target_pairs={{0,2},{1,3},{2,0},{3,1},{4,6},{5,7},{6,4},{7,5},{8,10},{9,11},{10,... | collective-permute-start | bytes 1966088 | tf_op jit(solution)/shard_map/ppermute | solution.py:82
  72.5 23.3 %collective-permute-start.17 = (bf16[1280,640]{1,0:T(8,128)(2,1)}, bf16[1280,640]{1,0:T(8,128)(2,1)}, u32[]{:S(2)}, u32[]{:S(2)}) collective-permute-start(bf16[1280,640]{1,0:T(8,128)(2,1)} %constant_dynamic-slice_fusion.2), channel_id=1, source_target_pairs={{0,1},{1,0},{2,3},{3,2},{4,5},{5,4},{6,7},{7,6},{8,9},{9,8},{10,11... | collective-permute-start | bytes 4915208 | tf_op jit(solution)/shard_map/ppermute | solution.py:82
  72.5 21.0 %collective-permute-start.18 = (bf16[640,640]{1,0:T(8,128)(2,1)}, bf16[640,640]{1,0:T(8,128)(2,1)}, u32[]{:S(2)}, u32[]{:S(2)}) collective-permute-start(bf16[640,640]{1,0:T(8,128)(2,1)} %copy-done.66), channel_id=1, source_target_pairs={{0,4},{1,5},{2,6},{3,7},{4,0},{5,1},{6,2},{7,3},{8,12},{9,13},{10,... | collective-permute-start | bytes 2457608 | tf_op jit(solution)/shard_map/ppermute | solution.py:82
  108.0 17.5 %collective-permute-start.21 = (bf16[128,2560]{1,0:T(8,128)(2,1)}, bf16[128,2560]{1,0:T(8,128)(2,1)}, u32[]{:S(2)}, u32[]{:S(2)}) collective-permute-start(bf16[128,2560]{1,0:T(8,128)(2,1)} %collective-permute-done.13.refs_1_), channel_id=1, source_target_pairs={{0,4},{1,5},{2,6},{3,7},{4,0},{5,1},{6,2},{7,3},{8,12},{9,13},{10,... | collective-permute-start | bytes 1966088 | tf_op jit(solution)/shard_map/ppermute | solution.py:82
  108.6 17.2 %collective-permute-start.24 = (bf16[128,2560]{1,0:T(8,128)(2,1)}, bf16[128,2560]{1,0:T(8,128)(2,1)}, u32[]{:S(2)}, u32[]{:S(2)}) collective-permute-start(bf16[128,2560]{1,0:T(8,128)(2,1)} %fusion.22), channel_id=1, source_target_pairs={{0,2},{1,3},{2,0},{3,1},{4,6},{5,7},{6,4},{7,5},{8,10},{9,11},{10,... | collective-permute-start | bytes 1966088 | tf_op jit(solution)/shard_map/ppermute | solution.py:82
  130.7 21.0 %collective-permute-start.27 = (bf16[128,2560]{1,0:T(8,128)(2,1)}, bf16[128,2560]{1,0:T(8,128)(2,1)}, u32[]{:S(2)}, u32[]{:S(2)}) collective-permute-start(bf16[128,2560]{1,0:T(8,128)(2,1)} %multiply_convert_fusion.refs_0_), channel_id=1, source_target_pairs={{0,1},{1,0},{2,3},{3,2},{4,5},{5,4},{6,7},{7,6},{8,9},{9,8},{10,11... | collective-permute-start | bytes 1966088 | tf_op jit(solution)/shard_map/ppermute | solution.py:82
  130.7 21.0 %collective-permute-start.28 = (bf16[128,2560]{1,0:T(8,128)(2,1)}, bf16[128,2560]{1,0:T(8,128)(2,1)}, u32[]{:S(2)}, u32[]{:S(2)}) collective-permute-start(bf16[128,2560]{1,0:T(8,128)(2,1)} %multiply_convert_fusion.refs_0_), channel_id=1, source_target_pairs={{0,2},{1,3},{2,0},{3,1},{4,6},{5,7},{6,4},{7,5},{8,10},{9,11},{10,... | collective-permute-start | bytes 1966088 | tf_op jit(solution)/shard_map/ppermute | solution.py:82
  132.2 19.5 %collective-permute-start.29 = (bf16[128,2560]{1,0:T(8,128)(2,1)}, bf16[128,2560]{1,0:T(8,128)(2,1)}, u32[]{:S(2)}, u32[]{:S(2)}) collective-permute-start(bf16[128,2560]{1,0:T(8,128)(2,1)} %multiply_convert_fusion.refs_0_), channel_id=1, source_target_pairs={{0,4},{1,5},{2,6},{3,7},{4,0},{5,1},{6,2},{7,3},{8,12},{9,13},{10,... | collective-permute-start | bytes 1966088 | tf_op jit(solution)/shard_map/ppermute | solution.py:82
  156.0 26.0 %collective-permute-start.32 = (bf16[128,2560]{1,0:T(8,128)(2,1)}, bf16[128,2560]{1,0:T(8,128)(2,1)}, u32[]{:S(2)}, u32[]{:S(2)}) collective-permute-start(bf16[128,2560]{1,0:T(8,128)(2,1)} %pad_maximum_fusion.4.refs_0_.refs_12_), channel_id=1, source_target_pairs={{0,2},{1,3},{2,0},{3,1},{4,6},{5,7},{6,4},{7,5},{8,10},{9,11},{10,... | collective-permute-start | bytes 1966088 | tf_op jit(solution)/shard_map/ppermute | solution.py:82
  156.5 25.4 %collective-permute-start.33 = (bf16[128,2560]{1,0:T(8,128)(2,1)}, bf16[128,2560]{1,0:T(8,128)(2,1)}, u32[]{:S(2)}, u32[]{:S(2)}) collective-permute-start(bf16[128,2560]{1,0:T(8,128)(2,1)} %collective-permute-done.28.refs_1_), channel_id=1, source_target_pairs={{0,4},{1,5},{2,6},{3,7},{4,0},{5,1},{6,2},{7,3},{8,12},{9,13},{10,... | collective-permute-start | bytes 1966088 | tf_op jit(solution)/shard_map/ppermute | solution.py:82
  158.2 23.7 %collective-permute-start.34 = (bf16[64,2560]{1,0:T(8,128)(2,1)}, bf16[64,2560]{1,0:T(8,128)(2,1)}, u32[]{:S(2)}, u32[]{:S(2)}) collective-permute-start(bf16[64,2560]{1,0:T(8,128)(2,1)} %slice.262), channel_id=1, source_target_pairs={{0,24},{1,25},{2,26},{3,27},{4,28},{5,29},{6,30},{7,31},{8,16},{9,... | collective-permute-start | bytes 983048 | tf_op jit(solution)/shard_map/ppermute | solution.py:82
  185.7 24.6 %collective-permute-start.36 = (bf16[128,2560]{1,0:T(8,128)(2,1)}, bf16[128,2560]{1,0:T(8,128)(2,1)}, u32[]{:S(2)}, u32[]{:S(2)}) collective-permute-start(bf16[128,2560]{1,0:T(8,128)(2,1)} %add_convert_fusion.1), channel_id=1, source_target_pairs={{0,2},{1,3},{2,0},{3,1},{4,6},{5,7},{6,4},{7,5},{8,10},{9,11},{10,... | collective-permute-start | bytes 1966088 | tf_op jit(solution)/shard_map/ppermute | solution.py:82
  187.2 23.1 %collective-permute-start.37 = (bf16[128,2560]{1,0:T(8,128)(2,1)}, bf16[128,2560]{1,0:T(8,128)(2,1)}, u32[]{:S(2)}, u32[]{:S(2)}) collective-permute-start(bf16[128,2560]{1,0:T(8,128)(2,1)} %collective-permute-done.33.refs_3_.refs_1_), channel_id=1, source_target_pairs={{0,1},{1,0},{2,3},{3,2},{4,5},{5,4},{6,7},{7,6},{8,9},{9,8},{10,11... | collective-permute-start | bytes 1966088 | tf_op jit(solution)/shard_map/ppermute | solution.py:82
  187.2 23.1 %collective-permute-start.38 = (bf16[64,2560]{1,0:T(8,128)(2,1)S(1)}, bf16[64,2560]{1,0:T(8,128)(2,1)}, u32[]{:S(2)}, u32[]{:S(2)}) collective-permute-start(bf16[64,2560]{1,0:T(8,128)(2,1)S(1)} %get-tuple-element.1663), channel_id=1, source_target_pairs={{0,24},{1,25},{2,26},{3,27},{4,28},{5,29},{6,30},{7,31},{8,16},{9,... | collective-permute-start | bytes 983048 | tf_op jit(solution)/shard_map/ppermute | solution.py:82
  190.7 19.6 %collective-permute-start.39 = (bf16[128,2560]{1,0:T(8,128)(2,1)}, bf16[128,2560]{1,0:T(8,128)(2,1)}, u32[]{:S(2)}, u32[]{:S(2)}) collective-permute-start(bf16[128,2560]{1,0:T(8,128)(2,1)} %collective-permute-done.29.refs_2_.refs_0_), channel_id=1, source_target_pairs={{0,1},{1,0},{2,3},{3,2},{4,5},{5,4},{6,7},{7,6},{8,9},{9,8},{10,11... | collective-permute-start | bytes 1966088 | tf_op jit(solution)/shard_map/ppermute | solution.py:82
  191.0 19.3 %collective-permute-start.40 = (bf16[128,2560]{1,0:T(8,128)(2,1)}, bf16[128,2560]{1,0:T(8,128)(2,1)}, u32[]{:S(2)}, u32[]{:S(2)}) collective-permute-start(bf16[128,2560]{1,0:T(8,128)(2,1)} %pad_maximum_fusion.5.refs_0_.refs_4_), channel_id=1, source_target_pairs={{0,4},{1,5},{2,6},{3,7},{4,0},{5,1},{6,2},{7,3},{8,12},{9,13},{10,... | collective-permute-start | bytes 1966088 | tf_op jit(solution)/shard_map/ppermute | solution.py:82
  219.3 19.0 %collective-permute-start.44 = (bf16[128,2560]{1,0:T(8,128)(2,1)}, bf16[128,2560]{1,0:T(8,128)(2,1)S(1)}, u32[]{:S(2)}, u32[]{:S(2)}) collective-permute-start(bf16[128,2560]{1,0:T(8,128)(2,1)} %pad_maximum_fusion.4.refs_0_.refs_12_), channel_id=1, source_target_pairs={{0,4},{1,5},{2,6},{3,7},{4,0},{5,1},{6,2},{7,3},{8,12},{9,13},{10,... | collective-permute-start | bytes 1966088 | tf_op jit(solution)/shard_map/ppermute | solution.py:82
  221.0 17.3 %collective-permute-start.45 = (bf16[128,2560]{1,0:T(8,128)(2,1)}, bf16[128,2560]{1,0:T(8,128)(2,1)}, u32[]{:S(2)}, u32[]{:S(2)}) collective-permute-start(bf16[128,2560]{1,0:T(8,128)(2,1)} %pad_maximum_fusion.4.refs_0_.refs_12_), channel_id=1, source_target_pairs={{0,1},{1,0},{2,3},{3,2},{4,5},{5,4},{6,7},{7,6},{8,9},{9,8},{10,11... | collective-permute-start | bytes 1966088 | tf_op jit(solution)/shard_map/ppermute | solution.py:82
  221.0 17.3 %collective-permute-start.43 = (bf16[128,2560]{1,0:T(8,128)(2,1)S(1)}, bf16[128,2560]{1,0:T(8,128)(2,1)}, u32[]{:S(2)}, u32[]{:S(2)}) collective-permute-start(bf16[128,2560]{1,0:T(8,128)(2,1)S(1)} %maximum_select_fusion.8), channel_id=1, source_target_pairs={{0,2},{1,3},{2,0},{3,1},{4,6},{5,7},{6,4},{7,5},{8,10},{9,11},{10,... | collective-permute-start | bytes 1966088 | tf_op jit(solution)/shard_map/ppermute | solution.py:82
  221.8 16.4 %collective-permute-start.47 = (bf16[128,2560]{1,0:T(8,128)(2,1)}, bf16[128,2560]{1,0:T(8,128)(2,1)}, u32[]{:S(2)}, u32[]{:S(2)}) collective-permute-start(bf16[128,2560]{1,0:T(8,128)(2,1)} %pad_maximum_fusion.5.refs_0_.refs_4_), channel_id=1, source_target_pairs={{0,1},{1,0},{2,3},{3,2},{4,5},{5,4},{6,7},{7,6},{8,9},{9,8},{10,11... | collective-permute-start | bytes 1966088 | tf_op jit(solution)/shard_map/ppermute | solution.py:82
  254.9 17.1 %collective-permute-start.57 = (bf16[128,2560]{1,0:T(8,128)(2,1)}, bf16[128,2560]{1,0:T(8,128)(2,1)}, u32[]{:S(2)}, u32[]{:S(2)}) collective-permute-start(bf16[128,2560]{1,0:T(8,128)(2,1)} %collective-permute-done.40.refs_2_.refs_8_), channel_id=1, source_target_pairs={{0,2},{1,3},{2,0},{3,1},{4,6},{5,7},{6,4},{7,5},{8,10},{9,11},{10,... | collective-permute-start | bytes 1966088 | tf_op jit(solution)/shard_map/ppermute | solution.py:82
  312.8 40.2 %collective-permute-start.69 = (bf16[256,1280]{1,0:T(8,128)(2,1)S(1)}, bf16[256,1280]{1,0:T(8,128)(2,1)}, u32[]{:S(2)}, u32[]{:S(2)}) collective-permute-start(bf16[256,1280]{1,0:T(8,128)(2,1)S(1)} %bitcast.124), channel_id=1, source_target_pairs={{0,1},{1,0},{2,3},{3,2},{4,5},{5,4},{6,7},{7,6},{8,9},{9,8},{10,11... | collective-permute-start | bytes 1966088 | tf_op jit(solution)/shard_map/ppermute | solution.py:82
  312.9 40.2 %collective-permute-start.70 = (bf16[256,1280]{1,0:T(8,128)(2,1)S(1)}, bf16[256,1280]{1,0:T(8,128)(2,1)}, u32[]{:S(2)}, u32[]{:S(2)}) collective-permute-start(bf16[256,1280]{1,0:T(8,128)(2,1)S(1)} %bitcast.125), channel_id=1, source_target_pairs={{0,4},{1,5},{2,6},{3,7},{4,0},{5,1},{6,2},{7,3},{8,12},{9,13},{10,... | collective-permute-start | bytes 1966088 | tf_op jit(solution)/shard_map/ppermute | solution.py:82
  314.2 38.8 %collective-permute-start.68 = (bf16[128,2560]{1,0:T(8,128)(2,1)}, bf16[128,2560]{1,0:T(8,128)(2,1)S(1)}, u32[]{:S(2)}, u32[]{:S(2)}) collective-permute-start(bf16[128,2560]{1,0:T(8,128)(2,1)} %slice.391), channel_id=1, source_target_pairs={{0,2},{1,3},{2,0},{3,1},{4,6},{5,7},{6,4},{7,5},{8,10},{9,11},{10,... | collective-permute-start | bytes 1966088 | tf_op jit(solution)/shard_map/ppermute | solution.py:82
  357.3 34.9 %collective-permute-start.79 = (bf16[320,2304]{1,0:T(8,128)(2,1)}, bf16[320,2304]{1,0:T(8,128)(2,1)}, u32[]{:S(2)}, u32[]{:S(2)}) collective-permute-start(bf16[320,2304]{1,0:T(8,128)(2,1)} %get-tuple-element.2296), channel_id=1, source_target_pairs={{0,8},{1,9},{2,10},{3,11},{4,12},{5,13},{6,14},{7,15},{8,0},{9,1},... | collective-permute-start | bytes 4423688 | tf_op jit(solution)/shard_map/ppermute | solution.py:82
  362.1 17.6 %collective-permute-start.73 = (bf16[256,1280]{1,0:T(8,128)(2,1)}, bf16[256,1280]{1,0:T(8,128)(2,1)}, u32[]{:S(2)}, u32[]{:S(2)}) collective-permute-start(bf16[256,1280]{1,0:T(8,128)(2,1)} %pad_maximum_fusion.8.refs_4_), channel_id=1, source_target_pairs={{0,1},{1,0},{2,3},{3,2},{4,5},{5,4},{6,7},{7,6},{8,9},{9,8},{10,11... | collective-permute-start | bytes 1966088 | tf_op jit(solution)/shard_map/ppermute | solution.py:82
  362.6 17.9 %collective-permute-start.74 = (bf16[256,1280]{1,0:T(8,128)(2,1)}, bf16[256,1280]{1,0:T(8,128)(2,1)}, u32[]{:S(2)}, u32[]{:S(2)}) collective-permute-start(bf16[256,1280]{1,0:T(8,128)(2,1)} %pad_maximum_fusion.8.refs_4_), channel_id=1, source_target_pairs={{0,4},{1,5},{2,6},{3,7},{4,0},{5,1},{6,2},{7,3},{8,12},{9,13},{10,... | collective-permute-start | bytes 1966088 | tf_op jit(solution)/shard_map/ppermute | solution.py:82
  392.1 44.5 %collective-permute-start.81 = (bf16[256,1280]{1,0:T(8,128)(2,1)S(1)}, bf16[256,1280]{1,0:T(8,128)(2,1)}, u32[]{:S(2)}, u32[]{:S(2)}) collective-permute-start(bf16[256,1280]{1,0:T(8,128)(2,1)S(1)} %bitcast.138), channel_id=1, source_target_pairs={{0,4},{1,5},{2,6},{3,7},{4,0},{5,1},{6,2},{7,3},{8,12},{9,13},{10,... | collective-permute-start | bytes 1966088 | tf_op jit(solution)/shard_map/ppermute | solution.py:82
  393.9 42.7 %collective-permute-start.82 = (bf16[160,1280]{1,0:T(8,128)(2,1)}, bf16[160,1280]{1,0:T(8,128)(2,1)S(1)}, u32[]{:S(2)}, u32[]{:S(2)}) collective-permute-start(bf16[160,1280]{1,0:T(8,128)(2,1)} %get-tuple-element.2509), channel_id=1, source_target_pairs={{0,8},{1,9},{2,10},{3,11},{4,12},{5,13},{6,14},{7,15},{8,16},{9,17... | collective-permute-start | bytes 1228808 | tf_op jit(solution)/shard_map/ppermute | solution.py:82
  395.2 41.4 %collective-permute-start.83 = (bf16[160,1280]{1,0:T(8,128)(2,1)}, bf16[160,1280]{1,0:T(8,128)(2,1)}, u32[]{:S(2)}, u32[]{:S(2)}) collective-permute-start(bf16[160,1280]{1,0:T(8,128)(2,1)} %get-tuple-element.2508), channel_id=1, source_target_pairs={{0,16},{1,17},{2,18},{3,19},{4,20},{5,21},{6,22},{7,23},{8,24},{9,... | collective-permute-start | bytes 1228808 | tf_op jit(solution)/shard_map/ppermute | solution.py:82
  396.2 40.5 %collective-permute-start.84 = (bf16[160,1280]{1,0:T(8,128)(2,1)}, bf16[160,1280]{1,0:T(8,128)(2,1)}, u32[]{:S(2)}, u32[]{:S(2)}) collective-permute-start(bf16[160,1280]{1,0:T(8,128)(2,1)} %get-tuple-element.2507), channel_id=1, source_target_pairs={{0,24},{1,25},{2,26},{3,27},{4,28},{5,29},{6,30},{7,31},{8,0},{9,1... | collective-permute-start | bytes 1228808 | tf_op jit(solution)/shard_map/ppermute | solution.py:82
  398.4 38.3 %collective-permute-start.85 = (bf16[1280,256]{1,0:T(8,128)(2,1)}, bf16[1280,256]{1,0:T(8,128)(2,1)S(1)}, u32[]{:S(2)}, u32[]{:S(2)}) collective-permute-start(bf16[1280,256]{1,0:T(8,128)(2,1)} %get-tuple-element.2327), channel_id=1, source_target_pairs={{0,4},{1,5},{2,6},{3,7},{4,0},{5,1},{6,2},{7,3},{8,12},{9,13},{10,... | collective-permute-start | bytes 1966088 | tf_op jit(solution)/shard_map/ppermute | solution.py:82
  436.7 33.0 %collective-permute-start.89 = (bf16[320,2304]{1,0:T(8,128)(2,1)}, bf16[320,2304]{1,0:T(8,128)(2,1)}, u32[]{:S(2)}, u32[]{:S(2)}) collective-permute-start(bf16[320,2304]{1,0:T(8,128)(2,1)} %get-tuple-element.2401), channel_id=1, source_target_pairs={{0,8},{1,9},{2,10},{3,11},{4,12},{5,13},{6,14},{7,15},{8,0},{9,1},... | collective-permute-start | bytes 4423688 | tf_op jit(solution)/shard_map/ppermute | solution.py:82
  470.8 37.7 %collective-permute-start.91 = (bf16[192,1280]{1,0:T(8,128)(2,1)}, bf16[192,1280]{1,0:T(8,128)(2,1)}, u32[]{:S(2)}, u32[]{:S(2)}) collective-permute-start(bf16[192,1280]{1,0:T(8,128)(2,1)} %get-tuple-element.2502), channel_id=1, source_target_pairs={{0,8},{1,9},{2,10},{3,11},{4,12},{5,13},{6,14},{7,15},{8,16},{9,17... | collective-permute-start | bytes 1474568 | tf_op jit(solution)/shard_map/ppermute | solution.py:82
  471.4 37.1 %collective-permute-start.92 = (bf16[192,1280]{1,0:T(8,128)(2,1)}, bf16[192,1280]{1,0:T(8,128)(2,1)}, u32[]{:S(2)}, u32[]{:S(2)}) collective-permute-start(bf16[192,1280]{1,0:T(8,128)(2,1)} %get-tuple-element.2501), channel_id=1, source_target_pairs={{0,16},{1,17},{2,18},{3,19},{4,20},{5,21},{6,22},{7,23},{8,24},{9,... | collective-permute-start | bytes 1474568 | tf_op jit(solution)/shard_map/ppermute | solution.py:82
  472.9 35.7 %collective-permute-start.93 = (bf16[192,1280]{1,0:T(8,128)(2,1)}, bf16[192,1280]{1,0:T(8,128)(2,1)}, u32[]{:S(2)}, u32[]{:S(2)}) collective-permute-start(bf16[192,1280]{1,0:T(8,128)(2,1)} %get-tuple-element.2500), channel_id=1, source_target_pairs={{0,24},{1,25},{2,26},{3,27},{4,28},{5,29},{6,30},{7,31},{8,0},{9,1... | collective-permute-start | bytes 1474568 | tf_op jit(solution)/shard_map/ppermute | solution.py:82
  475.7 32.9 %collective-permute-start.94 = (bf16[128,2560]{1,0:T(8,128)(2,1)S(1)}, bf16[128,2560]{1,0:T(8,128)(2,1)}, u32[]{:S(2)}, u32[]{:S(2)}) collective-permute-start(bf16[128,2560]{1,0:T(8,128)(2,1)S(1)} %slice.390), channel_id=1, source_target_pairs={{0,2},{1,3},{2,0},{3,1},{4,6},{5,7},{6,4},{7,5},{8,10},{9,11},{10,... | collective-permute-start | bytes 1966088 | tf_op jit(solution)/shard_map/ppermute | solution.py:82
  476.2 31.3 %collective-permute-start.95 = (f32[10,2560]{1,0:T(8,128)S(1)}, f32[10,2560]{1,0:T(8,128)}, u32[]{:S(2)}, u32[]{:S(2)}) collective-permute-start(f32[10,2560]{1,0:T(8,128)S(1)} %add.374), channel_id=1, source_target_pairs={{0,8},{1,9},{2,10},{3,11},{4,12},{5,13},{6,14},{7,15},{8,0},{9,1},... | collective-permute-start | bytes 307208 | tf_op jit(solution)/shard_map/ppermute | solution.py:82
  509.6 24.8 %collective-permute-start.96 = (bf16[160,1280]{1,0:T(8,128)(2,1)S(1)}, bf16[160,1280]{1,0:T(8,128)(2,1)S(1)}, u32[]{:S(2)}, u32[]{:S(2)}) collective-permute-start(bf16[160,1280]{1,0:T(8,128)(2,1)S(1)} %get-tuple-element.2505), channel_id=1, source_target_pairs={{0,16},{1,17},{2,18},{3,19},{4,20},{5,21},{6,22},{7,23},{8,24},{9,... | collective-permute-start | bytes 1228808 | tf_op jit(solution)/shard_map/ppermute | solution.py:82
  515.2 26.5 %collective-permute-start.100 = (bf16[160,1280]{1,0:T(8,128)(2,1)}, bf16[160,1280]{1,0:T(8,128)(2,1)}, u32[]{:S(2)}, u32[]{:S(2)}) collective-permute-start(bf16[160,1280]{1,0:T(8,128)(2,1)} %get-tuple-element.2504), channel_id=1, source_target_pairs={{0,24},{1,25},{2,26},{3,27},{4,28},{5,29},{6,30},{7,31},{8,0},{9,1... | collective-permute-start | bytes 1228808 | tf_op jit(solution)/shard_map/ppermute | solution.py:82
  518.5 28.1 %collective-permute-start.99 = (bf16[160,1280]{1,0:T(8,128)(2,1)}, bf16[160,1280]{1,0:T(8,128)(2,1)}, u32[]{:S(2)}, u32[]{:S(2)}) collective-permute-start(bf16[160,1280]{1,0:T(8,128)(2,1)} %get-tuple-element.2503), channel_id=1, source_target_pairs={{0,8},{1,9},{2,10},{3,11},{4,12},{5,13},{6,14},{7,15},{8,16},{9,17... | collective-permute-start | bytes 1228808 | tf_op jit(solution)/shard_map/ppermute | solution.py:82
  518.5 39.1 %collective-permute-start.101 = (bf16[320,1152]{1,0:T(8,128)(2,1)}, bf16[320,1152]{1,0:T(8,128)(2,1)}, u32[]{:S(2)}, u32[]{:S(2)}) collective-permute-start(bf16[320,1152]{1,0:T(8,128)(2,1)} %get-tuple-element.2470), channel_id=1, source_target_pairs={{0,8},{1,9},{2,10},{3,11},{4,12},{5,13},{6,14},{7,15},{8,0},{9,1},... | collective-permute-start | bytes 2211848 | tf_op jit(solution)/shard_map/ppermute | solution.py:82
  557.6 16.6 %collective-permute-start.102 = (f32[10,2560]{1,0:T(8,128)S(1)}, f32[10,2560]{1,0:T(8,128)S(1)}, u32[]{:S(2)}, u32[]{:S(2)}) collective-permute-start(f32[10,2560]{1,0:T(8,128)S(1)} %add.375), channel_id=1, source_target_pairs={{0,16},{1,17},{2,18},{3,19},{4,20},{5,21},{6,22},{7,23},{8,24},{9,... | collective-permute-start | bytes 307208 | tf_op jit(solution)/shard_map/ppermute | solution.py:82
  (157 other events, 1438.7 us)
